TPU v7x, 32 devices: a whole 2x2x4 slice. The times are simulated.
32 devices in a mesh: seq: 32 (over z, y, x, core), head: 1.
Axes of the slice: x: 2, y: 2, z: 4, core: 2. Of those that a mesh axis runs over, the one named last changes fastest.
Arguments:
- queries: bfloat16 [2048, 1536], P('seq', 'head'), may hold values from -6 to 6
- key_vectors: bfloat16 [2048, 512], P('seq', 'head'), may hold values from -6 to 6
- value_vectors: bfloat16 [2048, 512], P('seq', 'head'), may hold values from -6 to 6
- lengths: int32 [16], replicated, may hold values from 1 to 256, 2048 in all
- out_weight: bfloat16 [1536, 1536], P('head', 'seq'), may hold values from -0.15625 to 0.15625
- residual: bfloat16 [2048, 1536], P(('seq', 'head')), may hold values from -6 to 6
- norm_gain: float32 [1536], replicated, may hold values from 0.1 to 1.9
- route_ids: int32 [2048, 6], P(('seq', 'head')), may hold values from 0 to 63, all different within a row; in each aligned block of 64 rows (0 to 63, 64 to 127, ...) at most 6 rows name the same one
- route_logits: float32 [2048, 6], P(('seq', 'head')), may hold values from -8 to 340
- shared_gate_up: bfloat16 [1536, 2, 1024], P(None, None, ('seq', 'head')), may hold values from -0.15625 to 0.15625
- shared_down: bfloat16 [1024, 1536], P(('seq', 'head')), may hold values from -0.1875 to 0.1875
- expert_gate_up: bfloat16 [128, 1536, 2, 256], P('seq'), may hold values from -0.15625 to 0.15625
- expert_down: bfloat16 [128, 256, 1536], P('seq'), may hold values from -0.25 to 0.25
- cache_blocks: bfloat16 [32, 128, 8, 4, 128], P('seq', None, None, 'head'), may hold values from -6 to 6
- block_table: int32 [32], replicated, may hold values from 0 to 31, each once
Outputs:
- layer_out: bfloat16 [2048, 1536], P(('seq', 'head'))
- cache_out: bfloat16 [32, 128, 8, 4, 128], P(None, 'seq', None, 'head')
Inputs may be any that keep to these rules, and one draw needn't show every extreme that they name: The lengths sum to 2048. `route_ids`: each token names 6 different experts; among the tokens of one device no expert is named more than 6 times. `block_table`: every block appears once.
All inputs are finite; a program needn't handle non-finite values.
Results may differ from a plain program's by a relative error of at most 0.0095.
Values may be sent and summed in bfloat16 or wider, within the bound.
No kernel may reach another device: no remote copies, remote signals or barrier semaphores. Data moves between devices by JAX's collectives and lax.ppermute only.
A program may use at most 64 MiB of HBM per device.

v0:
```python
import math

import jax
import jax.numpy as jnp
from jax import lax
from jax.experimental import pallas as pl
from jax.experimental.pallas import tpu as pltpu
from jax.sharding import PartitionSpec as P

HD = 128
EXPERTS = 64
TOP = 6
REACH = 4
HALVES = 128
CAP = 6
Z_SIZE = 4
PLANE = 8
MIB = 1024 * 1024


NEGATIVE = -1e30
EPSILON = 1e-05


def from_behind(shard, axis, by):
    devices = lax.axis_size(axis)
    pairs = [(i, i + by) for i in range(devices) if 0 <= i + by < devices]
    return lax.ppermute(shard, axis, pairs)


def segment_of(positions, lengths):
    request_ends = jnp.cumsum(lengths)
    passed = (request_ends[None, :] <= positions[:, None]).astype(jnp.int32)
    return jnp.sum(passed, axis=1)


def shared_ffn(rows_in, gate_up_part, down_part):
    shared_both = jnp.einsum(
        "td,dcf->tcf", rows_in, gate_up_part, preferred_element_type=jnp.float32
    )
    shared_act = (jax.nn.silu(shared_both[:, 0]) * shared_both[:, 1]).astype(jnp.bfloat16)
    return jnp.dot(shared_act, down_part, preferred_element_type=jnp.float32)


def general_shards(
    queries,
    key_vectors,
    value_vectors,
    lengths,
    out_weight,
    residual,
    norm_gain,
    route_ids,
    route_logits,
    shared_gate_up,
    shared_down,
    expert_gate_up,
    expert_down,
    cache_blocks,
    block_table,
):
    handed = lax.all_to_all(cache_blocks, "seq", split_axis=1, concat_axis=0, tiled=True)
    cache_out = jnp.take(handed, block_table, axis=0)
    tok_rows = queries.shape[0]
    seq_index = lax.axis_index("seq")
    earlier = [
        from_behind((key_vectors, value_vectors), "seq", offset) for offset in range(REACH, 0, -1)
    ]
    window_keys = jnp.concatenate([member[0] for member in earlier] + [key_vectors], axis=0)
    window_values = jnp.concatenate([member[1] for member in earlier] + [value_vectors], axis=0)
    key_count = window_keys.shape[0]
    kv_heads = key_vectors.shape[1] // HD
    query_heads = queries.shape[1] // HD
    group_size = query_heads // kv_heads
    query_pos = seq_index * tok_rows + jnp.arange(tok_rows, dtype=jnp.int32)
    key_pos = (seq_index - REACH) * tok_rows + jnp.arange(key_count, dtype=jnp.int32)
    visible = (key_pos[None, :] >= 0) & (key_pos[None, :] <= query_pos[:, None])
    visible = visible & (
        segment_of(key_pos, lengths)[None, :] == segment_of(query_pos, lengths)[:, None]
    )
    query_part = queries.reshape(tok_rows, kv_heads, group_size, HD)
    key_part = window_keys.reshape(key_count, kv_heads, HD)
    value_part = window_values.reshape(key_count, kv_heads, HD)
    scores = jnp.einsum(
        "tkgd,wkd->kgtw", query_part, key_part, preferred_element_type=jnp.float32
    ) * (1.0 / math.sqrt(HD))
    scores = jnp.where(visible[None, None], scores, NEGATIVE)
    row_max = jnp.max(scores, axis=-1, keepdims=True)
    weights = jnp.exp(scores - row_max)
    row_total = jnp.sum(weights, axis=-1)
    weighted = jnp.einsum(
        "kgtw,wkd->tkgd",
        weights.astype(jnp.bfloat16),
        value_part,
        preferred_element_type=jnp.float32,
    )
    heads = (weighted / jnp.transpose(row_total, (2, 0, 1))[..., None]).astype(jnp.bfloat16)
    heads = heads.reshape(tok_rows, query_heads * HD)
    partial_out = jnp.dot(
        heads,
        lax.all_gather(out_weight, "seq", axis=1, tiled=True),
        preferred_element_type=jnp.float32,
    )
    attn_out = lax.psum_scatter(partial_out, "head", scatter_dimension=0, tiled=True)
    mixed = residual.astype(jnp.float32) + attn_out
    mean_square = jnp.mean(mixed * mixed, axis=-1, keepdims=True)
    normed = (mixed * lax.rsqrt(mean_square + EPSILON) * norm_gain).astype(jnp.bfloat16)
    gate_up_all, down_all = (
        lax.all_gather(shared_gate_up, ("seq", "head"), axis=2, tiled=True),
        lax.all_gather(shared_down, ("seq", "head"), axis=0, tiled=True),
    )
    shared_part = shared_ffn(normed, gate_up_all, down_all)
    own_tokens = normed.shape[0]
    width_model = normed.shape[1]
    flat_ids = route_ids.reshape(-1)
    onehot = (flat_ids[:, None] == jnp.arange(EXPERTS, dtype=jnp.int32)[None, :]).astype(jnp.int32)
    slot_rank = jnp.sum((jnp.cumsum(onehot, axis=0) - 1) * onehot, axis=1)
    first_slot = flat_ids * CAP + slot_rank
    second_slot = (flat_ids + EXPERTS) * CAP + slot_rank
    token_of = jnp.arange(flat_ids.shape[0], dtype=jnp.int32) // TOP
    routed_rows = normed[token_of]
    outgoing = jnp.zeros((HALVES * CAP, width_model), jnp.bfloat16)
    outgoing = outgoing.at[jnp.concatenate([first_slot, second_slot])].set(
        jnp.concatenate([routed_rows, routed_rows], axis=0)
    )
    local_halves = expert_gate_up.shape[0]
    outgoing = outgoing.reshape(HALVES // local_halves, local_halves, CAP, width_model)
    gate_up = jnp.einsum(
        "nsjd,sdcf->nsjcf",
        lax.all_to_all(outgoing, "seq", split_axis=0, concat_axis=0, tiled=True),
        expert_gate_up,
        preferred_element_type=jnp.float32,
    )
    expert_act = (jax.nn.silu(gate_up[:, :, :, 0]) * gate_up[:, :, :, 1]).astype(jnp.bfloat16)
    half_out = jnp.einsum(
        "nsjf,sfd->nsjd", expert_act, expert_down, preferred_element_type=jnp.float32
    ).astype(jnp.bfloat16)
    returned = lax.all_to_all(half_out, "seq", split_axis=0, concat_axis=0, tiled=True)
    returned = returned.reshape(HALVES * CAP, width_model)
    pair_sum = returned[first_slot].astype(jnp.float32) + returned[second_slot].astype(jnp.float32)
    route_probs = jax.nn.softmax(route_logits, axis=-1)
    routed = jnp.sum(
        route_probs[:, :, None] * pair_sum.reshape(own_tokens, TOP, width_model), axis=1
    )
    layer_out = (mixed + shared_part + routed).astype(jnp.bfloat16)
    return (layer_out, cache_out)


VMEM = pl.BlockSpec(memory_space=pltpu.VMEM)
SMEM = pl.BlockSpec(memory_space=pltpu.SMEM)
HBM = pl.BlockSpec(memory_space=pltpu.HBM)


def dot_rows(left, right):
    return lax.dot_general(left, right, (((1,), (1,)), ((), ())), preferred_element_type=jnp.float32)


def dot(left, right):
    return jnp.dot(left, right, preferred_element_type=jnp.float32)


def silu_times(gate, up):
    return (gate / (1.0 + jnp.exp(-gate)) * up).astype(jnp.bfloat16)


def attention_kernel(
    z_ref,
    first_ref,
    lengths_ref,
    q_ref,
    k4_ref,
    k3_ref,
    k2_ref,
    k1_ref,
    own_ref,
    residual_ref,
    info_ref,
    *out_refs,
):
    tokens, width = q_ref.shape
    part = width // Z_SIZE
    kv_width = own_ref.shape[1] // 2
    kv_heads = kv_width // HD
    group = width // HD // kv_heads
    blocks = [k4_ref, k3_ref, k2_ref, k1_ref, own_ref]
    keys = len(blocks) * tokens
    first = first_ref[0]
    query_pos = first + lax.broadcasted_iota(jnp.int32, (tokens, keys), 0)
    key_pos = first - (keys - tokens) + lax.broadcasted_iota(jnp.int32, (tokens, keys), 1)
    start = jnp.zeros((tokens, keys), jnp.int32)
    end = jnp.int32(0)
    for request in range(lengths_ref.shape[0]):
        end = end + lengths_ref[request]
        start = jnp.maximum(start, jnp.where(query_pos >= end, end, 0))
    hidden = jnp.where((key_pos >= start) & (key_pos <= query_pos), 0.0, NEGATIVE)
    hidden = jnp.concatenate([hidden] * group, axis=0)
    scale = 1.0 / math.sqrt(HD)
    for step, out_ref in enumerate(out_refs):
        z = lax.rem(z_ref[0] + step, Z_SIZE)
        for column in range(Z_SIZE):

            @pl.when(z == column)
            def _(column=column, out_ref=out_ref):
                columns = slice(column * part, (column + 1) * part)
                out_ref[:, width : width + part] = residual_ref[:, columns]

        out_ref[:, width + part :] = info_ref[...]
    for kv in range(kv_heads):
        at = slice(kv * HD, (kv + 1) * HD)
        value_at = slice(kv_width + kv * HD, kv_width + (kv + 1) * HD)
        key = jnp.concatenate([block[:, at] for block in blocks], axis=0)
        value = jnp.concatenate([block[:, value_at] for block in blocks], axis=0)
        heads = [kv * group + member for member in range(group)]
        query = jnp.concatenate([q_ref[:, h * HD : (h + 1) * HD] for h in heads], axis=0)
        scores = dot_rows(query, key) * scale + hidden
        weights = jnp.exp(scores - jnp.max(scores, axis=-1, keepdims=True))
        total = jnp.sum(weights, axis=-1, keepdims=True)
        result = (dot(weights.astype(jnp.bfloat16), value) / total).astype(jnp.bfloat16)
        for member, h in enumerate(heads):
            for out_ref in out_refs:
                out_ref[:, h * HD : (h + 1) * HD] = result[member * tokens : (member + 1) * tokens]


def route_kernel(z_ref, ids_ref, logits_ref, out_ref, turned_ref):
    choices, tokens = ids_ref.shape
    turned_ref[...] = jnp.zeros(turned_ref.shape, jnp.float32)
    turned_ref[:choices, :tokens] = ids_ref[...].astype(jnp.float32)
    turned_ref[8 : 8 + choices, :tokens] = logits_ref[...]
    table = turned_ref[...].T[:tokens]
    lane = lax.broadcasted_iota(jnp.int32, table.shape, 1)
    ids = [table[:, c : c + 1].astype(jnp.int32) for c in range(choices)]
    logits = [table[:, 8 + c : 9 + c] for c in range(choices)]
    member = jnp.zeros(table.shape, jnp.float32)
    for one in ids:
        member = jnp.where(lane == one, 1.0, member)
    row = lax.broadcasted_iota(jnp.int32, (tokens, tokens), 0)
    earlier = jnp.where(lax.broadcasted_iota(jnp.int32, (tokens, tokens), 1) < row, 1.0, 0.0)
    ahead = dot(earlier.astype(jnp.bfloat16), member.astype(jnp.bfloat16))
    top = logits[0]
    for one in logits[1:]:
        top = jnp.maximum(top, one)
    powers = [jnp.exp(one - top) for one in logits]
    total = sum(powers[1:], powers[0])
    per_device = EXPERTS // 2 // PLANE
    out = jnp.zeros(table.shape, jnp.float32)
    for c, one in enumerate(ids):
        rank = jnp.sum(jnp.where(lane == one, ahead, 0.0), axis=1, keepdims=True)
        where_to = lax.div(one, per_device).astype(jnp.float32)
        first = (lax.rem(one, per_device) * Z_SIZE + z_ref[0]) * CAP
        out = jnp.where(lane == c, where_to, out)
        out = jnp.where(lane == 8 + c, first.astype(jnp.float32) + rank, out)
        out = jnp.where(lane == 16 + c, powers[c] / total, out)
    out_ref[...] = out.astype(jnp.bfloat16)


def regroup_kernel(z_ref, *refs):
    pieces, outs = refs[:PLANE], refs[PLANE:]
    for step, out in enumerate(outs):
        z = lax.rem(z_ref[0] + step, Z_SIZE)
        for at, piece in enumerate(pieces):
            out[at] = piece[z]


def source_z(z_ref, step):
    return lax.rem(z_ref[0] + Z_SIZE - step, Z_SIZE)


def project_kernel(z_ref, *refs):
    sent = refs[:Z_SIZE]
    weight_ref, mixed_ref, info_ref, rows_ref = refs[Z_SIZE:]
    for step, sent_ref in enumerate(sent):
        rows_ref[source_z(z_ref, step)] = sent_ref[...]
    rows = jnp.concatenate([rows_ref[z] for z in range(Z_SIZE)], axis=0)
    part, width = weight_ref.shape
    out = dot_rows(rows[:, :width], weight_ref[...])
    mixed_ref[...] = (out + rows[:, width : width + part].astype(jnp.float32)).astype(jnp.bfloat16)
    info_ref[...] = rows[:, width + part :]


def row_codes(info, first, parity, per_device):
    where_to = info(first).astype(jnp.int32) - PLANE * parity
    inside = info(first + 8).astype(jnp.int32)
    fits = (where_to >= 0) & (where_to < PLANE)
    return jnp.where(fits, where_to * per_device + inside, -1)


def tables_kernel(parity_ref, info_ref, onehot_ref, mix_ref):
    rows, tokens = onehot_ref.shape
    info = info_ref[...].astype(jnp.float32)
    turned = info.T
    codes = row_codes(lambda at: turned[at : at + 8], 0, parity_ref[0], rows // PLANE)
    row = lax.broadcasted_iota(jnp.int32, (rows, tokens), 0)
    chosen = codes[0:1, :] == row
    for choice in range(1, TOP):
        chosen = chosen | (codes[choice : choice + 1, :] == row)
    onehot_ref[...] = jnp.where(chosen, 1.0, 0.0).astype(jnp.bfloat16)
    column = lax.broadcasted_iota(jnp.int32, mix_ref.shape, 1)
    mix = jnp.zeros(mix_ref.shape, jnp.float32)
    for choice in range(TOP):
        code = row_codes(lambda at: info[:, at : at + 1], choice, parity_ref[0], rows // PLANE)
        mix = jnp.where(code == column, info[:, 16 + choice : 17 + choice], mix)
    mix_ref[...] = mix.astype(jnp.bfloat16)


def pick_kernel(z_ref, onehot_ref, gain_ref, *refs):
    parts = refs[:Z_SIZE]
    normed_ref, own_ref, out_hbm, mixed_ref, out_ref, sems = refs[Z_SIZE:]
    for step, part_ref in enumerate(parts):
        mixed_ref[source_z(z_ref, step)] = part_ref[...]
    columns = mixed_ref.shape[2]
    tokens = own_ref.shape[0]
    own = pl.ds(pl.multiple_of(z_ref[0] * tokens, tokens), tokens)
    for z in range(Z_SIZE):
        own_ref[:, z * columns : (z + 1) * columns] = mixed_ref[z, own, :].astype(jnp.float32)
    mixed = jnp.concatenate([mixed_ref[z] for z in range(Z_SIZE)], axis=1).astype(jnp.float32)
    mean_square = jnp.mean(mixed * mixed, axis=-1, keepdims=True)
    normed = (mixed * lax.rsqrt(mean_square + EPSILON) * gain_ref[...]).astype(jnp.bfloat16)
    normed_ref[...] = normed
    picked = out_ref.shape[1]
    copies = []
    for p in range(PLANE):
        onehot = onehot_ref[p * picked : (p + 1) * picked]
        out_ref[p] = dot(onehot, normed).astype(jnp.bfloat16)
        copy = pltpu.make_async_copy(out_ref.at[p], out_hbm.at[p], sems.at[p])
        copy.start()
        copies.append(copy)
    for copy in copies:
        copy.wait()


def shared_kernel(rows_ref, weight_ref, out_ref):
    parts, units, _ = weight_ref.shape
    units = units // 3
    gate_weight, up_weight, down_weight = [
        jnp.concatenate([weight_ref[p, at * units : (at + 1) * units] for p in range(parts)], axis=0)
        for at in range(3)
    ]
    rows = rows_ref[...]
    act = silu_times(dot_rows(rows, gate_weight), dot_rows(rows, up_weight))
    out_ref[...] = dot(act, down_weight)


def experts_kernel(
    rows_ref, gate_up_hbm, down_hbm, out_hbm, gate_up_ref, down_ref, out_ref, in_sems, out_sems
):
    halves = gate_up_ref.shape[0]
    fetches = []
    for half in range(halves):
        gate_up = pltpu.make_async_copy(
            gate_up_hbm.at[half], gate_up_ref.at[half], in_sems.at[0, half]
        )
        down = pltpu.make_async_copy(down_hbm.at[half], down_ref.at[half], in_sems.at[1, half])
        gate_up.start()
        down.start()
        fetches.append((gate_up, down))
    sources, rows, width = rows_ref.shape
    per_half = rows // halves
    copies = []
    for pair in range(halves // 2):
        both = pl.ds(2 * pair * per_half, 2 * per_half)
        arrived = rows_ref[:, both, :].astype(jnp.float32)
        results = []
        for member in range(2):
            half = 2 * pair + member
            own = arrived[:, member * per_half : (member + 1) * per_half]
            own = own.reshape(sources * per_half, width).astype(jnp.bfloat16)
            fetches[half][0].wait()
            act = silu_times(dot(own, gate_up_ref[half, 0]), dot(own, gate_up_ref[half, 1]))
            fetches[half][1].wait()
            results.append(dot(act, down_ref[half]).reshape(sources, per_half, width))
        out_ref[:, both, :] = jnp.concatenate(results, axis=1).astype(jnp.bfloat16)
        copy = pltpu.make_async_copy(out_ref.at[:, both], out_hbm.at[:, both], out_sems.at[pair])
        copy.start()
        copies.append(copy)
    for copy in copies:
        copy.wait()


def combine_kernel(z_ref, mix_ref, rows_ref, shared_ref, *refs):
    outs, sum_ref = refs[:Z_SIZE], refs[Z_SIZE]
    tokens = outs[0].shape[0]
    sum_ref[...] = dot(mix_ref[...], rows_ref[...]) + shared_ref[...]
    for step, out_ref in enumerate(outs):
        z = lax.rem(z_ref[0] + step, Z_SIZE)
        rows = pl.ds(pl.multiple_of(z * tokens, tokens), tokens)
        out_ref[...] = sum_ref[rows, :].astype(jnp.bfloat16)


def final_kernel(mixed_ref, *refs):
    total = mixed_ref[...]
    for part_ref in refs[:Z_SIZE]:
        total = total + part_ref[...].astype(jnp.float32)
    refs[Z_SIZE][...] = total.astype(jnp.bfloat16)


def reorder_kernel(me_ref, table_ref, from_ref, to_ref):
    me = me_ref[0]
    for block in range(to_ref.shape[0]):
        source = table_ref[block]
        z_steps = lax.rem(lax.div(me, PLANE) - lax.div(source, PLANE) + Z_SIZE, Z_SIZE)
        steps = lax.rem(lax.rem(me, PLANE) - lax.rem(source, PLANE) + PLANE, PLANE)
        to_ref[block] = from_ref[z_steps * PLANE + steps]


def params(mib=16):
    return pltpu.CompilerParams(vmem_limit_bytes=mib * MIB)


def cost(flops, moved):
    return pl.CostEstimate(flops=int(flops), bytes_accessed=int(moved), transcendentals=0)


def shards(
    queries,
    key_vectors,
    value_vectors,
    lengths,
    out_weight,
    residual,
    norm_gain,
    route_ids,
    route_logits,
    shared_gate_up,
    shared_down,
    expert_gate_up,
    expert_down,
    cache_blocks,
    block_table,
):
    tokens, width = residual.shape
    devices = lax.axis_size("seq")
    me = lax.axis_index("seq")
    z_index, plane_index = lax.div(me, PLANE), lax.rem(me, PLANE)
    planes = [[p + PLANE * z for p in range(PLANE)] for z in range(Z_SIZE)]
    bf16, f32 = jnp.bfloat16, jnp.float32
    shape = jax.ShapeDtypeStruct
    scalar = lambda value: jnp.reshape(value, (1,)).astype(jnp.int32)
    all_tokens = Z_SIZE * tokens
    part = width // Z_SIZE

    def exchange(array, groups):
        return lax.all_to_all(
            array, "seq", split_axis=0, concat_axis=0, tiled=True, axis_index_groups=groups
        )

    own_kv = jnp.concatenate([key_vectors, value_vectors], axis=1)
    behind = [from_behind(own_kv, "seq", offset) for offset in range(REACH, 0, -1)]

    turned_weight = lax.all_gather(
        out_weight.T, "seq", axis=0, tiled=True, axis_index_groups=planes
    )
    info = pl.pallas_call(
        route_kernel,
        out_shape=shape((tokens, 128), bf16),
        in_specs=[SMEM] + [VMEM] * 2,
        out_specs=VMEM,
        scratch_shapes=[pltpu.VMEM((128, 128), f32)],
        compiler_params=params(),
        cost_estimate=cost(MIB, MIB),
        name="route",
    )(scalar(z_index), route_ids.T, route_logits.T)

    def along_z(arrays):
        return [arrays[0]] + [
            lax.ppermute(arrays[step], "seq", z_pairs[step]) for step in range(1, Z_SIZE)
        ]

    z_pairs = [
        [
            (z * PLANE + p, (z + step) % Z_SIZE * PLANE + p)
            for z in range(Z_SIZE)
            for p in range(PLANE)
        ]
        for step in range(Z_SIZE)
    ]
    z_scalar = scalar(z_index)
    gain = norm_gain.reshape(1, width)
    own_shared = jnp.concatenate(
        [jnp.transpose(shared_gate_up, (1, 2, 0)).reshape(-1, width), shared_down], axis=0
    )
    info, own_shared = lax.optimization_barrier((info, own_shared))
    shared_weight = lax.all_gather(own_shared, "seq", axis=0, axis_index_groups=planes)

    sent_width = width + part + info.shape[1]
    sent = pl.pallas_call(
        attention_kernel,
        out_shape=[shape((tokens, sent_width), bf16)] * Z_SIZE,
        in_specs=[SMEM] * 3 + [VMEM] * 8,
        out_specs=[VMEM] * Z_SIZE,
        compiler_params=params(),
        cost_estimate=cost(4 * tokens * 5 * tokens * width, 3 * MIB),
        name="attention",
    )(z_scalar, scalar(me * tokens), lengths, queries, *behind, own_kv, residual, info)

    gathered = along_z(sent)
    gathered, cache_blocks, expert_gate_up = lax.optimization_barrier(
        (gathered, cache_blocks, expert_gate_up)
    )

    _, block_tokens, layers, kv_heads, head_size = cache_blocks.shape
    per_device = block_tokens // devices
    cache_view = cache_blocks.reshape(Z_SIZE, PLANE, per_device * layers, kv_heads, head_size)
    in_plane = []
    for step in range(PLANE):
        piece = lax.dynamic_index_in_dim(
            cache_view, lax.rem(plane_index + step, PLANE), axis=1, keepdims=False
        )
        if step:
            pairs = [
                (z * PLANE + p, z * PLANE + (p + step) % PLANE)
                for z in range(Z_SIZE)
                for p in range(PLANE)
            ]
            piece = lax.ppermute(piece, "seq", pairs)
        in_plane.append(piece)
    gate_up = jnp.transpose(expert_gate_up, (0, 2, 1, 3))

    mixed_part, info = pl.pallas_call(
        project_kernel,
        out_shape=[shape((all_tokens, part), bf16), shape((all_tokens, 128), bf16)],
        in_specs=[SMEM] + [VMEM] * (Z_SIZE + 1),
        out_specs=[VMEM] * 2,
        scratch_shapes=[pltpu.VMEM((Z_SIZE, tokens, sent_width), bf16)],
        compiler_params=params(),
        cost_estimate=cost(2 * all_tokens * width * part, 3 * MIB),
        name="project",
    )(z_scalar, *gathered, turned_weight)
    mixed = along_z([mixed_part] * Z_SIZE)

    local_halves, _, _, half_ff = expert_gate_up.shape
    per_half = Z_SIZE * CAP
    picked = local_halves * per_half
    onehot, mix = pl.pallas_call(
        tables_kernel,
        out_shape=[
            shape((PLANE * picked, all_tokens), bf16),
            shape((all_tokens, PLANE * picked), bf16),
        ],
        in_specs=[SMEM, VMEM],
        out_specs=[VMEM] * 2,
        compiler_params=params(),
        cost_estimate=cost(20 * PLANE * picked * all_tokens, MIB),
        name="tables",
    )(scalar(lax.rem(z_index, 2)), info)
    normed, own_mixed, outgoing = pl.pallas_call(
        pick_kernel,
        out_shape=[
            shape((all_tokens, width), bf16),
            shape((tokens, width), f32),
            shape((PLANE, picked, width), bf16),
        ],
        in_specs=[SMEM] + [VMEM] * (2 + Z_SIZE),
        out_specs=[VMEM, VMEM, HBM],
        scratch_shapes=[
            pltpu.VMEM((Z_SIZE, all_tokens, part), bf16),
            pltpu.VMEM((PLANE, picked, width), bf16),
            pltpu.SemaphoreType.DMA((PLANE,)),
        ],
        compiler_params=params(20),
        cost_estimate=cost(2 * PLANE * picked * all_tokens * width, 5 * MIB),
        name="pick",
    )(z_scalar, onehot, gain, *mixed)

    outgoing, in_plane = lax.optimization_barrier((outgoing, in_plane))
    arrived = exchange(outgoing, planes)
    grouped = pl.pallas_call(
        regroup_kernel,
        out_shape=[shape((PLANE,) + in_plane[0].shape[1:], bf16)] * Z_SIZE,
        in_specs=[SMEM] + [VMEM] * PLANE,
        out_specs=[VMEM] * Z_SIZE,
        compiler_params=params(),
        cost_estimate=cost(0, 2 * MIB),
        name="regroup",
    )(z_scalar, *in_plane)
    arrived_cache = [grouped[0]]
    for step in range(1, Z_SIZE):
        arrived_cache.append(lax.ppermute(grouped[step], "seq", z_pairs[step]))

    arrived, shared_weight = lax.optimization_barrier((arrived, shared_weight))
    shared_part = pl.pallas_call(
        shared_kernel,
        out_shape=shape((all_tokens, width), f32),
        in_specs=[VMEM] * 2,
        out_specs=VMEM,
        compiler_params=params(24),
        cost_estimate=cost(6 * all_tokens * 256 * width, 5 * MIB),
        name="shared_expert",
    )(normed, shared_weight)

    returning = pl.pallas_call(
        experts_kernel,
        out_shape=shape((PLANE, picked, width), bf16),
        in_specs=[VMEM, HBM, HBM],
        out_specs=HBM,
        scratch_shapes=[
            pltpu.VMEM((local_halves, 2, width, half_ff), bf16),
            pltpu.VMEM((local_halves, half_ff, width), bf16),
            pltpu.VMEM((PLANE, picked, width), bf16),
            pltpu.SemaphoreType.DMA((2, local_halves)),
            pltpu.SemaphoreType.DMA((local_halves // 2,)),
        ],
        compiler_params=params(40),
        cost_estimate=cost(6 * PLANE * picked * half_ff * width, 14 * MIB),
        name="experts",
    )(arrived, gate_up, expert_down)
    returning, arrived_cache = lax.optimization_barrier((returning, arrived_cache))
    returned = exchange(returning, planes).reshape(PLANE * picked, width)

    arrived_cache = jnp.concatenate(arrived_cache)
    cache_out = pl.pallas_call(
        reorder_kernel,
        out_shape=shape(arrived_cache.shape, bf16),
        in_specs=[SMEM, SMEM, VMEM],
        out_specs=VMEM,
        compiler_params=params(),
        cost_estimate=cost(0, 2 * arrived_cache.size * 2),
        name="reorder",
    )(scalar(me), block_table, arrived_cache)
    cache_out = cache_out.reshape(devices, per_device, layers, kv_heads, head_size)

    sums = pl.pallas_call(
        combine_kernel,
        out_shape=[shape((tokens, width), bf16)] * Z_SIZE,
        in_specs=[SMEM] + [VMEM] * 3,
        out_specs=[VMEM] * Z_SIZE,
        scratch_shapes=[pltpu.VMEM((all_tokens, width), f32)],
        compiler_params=params(24),
        cost_estimate=cost(2 * all_tokens * PLANE * picked * width, 3 * MIB),
        name="combine",
    )(z_scalar, mix, returned, shared_part)
    layer_out = pl.pallas_call(
        final_kernel,
        out_shape=shape((tokens, width), bf16),
        in_specs=[VMEM] * (1 + Z_SIZE),
        out_specs=VMEM,
        compiler_params=params(),
        cost_estimate=cost(5 * tokens * width, 2 * MIB),
        name="final",
    )(own_mixed, *along_z(sums))
    return (layer_out, cache_out)


def solution(mesh):
    in_specs = (
        P("seq", "head"),
        P("seq", "head"),
        P("seq", "head"),
        P(),
        P("head", "seq"),
        P(("seq", "head"), None),
        P(),
        P(("seq", "head"), None),
        P(("seq", "head"), None),
        P(None, None, ("seq", "head")),
        P(("seq", "head"), None),
        P("seq", None, None, None),
        P("seq", None, None),
        P("seq", None, None, "head", None),
        P(),
    )
    out_specs = (P(("seq", "head"), None), P(None, "seq", None, "head", None))
    planes_fit = mesh.shape["seq"] == Z_SIZE * PLANE and mesh.shape["head"] == 1
    body = shards if planes_fit else general_shards
    return jax.shard_map(body, mesh=mesh, in_specs=in_specs, out_specs=out_specs, check_vma=False)
```

profile of v0, /device:TPU:10, one launch (start us, length us, event | category | flops | bytes accessed | tf_op | source)
XLA Modules:
  0.0 202.0 jit_solution(12619881018991136886)
XLA Ops:
  16.0 3.4 %collective-permute-start.2 = (bf16[64,1024]{1,0:T(8,128)(2,1)S(1)}, bf16[64,1024]{1,0:T(8,128)(2,1)S(1)}, u32[]{:S(2)}, u32[]{:S(2)}) collective-permute-start(bf16[64,1024]{1,0:T(8,128)(2,1)S(1)} %constant_dynamic-update-slice_fusion.own_ref), channel_id=1, source_target_pairs={{0,2},{1,3},{2,4},{3,5},{4,6},{5,7},{6,8},{7,9},{8,10},{9,11},{10,... | collective-permute-start | bytes 393224 | tf_op jit(solution)/shard_map/ppermute | solution.py:28
  19.4 4.3 %collective-permute-start.1 = (bf16[64,1024]{1,0:T(8,128)(2,1)S(1)}, bf16[64,1024]{1,0:T(8,128)(2,1)S(1)}, u32[]{:S(2)}, u32[]{:S(2)}) collective-permute-start(bf16[64,1024]{1,0:T(8,128)(2,1)S(1)} %constant_dynamic-update-slice_fusion.own_ref), channel_id=1, source_target_pairs={{0,3},{1,4},{2,5},{3,6},{4,7},{5,8},{6,9},{7,10},{8,11},{9,12},{10... | collective-permute-start | bytes 393224 | tf_op jit(solution)/shard_map/ppermute | solution.py:28
  23.7 3.4 %collective-permute-start = (bf16[64,1024]{1,0:T(8,128)(2,1)S(1)}, bf16[64,1024]{1,0:T(8,128)(2,1)S(1)}, u32[]{:S(2)}, u32[]{:S(2)}) collective-permute-start(bf16[64,1024]{1,0:T(8,128)(2,1)S(1)} %constant_dynamic-update-slice_fusion.own_ref), channel_id=1, source_target_pairs={{0,4},{1,5},{2,6},{3,7},{4,8},{5,9},{6,10},{7,11},{8,12},{9,13},{1... | collective-permute-start | bytes 393224 | tf_op jit(solution)/shard_map/ppermute | solution.py:28
  27.2 4.3 %collective-permute-done.k4_ref = bf16[64,1024]{1,0:T(8,128)(2,1)S(1)} collective-permute-done((bf16[64,1024]{1,0:T(8,128)(2,1)S(1)}, bf16[64,1024]{1,0:T(8,128)(2,1)S(1)}, u32[]{:S(2)}, u32[]{:S(2)}) %collective-permute-start) | collective-permute-done | bytes 131104 | tf_op jit(solution)/shard_map/ppermute | solution.py:28
  34.0 2.1 %attention.1 = (bf16[64,2048]{1,0:T(8,128)(2,1)S(1)}, bf16[64,2048]{1,0:T(8,128)(2,1)S(1)}, bf16[64,2048]{1,0:T(8,128)(2,1)S(1)}, bf16[64,2048]{1,0:T(8,128)(2,1)S(1)}) custom-call(s32[1]{0:T(128)} %bitcast.z_ref, s32[1]{0:T(128)} %bitcast.2.first_ref, s32[16]{0:T(128)S(1)} %copy-done.27, bf16[64,1536]{1,0:T(8,128)(2,1)S(1)} %copy-done.13, ...), custom_call_target="tpu_custom_call" | custom-call | flops 125829120 | bytes 3145728 | tf_op jit(solution)/shard_map/attention/pallas_call | solution.py:485
  40.1 15.4 %collective-permute-done.4.refs_1_ = bf16[64,2048]{1,0:T(8,128)(2,1)S(1)} collective-permute-done((bf16[64,2048]{1,0:T(8,128)(2,1)S(1)}, bf16[64,2048]{1,0:T(8,128)(2,1)S(1)}, u32[]{:S(2)}, u32[]{:S(2)}) %collective-permute-start.4) | collective-permute-done | bytes 262176 | tf_op jit(solution)/shard_map/ppermute | solution.py:465
  55.5 2.8 %collective-permute-done.5.refs_2_ = bf16[64,2048]{1,0:T(8,128)(2,1)S(1)} collective-permute-done((bf16[64,2048]{1,0:T(8,128)(2,1)S(1)}, bf16[64,2048]{1,0:T(8,128)(2,1)S(1)}, u32[]{:S(2)}, u32[]{:S(2)}) %collective-permute-start.5) | collective-permute-done | bytes 262176 | tf_op jit(solution)/shard_map/ppermute | solution.py:465
  58.3 2.4 %collective-permute-done.6.refs_3_ = bf16[64,2048]{1,0:T(8,128)(2,1)S(1)} collective-permute-done((bf16[64,2048]{1,0:T(8,128)(2,1)S(1)}, bf16[64,2048]{1,0:T(8,128)(2,1)S(1)}, u32[]{:S(2)}, u32[]{:S(2)}) %collective-permute-start.6) | collective-permute-done | bytes 262176 | tf_op jit(solution)/shard_map/ppermute | solution.py:465
  63.7 2.8 %collective-permute-start.7 = (bf16[256,384]{1,0:T(8,128)(2,1)S(1)}, bf16[256,384]{1,0:T(8,128)(2,1)S(1)}, u32[]{:S(2)}, u32[]{:S(2)}) collective-permute-start(bf16[256,384]{1,0:T(8,128)(2,1)S(1)} %get-tuple-element.56.refs_0_), channel_id=1, source_target_pairs={{0,8},{1,9},{2,10},{3,11},{4,12},{5,13},{6,14},{7,15},{8,16},{9,17... | collective-permute-start | bytes 589832 | tf_op jit(solution)/shard_map/ppermute | solution.py:465
  69.1 4.6 %collective-permute-done.16.refs_7_ = bf16[4,32,4,128]{3,2,1,0:T(4,128)(2,1)S(1)} collective-permute-done((bf16[4,32,4,128]{3,2,1,0:T(4,128)(2,1)S(1)}, bf16[4,32,4,128]{3,2,1,0:T(4,128)(2,1)S(1)}, u32[]{:S(2)}, u32[]{:S(2)}) %collective-permute-start.16) | collective-permute-done | bytes 131104 | tf_op jit(solution)/shard_map/ppermute | solution.py:514
  78.9 2.4 %collective-permute-start.11 = (bf16[4,32,4,128]{3,2,1,0:T(4,128)(2,1)}, bf16[4,32,4,128]{3,2,1,0:T(4,128)(2,1)S(1)}, u32[]{:S(2)}, u32[]{:S(2)}) collective-permute-start(bf16[4,32,4,128]{3,2,1,0:T(4,128)(2,1)} %get-tuple-element.93), channel_id=1, source_target_pairs={{0,2},{1,3},{2,4},{3,5},{4,6},{5,7},{6,0},{7,1},{8,10},{9,11},{10,... | collective-permute-start | bytes 393224 | tf_op jit(solution)/shard_map/ppermute | solution.py:514
  84.0 3.0 %pick.1 = (bf16[256,1536]{1,0:T(8,128)(2,1)S(1)}, f32[64,1536]{1,0:T(8,128)S(1)}, bf16[8,96,1536]{2,1,0:T(8,128)(2,1)S(1)}) custom-call(s32[1]{0:T(128)} %bitcast.z_ref, bf16[768,256]{1,0:T(8,128)(2,1)S(1)} %get-tuple-element.55.onehot_ref, f32[1,1536]{1,0:T(1,128)S(1)} %reshape.36.gain_ref, bf16[256,384]{1,0:T(8,128)(2,1)S(1)} %get-tuple-element.56.refs_0_, ...), custom_call_target="tpu_custom_call" | custom-call | flops 603979776 | bytes 5242880 | tf_op jit(solution)/shard_map/pick/pallas_call | solution.py:545
  92.4 4.6 %all-to-all-start = ((bf16[8,96,1536]{2,1,0:T(8,128)(2,1)}), bf16[8,96,1536]{2,1,0:T(8,128)(2,1)S(1)}, u32[]{:S(2)}, u32[]{:S(2)}) async-start(bf16[8,96,1536]{2,1,0:T(8,128)(2,1)} %copy-done.6), calls=%async_computation | async-start | bytes 4718592 | tf_op jit(solution)/shard_map/all_to_all | solution.py:442
  105.2 4.0 %collective-permute-start.18 = (bf16[8,32,4,128]{3,2,1,0:T(4,128)(2,1)}, bf16[8,32,4,128]{3,2,1,0:T(4,128)(2,1)}, u32[]{:S(2)}, u32[]{:S(2)}) collective-permute-start(bf16[8,32,4,128]{3,2,1,0:T(4,128)(2,1)} %get-tuple-element.75), channel_id=1, source_target_pairs={{0,16},{1,17},{2,18},{3,19},{4,20},{5,21},{6,22},{7,23},{8,24},{9,... | collective-permute-start | bytes 786440 | tf_op jit(solution)/shard_map/ppermute | solution.py:577
  109.3 6.3 %copy.35 = bf16[4,1536,2,256]{3,1,2,0:T(8,128)(2,1)} copy(bf16[4,1536,2,256]{3,2,1,0:T(2,128)(2,1)} %param.26) | data formatting | bytes 12582912 | tf_op jit(solution)/shard_map/optimization_barrier | solution.py:496
  115.5 9.4 %all-to-all-done.rows_ref = bf16[8,96,1536]{2,1,0:T(8,128)(2,1)S(1)} async-done(((bf16[8,96,1536]{2,1,0:T(8,128)(2,1)}), bf16[8,96,1536]{2,1,0:T(8,128)(2,1)S(1)}, u32[]{:S(2)}, u32[]{:S(2)}) %all-to-all-start) | async-done | bytes 2359328 | tf_op jit(solution)/shard_map/all_to_all | solution.py:442
  124.9 2.8 %copy-done = bf16[4,1536,2,256]{3,1,2,0:T(8,128)(2,1)S(1)} copy-done((bf16[4,1536,2,256]{3,1,2,0:T(8,128)(2,1)S(1)}, bf16[4,1536,2,256]{3,1,2,0:T(8,128)(2,1)}, u32[]{:S(2)}) %copy-start) | copy-done | bytes 6291480
  129.6 4.5 %experts.1 = bf16[8,96,1536]{2,1,0:T(8,128)(2,1)S(1)} custom-call(bf16[8,96,1536]{2,1,0:T(8,128)(2,1)S(1)} %all-to-all-done.rows_ref, bf16[4,2,1536,256]{3,2,1,0:T(8,128)(2,1)S(1)} %bitcast.49, bf16[4,256,1536]{2,1,0:T(8,128)(2,1)S(1)} %copy-done.4), custom_call_target="tpu_custom_call" | custom-call | flops 1811939328 | bytes 14680064 | tf_op jit(solution)/shard_map/experts/pallas_call | solution.py:590
  136.2 5.0 %all-to-all-start.1 = ((bf16[8,96,1536]{2,1,0:T(8,128)(2,1)}), bf16[8,96,1536]{2,1,0:T(8,128)(2,1)S(1)}, u32[]{:S(2)}, u32[]{:S(2)}) async-start(bf16[8,96,1536]{2,1,0:T(8,128)(2,1)} %copy-done.1), calls=%async_computation.1 | async-start | bytes 4718592 | tf_op jit(solution)/shard_map/all_to_all | solution.py:442
  145.0 24.2 %all-to-all-done.1 = bf16[8,96,1536]{2,1,0:T(8,128)(2,1)S(1)} async-done(((bf16[8,96,1536]{2,1,0:T(8,128)(2,1)}), bf16[8,96,1536]{2,1,0:T(8,128)(2,1)S(1)}, u32[]{:S(2)}, u32[]{:S(2)}) %all-to-all-start.1) | async-done | bytes 2359328 | tf_op jit(solution)/shard_map/all_to_all | solution.py:442
  171.6 2.1 %collective-permute-start.20 = (bf16[64,1536]{1,0:T(8,128)(2,1)S(1)}, bf16[64,1536]{1,0:T(8,128)(2,1)S(1)}, u32[]{:S(2)}, u32[]{:S(2)}) collective-permute-start(bf16[64,1536]{1,0:T(8,128)(2,1)S(1)} %get-tuple-element.81), channel_id=1, source_target_pairs={{0,8},{1,9},{2,10},{3,11},{4,12},{5,13},{6,14},{7,15},{8,16},{9,17... | collective-permute-start | bytes 589832 | tf_op jit(solution)/shard_map/ppermute | solution.py:465
  173.7 4.0 %collective-permute-start.21 = (bf16[64,1536]{1,0:T(8,128)(2,1)S(1)}, bf16[64,1536]{1,0:T(8,128)(2,1)S(1)}, u32[]{:S(2)}, u32[]{:S(2)}) collective-permute-start(bf16[64,1536]{1,0:T(8,128)(2,1)S(1)} %get-tuple-element.82), channel_id=1, source_target_pairs={{0,16},{1,17},{2,18},{3,19},{4,20},{5,21},{6,22},{7,23},{8,24},{9,... | collective-permute-start | bytes 589832 | tf_op jit(solution)/shard_map/ppermute | solution.py:465
  181.4 9.3 %collective-permute-done.21.refs_2_ = bf16[64,1536]{1,0:T(8,128)(2,1)S(1)} collective-permute-done((bf16[64,1536]{1,0:T(8,128)(2,1)S(1)}, bf16[64,1536]{1,0:T(8,128)(2,1)S(1)}, u32[]{:S(2)}, u32[]{:S(2)}) %collective-permute-start.21) | collective-permute-done | bytes 196640 | tf_op jit(solution)/shard_map/ppermute | solution.py:465
  190.7 3.7 %collective-permute-done.22.refs_3_ = bf16[64,1536]{1,0:T(8,128)(2,1)S(1)} collective-permute-done((bf16[64,1536]{1,0:T(8,128)(2,1)S(1)}, bf16[64,1536]{1,0:T(8,128)(2,1)S(1)}, u32[]{:S(2)}, u32[]{:S(2)}) %collective-permute-start.22) | collective-permute-done | bytes 196640 | tf_op jit(solution)/shard_map/ppermute | solution.py:465
  (114 shorter events, 56.8 us)
Async XLA Ops:
  7.2 53.6 %all-gather.4.cloned.1.call-start = ((), (), s32[]{:S(2)}) async-start(), calls=%async_computation.2 | async-start | bytes 1327104 | tf_op jit(solution)/shard_map/all_gather | solution.py:449
  7.9 107.6 %all-gather.6.cloned.1.call-start = ((), (), s32[]{:S(2)}) async-start(), calls=%async_computation.3 | async-start | bytes 2654208 | tf_op jit(solution)/shard_map/all_gather | solution.py:482
  14.1 13.1 %collective-permute-start.3 = (bf16[64,1024]{1,0:T(8,128)(2,1)S(1)}, bf16[64,1024]{1,0:T(8,128)(2,1)S(1)}, u32[]{:S(2)}, u32[]{:S(2)}) collective-permute-start(bf16[64,1024]{1,0:T(8,128)(2,1)S(1)} %constant_dynamic-update-slice_fusion.own_ref), channel_id=1, source_target_pairs={{0,1},{1,2},{2,3},{3,4},{4,5},{5,6},{6,7},{7,8},{8,9},{9,10},{10,1... | collective-permute-start | bytes 393224 | tf_op jit(solution)/shard_map/ppermute | solution.py:28
  16.0 11.2 %collective-permute-start.2 = (bf16[64,1024]{1,0:T(8,128)(2,1)S(1)}, bf16[64,1024]{1,0:T(8,128)(2,1)S(1)}, u32[]{:S(2)}, u32[]{:S(2)}) collective-permute-start(bf16[64,1024]{1,0:T(8,128)(2,1)S(1)} %constant_dynamic-update-slice_fusion.own_ref), channel_id=1, source_target_pairs={{0,2},{1,3},{2,4},{3,5},{4,6},{5,7},{6,8},{7,9},{8,10},{9,11},{10,... | collective-permute-start | bytes 393224 | tf_op jit(solution)/shard_map/ppermute | solution.py:28
  36.1 19.5 %collective-permute-start.4 = (bf16[64,2048]{1,0:T(8,128)(2,1)S(1)}, bf16[64,2048]{1,0:T(8,128)(2,1)S(1)}, u32[]{:S(2)}, u32[]{:S(2)}) collective-permute-start(bf16[64,2048]{1,0:T(8,128)(2,1)S(1)} %get-tuple-element.47), channel_id=1, source_target_pairs={{0,8},{1,9},{2,10},{3,11},{4,12},{5,13},{6,14},{7,15},{8,16},{9,17... | collective-permute-start | bytes 786440 | tf_op jit(solution)/shard_map/ppermute | solution.py:465
  37.7 20.7 %collective-permute-start.5 = (bf16[64,2048]{1,0:T(8,128)(2,1)S(1)}, bf16[64,2048]{1,0:T(8,128)(2,1)S(1)}, u32[]{:S(2)}, u32[]{:S(2)}) collective-permute-start(bf16[64,2048]{1,0:T(8,128)(2,1)S(1)} %get-tuple-element.48), channel_id=1, source_target_pairs={{0,16},{1,17},{2,18},{3,19},{4,20},{5,21},{6,22},{7,23},{8,24},{9,... | collective-permute-start | bytes 786440 | tf_op jit(solution)/shard_map/ppermute | solution.py:465
  38.2 22.6 %collective-permute-start.6 = (bf16[64,2048]{1,0:T(8,128)(2,1)S(1)}, bf16[64,2048]{1,0:T(8,128)(2,1)S(1)}, u32[]{:S(2)}, u32[]{:S(2)}) collective-permute-start(bf16[64,2048]{1,0:T(8,128)(2,1)S(1)} %get-tuple-element.49), channel_id=1, source_target_pairs={{0,24},{1,25},{2,26},{3,27},{4,28},{5,29},{6,30},{7,31},{8,0},{9,1... | collective-permute-start | bytes 786440 | tf_op jit(solution)/shard_map/ppermute | solution.py:465
  62.6 16.2 %collective-permute-start.9 = (bf16[256,384]{1,0:T(8,128)(2,1)S(1)}, bf16[256,384]{1,0:T(8,128)(2,1)S(1)}, u32[]{:S(2)}, u32[]{:S(2)}) collective-permute-start(bf16[256,384]{1,0:T(8,128)(2,1)S(1)} %get-tuple-element.56.refs_0_), channel_id=1, source_target_pairs={{0,24},{1,25},{2,26},{3,27},{4,28},{5,29},{6,30},{7,31},{8,0},{9,1... | collective-permute-start | bytes 589832 | tf_op jit(solution)/shard_map/ppermute | solution.py:465
  62.7 16.2 %collective-permute-start.8 = (bf16[256,384]{1,0:T(8,128)(2,1)S(1)}, bf16[256,384]{1,0:T(8,128)(2,1)S(1)}, u32[]{:S(2)}, u32[]{:S(2)}) collective-permute-start(bf16[256,384]{1,0:T(8,128)(2,1)S(1)} %get-tuple-element.56.refs_0_), channel_id=1, source_target_pairs={{0,16},{1,17},{2,18},{3,19},{4,20},{5,21},{6,22},{7,23},{8,24},{9,... | collective-permute-start | bytes 589832 | tf_op jit(solution)/shard_map/ppermute | solution.py:465
  63.7 17.5 %collective-permute-start.7 = (bf16[256,384]{1,0:T(8,128)(2,1)S(1)}, bf16[256,384]{1,0:T(8,128)(2,1)S(1)}, u32[]{:S(2)}, u32[]{:S(2)}) collective-permute-start(bf16[256,384]{1,0:T(8,128)(2,1)S(1)} %get-tuple-element.56.refs_0_), channel_id=1, source_target_pairs={{0,8},{1,9},{2,10},{3,11},{4,12},{5,13},{6,14},{7,15},{8,16},{9,17... | collective-permute-start | bytes 589832 | tf_op jit(solution)/shard_map/ppermute | solution.py:465
  67.8 9.4 %collective-permute-start.15 = (bf16[4,32,4,128]{3,2,1,0:T(4,128)(2,1)S(1)}, bf16[4,32,4,128]{3,2,1,0:T(4,128)(2,1)S(1)}, u32[]{:S(2)}, u32[]{:S(2)}) collective-permute-start(bf16[4,32,4,128]{3,2,1,0:T(4,128)(2,1)S(1)} %get-tuple-element.89), channel_id=1, source_target_pairs={{0,6},{1,7},{2,0},{3,1},{4,2},{5,3},{6,4},{7,5},{8,14},{9,15},{10,... | collective-permute-start | bytes 393224 | tf_op jit(solution)/shard_map/ppermute | solution.py:514
  73.7 15.4 %collective-permute-start.14 = (bf16[4,32,4,128]{3,2,1,0:T(4,128)(2,1)}, bf16[4,32,4,128]{3,2,1,0:T(4,128)(2,1)S(1)}, u32[]{:S(2)}, u32[]{:S(2)}) collective-permute-start(bf16[4,32,4,128]{3,2,1,0:T(4,128)(2,1)} %get-tuple-element.90), channel_id=1, source_target_pairs={{0,5},{1,6},{2,7},{3,0},{4,1},{5,2},{6,3},{7,4},{8,13},{9,14},{10,... | collective-permute-start | bytes 393224 | tf_op jit(solution)/shard_map/ppermute | solution.py:514
  77.3 12.5 %collective-permute-start.13 = (bf16[4,32,4,128]{3,2,1,0:T(4,128)(2,1)}, bf16[4,32,4,128]{3,2,1,0:T(4,128)(2,1)S(1)}, u32[]{:S(2)}, u32[]{:S(2)}) collective-permute-start(bf16[4,32,4,128]{3,2,1,0:T(4,128)(2,1)} %get-tuple-element.91), channel_id=1, source_target_pairs={{0,4},{1,5},{2,6},{3,7},{4,0},{5,1},{6,2},{7,3},{8,12},{9,13},{10,... | collective-permute-start | bytes 393224 | tf_op jit(solution)/shard_map/ppermute | solution.py:514
  78.9 11.6 %collective-permute-start.12 = (bf16[4,32,4,128]{3,2,1,0:T(4,128)(2,1)}, bf16[4,32,4,128]{3,2,1,0:T(4,128)(2,1)S(1)}, u32[]{:S(2)}, u32[]{:S(2)}) collective-permute-start(bf16[4,32,4,128]{3,2,1,0:T(4,128)(2,1)} %get-tuple-element.92), channel_id=1, source_target_pairs={{0,3},{1,4},{2,5},{3,6},{4,7},{5,0},{6,1},{7,2},{8,11},{9,12},{10,... | collective-permute-start | bytes 393224 | tf_op jit(solution)/shard_map/ppermute | solution.py:514
  78.9 12.2 %collective-permute-start.11 = (bf16[4,32,4,128]{3,2,1,0:T(4,128)(2,1)}, bf16[4,32,4,128]{3,2,1,0:T(4,128)(2,1)S(1)}, u32[]{:S(2)}, u32[]{:S(2)}) collective-permute-start(bf16[4,32,4,128]{3,2,1,0:T(4,128)(2,1)} %get-tuple-element.93), channel_id=1, source_target_pairs={{0,2},{1,3},{2,4},{3,5},{4,6},{5,7},{6,0},{7,1},{8,10},{9,11},{10,... | collective-permute-start | bytes 393224 | tf_op jit(solution)/shard_map/ppermute | solution.py:514
  81.3 10.5 %collective-permute-start.10 = (bf16[4,32,4,128]{3,2,1,0:T(4,128)(2,1)S(1)}, bf16[4,32,4,128]{3,2,1,0:T(4,128)(2,1)S(1)}, u32[]{:S(2)}, u32[]{:S(2)}) collective-permute-start(bf16[4,32,4,128]{3,2,1,0:T(4,128)(2,1)S(1)} %get-tuple-element.94), channel_id=1, source_target_pairs={{0,1},{1,2},{2,3},{3,4},{4,5},{5,6},{6,7},{7,0},{8,9},{9,10},{10,1... | collective-permute-start | bytes 393224 | tf_op jit(solution)/shard_map/ppermute | solution.py:514
  92.4 32.5 %all-to-all-start = ((bf16[8,96,1536]{2,1,0:T(8,128)(2,1)}), bf16[8,96,1536]{2,1,0:T(8,128)(2,1)S(1)}, u32[]{:S(2)}, u32[]{:S(2)}) async-start(bf16[8,96,1536]{2,1,0:T(8,128)(2,1)} %copy-done.6), calls=%async_computation | async-start | bytes 4718592 | tf_op jit(solution)/shard_map/all_to_all | solution.py:442
  103.2 32.3 %collective-permute-start.17 = (bf16[8,32,4,128]{3,2,1,0:T(4,128)(2,1)}, bf16[8,32,4,128]{3,2,1,0:T(4,128)(2,1)S(1)}, u32[]{:S(2)}, u32[]{:S(2)}) collective-permute-start(bf16[8,32,4,128]{3,2,1,0:T(4,128)(2,1)} %get-tuple-element.74), channel_id=1, source_target_pairs={{0,8},{1,9},{2,10},{3,11},{4,12},{5,13},{6,14},{7,15},{8,16},{9,17... | collective-permute-start | bytes 786440 | tf_op jit(solution)/shard_map/ppermute | solution.py:577
  105.2 30.3 %collective-permute-start.18 = (bf16[8,32,4,128]{3,2,1,0:T(4,128)(2,1)}, bf16[8,32,4,128]{3,2,1,0:T(4,128)(2,1)}, u32[]{:S(2)}, u32[]{:S(2)}) collective-permute-start(bf16[8,32,4,128]{3,2,1,0:T(4,128)(2,1)} %get-tuple-element.75), channel_id=1, source_target_pairs={{0,16},{1,17},{2,18},{3,19},{4,20},{5,21},{6,22},{7,23},{8,24},{9,... | collective-permute-start | bytes 786440 | tf_op jit(solution)/shard_map/ppermute | solution.py:577
  109.3 26.2 %collective-permute-start.19 = (bf16[8,32,4,128]{3,2,1,0:T(4,128)(2,1)}, bf16[8,32,4,128]{3,2,1,0:T(4,128)(2,1)}, u32[]{:S(2)}, u32[]{:S(2)}) collective-permute-start(bf16[8,32,4,128]{3,2,1,0:T(4,128)(2,1)} %get-tuple-element.76), channel_id=1, source_target_pairs={{0,24},{1,25},{2,26},{3,27},{4,28},{5,29},{6,30},{7,31},{8,0},{9,1... | collective-permute-start | bytes 786440 | tf_op jit(solution)/shard_map/ppermute | solution.py:577
  136.2 33.0 %all-to-all-start.1 = ((bf16[8,96,1536]{2,1,0:T(8,128)(2,1)}), bf16[8,96,1536]{2,1,0:T(8,128)(2,1)S(1)}, u32[]{:S(2)}, u32[]{:S(2)}) async-start(bf16[8,96,1536]{2,1,0:T(8,128)(2,1)} %copy-done.1), calls=%async_computation.1 | async-start | bytes 4718592 | tf_op jit(solution)/shard_map/all_to_all | solution.py:442
  171.6 9.8 %collective-permute-start.20 = (bf16[64,1536]{1,0:T(8,128)(2,1)S(1)}, bf16[64,1536]{1,0:T(8,128)(2,1)S(1)}, u32[]{:S(2)}, u32[]{:S(2)}) collective-permute-start(bf16[64,1536]{1,0:T(8,128)(2,1)S(1)} %get-tuple-element.81), channel_id=1, source_target_pairs={{0,8},{1,9},{2,10},{3,11},{4,12},{5,13},{6,14},{7,15},{8,16},{9,17... | collective-permute-start | bytes 589832 | tf_op jit(solution)/shard_map/ppermute | solution.py:465
  173.7 17.0 %collective-permute-start.21 = (bf16[64,1536]{1,0:T(8,128)(2,1)S(1)}, bf16[64,1536]{1,0:T(8,128)(2,1)S(1)}, u32[]{:S(2)}, u32[]{:S(2)}) collective-permute-start(bf16[64,1536]{1,0:T(8,128)(2,1)S(1)} %get-tuple-element.82), channel_id=1, source_target_pairs={{0,16},{1,17},{2,18},{3,19},{4,20},{5,21},{6,22},{7,23},{8,24},{9,... | collective-permute-start | bytes 589832 | tf_op jit(solution)/shard_map/ppermute | solution.py:465
  177.6 16.7 %collective-permute-start.22 = (bf16[64,1536]{1,0:T(8,128)(2,1)S(1)}, bf16[64,1536]{1,0:T(8,128)(2,1)S(1)}, u32[]{:S(2)}, u32[]{:S(2)}) collective-permute-start(bf16[64,1536]{1,0:T(8,128)(2,1)S(1)} %get-tuple-element.83), channel_id=1, source_target_pairs={{0,24},{1,25},{2,26},{3,27},{4,28},{5,29},{6,30},{7,31},{8,0},{9,1... | collective-permute-start | bytes 589832 | tf_op jit(solution)/shard_map/ppermute | solution.py:465
  (35 other events, 209.6 us)
Sparse Core Ops, SparseCore 0:
  9.9 33.8 all-gather.3
  45.6 30.4 all-gather.5
where the time goes:
time: 203 us; the launch traced here: 202 us
  waiting for transfers between devices  79.5 us (39%)
  starting transfers between devices  49.1 us (24%)
  local copies, waits for them, and re-layouts  36.7 us (18%)
  Pallas kernels  18.7 us (9%)
  between operations  14.3 us (7%)
  other arithmetic  3.67 us (2%)
    ppermute x9, waiting for transfers between devices, along_z(): lax.ppermute(arrays[step], 'seq', z_pairs[step])  34.6 us
    all_to_all x2, waiting for transfers between devices, exchange(): lax.all_to_all(array, 'seq', split_axis=0, concat_axis=0, tiled=True, axi...  33.6 us
    unnamed x65, local copies, waits for them, and re-layouts  28.4 us
    ppermute x9, starting transfers between devices, along_z(): lax.ppermute(arrays[step], 'seq', z_pairs[step])  14.1 us
    ppermute x4, starting transfers between devices, from_behind(): return lax.ppermute(shard, axis, pairs)  13.1 us
    all_to_all x2, starting transfers between devices, exchange(): lax.all_to_all(array, 'seq', split_axis=0, concat_axis=0, tiled=True, axi...  9.62 us
    optimization_barrier x1, local copies, waits for them, and re-layouts, shards(): lax.optimization_barrier((gathered, cache_blocks, expert_gate_up))  6.27 us
    ppermute x7, starting transfers between devices, shards(): piece = lax.ppermute(piece, 'seq', pairs)  6.22 us
  transfers between devices with their start and end apart: 27, of which 11 were waited for; matrix products, arithmetic and copies ran while one was open for 6% of the time, Pallas kernels for 8%

commit v1 on v0

--- a/solution.py
+++ b/solution.py
@@ -337,15 +337,34 @@
     ]
     rows = rows_ref[...]
     act = silu_times(dot_rows(rows, gate_weight), dot_rows(rows, up_weight))
-    out_ref[...] = dot(act, down_weight)
+    out_ref[...] = dot(act, down_weight).astype(jnp.bfloat16)
 
 
 def experts_kernel(
-    rows_ref, gate_up_hbm, down_hbm, out_hbm, gate_up_ref, down_ref, out_ref, in_sems, out_sems
+    rows_hbm,
+    gate_up_hbm,
+    down_hbm,
+    out_hbm,
+    rows_ref,
+    gate_up_ref,
+    down_ref,
+    out_ref,
+    in_sems,
+    row_sems,
+    out_sems,
 ):
     halves = gate_up_ref.shape[0]
-    fetches = []
+    sources, rows, width = rows_ref.shape
+    per_half = rows // halves
+    fetches, row_fetches = [], []
     for half in range(halves):
+        if half % 2 == 0:
+            both = pl.ds(half * per_half, 2 * per_half)
+            fetch = pltpu.make_async_copy(
+                rows_hbm.at[:, both], rows_ref.at[:, both], row_sems.at[half // 2]
+            )
+            fetch.start()
+            row_fetches.append(fetch)
         gate_up = pltpu.make_async_copy(
             gate_up_hbm.at[half], gate_up_ref.at[half], in_sems.at[0, half]
         )
@@ -353,11 +372,10 @@
         gate_up.start()
         down.start()
         fetches.append((gate_up, down))
-    sources, rows, width = rows_ref.shape
-    per_half = rows // halves
     copies = []
     for pair in range(halves // 2):
         both = pl.ds(2 * pair * per_half, 2 * per_half)
+        row_fetches[pair].wait()
         arrived = rows_ref[:, both, :].astype(jnp.float32)
         results = []
         for member in range(2):
@@ -379,7 +397,7 @@
 def combine_kernel(z_ref, mix_ref, rows_ref, shared_ref, *refs):
     outs, sum_ref = refs[:Z_SIZE], refs[Z_SIZE]
     tokens = outs[0].shape[0]
-    sum_ref[...] = dot(mix_ref[...], rows_ref[...]) + shared_ref[...]
+    sum_ref[...] = dot(mix_ref[...], rows_ref[...]) + shared_ref[...].astype(jnp.float32)
     for step, out_ref in enumerate(outs):
         z = lax.rem(z_ref[0] + step, Z_SIZE)
         rows = pl.ds(pl.multiple_of(z * tokens, tokens), tokens)
@@ -446,6 +464,10 @@
     own_kv = jnp.concatenate([key_vectors, value_vectors], axis=1)
     behind = [from_behind(own_kv, "seq", offset) for offset in range(REACH, 0, -1)]
 
+    behind[-1], route_ids, route_logits, shared_gate_up, shared_down = lax.optimization_barrier(
+        (behind[-1], route_ids, route_logits, shared_gate_up, shared_down)
+    )
+
     turned_weight = lax.all_gather(
         out_weight.T, "seq", axis=0, tiled=True, axis_index_groups=planes
     )
@@ -487,14 +509,42 @@
         out_shape=[shape((tokens, sent_width), bf16)] * Z_SIZE,
         in_specs=[SMEM] * 3 + [VMEM] * 8,
         out_specs=[VMEM] * Z_SIZE,
-        compiler_params=params(),
+        compiler_params=params(58),
         cost_estimate=cost(4 * tokens * 5 * tokens * width, 3 * MIB),
         name="attention",
     )(z_scalar, scalar(me * tokens), lengths, queries, *behind, own_kv, residual, info)
 
     gathered = along_z(sent)
-    gathered, cache_blocks, expert_gate_up = lax.optimization_barrier(
-        (gathered, cache_blocks, expert_gate_up)
+
+    mixed_part, info = pl.pallas_call(
+        project_kernel,
+        out_shape=[shape((all_tokens, part), bf16), shape((all_tokens, 128), bf16)],
+        in_specs=[SMEM] + [VMEM] * (Z_SIZE + 1),
+        out_specs=[VMEM] * 2,
+        scratch_shapes=[pltpu.VMEM((Z_SIZE, tokens, sent_width), bf16)],
+        compiler_params=params(),
+        cost_estimate=cost(2 * all_tokens * width * part, 3 * MIB),
+        name="project",
+    )(z_scalar, *gathered, turned_weight)
+    mixed = along_z([mixed_part] * Z_SIZE)
+
+    local_halves, _, _, half_ff = expert_gate_up.shape
+    per_half = Z_SIZE * CAP
+    picked = local_halves * per_half
+    onehot, mix = pl.pallas_call(
+        tables_kernel,
+        out_shape=[
+            shape((PLANE * picked, all_tokens), bf16),
+            shape((all_tokens, PLANE * picked), bf16),
+        ],
+        in_specs=[SMEM, VMEM],
+        out_specs=[VMEM] * 2,
+        compiler_params=params(),
+        cost_estimate=cost(20 * PLANE * picked * all_tokens, MIB),
+        name="tables",
+    )(scalar(lax.rem(z_index, 2)), info)
+    onehot, cache_blocks, expert_gate_up = lax.optimization_barrier(
+        (onehot, cache_blocks, expert_gate_up)
     )
 
     _, block_tokens, layers, kv_heads, head_size = cache_blocks.shape
@@ -515,33 +565,6 @@
         in_plane.append(piece)
     gate_up = jnp.transpose(expert_gate_up, (0, 2, 1, 3))
 
-    mixed_part, info = pl.pallas_call(
-        project_kernel,
-        out_shape=[shape((all_tokens, part), bf16), shape((all_tokens, 128), bf16)],
-        in_specs=[SMEM] + [VMEM] * (Z_SIZE + 1),
-        out_specs=[VMEM] * 2,
-        scratch_shapes=[pltpu.VMEM((Z_SIZE, tokens, sent_width), bf16)],
-        compiler_params=params(),
-        cost_estimate=cost(2 * all_tokens * width * part, 3 * MIB),
-        name="project",
-    )(z_scalar, *gathered, turned_weight)
-    mixed = along_z([mixed_part] * Z_SIZE)
-
-    local_halves, _, _, half_ff = expert_gate_up.shape
-    per_half = Z_SIZE * CAP
-    picked = local_halves * per_half
-    onehot, mix = pl.pallas_call(
-        tables_kernel,
-        out_shape=[
-            shape((PLANE * picked, all_tokens), bf16),
-            shape((all_tokens, PLANE * picked), bf16),
-        ],
-        in_specs=[SMEM, VMEM],
-        out_specs=[VMEM] * 2,
-        compiler_params=params(),
-        cost_estimate=cost(20 * PLANE * picked * all_tokens, MIB),
-        name="tables",
-    )(scalar(lax.rem(z_index, 2)), info)
     normed, own_mixed, outgoing = pl.pallas_call(
         pick_kernel,
         out_shape=[
@@ -556,12 +579,11 @@
             pltpu.VMEM((PLANE, picked, width), bf16),
             pltpu.SemaphoreType.DMA((PLANE,)),
         ],
-        compiler_params=params(20),
+        compiler_params=params(58),
         cost_estimate=cost(2 * PLANE * picked * all_tokens * width, 5 * MIB),
         name="pick",
     )(z_scalar, onehot, gain, *mixed)
 
-    outgoing, in_plane = lax.optimization_barrier((outgoing, in_plane))
     arrived = exchange(outgoing, planes)
     grouped = pl.pallas_call(
         regroup_kernel,
@@ -579,7 +601,7 @@
     arrived, shared_weight = lax.optimization_barrier((arrived, shared_weight))
     shared_part = pl.pallas_call(
         shared_kernel,
-        out_shape=shape((all_tokens, width), f32),
+        out_shape=shape((all_tokens, width), bf16),
         in_specs=[VMEM] * 2,
         out_specs=VMEM,
         compiler_params=params(24),
@@ -590,16 +612,18 @@
     returning = pl.pallas_call(
         experts_kernel,
         out_shape=shape((PLANE, picked, width), bf16),
-        in_specs=[VMEM, HBM, HBM],
+        in_specs=[HBM, HBM, HBM],
         out_specs=HBM,
         scratch_shapes=[
+            pltpu.VMEM((PLANE, picked, width), bf16),
             pltpu.VMEM((local_halves, 2, width, half_ff), bf16),
             pltpu.VMEM((local_halves, half_ff, width), bf16),
             pltpu.VMEM((PLANE, picked, width), bf16),
             pltpu.SemaphoreType.DMA((2, local_halves)),
             pltpu.SemaphoreType.DMA((local_halves // 2,)),
+            pltpu.SemaphoreType.DMA((local_halves // 2,)),
         ],
-        compiler_params=params(40),
+        compiler_params=params(58),
         cost_estimate=cost(6 * PLANE * picked * half_ff * width, 14 * MIB),
         name="experts",
     )(arrived, gate_up, expert_down)

time: 203 us -> 226 us (1.11)
  waiting for transfers between devices: 79.5 us -> 113 us
  local copies, waits for them, and re-layouts: 36.7 us -> 21.7 us
  Pallas kernels: 18.7 us -> 24.6 us
    ppermute x7, waiting for transfers between devices: 6.2 us -> 30 us  [shards(): piece = lax.ppermute(piece, 'seq', pairs)]
    unnamed x65 -> x47, local copies, waits for them, and re-layouts: 28.4 us -> 12.1 us
    ppermute x9, waiting for transfers between devices: 34.6 us -> 44.7 us  [along_z(): lax.ppermute(arrays[step], 'seq', z_pairs[step])]
    all_to_all x2, waiting for transfers between devices: 33.6 us -> 24.3 us  [exchange(): lax.all_to_all(array, 'seq', split_axis=0, concat_axis=0, tiled=True, axi...]
    ppermute x3, waiting for transfers between devices: 0.01 us -> 4.79 us  [shards(): arrived_cache.append(lax.ppermute(grouped[step], 'seq', z_pairs[step]))]
    ppermute x4, waiting for transfers between devices: 4.3 us -> 8.23 us  [from_behind(): return lax.ppermute(shard, axis, pairs)]
    pallas_call x1, Pallas kernels: 4.45 us -> 7.96 us  [shards(): pl.pallas_call(experts_kernel, out_shape=shape((PLANE, picked, width), bf...]
  transfers between devices with their start and end apart: 27 -> 27, of which waited for: 11 -> 18; matrix products, arithmetic and copies ran while one was open for 6% -> 6% of each run, Pallas kernels for 8% -> 10%
where the time goes in v1:
time: 226 us; the launch traced here: 225 us
  waiting for transfers between devices  113 us (50%)
  starting transfers between devices  48.1 us (21%)
  Pallas kernels  24.6 us (11%)
  local copies, waits for them, and re-layouts  21.7 us (10%)
  between operations  14.3 us (6%)
  other arithmetic  3.58 us (2%)
    ppermute x9, waiting for transfers between devices, along_z(): lax.ppermute(arrays[step], 'seq', z_pairs[step])  44.7 us
    ppermute x7, waiting for transfers between devices, shards(): piece = lax.ppermute(piece, 'seq', pairs)  30 us
    all_to_all x2, waiting for transfers between devices, exchange(): lax.all_to_all(array, 'seq', split_axis=0, concat_axis=0, tiled=True, axi...  24.3 us
    ppermute x9, starting transfers between devices, along_z(): lax.ppermute(arrays[step], 'seq', z_pairs[step])  12.9 us
    ppermute x4, starting transfers between devices, from_behind(): return lax.ppermute(shard, axis, pairs)  12.5 us
    unnamed x47, local copies, waits for them, and re-layouts  12.1 us
    all_to_all x2, starting transfers between devices, exchange(): lax.all_to_all(array, 'seq', split_axis=0, concat_axis=0, tiled=True, axi...  9.89 us
    ppermute x4, waiting for transfers between devices, from_behind(): return lax.ppermute(shard, axis, pairs)  8.23 us
  transfers between devices with their start and end apart: 27, of which 18 were waited for; matrix products, arithmetic and copies ran while one was open for 6% of the time, Pallas kernels for 10%

profile of v1, /device:TPU:10, one launch (start us, length us, event | category | flops | bytes accessed | tf_op | source)
XLA Modules:
  0.0 224.9 jit_solution(15905495661734357322)
XLA Ops:
  11.6 4.4 %collective-permute-done.3.k1_ref = bf16[64,1024]{1,0:T(8,128)(2,1)S(1)} collective-permute-done((bf16[64,1024]{1,0:T(8,128)(2,1)S(1)}, bf16[64,1024]{1,0:T(8,128)(2,1)S(1)}, u32[]{:S(2)}, u32[]{:S(2)}) %collective-permute-start.3) | collective-permute-done | bytes 131104 | tf_op jit(solution)/shard_map/ppermute | solution.py:28
  20.9 4.3 %collective-permute-start.2 = (bf16[64,1024]{1,0:T(8,128)(2,1)S(1)}, bf16[64,1024]{1,0:T(8,128)(2,1)S(1)}, u32[]{:S(2)}, u32[]{:S(2)}) collective-permute-start(bf16[64,1024]{1,0:T(8,128)(2,1)S(1)} %constant_dynamic-update-slice_fusion.own_ref), channel_id=1, source_target_pairs={{0,2},{1,3},{2,4},{3,5},{4,6},{5,7},{6,8},{7,9},{8,10},{9,11},{10,... | collective-permute-start | bytes 393224 | tf_op jit(solution)/shard_map/ppermute | solution.py:28
  27.2 4.3 %collective-permute-start = (bf16[64,1024]{1,0:T(8,128)(2,1)S(1)}, bf16[64,1024]{1,0:T(8,128)(2,1)S(1)}, u32[]{:S(2)}, u32[]{:S(2)}) collective-permute-start(bf16[64,1024]{1,0:T(8,128)(2,1)S(1)} %constant_dynamic-update-slice_fusion.own_ref), channel_id=1, source_target_pairs={{0,4},{1,5},{2,6},{3,7},{4,8},{5,9},{6,10},{7,11},{8,12},{9,13},{1... | collective-permute-start | bytes 393224 | tf_op jit(solution)/shard_map/ppermute | solution.py:28
  31.5 2.4 %collective-permute-done.1.k3_ref = bf16[64,1024]{1,0:T(8,128)(2,1)S(1)} collective-permute-done((bf16[64,1024]{1,0:T(8,128)(2,1)S(1)}, bf16[64,1024]{1,0:T(8,128)(2,1)S(1)}, u32[]{:S(2)}, u32[]{:S(2)}) %collective-permute-start.1) | collective-permute-done | bytes 131104 | tf_op jit(solution)/shard_map/ppermute | solution.py:28
  36.1 3.8 %attention.1 = (bf16[64,2048]{1,0:T(8,128)(2,1)}, bf16[64,2048]{1,0:T(8,128)(2,1)}, bf16[64,2048]{1,0:T(8,128)(2,1)}, bf16[64,2048]{1,0:T(8,128)(2,1)}) custom-call(s32[1]{0:T(128)} %bitcast.z_ref, s32[1]{0:T(128)} %bitcast.2.first_ref, s32[16]{0:T(128)} %lengths_ref.1, bf16[64,1536]{1,0:T(8,128)(2,1)} %q_ref.1, bf16[64,1024]{1,0:T(8,128)(2,1)} %copy-done.18, ...), custom_call_target="tpu_custom_call" | custom-call | flops 125829120 | bytes 3145728 | tf_op jit(solution)/shard_map/attention/pallas_call | solution.py:507
  45.8 3.3 %collective-permute-done.4.refs_1_ = bf16[64,2048]{1,0:T(8,128)(2,1)S(1)} collective-permute-done((bf16[64,2048]{1,0:T(8,128)(2,1)}, bf16[64,2048]{1,0:T(8,128)(2,1)S(1)}, u32[]{:S(2)}, u32[]{:S(2)}) %collective-permute-start.4) | collective-permute-done | bytes 262176 | tf_op jit(solution)/shard_map/ppermute | solution.py:487
  49.1 16.1 %collective-permute-done.5.refs_2_ = bf16[64,2048]{1,0:T(8,128)(2,1)S(1)} collective-permute-done((bf16[64,2048]{1,0:T(8,128)(2,1)}, bf16[64,2048]{1,0:T(8,128)(2,1)S(1)}, u32[]{:S(2)}, u32[]{:S(2)}) %collective-permute-start.5) | collective-permute-done | bytes 262176 | tf_op jit(solution)/shard_map/ppermute | solution.py:487
  71.5 2.8 %collective-permute-start.7 = (bf16[256,384]{1,0:T(8,128)(2,1)S(1)}, bf16[256,384]{1,0:T(8,128)(2,1)S(1)}, u32[]{:S(2)}, u32[]{:S(2)}) collective-permute-start(bf16[256,384]{1,0:T(8,128)(2,1)S(1)} %get-tuple-element.51.refs_0_), channel_id=1, source_target_pairs={{0,8},{1,9},{2,10},{3,11},{4,12},{5,13},{6,14},{7,15},{8,16},{9,17... | collective-permute-start | bytes 589832 | tf_op jit(solution)/shard_map/ppermute | solution.py:487
  77.6 8.8 %collective-permute-done.9.refs_3_ = bf16[256,384]{1,0:T(8,128)(2,1)S(1)} collective-permute-done((bf16[256,384]{1,0:T(8,128)(2,1)S(1)}, bf16[256,384]{1,0:T(8,128)(2,1)S(1)}, u32[]{:S(2)}, u32[]{:S(2)}) %collective-permute-start.9) | collective-permute-done | bytes 196640 | tf_op jit(solution)/shard_map/ppermute | solution.py:487
  89.3 4.5 %pick.1 = (bf16[256,1536]{1,0:T(8,128)(2,1)}, f32[64,1536]{1,0:T(8,128)}, bf16[8,96,1536]{2,1,0:T(8,128)(2,1)}) custom-call(s32[1]{0:T(128)} %bitcast.z_ref, bf16[768,256]{1,0:T(8,128)(2,1)} %copy-done.11, f32[1,1536]{1,0:T(1,128)} %reshape.36.gain_ref, bf16[256,384]{1,0:T(8,128)(2,1)} %copy-done.12, bf16[256,384]{1,0:T(8,128)(2,1)} %copy-done.22, ...), custom_call_target="tpu_custom_call" | custom-call | flops 603979776 | bytes 5242880 | tf_op jit(solution)/shard_map/pick/pallas_call | solution.py:568
  93.8 5.2 %all-to-all-start = ((bf16[8,96,1536]{2,1,0:T(8,128)(2,1)}), bf16[8,96,1536]{2,1,0:T(8,128)(2,1)S(1)}, u32[]{:S(2)}, u32[]{:S(2)}) async-start(bf16[8,96,1536]{2,1,0:T(8,128)(2,1)} %get-tuple-element.54), calls=%async_computation | async-start | bytes 4718592 | tf_op jit(solution)/shard_map/all_to_all | solution.py:460
  101.0 2.6 %collective-permute-start.15 = (bf16[4,32,4,128]{3,2,1,0:T(4,128)(2,1)S(1)}, bf16[4,32,4,128]{3,2,1,0:T(4,128)(2,1)S(1)}, u32[]{:S(2)}, u32[]{:S(2)}) collective-permute-start(bf16[4,32,4,128]{3,2,1,0:T(4,128)(2,1)S(1)} %get-tuple-element.75), channel_id=1, source_target_pairs={{0,6},{1,7},{2,0},{3,1},{4,2},{5,3},{6,4},{7,5},{8,14},{9,15},{10,... | collective-permute-start | bytes 393224 | tf_op jit(solution)/shard_map/ppermute | solution.py:564
  104.2 2.4 %collective-permute-start.12 = (bf16[4,32,4,128]{3,2,1,0:T(4,128)(2,1)S(1)}, bf16[4,32,4,128]{3,2,1,0:T(4,128)(2,1)S(1)}, u32[]{:S(2)}, u32[]{:S(2)}) collective-permute-start(bf16[4,32,4,128]{3,2,1,0:T(4,128)(2,1)S(1)} %get-tuple-element.78), channel_id=1, source_target_pairs={{0,3},{1,4},{2,5},{3,6},{4,7},{5,0},{6,1},{7,2},{8,11},{9,12},{10,... | collective-permute-start | bytes 393224 | tf_op jit(solution)/shard_map/ppermute | solution.py:564
  106.5 21.8 %collective-permute-done.16.refs_7_ = bf16[4,32,4,128]{3,2,1,0:T(4,128)(2,1)S(1)} collective-permute-done((bf16[4,32,4,128]{3,2,1,0:T(4,128)(2,1)S(1)}, bf16[4,32,4,128]{3,2,1,0:T(4,128)(2,1)S(1)}, u32[]{:S(2)}, u32[]{:S(2)}) %collective-permute-start.16) | collective-permute-done | bytes 131104 | tf_op jit(solution)/shard_map/ppermute | solution.py:564
  130.0 2.7 %collective-permute-done.15.refs_6_ = bf16[4,32,4,128]{3,2,1,0:T(4,128)(2,1)S(1)} collective-permute-done((bf16[4,32,4,128]{3,2,1,0:T(4,128)(2,1)S(1)}, bf16[4,32,4,128]{3,2,1,0:T(4,128)(2,1)S(1)}, u32[]{:S(2)}, u32[]{:S(2)}) %collective-permute-start.15) | collective-permute-done | bytes 131104 | tf_op jit(solution)/shard_map/ppermute | solution.py:564
  133.3 4.9 %collective-permute-done.13.refs_4_ = bf16[4,32,4,128]{3,2,1,0:T(4,128)(2,1)S(1)} collective-permute-done((bf16[4,32,4,128]{3,2,1,0:T(4,128)(2,1)S(1)}, bf16[4,32,4,128]{3,2,1,0:T(4,128)(2,1)S(1)}, u32[]{:S(2)}, u32[]{:S(2)}) %collective-permute-start.13) | collective-permute-done | bytes 131104 | tf_op jit(solution)/shard_map/ppermute | solution.py:564
  139.0 2.5 %collective-permute-start.17 = (bf16[8,32,4,128]{3,2,1,0:T(4,128)(2,1)S(1)}, bf16[8,32,4,128]{3,2,1,0:T(4,128)(2,1)}, u32[]{:S(2)}, u32[]{:S(2)}) collective-permute-start(bf16[8,32,4,128]{3,2,1,0:T(4,128)(2,1)S(1)} %get-tuple-element.60), channel_id=1, source_target_pairs={{0,8},{1,9},{2,10},{3,11},{4,12},{5,13},{6,14},{7,15},{8,16},{9,17... | collective-permute-start | bytes 786440 | tf_op jit(solution)/shard_map/ppermute | solution.py:599
  141.5 3.0 %collective-permute-start.18 = (bf16[8,32,4,128]{3,2,1,0:T(4,128)(2,1)S(1)}, bf16[8,32,4,128]{3,2,1,0:T(4,128)(2,1)}, u32[]{:S(2)}, u32[]{:S(2)}) collective-permute-start(bf16[8,32,4,128]{3,2,1,0:T(4,128)(2,1)S(1)} %get-tuple-element.61), channel_id=1, source_target_pairs={{0,16},{1,17},{2,18},{3,19},{4,20},{5,21},{6,22},{7,23},{8,24},{9,... | collective-permute-start | bytes 786440 | tf_op jit(solution)/shard_map/ppermute | solution.py:599
  144.4 6.3 %copy.35 = bf16[4,1536,2,256]{3,1,2,0:T(8,128)(2,1)} copy(bf16[4,1536,2,256]{3,2,1,0:T(2,128)(2,1)} %param.26) | data formatting | bytes 12582912 | tf_op jit(solution)/shard_map/optimization_barrier | solution.py:546
  152.2 8.0 %experts.1 = bf16[8,96,1536]{2,1,0:T(8,128)(2,1)} custom-call(bf16[8,96,1536]{2,1,0:T(8,128)(2,1)} %copy-done.13, bf16[4,2,1536,256]{3,2,1,0:T(8,128)(2,1)} %bitcast.53, bf16[4,256,1536]{2,1,0:T(8,128)(2,1)} %down_hbm.1), custom_call_target="tpu_custom_call" | custom-call | flops 1811939328 | bytes 14680064 | tf_op jit(solution)/shard_map/experts/pallas_call | solution.py:612
  162.3 2.7 %collective-permute-done.19 = bf16[8,32,4,128]{3,2,1,0:T(4,128)(2,1)} collective-permute-done((bf16[8,32,4,128]{3,2,1,0:T(4,128)(2,1)S(1)}, bf16[8,32,4,128]{3,2,1,0:T(4,128)(2,1)}, u32[]{:S(2)}, u32[]{:S(2)}) %collective-permute-start.19) | collective-permute-done | bytes 262176 | tf_op jit(solution)/shard_map/ppermute | solution.py:599
  165.0 4.7 %all-to-all-start.1 = ((bf16[8,96,1536]{2,1,0:T(8,128)(2,1)}), bf16[8,96,1536]{2,1,0:T(8,128)(2,1)S(1)}, u32[]{:S(2)}, u32[]{:S(2)}) async-start(bf16[8,96,1536]{2,1,0:T(8,128)(2,1)} %experts.1), calls=%async_computation.1 | async-start | bytes 4718592 | tf_op jit(solution)/shard_map/all_to_all | solution.py:460
  173.4 24.3 %all-to-all-done.1 = bf16[8,96,1536]{2,1,0:T(8,128)(2,1)S(1)} async-done(((bf16[8,96,1536]{2,1,0:T(8,128)(2,1)}), bf16[8,96,1536]{2,1,0:T(8,128)(2,1)S(1)}, u32[]{:S(2)}, u32[]{:S(2)}) %all-to-all-start.1) | async-done | bytes 2359328 | tf_op jit(solution)/shard_map/all_to_all | solution.py:460
  206.4 9.6 %collective-permute-done.21.refs_2_ = bf16[64,1536]{1,0:T(8,128)(2,1)S(1)} collective-permute-done((bf16[64,1536]{1,0:T(8,128)(2,1)S(1)}, bf16[64,1536]{1,0:T(8,128)(2,1)S(1)}, u32[]{:S(2)}, u32[]{:S(2)}) %collective-permute-start.21) | collective-permute-done | bytes 196640 | tf_op jit(solution)/shard_map/ppermute | solution.py:487
  (96 shorter events, 55.3 us)
Async XLA Ops:
  7.2 60.2 %all-gather.4.cloned.1.call-start = ((), (), s32[]{:S(2)}) async-start(), calls=%async_computation.2 | async-start | bytes 1327104 | tf_op jit(solution)/shard_map/all_gather | solution.py:471
  7.9 142.8 %all-gather.6.cloned.1.call-start = ((), (), s32[]{:S(2)}) async-start(), calls=%async_computation.3 | async-start | bytes 2654208 | tf_op jit(solution)/shard_map/all_gather | solution.py:504
  20.9 10.6 %collective-permute-start.2 = (bf16[64,1024]{1,0:T(8,128)(2,1)S(1)}, bf16[64,1024]{1,0:T(8,128)(2,1)S(1)}, u32[]{:S(2)}, u32[]{:S(2)}) collective-permute-start(bf16[64,1024]{1,0:T(8,128)(2,1)S(1)} %constant_dynamic-update-slice_fusion.own_ref), channel_id=1, source_target_pairs={{0,2},{1,3},{2,4},{3,5},{4,6},{5,7},{6,8},{7,9},{8,10},{9,11},{10,... | collective-permute-start | bytes 393224 | tf_op jit(solution)/shard_map/ppermute | solution.py:28
  25.2 8.7 %collective-permute-start.1 = (bf16[64,1024]{1,0:T(8,128)(2,1)S(1)}, bf16[64,1024]{1,0:T(8,128)(2,1)S(1)}, u32[]{:S(2)}, u32[]{:S(2)}) collective-permute-start(bf16[64,1024]{1,0:T(8,128)(2,1)S(1)} %constant_dynamic-update-slice_fusion.own_ref), channel_id=1, source_target_pairs={{0,3},{1,4},{2,5},{3,6},{4,7},{5,8},{6,9},{7,10},{8,11},{9,12},{10... | collective-permute-start | bytes 393224 | tf_op jit(solution)/shard_map/ppermute | solution.py:28
  27.2 8.2 %collective-permute-start = (bf16[64,1024]{1,0:T(8,128)(2,1)S(1)}, bf16[64,1024]{1,0:T(8,128)(2,1)S(1)}, u32[]{:S(2)}, u32[]{:S(2)}) collective-permute-start(bf16[64,1024]{1,0:T(8,128)(2,1)S(1)} %constant_dynamic-update-slice_fusion.own_ref), channel_id=1, source_target_pairs={{0,4},{1,5},{2,6},{3,7},{4,8},{5,9},{6,10},{7,11},{8,12},{9,13},{1... | collective-permute-start | bytes 393224 | tf_op jit(solution)/shard_map/ppermute | solution.py:28
  39.9 9.2 %collective-permute-start.4 = (bf16[64,2048]{1,0:T(8,128)(2,1)}, bf16[64,2048]{1,0:T(8,128)(2,1)S(1)}, u32[]{:S(2)}, u32[]{:S(2)}) collective-permute-start(bf16[64,2048]{1,0:T(8,128)(2,1)} %get-tuple-element.45), channel_id=1, source_target_pairs={{0,8},{1,9},{2,10},{3,11},{4,12},{5,13},{6,14},{7,15},{8,16},{9,17... | collective-permute-start | bytes 786440 | tf_op jit(solution)/shard_map/ppermute | solution.py:487
  41.5 23.7 %collective-permute-start.5 = (bf16[64,2048]{1,0:T(8,128)(2,1)}, bf16[64,2048]{1,0:T(8,128)(2,1)S(1)}, u32[]{:S(2)}, u32[]{:S(2)}) collective-permute-start(bf16[64,2048]{1,0:T(8,128)(2,1)} %get-tuple-element.46), channel_id=1, source_target_pairs={{0,16},{1,17},{2,18},{3,19},{4,20},{5,21},{6,22},{7,23},{8,24},{9,... | collective-permute-start | bytes 786440 | tf_op jit(solution)/shard_map/ppermute | solution.py:487
  43.8 23.6 %collective-permute-start.6 = (bf16[64,2048]{1,0:T(8,128)(2,1)}, bf16[64,2048]{1,0:T(8,128)(2,1)S(1)}, u32[]{:S(2)}, u32[]{:S(2)}) collective-permute-start(bf16[64,2048]{1,0:T(8,128)(2,1)} %get-tuple-element.47), channel_id=1, source_target_pairs={{0,24},{1,25},{2,26},{3,27},{4,28},{5,29},{6,30},{7,31},{8,0},{9,1... | collective-permute-start | bytes 786440 | tf_op jit(solution)/shard_map/ppermute | solution.py:487
  70.2 16.2 %collective-permute-start.9 = (bf16[256,384]{1,0:T(8,128)(2,1)S(1)}, bf16[256,384]{1,0:T(8,128)(2,1)S(1)}, u32[]{:S(2)}, u32[]{:S(2)}) collective-permute-start(bf16[256,384]{1,0:T(8,128)(2,1)S(1)} %get-tuple-element.51.refs_0_), channel_id=1, source_target_pairs={{0,24},{1,25},{2,26},{3,27},{4,28},{5,29},{6,30},{7,31},{8,0},{9,1... | collective-permute-start | bytes 589832 | tf_op jit(solution)/shard_map/ppermute | solution.py:487
  70.3 16.2 %collective-permute-start.8 = (bf16[256,384]{1,0:T(8,128)(2,1)S(1)}, bf16[256,384]{1,0:T(8,128)(2,1)S(1)}, u32[]{:S(2)}, u32[]{:S(2)}) collective-permute-start(bf16[256,384]{1,0:T(8,128)(2,1)S(1)} %get-tuple-element.51.refs_0_), channel_id=1, source_target_pairs={{0,16},{1,17},{2,18},{3,19},{4,20},{5,21},{6,22},{7,23},{8,24},{9,... | collective-permute-start | bytes 589832 | tf_op jit(solution)/shard_map/ppermute | solution.py:487
  71.5 17.1 %collective-permute-start.7 = (bf16[256,384]{1,0:T(8,128)(2,1)S(1)}, bf16[256,384]{1,0:T(8,128)(2,1)S(1)}, u32[]{:S(2)}, u32[]{:S(2)}) collective-permute-start(bf16[256,384]{1,0:T(8,128)(2,1)S(1)} %get-tuple-element.51.refs_0_), channel_id=1, source_target_pairs={{0,8},{1,9},{2,10},{3,11},{4,12},{5,13},{6,14},{7,15},{8,16},{9,17... | collective-permute-start | bytes 589832 | tf_op jit(solution)/shard_map/ppermute | solution.py:487
  93.8 56.9 %all-to-all-start = ((bf16[8,96,1536]{2,1,0:T(8,128)(2,1)}), bf16[8,96,1536]{2,1,0:T(8,128)(2,1)S(1)}, u32[]{:S(2)}, u32[]{:S(2)}) async-start(bf16[8,96,1536]{2,1,0:T(8,128)(2,1)} %get-tuple-element.54), calls=%async_computation | async-start | bytes 4718592 | tf_op jit(solution)/shard_map/all_to_all | solution.py:460
  100.9 27.5 %collective-permute-start.16 = (bf16[4,32,4,128]{3,2,1,0:T(4,128)(2,1)S(1)}, bf16[4,32,4,128]{3,2,1,0:T(4,128)(2,1)S(1)}, u32[]{:S(2)}, u32[]{:S(2)}) collective-permute-start(bf16[4,32,4,128]{3,2,1,0:T(4,128)(2,1)S(1)} %get-tuple-element.74), channel_id=1, source_target_pairs={{0,7},{1,0},{2,1},{3,2},{4,3},{5,4},{6,5},{7,6},{8,15},{9,8},{10,9... | collective-permute-start | bytes 393224 | tf_op jit(solution)/shard_map/ppermute | solution.py:564
  101.0 31.7 %collective-permute-start.15 = (bf16[4,32,4,128]{3,2,1,0:T(4,128)(2,1)S(1)}, bf16[4,32,4,128]{3,2,1,0:T(4,128)(2,1)S(1)}, u32[]{:S(2)}, u32[]{:S(2)}) collective-permute-start(bf16[4,32,4,128]{3,2,1,0:T(4,128)(2,1)S(1)} %get-tuple-element.75), channel_id=1, source_target_pairs={{0,6},{1,7},{2,0},{3,1},{4,2},{5,3},{6,4},{7,5},{8,14},{9,15},{10,... | collective-permute-start | bytes 393224 | tf_op jit(solution)/shard_map/ppermute | solution.py:564
  103.6 29.6 %collective-permute-start.14 = (bf16[4,32,4,128]{3,2,1,0:T(4,128)(2,1)S(1)}, bf16[4,32,4,128]{3,2,1,0:T(4,128)(2,1)S(1)}, u32[]{:S(2)}, u32[]{:S(2)}) collective-permute-start(bf16[4,32,4,128]{3,2,1,0:T(4,128)(2,1)S(1)} %get-tuple-element.76), channel_id=1, source_target_pairs={{0,5},{1,6},{2,7},{3,0},{4,1},{5,2},{6,3},{7,4},{8,13},{9,14},{10,... | collective-permute-start | bytes 393224 | tf_op jit(solution)/shard_map/ppermute | solution.py:564
  103.6 34.5 %collective-permute-start.13 = (bf16[4,32,4,128]{3,2,1,0:T(4,128)(2,1)S(1)}, bf16[4,32,4,128]{3,2,1,0:T(4,128)(2,1)S(1)}, u32[]{:S(2)}, u32[]{:S(2)}) collective-permute-start(bf16[4,32,4,128]{3,2,1,0:T(4,128)(2,1)S(1)} %get-tuple-element.77), channel_id=1, source_target_pairs={{0,4},{1,5},{2,6},{3,7},{4,0},{5,1},{6,2},{7,3},{8,12},{9,13},{10,... | collective-permute-start | bytes 393224 | tf_op jit(solution)/shard_map/ppermute | solution.py:564
  104.2 34.0 %collective-permute-start.12 = (bf16[4,32,4,128]{3,2,1,0:T(4,128)(2,1)S(1)}, bf16[4,32,4,128]{3,2,1,0:T(4,128)(2,1)S(1)}, u32[]{:S(2)}, u32[]{:S(2)}) collective-permute-start(bf16[4,32,4,128]{3,2,1,0:T(4,128)(2,1)S(1)} %get-tuple-element.78), channel_id=1, source_target_pairs={{0,3},{1,4},{2,5},{3,6},{4,7},{5,0},{6,1},{7,2},{8,11},{9,12},{10,... | collective-permute-start | bytes 393224 | tf_op jit(solution)/shard_map/ppermute | solution.py:564
  128.4 9.8 %collective-permute-start.11 = (bf16[4,32,4,128]{3,2,1,0:T(4,128)(2,1)S(1)}, bf16[4,32,4,128]{3,2,1,0:T(4,128)(2,1)S(1)}, u32[]{:S(2)}, u32[]{:S(2)}) collective-permute-start(bf16[4,32,4,128]{3,2,1,0:T(4,128)(2,1)S(1)} %get-tuple-element.79), channel_id=1, source_target_pairs={{0,2},{1,3},{2,4},{3,5},{4,6},{5,7},{6,0},{7,1},{8,10},{9,11},{10,... | collective-permute-start | bytes 393224 | tf_op jit(solution)/shard_map/ppermute | solution.py:564
  139.0 21.2 %collective-permute-start.17 = (bf16[8,32,4,128]{3,2,1,0:T(4,128)(2,1)S(1)}, bf16[8,32,4,128]{3,2,1,0:T(4,128)(2,1)}, u32[]{:S(2)}, u32[]{:S(2)}) collective-permute-start(bf16[8,32,4,128]{3,2,1,0:T(4,128)(2,1)S(1)} %get-tuple-element.60), channel_id=1, source_target_pairs={{0,8},{1,9},{2,10},{3,11},{4,12},{5,13},{6,14},{7,15},{8,16},{9,17... | collective-permute-start | bytes 786440 | tf_op jit(solution)/shard_map/ppermute | solution.py:599
  141.5 20.8 %collective-permute-start.18 = (bf16[8,32,4,128]{3,2,1,0:T(4,128)(2,1)S(1)}, bf16[8,32,4,128]{3,2,1,0:T(4,128)(2,1)}, u32[]{:S(2)}, u32[]{:S(2)}) collective-permute-start(bf16[8,32,4,128]{3,2,1,0:T(4,128)(2,1)S(1)} %get-tuple-element.61), channel_id=1, source_target_pairs={{0,16},{1,17},{2,18},{3,19},{4,20},{5,21},{6,22},{7,23},{8,24},{9,... | collective-permute-start | bytes 786440 | tf_op jit(solution)/shard_map/ppermute | solution.py:599
  144.4 20.5 %collective-permute-start.19 = (bf16[8,32,4,128]{3,2,1,0:T(4,128)(2,1)S(1)}, bf16[8,32,4,128]{3,2,1,0:T(4,128)(2,1)}, u32[]{:S(2)}, u32[]{:S(2)}) collective-permute-start(bf16[8,32,4,128]{3,2,1,0:T(4,128)(2,1)S(1)} %get-tuple-element.62), channel_id=1, source_target_pairs={{0,24},{1,25},{2,26},{3,27},{4,28},{5,29},{6,30},{7,31},{8,0},{9,1... | collective-permute-start | bytes 786440 | tf_op jit(solution)/shard_map/ppermute | solution.py:599
  165.0 32.7 %all-to-all-start.1 = ((bf16[8,96,1536]{2,1,0:T(8,128)(2,1)}), bf16[8,96,1536]{2,1,0:T(8,128)(2,1)S(1)}, u32[]{:S(2)}, u32[]{:S(2)}) async-start(bf16[8,96,1536]{2,1,0:T(8,128)(2,1)} %experts.1), calls=%async_computation.1 | async-start | bytes 4718592 | tf_op jit(solution)/shard_map/all_to_all | solution.py:460
  198.7 17.3 %collective-permute-start.21 = (bf16[64,1536]{1,0:T(8,128)(2,1)S(1)}, bf16[64,1536]{1,0:T(8,128)(2,1)S(1)}, u32[]{:S(2)}, u32[]{:S(2)}) collective-permute-start(bf16[64,1536]{1,0:T(8,128)(2,1)S(1)} %get-tuple-element.68), channel_id=1, source_target_pairs={{0,16},{1,17},{2,18},{3,19},{4,20},{5,21},{6,22},{7,23},{8,24},{9,... | collective-permute-start | bytes 589832 | tf_op jit(solution)/shard_map/ppermute | solution.py:487
  199.5 17.7 %collective-permute-start.22 = (bf16[64,1536]{1,0:T(8,128)(2,1)S(1)}, bf16[64,1536]{1,0:T(8,128)(2,1)S(1)}, u32[]{:S(2)}, u32[]{:S(2)}) collective-permute-start(bf16[64,1536]{1,0:T(8,128)(2,1)S(1)} %get-tuple-element.69), channel_id=1, source_target_pairs={{0,24},{1,25},{2,26},{3,27},{4,28},{5,29},{6,30},{7,31},{8,0},{9,1... | collective-permute-start | bytes 589832 | tf_op jit(solution)/shard_map/ppermute | solution.py:487
  (26 other events, 199.6 us)
Sparse Core Ops, SparseCore 0:
  9.9 29.4 all-gather.3
  41.2 30.6 all-gather.5

commit v2 on v1

--- a/solution.py
+++ b/solution.py
@@ -253,12 +253,11 @@
     out_ref[...] = out.astype(jnp.bfloat16)
 
 
-def regroup_kernel(z_ref, *refs):
-    pieces, outs = refs[:PLANE], refs[PLANE:]
+def regroup_kernel(z_ref, pieces_ref, *outs):
     for step, out in enumerate(outs):
         z = lax.rem(z_ref[0] + step, Z_SIZE)
-        for at, piece in enumerate(pieces):
-            out[at] = piece[z]
+        for at in range(PLANE):
+            out[at] = pieces_ref[at, z]
 
 
 def source_z(z_ref, step):
@@ -416,8 +415,7 @@
     for block in range(to_ref.shape[0]):
         source = table_ref[block]
         z_steps = lax.rem(lax.div(me, PLANE) - lax.div(source, PLANE) + Z_SIZE, Z_SIZE)
-        steps = lax.rem(lax.rem(me, PLANE) - lax.rem(source, PLANE) + PLANE, PLANE)
-        to_ref[block] = from_ref[z_steps * PLANE + steps]
+        to_ref[block] = from_ref[z_steps * PLANE + lax.rem(source, PLANE)]
 
 
 def params(mib=16):
@@ -448,7 +446,7 @@
     tokens, width = residual.shape
     devices = lax.axis_size("seq")
     me = lax.axis_index("seq")
-    z_index, plane_index = lax.div(me, PLANE), lax.rem(me, PLANE)
+    z_index = lax.div(me, PLANE)
     planes = [[p + PLANE * z for p in range(PLANE)] for z in range(Z_SIZE)]
     bf16, f32 = jnp.bfloat16, jnp.float32
     shape = jax.ShapeDtypeStruct
@@ -463,10 +461,6 @@
 
     own_kv = jnp.concatenate([key_vectors, value_vectors], axis=1)
     behind = [from_behind(own_kv, "seq", offset) for offset in range(REACH, 0, -1)]
-
-    behind[-1], route_ids, route_logits, shared_gate_up, shared_down = lax.optimization_barrier(
-        (behind[-1], route_ids, route_logits, shared_gate_up, shared_down)
-    )
 
     turned_weight = lax.all_gather(
         out_weight.T, "seq", axis=0, tiled=True, axis_index_groups=planes
@@ -500,8 +494,6 @@
     own_shared = jnp.concatenate(
         [jnp.transpose(shared_gate_up, (1, 2, 0)).reshape(-1, width), shared_down], axis=0
     )
-    info, own_shared = lax.optimization_barrier((info, own_shared))
-    shared_weight = lax.all_gather(own_shared, "seq", axis=0, axis_index_groups=planes)
 
     sent_width = width + part + info.shape[1]
     sent = pl.pallas_call(
@@ -514,6 +506,8 @@
         name="attention",
     )(z_scalar, scalar(me * tokens), lengths, queries, *behind, own_kv, residual, info)
 
+    sent, own_shared = lax.optimization_barrier((sent, own_shared))
+    shared_weight = lax.all_gather(own_shared, "seq", axis=0, axis_index_groups=planes)
     gathered = along_z(sent)
 
     mixed_part, info = pl.pallas_call(
@@ -550,19 +544,7 @@
     _, block_tokens, layers, kv_heads, head_size = cache_blocks.shape
     per_device = block_tokens // devices
     cache_view = cache_blocks.reshape(Z_SIZE, PLANE, per_device * layers, kv_heads, head_size)
-    in_plane = []
-    for step in range(PLANE):
-        piece = lax.dynamic_index_in_dim(
-            cache_view, lax.rem(plane_index + step, PLANE), axis=1, keepdims=False
-        )
-        if step:
-            pairs = [
-                (z * PLANE + p, z * PLANE + (p + step) % PLANE)
-                for z in range(Z_SIZE)
-                for p in range(PLANE)
-            ]
-            piece = lax.ppermute(piece, "seq", pairs)
-        in_plane.append(piece)
+    in_plane = exchange(jnp.transpose(cache_view, (1, 0, 2, 3, 4)), planes)
     gate_up = jnp.transpose(expert_gate_up, (0, 2, 1, 3))
 
     normed, own_mixed, outgoing = pl.pallas_call(
@@ -587,13 +569,13 @@
     arrived = exchange(outgoing, planes)
     grouped = pl.pallas_call(
         regroup_kernel,
-        out_shape=[shape((PLANE,) + in_plane[0].shape[1:], bf16)] * Z_SIZE,
-        in_specs=[SMEM] + [VMEM] * PLANE,
+        out_shape=[shape((PLANE,) + in_plane.shape[2:], bf16)] * Z_SIZE,
+        in_specs=[SMEM, VMEM],
         out_specs=[VMEM] * Z_SIZE,
         compiler_params=params(),
         cost_estimate=cost(0, 2 * MIB),
         name="regroup",
-    )(z_scalar, *in_plane)
+    )(z_scalar, in_plane)
     arrived_cache = [grouped[0]]
     for step in range(1, Z_SIZE):
         arrived_cache.append(lax.ppermute(grouped[step], "seq", z_pairs[step]))

time: 226 us -> 199 us (0.88)
  waiting for transfers between devices: 113 us -> 90.2 us
  starting transfers between devices: 48.1 us -> 45.8 us
    ppermute x7 -> x0, waiting for transfers between devices: 30 us -> none  [shards(): piece = lax.ppermute(piece, 'seq', pairs)]
    all_to_all x2 -> x3, waiting for transfers between devices: 24.3 us -> 39.9 us  [exchange(): lax.all_to_all(array, 'seq', split_axis=0, concat_axis=0, tiled=True, axi...]
    ppermute x4, waiting for transfers between devices: 8.23 us -> 0.01 us  [from_behind(): return lax.ppermute(shard, axis, pairs)]
    ppermute x7 -> x0, starting transfers between devices: 7.29 us -> none  [shards(): piece = lax.ppermute(piece, 'seq', pairs)]
    ppermute x9, waiting for transfers between devices: 44.7 us -> 49.6 us  [along_z(): lax.ppermute(arrays[step], 'seq', z_pairs[step])]
    ppermute x3, waiting for transfers between devices: 4.79 us -> 0.01 us  [shards(): arrived_cache.append(lax.ppermute(grouped[step], 'seq', z_pairs[step]))]
    all_to_all x2 -> x3, starting transfers between devices: 9.89 us -> 14 us  [exchange(): lax.all_to_all(array, 'seq', split_axis=0, concat_axis=0, tiled=True, axi...]
    unnamed x47 -> x59, local copies, waits for them, and re-layouts: 12.1 us -> 11.5 us
  transfers between devices with their start and end apart: 27 -> 21, of which waited for: 18 -> 10; matrix products, arithmetic and copies ran while one was open for 6% -> 6% of each run, Pallas kernels for 10% -> 11%
where the time goes in v2:
time: 199 us; the launch traced here: 198 us
  waiting for transfers between devices  90.2 us (45%)
  starting transfers between devices  45.8 us (23%)
  Pallas kernels  24.5 us (12%)
  local copies, waits for them, and re-layouts  20.7 us (10%)
  between operations  14.4 us (7%)
  other arithmetic  2.47 us (1%)
    ppermute x9, waiting for transfers between devices, along_z(): lax.ppermute(arrays[step], 'seq', z_pairs[step])  49.6 us
    all_to_all x3, waiting for transfers between devices, exchange(): lax.all_to_all(array, 'seq', split_axis=0, concat_axis=0, tiled=True, axi...  39.9 us
    all_to_all x3, starting transfers between devices, exchange(): lax.all_to_all(array, 'seq', split_axis=0, concat_axis=0, tiled=True, axi...  14 us
    ppermute x9, starting transfers between devices, along_z(): lax.ppermute(arrays[step], 'seq', z_pairs[step])  13.3 us
    ppermute x4, starting transfers between devices, from_behind(): return lax.ppermute(shard, axis, pairs)  13.1 us
    unnamed x59, local copies, waits for them, and re-layouts  11.5 us
    pallas_call x1, Pallas kernels, shards(): pl.pallas_call(experts_kernel, out_shape=shape((PLANE, picked, width), bf...  7.97 us
    optimization_barrier x1, local copies, waits for them, and re-layouts, shards(): lax.optimization_barrier((onehot, cache_blocks, expert_gate_up))  6.29 us
  transfers between devices with their start and end apart: 21, of which 10 were waited for; matrix products, arithmetic and copies ran while one was open for 6% of the time, Pallas kernels for 11%

profile of v2, /device:TPU:10, one launch (start us, length us, event | category | flops | bytes accessed | tf_op | source)
XLA Modules:
  0.0 197.9 jit_solution(8967839913920636752)
XLA Ops:
  11.6 3.4 %collective-permute-start.2 = (bf16[64,1024]{1,0:T(8,128)(2,1)S(1)}, bf16[64,1024]{1,0:T(8,128)(2,1)S(1)}, u32[]{:S(2)}, u32[]{:S(2)}) collective-permute-start(bf16[64,1024]{1,0:T(8,128)(2,1)S(1)} %constant_dynamic-update-slice_fusion.own_ref), channel_id=1, source_target_pairs={{0,2},{1,3},{2,4},{3,5},{4,6},{5,7},{6,8},{7,9},{8,10},{9,11},{10,... | collective-permute-start | bytes 393224 | tf_op jit(solution)/shard_map/ppermute | solution.py:28
  15.0 4.3 %collective-permute-start.1 = (bf16[64,1024]{1,0:T(8,128)(2,1)S(1)}, bf16[64,1024]{1,0:T(8,128)(2,1)S(1)}, u32[]{:S(2)}, u32[]{:S(2)}) collective-permute-start(bf16[64,1024]{1,0:T(8,128)(2,1)S(1)} %constant_dynamic-update-slice_fusion.own_ref), channel_id=1, source_target_pairs={{0,3},{1,4},{2,5},{3,6},{4,7},{5,8},{6,9},{7,10},{8,11},{9,12},{10... | collective-permute-start | bytes 393224 | tf_op jit(solution)/shard_map/ppermute | solution.py:28
  19.3 3.4 %collective-permute-start = (bf16[64,1024]{1,0:T(8,128)(2,1)S(1)}, bf16[64,1024]{1,0:T(8,128)(2,1)S(1)}, u32[]{:S(2)}, u32[]{:S(2)}) collective-permute-start(bf16[64,1024]{1,0:T(8,128)(2,1)S(1)} %constant_dynamic-update-slice_fusion.own_ref), channel_id=1, source_target_pairs={{0,4},{1,5},{2,6},{3,7},{4,8},{5,9},{6,10},{7,11},{8,12},{9,13},{1... | collective-permute-start | bytes 393224 | tf_op jit(solution)/shard_map/ppermute | solution.py:28
  28.5 3.8 %attention.1 = (bf16[64,2048]{1,0:T(8,128)(2,1)}, bf16[64,2048]{1,0:T(8,128)(2,1)}, bf16[64,2048]{1,0:T(8,128)(2,1)}, bf16[64,2048]{1,0:T(8,128)(2,1)}) custom-call(s32[1]{0:T(128)} %bitcast.z_ref, s32[1]{0:T(128)} %bitcast.2.first_ref, s32[16]{0:T(128)} %lengths_ref.1, bf16[64,1536]{1,0:T(8,128)(2,1)} %q_ref.1, bf16[64,1024]{1,0:T(8,128)(2,1)} %copy-done.24, ...), custom_call_target="tpu_custom_call" | custom-call | flops 125829120 | bytes 3145728 | tf_op jit(solution)/shard_map/attention/pallas_call | solution.py:499
  35.7 16.6 %collective-permute-done.4.refs_1_ = bf16[64,2048]{1,0:T(8,128)(2,1)S(1)} collective-permute-done((bf16[64,2048]{1,0:T(8,128)(2,1)}, bf16[64,2048]{1,0:T(8,128)(2,1)S(1)}, u32[]{:S(2)}, u32[]{:S(2)}) %collective-permute-start.4) | collective-permute-done | bytes 262176 | tf_op jit(solution)/shard_map/ppermute | solution.py:481
  52.3 3.5 %collective-permute-done.5.refs_2_ = bf16[64,2048]{1,0:T(8,128)(2,1)S(1)} collective-permute-done((bf16[64,2048]{1,0:T(8,128)(2,1)}, bf16[64,2048]{1,0:T(8,128)(2,1)S(1)}, u32[]{:S(2)}, u32[]{:S(2)}) %collective-permute-start.5) | collective-permute-done | bytes 262176 | tf_op jit(solution)/shard_map/ppermute | solution.py:481
  64.4 4.3 %all-to-all-start.1 = ((bf16[8,4,32,4,128]{4,3,2,1,0:T(4,128)(2,1)}), bf16[8,4,32,4,128]{4,3,2,1,0:T(4,128)(2,1)S(1)}, u32[]{:S(2)}, u32[]{:S(2)}) async-start(bf16[8,4,32,4,128]{4,3,2,1,0:T(4,128)(2,1)} %bitcast.19), calls=%async_computation.1 | async-start | bytes 2097152 | tf_op jit(solution)/shard_map/all_to_all | solution.py:458
  70.3 2.9 %collective-permute-start.7 = (bf16[256,384]{1,0:T(8,128)(2,1)S(1)}, bf16[256,384]{1,0:T(8,128)(2,1)S(1)}, u32[]{:S(2)}, u32[]{:S(2)}) collective-permute-start(bf16[256,384]{1,0:T(8,128)(2,1)S(1)} %get-tuple-element.47.refs_0_), channel_id=1, source_target_pairs={{0,8},{1,9},{2,10},{3,11},{4,12},{5,13},{6,14},{7,15},{8,16},{9,17... | collective-permute-start | bytes 589832 | tf_op jit(solution)/shard_map/ppermute | solution.py:481
  73.8 11.0 %collective-permute-done.9.refs_3_ = bf16[256,384]{1,0:T(8,128)(2,1)S(1)} collective-permute-done((bf16[256,384]{1,0:T(8,128)(2,1)S(1)}, bf16[256,384]{1,0:T(8,128)(2,1)S(1)}, u32[]{:S(2)}, u32[]{:S(2)}) %collective-permute-start.9) | collective-permute-done | bytes 196640 | tf_op jit(solution)/shard_map/ppermute | solution.py:481
  84.9 2.6 %collective-permute-done.7.refs_1_ = bf16[256,384]{1,0:T(8,128)(2,1)S(1)} collective-permute-done((bf16[256,384]{1,0:T(8,128)(2,1)S(1)}, bf16[256,384]{1,0:T(8,128)(2,1)S(1)}, u32[]{:S(2)}, u32[]{:S(2)}) %collective-permute-start.7) | collective-permute-done | bytes 196640 | tf_op jit(solution)/shard_map/ppermute | solution.py:481
  88.1 4.5 %pick.1 = (bf16[256,1536]{1,0:T(8,128)(2,1)}, f32[64,1536]{1,0:T(8,128)}, bf16[8,96,1536]{2,1,0:T(8,128)(2,1)}) custom-call(s32[1]{0:T(128)} %bitcast.z_ref, bf16[768,256]{1,0:T(8,128)(2,1)} %copy-done.11, f32[1,1536]{1,0:T(1,128)} %reshape.36.gain_ref, bf16[256,384]{1,0:T(8,128)(2,1)} %copy-done.12, bf16[256,384]{1,0:T(8,128)(2,1)} %copy-done.28, ...), custom_call_target="tpu_custom_call" | custom-call | flops 603979776 | bytes 5242880 | tf_op jit(solution)/shard_map/pick/pallas_call | solution.py:550
  92.7 4.6 %all-to-all-start = ((bf16[8,96,1536]{2,1,0:T(8,128)(2,1)}), bf16[8,96,1536]{2,1,0:T(8,128)(2,1)}, u32[]{:S(2)}, u32[]{:S(2)}) async-start(bf16[8,96,1536]{2,1,0:T(8,128)(2,1)} %get-tuple-element.50), calls=%async_computation | async-start | bytes 4718592 | tf_op jit(solution)/shard_map/all_to_all | solution.py:458
  98.1 2.5 %collective-permute-start.10 = (bf16[8,32,4,128]{3,2,1,0:T(4,128)(2,1)S(1)}, bf16[8,32,4,128]{3,2,1,0:T(4,128)(2,1)S(1)}, u32[]{:S(2)}, u32[]{:S(2)}) collective-permute-start(bf16[8,32,4,128]{3,2,1,0:T(4,128)(2,1)S(1)} %get-tuple-element.56), channel_id=1, source_target_pairs={{0,8},{1,9},{2,10},{3,11},{4,12},{5,13},{6,14},{7,15},{8,16},{9,17... | collective-permute-start | bytes 786440 | tf_op jit(solution)/shard_map/ppermute | solution.py:581
  100.6 2.9 %collective-permute-start.11 = (bf16[8,32,4,128]{3,2,1,0:T(4,128)(2,1)S(1)}, bf16[8,32,4,128]{3,2,1,0:T(4,128)(2,1)S(1)}, u32[]{:S(2)}, u32[]{:S(2)}) collective-permute-start(bf16[8,32,4,128]{3,2,1,0:T(4,128)(2,1)S(1)} %get-tuple-element.57), channel_id=1, source_target_pairs={{0,16},{1,17},{2,18},{3,19},{4,20},{5,21},{6,22},{7,23},{8,24},{9,... | collective-permute-start | bytes 786440 | tf_op jit(solution)/shard_map/ppermute | solution.py:581
  103.4 6.3 %copy.25 = bf16[4,1536,2,256]{3,1,2,0:T(8,128)(2,1)} copy(bf16[4,1536,2,256]{3,2,1,0:T(2,128)(2,1)} %param.26) | data formatting | bytes 12582912 | tf_op jit(solution)/shard_map/optimization_barrier | solution.py:540
  109.7 15.7 %all-to-all-done.rows_hbm = bf16[8,96,1536]{2,1,0:T(8,128)(2,1)} async-done(((bf16[8,96,1536]{2,1,0:T(8,128)(2,1)}), bf16[8,96,1536]{2,1,0:T(8,128)(2,1)}, u32[]{:S(2)}, u32[]{:S(2)}) %all-to-all-start) | async-done | bytes 2359328 | tf_op jit(solution)/shard_map/all_to_all | solution.py:458
  125.4 8.0 %experts.1 = bf16[8,96,1536]{2,1,0:T(8,128)(2,1)} custom-call(bf16[8,96,1536]{2,1,0:T(8,128)(2,1)} %all-to-all-done.rows_hbm, bf16[4,2,1536,256]{3,2,1,0:T(8,128)(2,1)} %bitcast.24, bf16[4,256,1536]{2,1,0:T(8,128)(2,1)} %down_hbm.1), custom_call_target="tpu_custom_call" | custom-call | flops 1811939328 | bytes 14680064 | tf_op jit(solution)/shard_map/experts/pallas_call | solution.py:594
  134.2 5.0 %all-to-all-start.2 = ((bf16[8,96,1536]{2,1,0:T(8,128)(2,1)}), bf16[8,96,1536]{2,1,0:T(8,128)(2,1)S(1)}, u32[]{:S(2)}, u32[]{:S(2)}) async-start(bf16[8,96,1536]{2,1,0:T(8,128)(2,1)} %experts.1), calls=%async_computation.2 | async-start | bytes 4718592 | tf_op jit(solution)/shard_map/all_to_all | solution.py:458
  143.0 24.3 %all-to-all-done.2 = bf16[8,96,1536]{2,1,0:T(8,128)(2,1)S(1)} async-done(((bf16[8,96,1536]{2,1,0:T(8,128)(2,1)}), bf16[8,96,1536]{2,1,0:T(8,128)(2,1)S(1)}, u32[]{:S(2)}, u32[]{:S(2)}) %all-to-all-start.2) | async-done | bytes 2359328 | tf_op jit(solution)/shard_map/all_to_all | solution.py:458
  168.2 2.5 %collective-permute-start.13 = (bf16[64,1536]{1,0:T(8,128)(2,1)S(1)}, bf16[64,1536]{1,0:T(8,128)(2,1)S(1)}, u32[]{:S(2)}, u32[]{:S(2)}) collective-permute-start(bf16[64,1536]{1,0:T(8,128)(2,1)S(1)} %get-tuple-element.63), channel_id=1, source_target_pairs={{0,8},{1,9},{2,10},{3,11},{4,12},{5,13},{6,14},{7,15},{8,16},{9,17... | collective-permute-start | bytes 589832 | tf_op jit(solution)/shard_map/ppermute | solution.py:481
  170.8 2.8 %collective-permute-start.14 = (bf16[64,1536]{1,0:T(8,128)(2,1)S(1)}, bf16[64,1536]{1,0:T(8,128)(2,1)S(1)}, u32[]{:S(2)}, u32[]{:S(2)}) collective-permute-start(bf16[64,1536]{1,0:T(8,128)(2,1)S(1)} %get-tuple-element.64), channel_id=1, source_target_pairs={{0,16},{1,17},{2,18},{3,19},{4,20},{5,21},{6,22},{7,23},{8,24},{9,... | collective-permute-start | bytes 589832 | tf_op jit(solution)/shard_map/ppermute | solution.py:481
  176.1 8.2 %collective-permute-done.13.refs_1_ = bf16[64,1536]{1,0:T(8,128)(2,1)S(1)} collective-permute-done((bf16[64,1536]{1,0:T(8,128)(2,1)S(1)}, bf16[64,1536]{1,0:T(8,128)(2,1)S(1)}, u32[]{:S(2)}, u32[]{:S(2)}) %collective-permute-start.13) | collective-permute-done | bytes 196640 | tf_op jit(solution)/shard_map/ppermute | solution.py:481
  184.3 3.5 %collective-permute-done.14.refs_2_ = bf16[64,1536]{1,0:T(8,128)(2,1)S(1)} collective-permute-done((bf16[64,1536]{1,0:T(8,128)(2,1)S(1)}, bf16[64,1536]{1,0:T(8,128)(2,1)S(1)}, u32[]{:S(2)}, u32[]{:S(2)}) %collective-permute-start.14) | collective-permute-done | bytes 196640 | tf_op jit(solution)/shard_map/ppermute | solution.py:481
  187.8 2.5 %collective-permute-done.15.refs_3_ = bf16[64,1536]{1,0:T(8,128)(2,1)S(1)} collective-permute-done((bf16[64,1536]{1,0:T(8,128)(2,1)S(1)}, bf16[64,1536]{1,0:T(8,128)(2,1)S(1)}, u32[]{:S(2)}, u32[]{:S(2)}) %collective-permute-start.15) | collective-permute-done | bytes 196640 | tf_op jit(solution)/shard_map/ppermute | solution.py:481
  (96 shorter events, 34.4 us)
Async XLA Ops:
  7.2 50.3 %all-gather.4.cloned.1.call-start = ((), (), s32[]{:S(2)}) async-start(), calls=%async_computation.3 | async-start | bytes 1327104 | tf_op jit(solution)/shard_map/all_gather | solution.py:465
  7.9 101.8 %all-gather.6.cloned.1.call-start = ((), (), s32[]{:S(2)}) async-start(), calls=%async_computation.4 | async-start | bytes 2654208 | tf_op jit(solution)/shard_map/all_gather | solution.py:510
  9.6 18.1 %collective-permute-start.3 = (bf16[64,1024]{1,0:T(8,128)(2,1)S(1)}, bf16[64,1024]{1,0:T(8,128)(2,1)S(1)}, u32[]{:S(2)}, u32[]{:S(2)}) collective-permute-start(bf16[64,1024]{1,0:T(8,128)(2,1)S(1)} %constant_dynamic-update-slice_fusion.own_ref), channel_id=1, source_target_pairs={{0,1},{1,2},{2,3},{3,4},{4,5},{5,6},{6,7},{7,8},{8,9},{9,10},{10,1... | collective-permute-start | bytes 393224 | tf_op jit(solution)/shard_map/ppermute | solution.py:28
  11.6 16.2 %collective-permute-start.2 = (bf16[64,1024]{1,0:T(8,128)(2,1)S(1)}, bf16[64,1024]{1,0:T(8,128)(2,1)S(1)}, u32[]{:S(2)}, u32[]{:S(2)}) collective-permute-start(bf16[64,1024]{1,0:T(8,128)(2,1)S(1)} %constant_dynamic-update-slice_fusion.own_ref), channel_id=1, source_target_pairs={{0,2},{1,3},{2,4},{3,5},{4,6},{5,7},{6,8},{7,9},{8,10},{9,11},{10,... | collective-permute-start | bytes 393224 | tf_op jit(solution)/shard_map/ppermute | solution.py:28
  15.0 12.8 %collective-permute-start.1 = (bf16[64,1024]{1,0:T(8,128)(2,1)S(1)}, bf16[64,1024]{1,0:T(8,128)(2,1)S(1)}, u32[]{:S(2)}, u32[]{:S(2)}) collective-permute-start(bf16[64,1024]{1,0:T(8,128)(2,1)S(1)} %constant_dynamic-update-slice_fusion.own_ref), channel_id=1, source_target_pairs={{0,3},{1,4},{2,5},{3,6},{4,7},{5,8},{6,9},{7,10},{8,11},{9,12},{10... | collective-permute-start | bytes 393224 | tf_op jit(solution)/shard_map/ppermute | solution.py:28
  19.3 8.5 %collective-permute-start = (bf16[64,1024]{1,0:T(8,128)(2,1)S(1)}, bf16[64,1024]{1,0:T(8,128)(2,1)S(1)}, u32[]{:S(2)}, u32[]{:S(2)}) collective-permute-start(bf16[64,1024]{1,0:T(8,128)(2,1)S(1)} %constant_dynamic-update-slice_fusion.own_ref), channel_id=1, source_target_pairs={{0,4},{1,5},{2,6},{3,7},{4,8},{5,9},{6,10},{7,11},{8,12},{9,13},{1... | collective-permute-start | bytes 393224 | tf_op jit(solution)/shard_map/ppermute | solution.py:28
  24.1 38.8 %copy-start.13 = (bf16[1,128,8,4,128]{4,3,2,1,0:T(4,128)(2,1)S(1)}, bf16[1,128,8,4,128]{4,3,2,1,0:T(4,128)(2,1)}, u32[]{:S(2)}) copy-start(bf16[1,128,8,4,128]{4,3,2,1,0:T(4,128)(2,1)} %param.28) | copy-start | bytes 3145732
  32.3 19.9 %collective-permute-start.4 = (bf16[64,2048]{1,0:T(8,128)(2,1)}, bf16[64,2048]{1,0:T(8,128)(2,1)S(1)}, u32[]{:S(2)}, u32[]{:S(2)}) collective-permute-start(bf16[64,2048]{1,0:T(8,128)(2,1)} %get-tuple-element.41), channel_id=1, source_target_pairs={{0,8},{1,9},{2,10},{3,11},{4,12},{5,13},{6,14},{7,15},{8,16},{9,17... | collective-permute-start | bytes 786440 | tf_op jit(solution)/shard_map/ppermute | solution.py:481
  33.9 21.8 %collective-permute-start.5 = (bf16[64,2048]{1,0:T(8,128)(2,1)}, bf16[64,2048]{1,0:T(8,128)(2,1)S(1)}, u32[]{:S(2)}, u32[]{:S(2)}) collective-permute-start(bf16[64,2048]{1,0:T(8,128)(2,1)} %get-tuple-element.42), channel_id=1, source_target_pairs={{0,16},{1,17},{2,18},{3,19},{4,20},{5,21},{6,22},{7,23},{8,24},{9,... | collective-permute-start | bytes 786440 | tf_op jit(solution)/shard_map/ppermute | solution.py:481
  35.2 22.2 %collective-permute-start.6 = (bf16[64,2048]{1,0:T(8,128)(2,1)}, bf16[64,2048]{1,0:T(8,128)(2,1)S(1)}, u32[]{:S(2)}, u32[]{:S(2)}) collective-permute-start(bf16[64,2048]{1,0:T(8,128)(2,1)} %get-tuple-element.43), channel_id=1, source_target_pairs={{0,24},{1,25},{2,26},{3,27},{4,28},{5,29},{6,30},{7,31},{8,0},{9,1... | collective-permute-start | bytes 786440 | tf_op jit(solution)/shard_map/ppermute | solution.py:481
  60.2 27.2 %copy-start.12 = (bf16[256,384]{1,0:T(8,128)(2,1)}, bf16[256,384]{1,0:T(8,128)(2,1)S(1)}, u32[]{:S(2)}) copy-start(bf16[256,384]{1,0:T(8,128)(2,1)S(1)} %get-tuple-element.47.refs_0_) | copy-start | bytes 589828
  64.4 28.3 %all-to-all-start.1 = ((bf16[8,4,32,4,128]{4,3,2,1,0:T(4,128)(2,1)}), bf16[8,4,32,4,128]{4,3,2,1,0:T(4,128)(2,1)S(1)}, u32[]{:S(2)}, u32[]{:S(2)}) async-start(bf16[8,4,32,4,128]{4,3,2,1,0:T(4,128)(2,1)} %bitcast.19), calls=%async_computation.1 | async-start | bytes 2097152 | tf_op jit(solution)/shard_map/all_to_all | solution.py:458
  68.7 16.2 %collective-permute-start.9 = (bf16[256,384]{1,0:T(8,128)(2,1)S(1)}, bf16[256,384]{1,0:T(8,128)(2,1)S(1)}, u32[]{:S(2)}, u32[]{:S(2)}) collective-permute-start(bf16[256,384]{1,0:T(8,128)(2,1)S(1)} %get-tuple-element.47.refs_0_), channel_id=1, source_target_pairs={{0,24},{1,25},{2,26},{3,27},{4,28},{5,29},{6,30},{7,31},{8,0},{9,1... | collective-permute-start | bytes 589832 | tf_op jit(solution)/shard_map/ppermute | solution.py:481
  68.7 16.2 %collective-permute-start.8 = (bf16[256,384]{1,0:T(8,128)(2,1)S(1)}, bf16[256,384]{1,0:T(8,128)(2,1)S(1)}, u32[]{:S(2)}, u32[]{:S(2)}) collective-permute-start(bf16[256,384]{1,0:T(8,128)(2,1)S(1)} %get-tuple-element.47.refs_0_), channel_id=1, source_target_pairs={{0,16},{1,17},{2,18},{3,19},{4,20},{5,21},{6,22},{7,23},{8,24},{9,... | collective-permute-start | bytes 589832 | tf_op jit(solution)/shard_map/ppermute | solution.py:481
  70.3 17.2 %collective-permute-start.7 = (bf16[256,384]{1,0:T(8,128)(2,1)S(1)}, bf16[256,384]{1,0:T(8,128)(2,1)S(1)}, u32[]{:S(2)}, u32[]{:S(2)}) collective-permute-start(bf16[256,384]{1,0:T(8,128)(2,1)S(1)} %get-tuple-element.47.refs_0_), channel_id=1, source_target_pairs={{0,8},{1,9},{2,10},{3,11},{4,12},{5,13},{6,14},{7,15},{8,16},{9,17... | collective-permute-start | bytes 589832 | tf_op jit(solution)/shard_map/ppermute | solution.py:481
  92.7 32.7 %all-to-all-start = ((bf16[8,96,1536]{2,1,0:T(8,128)(2,1)}), bf16[8,96,1536]{2,1,0:T(8,128)(2,1)}, u32[]{:S(2)}, u32[]{:S(2)}) async-start(bf16[8,96,1536]{2,1,0:T(8,128)(2,1)} %get-tuple-element.50), calls=%async_computation | async-start | bytes 4718592 | tf_op jit(solution)/shard_map/all_to_all | solution.py:458
  98.1 35.3 %collective-permute-start.10 = (bf16[8,32,4,128]{3,2,1,0:T(4,128)(2,1)S(1)}, bf16[8,32,4,128]{3,2,1,0:T(4,128)(2,1)S(1)}, u32[]{:S(2)}, u32[]{:S(2)}) collective-permute-start(bf16[8,32,4,128]{3,2,1,0:T(4,128)(2,1)S(1)} %get-tuple-element.56), channel_id=1, source_target_pairs={{0,8},{1,9},{2,10},{3,11},{4,12},{5,13},{6,14},{7,15},{8,16},{9,17... | collective-permute-start | bytes 786440 | tf_op jit(solution)/shard_map/ppermute | solution.py:581
  100.6 32.8 %collective-permute-start.11 = (bf16[8,32,4,128]{3,2,1,0:T(4,128)(2,1)S(1)}, bf16[8,32,4,128]{3,2,1,0:T(4,128)(2,1)S(1)}, u32[]{:S(2)}, u32[]{:S(2)}) collective-permute-start(bf16[8,32,4,128]{3,2,1,0:T(4,128)(2,1)S(1)} %get-tuple-element.57), channel_id=1, source_target_pairs={{0,16},{1,17},{2,18},{3,19},{4,20},{5,21},{6,22},{7,23},{8,24},{9,... | collective-permute-start | bytes 786440 | tf_op jit(solution)/shard_map/ppermute | solution.py:581
  103.4 30.0 %collective-permute-start.12 = (bf16[8,32,4,128]{3,2,1,0:T(4,128)(2,1)S(1)}, bf16[8,32,4,128]{3,2,1,0:T(4,128)(2,1)S(1)}, u32[]{:S(2)}, u32[]{:S(2)}) collective-permute-start(bf16[8,32,4,128]{3,2,1,0:T(4,128)(2,1)S(1)} %get-tuple-element.58), channel_id=1, source_target_pairs={{0,24},{1,25},{2,26},{3,27},{4,28},{5,29},{6,30},{7,31},{8,0},{9,1... | collective-permute-start | bytes 786440 | tf_op jit(solution)/shard_map/ppermute | solution.py:581
  134.2 33.0 %all-to-all-start.2 = ((bf16[8,96,1536]{2,1,0:T(8,128)(2,1)}), bf16[8,96,1536]{2,1,0:T(8,128)(2,1)S(1)}, u32[]{:S(2)}, u32[]{:S(2)}) async-start(bf16[8,96,1536]{2,1,0:T(8,128)(2,1)} %experts.1), calls=%async_computation.2 | async-start | bytes 4718592 | tf_op jit(solution)/shard_map/all_to_all | solution.py:458
  168.2 22.1 %copy-start.3 = (f32[64,1536]{1,0:T(8,128)S(1)}, f32[64,1536]{1,0:T(8,128)}, u32[]{:S(2)}) copy-start(f32[64,1536]{1,0:T(8,128)} %get-tuple-element.48.mixed_ref) | copy-start | bytes 1179652
  168.2 16.1 %collective-permute-start.13 = (bf16[64,1536]{1,0:T(8,128)(2,1)S(1)}, bf16[64,1536]{1,0:T(8,128)(2,1)S(1)}, u32[]{:S(2)}, u32[]{:S(2)}) collective-permute-start(bf16[64,1536]{1,0:T(8,128)(2,1)S(1)} %get-tuple-element.63), channel_id=1, source_target_pairs={{0,8},{1,9},{2,10},{3,11},{4,12},{5,13},{6,14},{7,15},{8,16},{9,17... | collective-permute-start | bytes 589832 | tf_op jit(solution)/shard_map/ppermute | solution.py:481
  170.8 17.0 %collective-permute-start.14 = (bf16[64,1536]{1,0:T(8,128)(2,1)S(1)}, bf16[64,1536]{1,0:T(8,128)(2,1)S(1)}, u32[]{:S(2)}, u32[]{:S(2)}) collective-permute-start(bf16[64,1536]{1,0:T(8,128)(2,1)S(1)} %get-tuple-element.64), channel_id=1, source_target_pairs={{0,16},{1,17},{2,18},{3,19},{4,20},{5,21},{6,22},{7,23},{8,24},{9,... | collective-permute-start | bytes 589832 | tf_op jit(solution)/shard_map/ppermute | solution.py:481
  173.6 16.7 %collective-permute-start.15 = (bf16[64,1536]{1,0:T(8,128)(2,1)S(1)}, bf16[64,1536]{1,0:T(8,128)(2,1)S(1)}, u32[]{:S(2)}, u32[]{:S(2)}) collective-permute-start(bf16[64,1536]{1,0:T(8,128)(2,1)S(1)} %get-tuple-element.65), channel_id=1, source_target_pairs={{0,24},{1,25},{2,26},{3,27},{4,28},{5,29},{6,30},{7,31},{8,0},{9,1... | collective-permute-start | bytes 589832 | tf_op jit(solution)/shard_map/ppermute | solution.py:481
  (26 other events, 83.2 us)
Sparse Core Ops, SparseCore 0:
  9.9 30.4 all-gather.3
  42.3 29.0 all-gather.5

commit v3 on v0

--- a/solution.py
+++ b/solution.py
@@ -273,7 +273,9 @@
     rows = jnp.concatenate([rows_ref[z] for z in range(Z_SIZE)], axis=0)
     part, width = weight_ref.shape
     out = dot_rows(rows[:, :width], weight_ref[...])
-    mixed_ref[...] = (out + rows[:, width : width + part].astype(jnp.float32)).astype(jnp.bfloat16)
+    mixed = (out + rows[:, width : width + part].astype(jnp.float32)).astype(jnp.bfloat16)
+    for z in range(Z_SIZE):
+        mixed_ref[z] = mixed
     info_ref[...] = rows[:, width + part :]
 
 
@@ -302,20 +304,14 @@
     mix_ref[...] = mix.astype(jnp.bfloat16)
 
 
-def pick_kernel(z_ref, onehot_ref, gain_ref, *refs):
-    parts = refs[:Z_SIZE]
-    normed_ref, own_ref, out_hbm, mixed_ref, out_ref, sems = refs[Z_SIZE:]
-    for step, part_ref in enumerate(parts):
-        mixed_ref[source_z(z_ref, step)] = part_ref[...]
-    columns = mixed_ref.shape[2]
-    tokens = own_ref.shape[0]
-    own = pl.ds(pl.multiple_of(z_ref[0] * tokens, tokens), tokens)
-    for z in range(Z_SIZE):
-        own_ref[:, z * columns : (z + 1) * columns] = mixed_ref[z, own, :].astype(jnp.float32)
+def norm(mixed_ref, gain_ref):
     mixed = jnp.concatenate([mixed_ref[z] for z in range(Z_SIZE)], axis=1).astype(jnp.float32)
     mean_square = jnp.mean(mixed * mixed, axis=-1, keepdims=True)
-    normed = (mixed * lax.rsqrt(mean_square + EPSILON) * gain_ref[...]).astype(jnp.bfloat16)
-    normed_ref[...] = normed
+    return (mixed * lax.rsqrt(mean_square + EPSILON) * gain_ref[...]).astype(jnp.bfloat16)
+
+
+def pick_kernel(onehot_ref, gain_ref, mixed_ref, out_hbm, out_ref, sems):
+    normed = norm(mixed_ref, gain_ref)
     picked = out_ref.shape[1]
     copies = []
     for p in range(PLANE):
@@ -328,45 +324,75 @@
         copy.wait()
 
 
-def shared_kernel(rows_ref, weight_ref, out_ref):
+def shared_kernel(z_ref, gain_ref, mixed_ref, weight_ref, out_ref, own_ref):
+    tokens, columns = own_ref.shape[0], mixed_ref.shape[2]
+    own = pl.ds(pl.multiple_of(z_ref[0] * tokens, tokens), tokens)
+    for z in range(Z_SIZE):
+        own_ref[:, z * columns : (z + 1) * columns] = mixed_ref[z, own, :].astype(jnp.float32)
     parts, units, _ = weight_ref.shape
     units = units // 3
     gate_weight, up_weight, down_weight = [
         jnp.concatenate([weight_ref[p, at * units : (at + 1) * units] for p in range(parts)], axis=0)
         for at in range(3)
     ]
-    rows = rows_ref[...]
+    rows = norm(mixed_ref, gain_ref)
     act = silu_times(dot_rows(rows, gate_weight), dot_rows(rows, up_weight))
-    out_ref[...] = dot(act, down_weight)
+    out_ref[...] = dot(act, down_weight).astype(jnp.bfloat16)
 
 
 def experts_kernel(
-    rows_ref, gate_up_hbm, down_hbm, out_hbm, gate_up_ref, down_ref, out_ref, in_sems, out_sems
+    rows_hbm,
+    gate_up_hbm,
+    down_hbm,
+    out_hbm,
+    rows_ref,
+    gate_up_ref,
+    down_ref,
+    out_ref,
+    in_sems,
+    row_sems,
+    out_sems,
 ):
     halves = gate_up_ref.shape[0]
-    fetches = []
-    for half in range(halves):
-        gate_up = pltpu.make_async_copy(
-            gate_up_hbm.at[half], gate_up_ref.at[half], in_sems.at[0, half]
-        )
-        down = pltpu.make_async_copy(down_hbm.at[half], down_ref.at[half], in_sems.at[1, half])
-        gate_up.start()
-        down.start()
-        fetches.append((gate_up, down))
     sources, rows, width = rows_ref.shape
     per_half = rows // halves
+    row_fetches = [
+        pltpu.make_async_copy(
+            rows_hbm.at[:, pl.ds(2 * pair * per_half, 2 * per_half)],
+            rows_ref.at[:, pl.ds(2 * pair * per_half, 2 * per_half)],
+            row_sems.at[pair],
+        )
+        for pair in range(halves // 2)
+    ]
+    gate_up_fetches = [
+        pltpu.make_async_copy(gate_up_hbm.at[half], gate_up_ref.at[half], in_sems.at[0, half])
+        for half in range(halves)
+    ]
+    down_fetches = [
+        pltpu.make_async_copy(down_hbm.at[half], down_ref.at[half], in_sems.at[1, half])
+        for half in range(halves)
+    ]
+    row_fetches[0].start()
+    gate_up_fetches[0].start()
+    down_fetches[0].start()
     copies = []
     for pair in range(halves // 2):
         both = pl.ds(2 * pair * per_half, 2 * per_half)
+        row_fetches[pair].wait()
+        if pair + 1 < halves // 2:
+            row_fetches[pair + 1].start()
         arrived = rows_ref[:, both, :].astype(jnp.float32)
         results = []
         for member in range(2):
             half = 2 * pair + member
             own = arrived[:, member * per_half : (member + 1) * per_half]
             own = own.reshape(sources * per_half, width).astype(jnp.bfloat16)
-            fetches[half][0].wait()
+            gate_up_fetches[half].wait()
+            if half + 1 < halves:
+                gate_up_fetches[half + 1].start()
+                down_fetches[half + 1].start()
             act = silu_times(dot(own, gate_up_ref[half, 0]), dot(own, gate_up_ref[half, 1]))
-            fetches[half][1].wait()
+            down_fetches[half].wait()
             results.append(dot(act, down_ref[half]).reshape(sources, per_half, width))
         out_ref[:, both, :] = jnp.concatenate(results, axis=1).astype(jnp.bfloat16)
         copy = pltpu.make_async_copy(out_ref.at[:, both], out_hbm.at[:, both], out_sems.at[pair])
@@ -379,7 +405,7 @@
 def combine_kernel(z_ref, mix_ref, rows_ref, shared_ref, *refs):
     outs, sum_ref = refs[:Z_SIZE], refs[Z_SIZE]
     tokens = outs[0].shape[0]
-    sum_ref[...] = dot(mix_ref[...], rows_ref[...]) + shared_ref[...]
+    sum_ref[...] = dot(mix_ref[...], rows_ref[...]) + shared_ref[...].astype(jnp.float32)
     for step, out_ref in enumerate(outs):
         z = lax.rem(z_ref[0] + step, Z_SIZE)
         rows = pl.ds(pl.multiple_of(z * tokens, tokens), tokens)
@@ -431,6 +457,7 @@
     devices = lax.axis_size("seq")
     me = lax.axis_index("seq")
     z_index, plane_index = lax.div(me, PLANE), lax.rem(me, PLANE)
+    z_groups = [[p + PLANE * z for z in range(Z_SIZE)] for p in range(PLANE)]
     planes = [[p + PLANE * z for p in range(PLANE)] for z in range(Z_SIZE)]
     bf16, f32 = jnp.bfloat16, jnp.float32
     shape = jax.ShapeDtypeStruct
@@ -478,8 +505,6 @@
     own_shared = jnp.concatenate(
         [jnp.transpose(shared_gate_up, (1, 2, 0)).reshape(-1, width), shared_down], axis=0
     )
-    info, own_shared = lax.optimization_barrier((info, own_shared))
-    shared_weight = lax.all_gather(own_shared, "seq", axis=0, axis_index_groups=planes)
 
     sent_width = width + part + info.shape[1]
     sent = pl.pallas_call(
@@ -487,11 +512,13 @@
         out_shape=[shape((tokens, sent_width), bf16)] * Z_SIZE,
         in_specs=[SMEM] * 3 + [VMEM] * 8,
         out_specs=[VMEM] * Z_SIZE,
-        compiler_params=params(),
+        compiler_params=params(58),
         cost_estimate=cost(4 * tokens * 5 * tokens * width, 3 * MIB),
         name="attention",
     )(z_scalar, scalar(me * tokens), lengths, queries, *behind, own_kv, residual, info)
 
+    sent, own_shared = lax.optimization_barrier((sent, own_shared))
+    shared_weight = lax.all_gather(own_shared, "seq", axis=0, axis_index_groups=planes)
     gathered = along_z(sent)
     gathered, cache_blocks, expert_gate_up = lax.optimization_barrier(
         (gathered, cache_blocks, expert_gate_up)
@@ -517,15 +544,15 @@
 
     mixed_part, info = pl.pallas_call(
         project_kernel,
-        out_shape=[shape((all_tokens, part), bf16), shape((all_tokens, 128), bf16)],
+        out_shape=[shape((Z_SIZE, all_tokens, part), bf16), shape((all_tokens, 128), bf16)],
         in_specs=[SMEM] + [VMEM] * (Z_SIZE + 1),
         out_specs=[VMEM] * 2,
         scratch_shapes=[pltpu.VMEM((Z_SIZE, tokens, sent_width), bf16)],
-        compiler_params=params(),
+        compiler_params=params(58),
         cost_estimate=cost(2 * all_tokens * width * part, 3 * MIB),
         name="project",
     )(z_scalar, *gathered, turned_weight)
-    mixed = along_z([mixed_part] * Z_SIZE)
+    mixed = exchange(mixed_part, z_groups)
 
     local_halves, _, _, half_ff = expert_gate_up.shape
     per_half = Z_SIZE * CAP
@@ -542,24 +569,19 @@
         cost_estimate=cost(20 * PLANE * picked * all_tokens, MIB),
         name="tables",
     )(scalar(lax.rem(z_index, 2)), info)
-    normed, own_mixed, outgoing = pl.pallas_call(
+    outgoing = pl.pallas_call(
         pick_kernel,
-        out_shape=[
-            shape((all_tokens, width), bf16),
-            shape((tokens, width), f32),
-            shape((PLANE, picked, width), bf16),
-        ],
-        in_specs=[SMEM] + [VMEM] * (2 + Z_SIZE),
-        out_specs=[VMEM, VMEM, HBM],
+        out_shape=shape((PLANE, picked, width), bf16),
+        in_specs=[VMEM] * 3,
+        out_specs=HBM,
         scratch_shapes=[
-            pltpu.VMEM((Z_SIZE, all_tokens, part), bf16),
             pltpu.VMEM((PLANE, picked, width), bf16),
             pltpu.SemaphoreType.DMA((PLANE,)),
         ],
-        compiler_params=params(20),
-        cost_estimate=cost(2 * PLANE * picked * all_tokens * width, 5 * MIB),
+        compiler_params=params(58),
+        cost_estimate=cost(2 * PLANE * picked * all_tokens * width, 4 * MIB),
         name="pick",
-    )(z_scalar, onehot, gain, *mixed)
+    )(onehot, gain, mixed)
 
     outgoing, in_plane = lax.optimization_barrier((outgoing, in_plane))
     arrived = exchange(outgoing, planes)
@@ -568,7 +590,7 @@
         out_shape=[shape((PLANE,) + in_plane[0].shape[1:], bf16)] * Z_SIZE,
         in_specs=[SMEM] + [VMEM] * PLANE,
         out_specs=[VMEM] * Z_SIZE,
-        compiler_params=params(),
+        compiler_params=params(58),
         cost_estimate=cost(0, 2 * MIB),
         name="regroup",
     )(z_scalar, *in_plane)
@@ -577,29 +599,31 @@
         arrived_cache.append(lax.ppermute(grouped[step], "seq", z_pairs[step]))
 
     arrived, shared_weight = lax.optimization_barrier((arrived, shared_weight))
-    shared_part = pl.pallas_call(
+    shared_part, own_mixed = pl.pallas_call(
         shared_kernel,
-        out_shape=shape((all_tokens, width), f32),
-        in_specs=[VMEM] * 2,
-        out_specs=VMEM,
+        out_shape=[shape((all_tokens, width), bf16), shape((tokens, width), f32)],
+        in_specs=[SMEM] + [VMEM] * 3,
+        out_specs=[VMEM] * 2,
         compiler_params=params(24),
         cost_estimate=cost(6 * all_tokens * 256 * width, 5 * MIB),
         name="shared_expert",
-    )(normed, shared_weight)
+    )(z_scalar, gain, mixed, shared_weight)
 
     returning = pl.pallas_call(
         experts_kernel,
         out_shape=shape((PLANE, picked, width), bf16),
-        in_specs=[VMEM, HBM, HBM],
+        in_specs=[HBM, HBM, HBM],
         out_specs=HBM,
         scratch_shapes=[
+            pltpu.VMEM((PLANE, picked, width), bf16),
             pltpu.VMEM((local_halves, 2, width, half_ff), bf16),
             pltpu.VMEM((local_halves, half_ff, width), bf16),
             pltpu.VMEM((PLANE, picked, width), bf16),
             pltpu.SemaphoreType.DMA((2, local_halves)),
             pltpu.SemaphoreType.DMA((local_halves // 2,)),
+            pltpu.SemaphoreType.DMA((local_halves // 2,)),
         ],
-        compiler_params=params(40),
+        compiler_params=params(58),
         cost_estimate=cost(6 * PLANE * picked * half_ff * width, 14 * MIB),
         name="experts",
     )(arrived, gate_up, expert_down)

time: 203 us -> 198 us (0.975)
  local copies, waits for them, and re-layouts: 36.7 us -> 23.9 us
  Pallas kernels: 18.7 us -> 28.8 us
    unnamed x65 -> x73, local copies, waits for them, and re-layouts: 28.4 us -> 15 us
    all_to_all x2 -> x3, waiting for transfers between devices: 33.6 us -> 40.1 us  [exchange(): lax.all_to_all(array, 'seq', split_axis=0, concat_axis=0, tiled=True, axi...]
    ppermute x9 -> x6, starting transfers between devices: 14.1 us -> 8.69 us  [along_z(): lax.ppermute(arrays[step], 'seq', z_pairs[step])]
    all_to_all x2 -> x3, starting transfers between devices: 9.62 us -> 14.1 us  [exchange(): lax.all_to_all(array, 'seq', split_axis=0, concat_axis=0, tiled=True, axi...]
    ppermute x4, waiting for transfers between devices: 4.3 us -> 0.01 us  [from_behind(): return lax.ppermute(shard, axis, pairs)]
    pallas_call x1, Pallas kernels: 4.45 us -> 8.43 us  [shards(): pl.pallas_call(experts_kernel, out_shape=shape((PLANE, picked, width), bf...]
    pallas_call x3, Pallas kernels: 4.5 us -> 7.48 us  [the longest x1 3.4 us: shards(): pl.pallas_call(pick_kernel, out_shape=shape((PLANE, picked, width), bf16)...]
    ppermute x7, waiting for transfers between devices: 6.2 us -> 3.33 us  [shards(): piece = lax.ppermute(piece, 'seq', pairs)]
  transfers between devices with their start and end apart: 27 -> 25, of which waited for: 11 -> 9; matrix products, arithmetic and copies ran while one was open for 6% -> 7% of each run, Pallas kernels for 8% -> 14%
where the time goes in v3:
time: 198 us; the launch traced here: 197 us
  waiting for transfers between devices  78.5 us (40%)
  starting transfers between devices  47.6 us (24%)
  Pallas kernels  28.8 us (15%)
  local copies, waits for them, and re-layouts  23.9 us (12%)
  between operations  14.4 us (7%)
  other arithmetic  3.59 us (2%)
    all_to_all x3, waiting for transfers between devices, exchange(): lax.all_to_all(array, 'seq', split_axis=0, concat_axis=0, tiled=True, axi...  40.1 us
    ppermute x6, waiting for transfers between devices, along_z(): lax.ppermute(arrays[step], 'seq', z_pairs[step])  34.4 us
    unnamed x73, local copies, waits for them, and re-layouts  15 us
    all_to_all x3, starting transfers between devices, exchange(): lax.all_to_all(array, 'seq', split_axis=0, concat_axis=0, tiled=True, axi...  14.1 us
    ppermute x4, starting transfers between devices, from_behind(): return lax.ppermute(shard, axis, pairs)  13.1 us
    ppermute x6, starting transfers between devices, along_z(): lax.ppermute(arrays[step], 'seq', z_pairs[step])  8.69 us
    pallas_call x1, Pallas kernels, shards(): pl.pallas_call(experts_kernel, out_shape=shape((PLANE, picked, width), bf...  8.43 us
    ppermute x7, starting transfers between devices, shards(): piece = lax.ppermute(piece, 'seq', pairs)  6.32 us
  transfers between devices with their start and end apart: 25, of which 9 were waited for; matrix products, arithmetic and copies ran while one was open for 7% of the time, Pallas kernels for 14%

profile of v3, /device:TPU:10, one launch (start us, length us, event | category | flops | bytes accessed | tf_op | source)
XLA Modules:
  0.0 196.8 jit_solution(7491168337591194368)
XLA Ops:
  9.6 1.9 collective-permute-start.3
  11.6 3.4 %collective-permute-start.2 = (bf16[64,1024]{1,0:T(8,128)(2,1)S(1)}, bf16[64,1024]{1,0:T(8,128)(2,1)S(1)}, u32[]{:S(2)}, u32[]{:S(2)}) collective-permute-start(bf16[64,1024]{1,0:T(8,128)(2,1)S(1)} %constant_dynamic-update-slice_fusion.own_ref), channel_id=1, source_target_pairs={{0,2},{1,3},{2,4},{3,5},{4,6},{5,7},{6,8},{7,9},{8,10},{9,11},{10,... | collective-permute-start | bytes 393224 | tf_op jit(solution)/shard_map/ppermute | solution.py:28
  15.0 4.3 %collective-permute-start.1 = (bf16[64,1024]{1,0:T(8,128)(2,1)S(1)}, bf16[64,1024]{1,0:T(8,128)(2,1)S(1)}, u32[]{:S(2)}, u32[]{:S(2)}) collective-permute-start(bf16[64,1024]{1,0:T(8,128)(2,1)S(1)} %constant_dynamic-update-slice_fusion.own_ref), channel_id=1, source_target_pairs={{0,3},{1,4},{2,5},{3,6},{4,7},{5,8},{6,9},{7,10},{8,11},{9,12},{10... | collective-permute-start | bytes 393224 | tf_op jit(solution)/shard_map/ppermute | solution.py:28
  19.3 3.4 %collective-permute-start = (bf16[64,1024]{1,0:T(8,128)(2,1)S(1)}, bf16[64,1024]{1,0:T(8,128)(2,1)S(1)}, u32[]{:S(2)}, u32[]{:S(2)}) collective-permute-start(bf16[64,1024]{1,0:T(8,128)(2,1)S(1)} %constant_dynamic-update-slice_fusion.own_ref), channel_id=1, source_target_pairs={{0,4},{1,5},{2,6},{3,7},{4,8},{5,9},{6,10},{7,11},{8,12},{9,13},{1... | collective-permute-start | bytes 393224 | tf_op jit(solution)/shard_map/ppermute | solution.py:28
  28.5 3.8 %attention.1 = (bf16[64,2048]{1,0:T(8,128)(2,1)}, bf16[64,2048]{1,0:T(8,128)(2,1)}, bf16[64,2048]{1,0:T(8,128)(2,1)}, bf16[64,2048]{1,0:T(8,128)(2,1)}) custom-call(s32[1]{0:T(128)} %bitcast.z_ref, s32[1]{0:T(128)} %bitcast.1.first_ref, s32[16]{0:T(128)} %lengths_ref.1, bf16[64,1536]{1,0:T(8,128)(2,1)} %q_ref.1, bf16[64,1024]{1,0:T(8,128)(2,1)} %copy-done.27, ...), custom_call_target="tpu_custom_call" | custom-call | flops 125829120 | bytes 3145728 | tf_op jit(solution)/shard_map/attention/pallas_call | solution.py:510
  35.7 16.6 %collective-permute-done.4.refs_1_ = bf16[64,2048]{1,0:T(8,128)(2,1)S(1)} collective-permute-done((bf16[64,2048]{1,0:T(8,128)(2,1)}, bf16[64,2048]{1,0:T(8,128)(2,1)S(1)}, u32[]{:S(2)}, u32[]{:S(2)}) %collective-permute-start.4) | collective-permute-done | bytes 262176 | tf_op jit(solution)/shard_map/ppermute | solution.py:492
  52.3 3.5 %collective-permute-done.5.refs_2_ = bf16[64,2048]{1,0:T(8,128)(2,1)S(1)} collective-permute-done((bf16[64,2048]{1,0:T(8,128)(2,1)}, bf16[64,2048]{1,0:T(8,128)(2,1)S(1)}, u32[]{:S(2)}, u32[]{:S(2)}) %collective-permute-start.5) | collective-permute-done | bytes 262176 | tf_op jit(solution)/shard_map/ppermute | solution.py:492
  58.1 3.1 %project.1 = (bf16[4,256,384]{2,1,0:T(8,128)(2,1)}, bf16[256,128]{1,0:T(8,128)(2,1)}) custom-call(s32[1]{0:T(128)} %bitcast.z_ref, bf16[64,2048]{1,0:T(8,128)(2,1)} %get-tuple-element.55.refs_0_, bf16[64,2048]{1,0:T(8,128)(2,1)} %copy-done.17, bf16[64,2048]{1,0:T(8,128)(2,1)} %copy-done.18, bf16[64,2048]{1,0:T(8,128)(2,1)} %copy-done.19, ...), custom_call_target="tpu_custom_call" | custom-call | flops 301989888 | bytes 3145728 | tf_op jit(solution)/shard_map/project/pallas_call | solution.py:545
  61.2 4.6 %all-to-all-start = ((bf16[4,256,384]{2,1,0:T(8,128)(2,1)}), bf16[4,256,384]{2,1,0:T(8,128)(2,1)S(1)}, u32[]{:S(2)}, u32[]{:S(2)}) async-start(bf16[4,256,384]{2,1,0:T(8,128)(2,1)} %get-tuple-element.59), calls=%async_computation | async-start | bytes 1572864 | tf_op jit(solution)/shard_map/all_to_all | solution.py:469
  70.0 2.4 %collective-permute-start.9 = (bf16[4,32,4,128]{3,2,1,0:T(4,128)(2,1)S(1)}, bf16[4,32,4,128]{3,2,1,0:T(4,128)(2,1)S(1)}, u32[]{:S(2)}, u32[]{:S(2)}) collective-permute-start(bf16[4,32,4,128]{3,2,1,0:T(4,128)(2,1)S(1)} %get-tuple-element.96), channel_id=1, source_target_pairs={{0,3},{1,4},{2,5},{3,6},{4,7},{5,0},{6,1},{7,2},{8,11},{9,12},{10,... | collective-permute-start | bytes 393224 | tf_op jit(solution)/shard_map/ppermute | solution.py:541
  73.4 3.3 %collective-permute-done.12.refs_6_ = bf16[4,32,4,128]{3,2,1,0:T(4,128)(2,1)S(1)} collective-permute-done((bf16[4,32,4,128]{3,2,1,0:T(4,128)(2,1)S(1)}, bf16[4,32,4,128]{3,2,1,0:T(4,128)(2,1)S(1)}, u32[]{:S(2)}, u32[]{:S(2)}) %collective-permute-start.12) | collective-permute-done | bytes 131104 | tf_op jit(solution)/shard_map/ppermute | solution.py:541
  77.3 1.9 tables.1
  83.3 3.4 %pick.1 = bf16[8,96,1536]{2,1,0:T(8,128)(2,1)} custom-call(bf16[768,256]{1,0:T(8,128)(2,1)} %copy-done.7, f32[1,1536]{1,0:T(1,128)} %reshape.33.gain_ref, bf16[4,256,384]{2,1,0:T(8,128)(2,1)} %copy-done), custom_call_target="tpu_custom_call" | custom-call | flops 603979776 | bytes 4194304 | tf_op jit(solution)/shard_map/pick/pallas_call | solution.py:572
  87.6 4.4 %all-to-all-start.1 = ((bf16[8,96,1536]{2,1,0:T(8,128)(2,1)}), bf16[8,96,1536]{2,1,0:T(8,128)(2,1)S(1)}, u32[]{:S(2)}, u32[]{:S(2)}) async-start(bf16[8,96,1536]{2,1,0:T(8,128)(2,1)} %pick.1), calls=%async_computation.1 | async-start | bytes 4718592 | tf_op jit(solution)/shard_map/all_to_all | solution.py:469
  92.0 2.4 %regroup.1 = (bf16[8,32,4,128]{3,2,1,0:T(4,128)(2,1)}, bf16[8,32,4,128]{3,2,1,0:T(4,128)(2,1)}, bf16[8,32,4,128]{3,2,1,0:T(4,128)(2,1)}, bf16[8,32,4,128]{3,2,1,0:T(4,128)(2,1)}) custom-call(s32[1]{0:T(128)} %bitcast.z_ref, bf16[4,32,4,128]{3,2,1,0:T(4,128)(2,1)} %get-tuple-element.70.refs_0_, bf16[4,32,4,128]{3,2,1,0:T(4,128)(2,1)} %copy-done.34, ...), custom_call_target="tpu_custom_call" | custom-call | bytes 2097152 | tf_op jit(solution)/shard_map/regroup/pallas_call | solution.py:588
  95.1 4.2 %collective-permute-start.15 = (bf16[8,32,4,128]{3,2,1,0:T(4,128)(2,1)}, bf16[8,32,4,128]{3,2,1,0:T(4,128)(2,1)S(1)}, u32[]{:S(2)}, u32[]{:S(2)}) collective-permute-start(bf16[8,32,4,128]{3,2,1,0:T(4,128)(2,1)} %get-tuple-element.80), channel_id=1, source_target_pairs={{0,16},{1,17},{2,18},{3,19},{4,20},{5,21},{6,22},{7,23},{8,24},{9,... | collective-permute-start | bytes 786440 | tf_op jit(solution)/shard_map/ppermute | solution.py:599
  99.6 6.2 %copy.35 = bf16[4,1536,2,256]{3,1,2,0:T(8,128)(2,1)} copy(bf16[4,1536,2,256]{3,2,1,0:T(2,128)(2,1)} %param.26) | data formatting | bytes 12582912 | tf_op jit(solution)/shard_map/optimization_barrier | solution.py:523
  105.9 14.0 %all-to-all-done.1.rows_hbm = bf16[8,96,1536]{2,1,0:T(8,128)(2,1)S(1)} async-done(((bf16[8,96,1536]{2,1,0:T(8,128)(2,1)}), bf16[8,96,1536]{2,1,0:T(8,128)(2,1)S(1)}, u32[]{:S(2)}, u32[]{:S(2)}) %all-to-all-start.1) | async-done | bytes 2359328 | tf_op jit(solution)/shard_map/all_to_all | solution.py:469
  121.4 8.4 %experts.1 = bf16[8,96,1536]{2,1,0:T(8,128)(2,1)} custom-call(bf16[8,96,1536]{2,1,0:T(8,128)(2,1)} %copy-done.14, bf16[4,2,1536,256]{3,2,1,0:T(8,128)(2,1)} %bitcast.53, bf16[4,256,1536]{2,1,0:T(8,128)(2,1)} %down_hbm.1), custom_call_target="tpu_custom_call" | custom-call | flops 1811939328 | bytes 14680064 | tf_op jit(solution)/shard_map/experts/pallas_call | solution.py:612
  131.3 5.2 %all-to-all-start.2 = ((bf16[8,96,1536]{2,1,0:T(8,128)(2,1)}), bf16[8,96,1536]{2,1,0:T(8,128)(2,1)S(1)}, u32[]{:S(2)}, u32[]{:S(2)}) async-start(bf16[8,96,1536]{2,1,0:T(8,128)(2,1)} %experts.1), calls=%async_computation.2 | async-start | bytes 4718592 | tf_op jit(solution)/shard_map/all_to_all | solution.py:469
  140.0 24.4 %all-to-all-done.2 = bf16[8,96,1536]{2,1,0:T(8,128)(2,1)S(1)} async-done(((bf16[8,96,1536]{2,1,0:T(8,128)(2,1)}), bf16[8,96,1536]{2,1,0:T(8,128)(2,1)S(1)}, u32[]{:S(2)}, u32[]{:S(2)}) %all-to-all-start.2) | async-done | bytes 2359328 | tf_op jit(solution)/shard_map/all_to_all | solution.py:469
  168.3 4.2 %collective-permute-start.18 = (bf16[64,1536]{1,0:T(8,128)(2,1)S(1)}, bf16[64,1536]{1,0:T(8,128)(2,1)S(1)}, u32[]{:S(2)}, u32[]{:S(2)}) collective-permute-start(bf16[64,1536]{1,0:T(8,128)(2,1)S(1)} %get-tuple-element.86), channel_id=1, source_target_pairs={{0,16},{1,17},{2,18},{3,19},{4,20},{5,21},{6,22},{7,23},{8,24},{9,... | collective-permute-start | bytes 589832 | tf_op jit(solution)/shard_map/ppermute | solution.py:492
  176.5 8.8 %collective-permute-done.18.refs_2_ = bf16[64,1536]{1,0:T(8,128)(2,1)S(1)} collective-permute-done((bf16[64,1536]{1,0:T(8,128)(2,1)S(1)}, bf16[64,1536]{1,0:T(8,128)(2,1)S(1)}, u32[]{:S(2)}, u32[]{:S(2)}) %collective-permute-start.18) | collective-permute-done | bytes 196640 | tf_op jit(solution)/shard_map/ppermute | solution.py:492
  185.3 3.8 %collective-permute-done.19.refs_3_ = bf16[64,1536]{1,0:T(8,128)(2,1)S(1)} collective-permute-done((bf16[64,1536]{1,0:T(8,128)(2,1)S(1)}, bf16[64,1536]{1,0:T(8,128)(2,1)S(1)}, u32[]{:S(2)}, u32[]{:S(2)}) %collective-permute-start.19) | collective-permute-done | bytes 196640 | tf_op jit(solution)/shard_map/ppermute | solution.py:492
  (118 shorter events, 40.7 us)
Async XLA Ops:
  7.2 50.3 %all-gather.4.cloned.1.call-start = ((), (), s32[]{:S(2)}) async-start(), calls=%async_computation.3 | async-start | bytes 1327104 | tf_op jit(solution)/shard_map/all_gather | solution.py:476
  7.9 98.0 %all-gather.6.cloned.1.call-start = ((), (), s32[]{:S(2)}) async-start(), calls=%async_computation.4 | async-start | bytes 2654208 | tf_op jit(solution)/shard_map/all_gather | solution.py:521
  9.6 18.1 %collective-permute-start.3 = (bf16[64,1024]{1,0:T(8,128)(2,1)S(1)}, bf16[64,1024]{1,0:T(8,128)(2,1)S(1)}, u32[]{:S(2)}, u32[]{:S(2)}) collective-permute-start(bf16[64,1024]{1,0:T(8,128)(2,1)S(1)} %constant_dynamic-update-slice_fusion.own_ref), channel_id=1, source_target_pairs={{0,1},{1,2},{2,3},{3,4},{4,5},{5,6},{6,7},{7,8},{8,9},{9,10},{10,1... | collective-permute-start | bytes 393224 | tf_op jit(solution)/shard_map/ppermute | solution.py:28
  11.6 16.2 %collective-permute-start.2 = (bf16[64,1024]{1,0:T(8,128)(2,1)S(1)}, bf16[64,1024]{1,0:T(8,128)(2,1)S(1)}, u32[]{:S(2)}, u32[]{:S(2)}) collective-permute-start(bf16[64,1024]{1,0:T(8,128)(2,1)S(1)} %constant_dynamic-update-slice_fusion.own_ref), channel_id=1, source_target_pairs={{0,2},{1,3},{2,4},{3,5},{4,6},{5,7},{6,8},{7,9},{8,10},{9,11},{10,... | collective-permute-start | bytes 393224 | tf_op jit(solution)/shard_map/ppermute | solution.py:28
  15.0 12.8 %collective-permute-start.1 = (bf16[64,1024]{1,0:T(8,128)(2,1)S(1)}, bf16[64,1024]{1,0:T(8,128)(2,1)S(1)}, u32[]{:S(2)}, u32[]{:S(2)}) collective-permute-start(bf16[64,1024]{1,0:T(8,128)(2,1)S(1)} %constant_dynamic-update-slice_fusion.own_ref), channel_id=1, source_target_pairs={{0,3},{1,4},{2,5},{3,6},{4,7},{5,8},{6,9},{7,10},{8,11},{9,12},{10... | collective-permute-start | bytes 393224 | tf_op jit(solution)/shard_map/ppermute | solution.py:28
  19.3 8.5 %collective-permute-start = (bf16[64,1024]{1,0:T(8,128)(2,1)S(1)}, bf16[64,1024]{1,0:T(8,128)(2,1)S(1)}, u32[]{:S(2)}, u32[]{:S(2)}) collective-permute-start(bf16[64,1024]{1,0:T(8,128)(2,1)S(1)} %constant_dynamic-update-slice_fusion.own_ref), channel_id=1, source_target_pairs={{0,4},{1,5},{2,6},{3,7},{4,8},{5,9},{6,10},{7,11},{8,12},{9,13},{1... | collective-permute-start | bytes 393224 | tf_op jit(solution)/shard_map/ppermute | solution.py:28
  32.3 19.9 %collective-permute-start.4 = (bf16[64,2048]{1,0:T(8,128)(2,1)}, bf16[64,2048]{1,0:T(8,128)(2,1)S(1)}, u32[]{:S(2)}, u32[]{:S(2)}) collective-permute-start(bf16[64,2048]{1,0:T(8,128)(2,1)} %get-tuple-element.52), channel_id=1, source_target_pairs={{0,8},{1,9},{2,10},{3,11},{4,12},{5,13},{6,14},{7,15},{8,16},{9,17... | collective-permute-start | bytes 786440 | tf_op jit(solution)/shard_map/ppermute | solution.py:492
  34.0 21.8 %collective-permute-start.5 = (bf16[64,2048]{1,0:T(8,128)(2,1)}, bf16[64,2048]{1,0:T(8,128)(2,1)S(1)}, u32[]{:S(2)}, u32[]{:S(2)}) collective-permute-start(bf16[64,2048]{1,0:T(8,128)(2,1)} %get-tuple-element.53), channel_id=1, source_target_pairs={{0,16},{1,17},{2,18},{3,19},{4,20},{5,21},{6,22},{7,23},{8,24},{9,... | collective-permute-start | bytes 786440 | tf_op jit(solution)/shard_map/ppermute | solution.py:492
  35.2 22.2 %collective-permute-start.6 = (bf16[64,2048]{1,0:T(8,128)(2,1)}, bf16[64,2048]{1,0:T(8,128)(2,1)S(1)}, u32[]{:S(2)}, u32[]{:S(2)}) collective-permute-start(bf16[64,2048]{1,0:T(8,128)(2,1)} %get-tuple-element.54), channel_id=1, source_target_pairs={{0,24},{1,25},{2,26},{3,27},{4,28},{5,29},{6,30},{7,31},{8,0},{9,1... | collective-permute-start | bytes 786440 | tf_op jit(solution)/shard_map/ppermute | solution.py:492
  61.2 21.2 %all-to-all-start = ((bf16[4,256,384]{2,1,0:T(8,128)(2,1)}), bf16[4,256,384]{2,1,0:T(8,128)(2,1)S(1)}, u32[]{:S(2)}, u32[]{:S(2)}) async-start(bf16[4,256,384]{2,1,0:T(8,128)(2,1)} %get-tuple-element.59), calls=%async_computation | async-start | bytes 1572864 | tf_op jit(solution)/shard_map/all_to_all | solution.py:469
  67.0 9.6 %collective-permute-start.12 = (bf16[4,32,4,128]{3,2,1,0:T(4,128)(2,1)S(1)}, bf16[4,32,4,128]{3,2,1,0:T(4,128)(2,1)S(1)}, u32[]{:S(2)}, u32[]{:S(2)}) collective-permute-start(bf16[4,32,4,128]{3,2,1,0:T(4,128)(2,1)S(1)} %get-tuple-element.93), channel_id=1, source_target_pairs={{0,6},{1,7},{2,0},{3,1},{4,2},{5,3},{6,4},{7,5},{8,14},{9,15},{10,... | collective-permute-start | bytes 393224 | tf_op jit(solution)/shard_map/ppermute | solution.py:541
  68.8 17.9 %collective-permute-start.11 = (bf16[4,32,4,128]{3,2,1,0:T(4,128)(2,1)S(1)}, bf16[4,32,4,128]{3,2,1,0:T(4,128)(2,1)S(1)}, u32[]{:S(2)}, u32[]{:S(2)}) collective-permute-start(bf16[4,32,4,128]{3,2,1,0:T(4,128)(2,1)S(1)} %get-tuple-element.94), channel_id=1, source_target_pairs={{0,5},{1,6},{2,7},{3,0},{4,1},{5,2},{6,3},{7,4},{8,13},{9,14},{10,... | collective-permute-start | bytes 393224 | tf_op jit(solution)/shard_map/ppermute | solution.py:541
  69.9 16.9 %collective-permute-start.10 = (bf16[4,32,4,128]{3,2,1,0:T(4,128)(2,1)S(1)}, bf16[4,32,4,128]{3,2,1,0:T(4,128)(2,1)S(1)}, u32[]{:S(2)}, u32[]{:S(2)}) collective-permute-start(bf16[4,32,4,128]{3,2,1,0:T(4,128)(2,1)S(1)} %get-tuple-element.95), channel_id=1, source_target_pairs={{0,4},{1,5},{2,6},{3,7},{4,0},{5,1},{6,2},{7,3},{8,12},{9,13},{10,... | collective-permute-start | bytes 393224 | tf_op jit(solution)/shard_map/ppermute | solution.py:541
  70.0 16.7 %collective-permute-start.9 = (bf16[4,32,4,128]{3,2,1,0:T(4,128)(2,1)S(1)}, bf16[4,32,4,128]{3,2,1,0:T(4,128)(2,1)S(1)}, u32[]{:S(2)}, u32[]{:S(2)}) collective-permute-start(bf16[4,32,4,128]{3,2,1,0:T(4,128)(2,1)S(1)} %get-tuple-element.96), channel_id=1, source_target_pairs={{0,3},{1,4},{2,5},{3,6},{4,7},{5,0},{6,1},{7,2},{8,11},{9,12},{10,... | collective-permute-start | bytes 393224 | tf_op jit(solution)/shard_map/ppermute | solution.py:541
  72.4 14.4 %collective-permute-start.8 = (bf16[4,32,4,128]{3,2,1,0:T(4,128)(2,1)S(1)}, bf16[4,32,4,128]{3,2,1,0:T(4,128)(2,1)S(1)}, u32[]{:S(2)}, u32[]{:S(2)}) collective-permute-start(bf16[4,32,4,128]{3,2,1,0:T(4,128)(2,1)S(1)} %get-tuple-element.97), channel_id=1, source_target_pairs={{0,2},{1,3},{2,4},{3,5},{4,6},{5,7},{6,0},{7,1},{8,10},{9,11},{10,... | collective-permute-start | bytes 393224 | tf_op jit(solution)/shard_map/ppermute | solution.py:541
  76.7 10.1 %collective-permute-start.7 = (bf16[4,32,4,128]{3,2,1,0:T(4,128)(2,1)S(1)}, bf16[4,32,4,128]{3,2,1,0:T(4,128)(2,1)S(1)}, u32[]{:S(2)}, u32[]{:S(2)}) collective-permute-start(bf16[4,32,4,128]{3,2,1,0:T(4,128)(2,1)S(1)} %get-tuple-element.98), channel_id=1, source_target_pairs={{0,1},{1,2},{2,3},{3,4},{4,5},{5,6},{6,7},{7,0},{8,9},{9,10},{10,1... | collective-permute-start | bytes 393224 | tf_op jit(solution)/shard_map/ppermute | solution.py:541
  87.6 32.3 %all-to-all-start.1 = ((bf16[8,96,1536]{2,1,0:T(8,128)(2,1)}), bf16[8,96,1536]{2,1,0:T(8,128)(2,1)S(1)}, u32[]{:S(2)}, u32[]{:S(2)}) async-start(bf16[8,96,1536]{2,1,0:T(8,128)(2,1)} %pick.1), calls=%async_computation.1 | async-start | bytes 4718592 | tf_op jit(solution)/shard_map/all_to_all | solution.py:469
  94.3 35.5 %collective-permute-start.14 = (bf16[8,32,4,128]{3,2,1,0:T(4,128)(2,1)}, bf16[8,32,4,128]{3,2,1,0:T(4,128)(2,1)S(1)}, u32[]{:S(2)}, u32[]{:S(2)}) collective-permute-start(bf16[8,32,4,128]{3,2,1,0:T(4,128)(2,1)} %get-tuple-element.79), channel_id=1, source_target_pairs={{0,8},{1,9},{2,10},{3,11},{4,12},{5,13},{6,14},{7,15},{8,16},{9,17... | collective-permute-start | bytes 786440 | tf_op jit(solution)/shard_map/ppermute | solution.py:599
  95.1 34.7 %collective-permute-start.15 = (bf16[8,32,4,128]{3,2,1,0:T(4,128)(2,1)}, bf16[8,32,4,128]{3,2,1,0:T(4,128)(2,1)S(1)}, u32[]{:S(2)}, u32[]{:S(2)}) collective-permute-start(bf16[8,32,4,128]{3,2,1,0:T(4,128)(2,1)} %get-tuple-element.80), channel_id=1, source_target_pairs={{0,16},{1,17},{2,18},{3,19},{4,20},{5,21},{6,22},{7,23},{8,24},{9,... | collective-permute-start | bytes 786440 | tf_op jit(solution)/shard_map/ppermute | solution.py:599
  99.3 30.6 %collective-permute-start.16 = (bf16[8,32,4,128]{3,2,1,0:T(4,128)(2,1)}, bf16[8,32,4,128]{3,2,1,0:T(4,128)(2,1)S(1)}, u32[]{:S(2)}, u32[]{:S(2)}) collective-permute-start(bf16[8,32,4,128]{3,2,1,0:T(4,128)(2,1)} %get-tuple-element.81), channel_id=1, source_target_pairs={{0,24},{1,25},{2,26},{3,27},{4,28},{5,29},{6,30},{7,31},{8,0},{9,1... | collective-permute-start | bytes 786440 | tf_op jit(solution)/shard_map/ppermute | solution.py:599
  131.3 33.1 %all-to-all-start.2 = ((bf16[8,96,1536]{2,1,0:T(8,128)(2,1)}), bf16[8,96,1536]{2,1,0:T(8,128)(2,1)S(1)}, u32[]{:S(2)}, u32[]{:S(2)}) async-start(bf16[8,96,1536]{2,1,0:T(8,128)(2,1)} %experts.1), calls=%async_computation.2 | async-start | bytes 4718592 | tf_op jit(solution)/shard_map/all_to_all | solution.py:469
  167.5 9.0 %collective-permute-start.17 = (bf16[64,1536]{1,0:T(8,128)(2,1)S(1)}, bf16[64,1536]{1,0:T(8,128)(2,1)S(1)}, u32[]{:S(2)}, u32[]{:S(2)}) collective-permute-start(bf16[64,1536]{1,0:T(8,128)(2,1)S(1)} %get-tuple-element.85), channel_id=1, source_target_pairs={{0,8},{1,9},{2,10},{3,11},{4,12},{5,13},{6,14},{7,15},{8,16},{9,17... | collective-permute-start | bytes 589832 | tf_op jit(solution)/shard_map/ppermute | solution.py:492
  168.3 17.0 %collective-permute-start.18 = (bf16[64,1536]{1,0:T(8,128)(2,1)S(1)}, bf16[64,1536]{1,0:T(8,128)(2,1)S(1)}, u32[]{:S(2)}, u32[]{:S(2)}) collective-permute-start(bf16[64,1536]{1,0:T(8,128)(2,1)S(1)} %get-tuple-element.86), channel_id=1, source_target_pairs={{0,16},{1,17},{2,18},{3,19},{4,20},{5,21},{6,22},{7,23},{8,24},{9,... | collective-permute-start | bytes 589832 | tf_op jit(solution)/shard_map/ppermute | solution.py:492
  172.5 16.7 %collective-permute-start.19 = (bf16[64,1536]{1,0:T(8,128)(2,1)S(1)}, bf16[64,1536]{1,0:T(8,128)(2,1)S(1)}, u32[]{:S(2)}, u32[]{:S(2)}) collective-permute-start(bf16[64,1536]{1,0:T(8,128)(2,1)S(1)} %get-tuple-element.87), channel_id=1, source_target_pairs={{0,24},{1,25},{2,26},{3,27},{4,28},{5,29},{6,30},{7,31},{8,0},{9,1... | collective-permute-start | bytes 589832 | tf_op jit(solution)/shard_map/ppermute | solution.py:492
  (37 other events, 175.7 us)
Sparse Core Ops, SparseCore 0:
  9.9 30.4 all-gather.3
  42.3 29.0 all-gather.5

commit v4 on v3

--- a/solution.py
+++ b/solution.py
@@ -340,59 +340,32 @@
     out_ref[...] = dot(act, down_weight).astype(jnp.bfloat16)
 
 
-def experts_kernel(
-    rows_hbm,
-    gate_up_hbm,
-    down_hbm,
-    out_hbm,
-    rows_ref,
-    gate_up_ref,
-    down_ref,
-    out_ref,
-    in_sems,
-    row_sems,
-    out_sems,
-):
+def hold_kernel(*refs):
+    count = (len(refs) + 1) // 2
+    copies = []
+    for from_ref, to_ref in zip(refs[: count - 1], refs[count - 1 : -1]):
+        for at in range(to_ref.shape[0]):
+            copy = pltpu.make_async_copy(from_ref.at[at], to_ref.at[at], refs[-1].at[len(copies)])
+            copy.start()
+            copies.append(copy)
+    for copy in copies:
+        copy.wait()
+
+
+def experts_kernel(rows_ref, gate_up_ref, down_ref, out_hbm, out_ref, out_sems):
     halves = gate_up_ref.shape[0]
     sources, rows, width = rows_ref.shape
     per_half = rows // halves
-    row_fetches = [
-        pltpu.make_async_copy(
-            rows_hbm.at[:, pl.ds(2 * pair * per_half, 2 * per_half)],
-            rows_ref.at[:, pl.ds(2 * pair * per_half, 2 * per_half)],
-            row_sems.at[pair],
-        )
-        for pair in range(halves // 2)
-    ]
-    gate_up_fetches = [
-        pltpu.make_async_copy(gate_up_hbm.at[half], gate_up_ref.at[half], in_sems.at[0, half])
-        for half in range(halves)
-    ]
-    down_fetches = [
-        pltpu.make_async_copy(down_hbm.at[half], down_ref.at[half], in_sems.at[1, half])
-        for half in range(halves)
-    ]
-    row_fetches[0].start()
-    gate_up_fetches[0].start()
-    down_fetches[0].start()
     copies = []
     for pair in range(halves // 2):
         both = pl.ds(2 * pair * per_half, 2 * per_half)
-        row_fetches[pair].wait()
-        if pair + 1 < halves // 2:
-            row_fetches[pair + 1].start()
         arrived = rows_ref[:, both, :].astype(jnp.float32)
         results = []
         for member in range(2):
             half = 2 * pair + member
             own = arrived[:, member * per_half : (member + 1) * per_half]
             own = own.reshape(sources * per_half, width).astype(jnp.bfloat16)
-            gate_up_fetches[half].wait()
-            if half + 1 < halves:
-                gate_up_fetches[half + 1].start()
-                down_fetches[half + 1].start()
             act = silu_times(dot(own, gate_up_ref[half, 0]), dot(own, gate_up_ref[half, 1]))
-            down_fetches[half].wait()
             results.append(dot(act, down_ref[half]).reshape(sources, per_half, width))
         out_ref[:, both, :] = jnp.concatenate(results, axis=1).astype(jnp.bfloat16)
         copy = pltpu.make_async_copy(out_ref.at[:, both], out_hbm.at[:, both], out_sems.at[pair])
@@ -544,11 +517,11 @@
 
     mixed_part, info = pl.pallas_call(
         project_kernel,
-        out_shape=[shape((Z_SIZE, all_tokens, part), bf16), shape((all_tokens, 128), bf16)],
+        out_shape=[pltpu.HBM((Z_SIZE, all_tokens, part), bf16), shape((all_tokens, 128), bf16)],
         in_specs=[SMEM] + [VMEM] * (Z_SIZE + 1),
         out_specs=[VMEM] * 2,
         scratch_shapes=[pltpu.VMEM((Z_SIZE, tokens, sent_width), bf16)],
-        compiler_params=params(58),
+        compiler_params=params(),
         cost_estimate=cost(2 * all_tokens * width * part, 3 * MIB),
         name="project",
     )(z_scalar, *gathered, turned_weight)
@@ -571,14 +544,14 @@
     )(scalar(lax.rem(z_index, 2)), info)
     outgoing = pl.pallas_call(
         pick_kernel,
-        out_shape=shape((PLANE, picked, width), bf16),
+        out_shape=pltpu.HBM((PLANE, picked, width), bf16),
         in_specs=[VMEM] * 3,
         out_specs=HBM,
         scratch_shapes=[
             pltpu.VMEM((PLANE, picked, width), bf16),
             pltpu.SemaphoreType.DMA((PLANE,)),
         ],
-        compiler_params=params(58),
+        compiler_params=params(),
         cost_estimate=cost(2 * PLANE * picked * all_tokens * width, 4 * MIB),
         name="pick",
     )(onehot, gain, mixed)
@@ -590,15 +563,28 @@
         out_shape=[shape((PLANE,) + in_plane[0].shape[1:], bf16)] * Z_SIZE,
         in_specs=[SMEM] + [VMEM] * PLANE,
         out_specs=[VMEM] * Z_SIZE,
-        compiler_params=params(58),
+        compiler_params=params(),
         cost_estimate=cost(0, 2 * MIB),
         name="regroup",
     )(z_scalar, *in_plane)
+    grouped, gate_up, expert_down = lax.optimization_barrier((grouped, gate_up, expert_down))
+    gate_up, down = pl.pallas_call(
+        hold_kernel,
+        out_shape=[pltpu.VMEM(gate_up.shape, bf16), pltpu.VMEM(expert_down.shape, bf16)],
+        in_specs=[HBM] * 2,
+        out_specs=[VMEM] * 2,
+        scratch_shapes=[pltpu.SemaphoreType.DMA((2 * local_halves,))],
+        compiler_params=params(4),
+        cost_estimate=cost(0, 18 * MIB),
+        name="hold",
+    )(gate_up, expert_down)
     arrived_cache = [grouped[0]]
     for step in range(1, Z_SIZE):
         arrived_cache.append(lax.ppermute(grouped[step], "seq", z_pairs[step]))
 
-    arrived, shared_weight = lax.optimization_barrier((arrived, shared_weight))
+    arrived, gate_up, down, shared_weight = lax.optimization_barrier(
+        (arrived, gate_up, down, shared_weight)
+    )
     shared_part, own_mixed = pl.pallas_call(
         shared_kernel,
         out_shape=[shape((all_tokens, width), bf16), shape((tokens, width), f32)],
@@ -611,22 +597,17 @@
 
     returning = pl.pallas_call(
         experts_kernel,
-        out_shape=shape((PLANE, picked, width), bf16),
-        in_specs=[HBM, HBM, HBM],
+        out_shape=pltpu.HBM((PLANE, picked, width), bf16),
+        in_specs=[VMEM] * 3,
         out_specs=HBM,
         scratch_shapes=[
             pltpu.VMEM((PLANE, picked, width), bf16),
-            pltpu.VMEM((local_halves, 2, width, half_ff), bf16),
-            pltpu.VMEM((local_halves, half_ff, width), bf16),
-            pltpu.VMEM((PLANE, picked, width), bf16),
-            pltpu.SemaphoreType.DMA((2, local_halves)),
-            pltpu.SemaphoreType.DMA((local_halves // 2,)),
             pltpu.SemaphoreType.DMA((local_halves // 2,)),
         ],
-        compiler_params=params(58),
+        compiler_params=params(20),
         cost_estimate=cost(6 * PLANE * picked * half_ff * width, 14 * MIB),
         name="experts",
-    )(arrived, gate_up, expert_down)
+    )(arrived, gate_up, down)
     returning, arrived_cache = lax.optimization_barrier((returning, arrived_cache))
     returned = exchange(returning, planes).reshape(PLANE * picked, width)
 

time: 198 us -> 196 us (0.990)
  Pallas kernels: 28.8 us -> 20.4 us
  local copies, waits for them, and re-layouts: 23.9 us -> 29.5 us
    unnamed x73, local copies, waits for them, and re-layouts: 15 us -> 24.3 us
    pallas_call x3 -> x4, Pallas kernels: 14.9 us -> 7.86 us  [the longest x1 3.51 us: shards(): pl.pallas_call(experts_kernel, out_shape=pltpu.HBM((PLANE, picked, width)...]
    ppermute x7, waiting for transfers between devices: 3.33 us -> 0.81 us  [shards(): piece = lax.ppermute(piece, 'seq', pairs)]
    optimization_barrier x1, local copies, waits for them, and re-layouts: 6.25 us -> 3.79 us  [shards(): lax.optimization_barrier((gathered, cache_blocks, expert_gate_up))]
    ppermute x6, waiting for transfers between devices: 34.4 us -> 36.5 us  [along_z(): lax.ppermute(arrays[step], 'seq', z_pairs[step])]
  transfers between devices with their start and end apart: 25 -> 25, of which waited for: 9 -> 9; matrix products, arithmetic and copies ran while one was open for 7% -> 5% of each run, Pallas kernels for 14% -> 10%
where the time goes in v4:
time: 196 us; the launch traced here: 195 us
  waiting for transfers between devices  79.1 us (40%)
  starting transfers between devices  47.8 us (24%)
  local copies, waits for them, and re-layouts  29.5 us (15%)
  Pallas kernels  20.4 us (10%)
  between operations  14.4 us (7%)
  other arithmetic  3.57 us (2%)
    all_to_all x3, waiting for transfers between devices, exchange(): lax.all_to_all(array, 'seq', split_axis=0, concat_axis=0, tiled=True, axi...  41.1 us
    ppermute x6, waiting for transfers between devices, along_z(): lax.ppermute(arrays[step], 'seq', z_pairs[step])  36.5 us
    unnamed x73, local copies, waits for them, and re-layouts  24.3 us
    all_to_all x3, starting transfers between devices, exchange(): lax.all_to_all(array, 'seq', split_axis=0, concat_axis=0, tiled=True, axi...  13.5 us
    ppermute x4, starting transfers between devices, from_behind(): return lax.ppermute(shard, axis, pairs)  12 us
    ppermute x6, starting transfers between devices, along_z(): lax.ppermute(arrays[step], 'seq', z_pairs[step])  8.72 us
    ppermute x7, starting transfers between devices, shards(): piece = lax.ppermute(piece, 'seq', pairs)  8.22 us
    ppermute x3, starting transfers between devices, shards(): arrived_cache.append(lax.ppermute(grouped[step], 'seq', z_pairs[step]))  5.31 us
  transfers between devices with their start and end apart: 25, of which 9 were waited for; matrix products, arithmetic and copies ran while one was open for 5% of the time, Pallas kernels for 10%

profile of v4, /device:TPU:10, one launch (start us, length us, event | category | flops | bytes accessed | tf_op | source)
XLA Modules:
  0.0 194.8 jit_solution(10945774139218019224)
XLA Ops:
  9.6 3.4 %collective-permute-start = (bf16[64,1024]{1,0:T(8,128)(2,1)S(1)}, bf16[64,1024]{1,0:T(8,128)(2,1)S(1)}, u32[]{:S(2)}, u32[]{:S(2)}) collective-permute-start(bf16[64,1024]{1,0:T(8,128)(2,1)S(1)} %constant_dynamic-update-slice_fusion.own_ref), channel_id=1, source_target_pairs={{0,4},{1,5},{2,6},{3,7},{4,8},{5,9},{6,10},{7,11},{8,12},{9,13},{1... | collective-permute-start | bytes 393224 | tf_op jit(solution)/shard_map/ppermute | solution.py:28
  13.1 2.6 %collective-permute-start.1 = (bf16[64,1024]{1,0:T(8,128)(2,1)S(1)}, bf16[64,1024]{1,0:T(8,128)(2,1)S(1)}, u32[]{:S(2)}, u32[]{:S(2)}) collective-permute-start(bf16[64,1024]{1,0:T(8,128)(2,1)S(1)} %constant_dynamic-update-slice_fusion.own_ref), channel_id=1, source_target_pairs={{0,3},{1,4},{2,5},{3,6},{4,7},{5,8},{6,9},{7,10},{8,11},{9,12},{10... | collective-permute-start | bytes 393224 | tf_op jit(solution)/shard_map/ppermute | solution.py:28
  15.6 3.4 %collective-permute-start.2 = (bf16[64,1024]{1,0:T(8,128)(2,1)S(1)}, bf16[64,1024]{1,0:T(8,128)(2,1)S(1)}, u32[]{:S(2)}, u32[]{:S(2)}) collective-permute-start(bf16[64,1024]{1,0:T(8,128)(2,1)S(1)} %constant_dynamic-update-slice_fusion.own_ref), channel_id=1, source_target_pairs={{0,2},{1,3},{2,4},{3,5},{4,6},{5,7},{6,8},{7,9},{8,10},{9,11},{10,... | collective-permute-start | bytes 393224 | tf_op jit(solution)/shard_map/ppermute | solution.py:28
  19.0 2.6 %collective-permute-start.3 = (bf16[64,1024]{1,0:T(8,128)(2,1)S(1)}, bf16[64,1024]{1,0:T(8,128)(2,1)S(1)}, u32[]{:S(2)}, u32[]{:S(2)}) collective-permute-start(bf16[64,1024]{1,0:T(8,128)(2,1)S(1)} %constant_dynamic-update-slice_fusion.own_ref), channel_id=1, source_target_pairs={{0,1},{1,2},{2,3},{3,4},{4,5},{5,6},{6,7},{7,8},{8,9},{9,10},{10,1... | collective-permute-start | bytes 393224 | tf_op jit(solution)/shard_map/ppermute | solution.py:28
  26.8 3.9 %attention.1 = (bf16[64,2048]{1,0:T(8,128)(2,1)}, bf16[64,2048]{1,0:T(8,128)(2,1)}, bf16[64,2048]{1,0:T(8,128)(2,1)}, bf16[64,2048]{1,0:T(8,128)(2,1)}) custom-call(s32[1]{0:T(128)} %bitcast.z_ref, s32[1]{0:T(128)} %bitcast.1.first_ref, s32[16]{0:T(128)} %lengths_ref.1, bf16[64,1536]{1,0:T(8,128)(2,1)} %q_ref.1, bf16[64,1024]{1,0:T(8,128)(2,1)} %copy-done.31, ...), custom_call_target="tpu_custom_call" | custom-call | flops 125829120 | bytes 3145728 | tf_op jit(solution)/shard_map/attention/pallas_call | solution.py:483
  34.1 6.1 %collective-permute-done.4.refs_1_ = bf16[64,2048]{1,0:T(8,128)(2,1)S(1)} collective-permute-done((bf16[64,2048]{1,0:T(8,128)(2,1)}, bf16[64,2048]{1,0:T(8,128)(2,1)S(1)}, u32[]{:S(2)}, u32[]{:S(2)}) %collective-permute-start.4) | collective-permute-done | bytes 262176 | tf_op jit(solution)/shard_map/ppermute | solution.py:465
  40.2 16.0 %collective-permute-done.5.refs_2_ = bf16[64,2048]{1,0:T(8,128)(2,1)S(1)} collective-permute-done((bf16[64,2048]{1,0:T(8,128)(2,1)}, bf16[64,2048]{1,0:T(8,128)(2,1)S(1)}, u32[]{:S(2)}, u32[]{:S(2)}) %collective-permute-start.5) | collective-permute-done | bytes 262176 | tf_op jit(solution)/shard_map/ppermute | solution.py:465
  61.5 4.5 %all-to-all-start = ((bf16[4,256,384]{2,1,0:T(8,128)(2,1)}), bf16[4,256,384]{2,1,0:T(8,128)(2,1)S(1)}, u32[]{:S(2)}, u32[]{:S(2)}) async-start(bf16[4,256,384]{2,1,0:T(8,128)(2,1)} %get-tuple-element.69), calls=%async_computation | async-start | bytes 1572864 | tf_op jit(solution)/shard_map/all_to_all | solution.py:442
  73.4 2.2 %collective-permute-start.13 = (bf16[4,32,4,128]{3,2,1,0:T(4,128)(2,1)S(1)}, bf16[4,32,4,128]{3,2,1,0:T(4,128)(2,1)S(1)}, u32[]{:S(2)}, u32[]{:S(2)}) collective-permute-start(bf16[4,32,4,128]{3,2,1,0:T(4,128)(2,1)S(1)} %get-tuple-element.112), channel_id=1, source_target_pairs={{0,7},{1,0},{2,1},{3,2},{4,3},{5,4},{6,5},{7,6},{8,15},{9,8},{10,9... | collective-permute-start | bytes 393224 | tf_op jit(solution)/shard_map/ppermute | solution.py:514
  75.7 1.9 tables.1
  78.4 4.7 %all-to-all-done.mixed_ref = bf16[4,256,384]{2,1,0:T(8,128)(2,1)S(1)} async-done(((bf16[4,256,384]{2,1,0:T(8,128)(2,1)}), bf16[4,256,384]{2,1,0:T(8,128)(2,1)S(1)}, u32[]{:S(2)}, u32[]{:S(2)}) %all-to-all-start) | async-done | bytes 786464 | tf_op jit(solution)/shard_map/all_to_all | solution.py:442
  83.1 2.1 %pick.1 = bf16[8,96,1536]{2,1,0:T(8,128)(2,1)} custom-call(bf16[768,256]{1,0:T(8,128)(2,1)S(1)} %get-tuple-element.71.onehot_ref, f32[1,1536]{1,0:T(1,128)S(1)} %reshape.33.gain_ref, bf16[4,256,384]{2,1,0:T(8,128)(2,1)S(1)} %all-to-all-done.mixed_ref), custom_call_target="tpu_custom_call" | custom-call | flops 603979776 | bytes 4194304 | tf_op jit(solution)/shard_map/pick/pallas_call | solution.py:545
  88.5 3.9 %all-to-all-start.1 = ((bf16[8,96,1536]{2,1,0:T(8,128)(2,1)}), bf16[8,96,1536]{2,1,0:T(8,128)(2,1)S(1)}, u32[]{:S(2)}, u32[]{:S(2)}) async-start(bf16[8,96,1536]{2,1,0:T(8,128)(2,1)} %pick.1), calls=%async_computation.1 | async-start | bytes 4718592 | tf_op jit(solution)/shard_map/all_to_all | solution.py:442
  92.5 3.8 %copy.35 = bf16[4,1536,2,256]{3,1,2,0:T(8,128)(2,1)S(1)} copy(bf16[4,1536,2,256]{3,2,1,0:T(2,128)(2,1)} %param.26) | data formatting | bytes 12582912 | tf_op jit(solution)/shard_map/optimization_barrier | solution.py:496
  99.1 4.2 %collective-permute-start.15 = (bf16[8,32,4,128]{3,2,1,0:T(4,128)(2,1)}, bf16[8,32,4,128]{3,2,1,0:T(4,128)(2,1)}, u32[]{:S(2)}, u32[]{:S(2)}) collective-permute-start(bf16[8,32,4,128]{3,2,1,0:T(4,128)(2,1)} %get-tuple-element.100), channel_id=1, source_target_pairs={{0,16},{1,17},{2,18},{3,19},{4,20},{5,21},{6,22},{7,23},{8,24},{9,... | collective-permute-start | bytes 786440 | tf_op jit(solution)/shard_map/ppermute | solution.py:583
  104.0 2.6 %copy-done = bf16[4,2,1536,256]{3,2,1,0:T(8,128)(2,1)} copy-done((bf16[4,2,1536,256]{3,2,1,0:T(8,128)(2,1)}, bf16[4,2,1536,256]{3,2,1,0:T(8,128)(2,1)S(1)}, u32[]{:S(2)}) %copy-start) | copy-done | bytes 6291480
  108.3 12.0 %all-to-all-done.1.rows_ref = bf16[8,96,1536]{2,1,0:T(8,128)(2,1)S(1)} async-done(((bf16[8,96,1536]{2,1,0:T(8,128)(2,1)}), bf16[8,96,1536]{2,1,0:T(8,128)(2,1)S(1)}, u32[]{:S(2)}, u32[]{:S(2)}) %all-to-all-start.1) | async-done | bytes 2359328 | tf_op jit(solution)/shard_map/all_to_all | solution.py:442
  120.4 2.8 %copy-done.1 = bf16[4,2,1536,256]{3,2,1,0:T(8,128)(2,1)S(1)} copy-done((bf16[4,2,1536,256]{3,2,1,0:T(8,128)(2,1)S(1)}, bf16[4,2,1536,256]{3,2,1,0:T(8,128)(2,1)}, u32[]{:S(2)}) %copy-start.1) | copy-done | bytes 6291480
  125.0 3.5 %experts.1 = bf16[8,96,1536]{2,1,0:T(8,128)(2,1)} custom-call(bf16[8,96,1536]{2,1,0:T(8,128)(2,1)S(1)} %all-to-all-done.1.rows_ref, bf16[4,2,1536,256]{3,2,1,0:T(8,128)(2,1)S(1)} %copy-done.1, bf16[4,256,1536]{2,1,0:T(8,128)(2,1)S(1)} %copy-done.3), custom_call_target="tpu_custom_call" | custom-call | flops 1811939328 | bytes 14680064 | tf_op jit(solution)/shard_map/experts/pallas_call | solution.py:598
  129.3 5.0 %all-to-all-start.2 = ((bf16[8,96,1536]{2,1,0:T(8,128)(2,1)}), bf16[8,96,1536]{2,1,0:T(8,128)(2,1)S(1)}, u32[]{:S(2)}, u32[]{:S(2)}) async-start(bf16[8,96,1536]{2,1,0:T(8,128)(2,1)} %experts.1), calls=%async_computation.2 | async-start | bytes 4718592 | tf_op jit(solution)/shard_map/all_to_all | solution.py:442
  137.9 24.4 %all-to-all-done.2 = bf16[8,96,1536]{2,1,0:T(8,128)(2,1)S(1)} async-done(((bf16[8,96,1536]{2,1,0:T(8,128)(2,1)}), bf16[8,96,1536]{2,1,0:T(8,128)(2,1)S(1)}, u32[]{:S(2)}, u32[]{:S(2)}) %all-to-all-start.2) | async-done | bytes 2359328 | tf_op jit(solution)/shard_map/all_to_all | solution.py:442
  166.3 4.2 %collective-permute-start.18 = (bf16[64,1536]{1,0:T(8,128)(2,1)S(1)}, bf16[64,1536]{1,0:T(8,128)(2,1)S(1)}, u32[]{:S(2)}, u32[]{:S(2)}) collective-permute-start(bf16[64,1536]{1,0:T(8,128)(2,1)S(1)} %get-tuple-element.106), channel_id=1, source_target_pairs={{0,16},{1,17},{2,18},{3,19},{4,20},{5,21},{6,22},{7,23},{8,24},{9,... | collective-permute-start | bytes 589832 | tf_op jit(solution)/shard_map/ppermute | solution.py:465
  174.4 8.9 %collective-permute-done.18.refs_2_ = bf16[64,1536]{1,0:T(8,128)(2,1)S(1)} collective-permute-done((bf16[64,1536]{1,0:T(8,128)(2,1)S(1)}, bf16[64,1536]{1,0:T(8,128)(2,1)S(1)}, u32[]{:S(2)}, u32[]{:S(2)}) %collective-permute-start.18) | collective-permute-done | bytes 196640 | tf_op jit(solution)/shard_map/ppermute | solution.py:465
  183.3 3.8 %collective-permute-done.19.refs_3_ = bf16[64,1536]{1,0:T(8,128)(2,1)S(1)} collective-permute-done((bf16[64,1536]{1,0:T(8,128)(2,1)S(1)}, bf16[64,1536]{1,0:T(8,128)(2,1)S(1)}, u32[]{:S(2)}, u32[]{:S(2)}) %collective-permute-start.19) | collective-permute-done | bytes 196640 | tf_op jit(solution)/shard_map/ppermute | solution.py:465
  (119 shorter events, 47.7 us)
Async XLA Ops:
  7.2 50.6 %all-gather.4.cloned.1.call-start = ((), (), s32[]{:S(2)}) async-start(), calls=%async_computation.3 | async-start | bytes 1327104 | tf_op jit(solution)/shard_map/all_gather | solution.py:449
  7.9 100.4 %all-gather.6.cloned.1.call-start = ((), (), s32[]{:S(2)}) async-start(), calls=%async_computation.4 | async-start | bytes 2654208 | tf_op jit(solution)/shard_map/all_gather | solution.py:494
  9.6 16.4 %collective-permute-start = (bf16[64,1024]{1,0:T(8,128)(2,1)S(1)}, bf16[64,1024]{1,0:T(8,128)(2,1)S(1)}, u32[]{:S(2)}, u32[]{:S(2)}) collective-permute-start(bf16[64,1024]{1,0:T(8,128)(2,1)S(1)} %constant_dynamic-update-slice_fusion.own_ref), channel_id=1, source_target_pairs={{0,4},{1,5},{2,6},{3,7},{4,8},{5,9},{6,10},{7,11},{8,12},{9,13},{1... | collective-permute-start | bytes 393224 | tf_op jit(solution)/shard_map/ppermute | solution.py:28
  13.1 13.0 %collective-permute-start.1 = (bf16[64,1024]{1,0:T(8,128)(2,1)S(1)}, bf16[64,1024]{1,0:T(8,128)(2,1)S(1)}, u32[]{:S(2)}, u32[]{:S(2)}) collective-permute-start(bf16[64,1024]{1,0:T(8,128)(2,1)S(1)} %constant_dynamic-update-slice_fusion.own_ref), channel_id=1, source_target_pairs={{0,3},{1,4},{2,5},{3,6},{4,7},{5,8},{6,9},{7,10},{8,11},{9,12},{10... | collective-permute-start | bytes 393224 | tf_op jit(solution)/shard_map/ppermute | solution.py:28
  15.6 10.4 %collective-permute-start.2 = (bf16[64,1024]{1,0:T(8,128)(2,1)S(1)}, bf16[64,1024]{1,0:T(8,128)(2,1)S(1)}, u32[]{:S(2)}, u32[]{:S(2)}) collective-permute-start(bf16[64,1024]{1,0:T(8,128)(2,1)S(1)} %constant_dynamic-update-slice_fusion.own_ref), channel_id=1, source_target_pairs={{0,2},{1,3},{2,4},{3,5},{4,6},{5,7},{6,8},{7,9},{8,10},{9,11},{10,... | collective-permute-start | bytes 393224 | tf_op jit(solution)/shard_map/ppermute | solution.py:28
  19.0 7.1 %collective-permute-start.3 = (bf16[64,1024]{1,0:T(8,128)(2,1)S(1)}, bf16[64,1024]{1,0:T(8,128)(2,1)S(1)}, u32[]{:S(2)}, u32[]{:S(2)}) collective-permute-start(bf16[64,1024]{1,0:T(8,128)(2,1)S(1)} %constant_dynamic-update-slice_fusion.own_ref), channel_id=1, source_target_pairs={{0,1},{1,2},{2,3},{3,4},{4,5},{5,6},{6,7},{7,8},{8,9},{9,10},{10,1... | collective-permute-start | bytes 393224 | tf_op jit(solution)/shard_map/ppermute | solution.py:28
  30.7 9.4 %collective-permute-start.4 = (bf16[64,2048]{1,0:T(8,128)(2,1)}, bf16[64,2048]{1,0:T(8,128)(2,1)S(1)}, u32[]{:S(2)}, u32[]{:S(2)}) collective-permute-start(bf16[64,2048]{1,0:T(8,128)(2,1)} %get-tuple-element.62), channel_id=1, source_target_pairs={{0,8},{1,9},{2,10},{3,11},{4,12},{5,13},{6,14},{7,15},{8,16},{9,17... | collective-permute-start | bytes 786440 | tf_op jit(solution)/shard_map/ppermute | solution.py:465
  32.3 23.8 %collective-permute-start.5 = (bf16[64,2048]{1,0:T(8,128)(2,1)}, bf16[64,2048]{1,0:T(8,128)(2,1)S(1)}, u32[]{:S(2)}, u32[]{:S(2)}) collective-permute-start(bf16[64,2048]{1,0:T(8,128)(2,1)} %get-tuple-element.63), channel_id=1, source_target_pairs={{0,16},{1,17},{2,18},{3,19},{4,20},{5,21},{6,22},{7,23},{8,24},{9,... | collective-permute-start | bytes 786440 | tf_op jit(solution)/shard_map/ppermute | solution.py:465
  33.6 24.2 %collective-permute-start.6 = (bf16[64,2048]{1,0:T(8,128)(2,1)}, bf16[64,2048]{1,0:T(8,128)(2,1)S(1)}, u32[]{:S(2)}, u32[]{:S(2)}) collective-permute-start(bf16[64,2048]{1,0:T(8,128)(2,1)} %get-tuple-element.64), channel_id=1, source_target_pairs={{0,24},{1,25},{2,26},{3,27},{4,28},{5,29},{6,30},{7,31},{8,0},{9,1... | collective-permute-start | bytes 786440 | tf_op jit(solution)/shard_map/ppermute | solution.py:465
  61.5 21.6 %all-to-all-start = ((bf16[4,256,384]{2,1,0:T(8,128)(2,1)}), bf16[4,256,384]{2,1,0:T(8,128)(2,1)S(1)}, u32[]{:S(2)}, u32[]{:S(2)}) async-start(bf16[4,256,384]{2,1,0:T(8,128)(2,1)} %get-tuple-element.69), calls=%async_computation | async-start | bytes 1572864 | tf_op jit(solution)/shard_map/all_to_all | solution.py:442
  66.7 6.7 %collective-permute-start.8 = (bf16[4,32,4,128]{3,2,1,0:T(4,128)(2,1)S(1)}, bf16[4,32,4,128]{3,2,1,0:T(4,128)(2,1)S(1)}, u32[]{:S(2)}, u32[]{:S(2)}) collective-permute-start(bf16[4,32,4,128]{3,2,1,0:T(4,128)(2,1)S(1)} %get-tuple-element.117), channel_id=1, source_target_pairs={{0,2},{1,3},{2,4},{3,5},{4,6},{5,7},{6,0},{7,1},{8,10},{9,11},{10,... | collective-permute-start | bytes 393224 | tf_op jit(solution)/shard_map/ppermute | solution.py:514
  68.3 17.0 %collective-permute-start.9 = (bf16[4,32,4,128]{3,2,1,0:T(4,128)(2,1)S(1)}, bf16[4,32,4,128]{3,2,1,0:T(4,128)(2,1)S(1)}, u32[]{:S(2)}, u32[]{:S(2)}) collective-permute-start(bf16[4,32,4,128]{3,2,1,0:T(4,128)(2,1)S(1)} %get-tuple-element.116), channel_id=1, source_target_pairs={{0,3},{1,4},{2,5},{3,6},{4,7},{5,0},{6,1},{7,2},{8,11},{9,12},{10,... | collective-permute-start | bytes 393224 | tf_op jit(solution)/shard_map/ppermute | solution.py:514
  69.6 16.3 %collective-permute-start.10 = (bf16[4,32,4,128]{3,2,1,0:T(4,128)(2,1)S(1)}, bf16[4,32,4,128]{3,2,1,0:T(4,128)(2,1)S(1)}, u32[]{:S(2)}, u32[]{:S(2)}) collective-permute-start(bf16[4,32,4,128]{3,2,1,0:T(4,128)(2,1)S(1)} %get-tuple-element.115), channel_id=1, source_target_pairs={{0,4},{1,5},{2,6},{3,7},{4,0},{5,1},{6,2},{7,3},{8,12},{9,13},{10,... | collective-permute-start | bytes 393224 | tf_op jit(solution)/shard_map/ppermute | solution.py:514
  71.1 15.4 %collective-permute-start.11 = (bf16[4,32,4,128]{3,2,1,0:T(4,128)(2,1)S(1)}, bf16[4,32,4,128]{3,2,1,0:T(4,128)(2,1)S(1)}, u32[]{:S(2)}, u32[]{:S(2)}) collective-permute-start(bf16[4,32,4,128]{3,2,1,0:T(4,128)(2,1)S(1)} %get-tuple-element.114), channel_id=1, source_target_pairs={{0,5},{1,6},{2,7},{3,0},{4,1},{5,2},{6,3},{7,4},{8,13},{9,14},{10,... | collective-permute-start | bytes 393224 | tf_op jit(solution)/shard_map/ppermute | solution.py:514
  71.9 15.3 %collective-permute-start.12 = (bf16[4,32,4,128]{3,2,1,0:T(4,128)(2,1)S(1)}, bf16[4,32,4,128]{3,2,1,0:T(4,128)(2,1)S(1)}, u32[]{:S(2)}, u32[]{:S(2)}) collective-permute-start(bf16[4,32,4,128]{3,2,1,0:T(4,128)(2,1)S(1)} %get-tuple-element.113), channel_id=1, source_target_pairs={{0,6},{1,7},{2,0},{3,1},{4,2},{5,3},{6,4},{7,5},{8,14},{9,15},{10,... | collective-permute-start | bytes 393224 | tf_op jit(solution)/shard_map/ppermute | solution.py:514
  73.4 14.4 %collective-permute-start.13 = (bf16[4,32,4,128]{3,2,1,0:T(4,128)(2,1)S(1)}, bf16[4,32,4,128]{3,2,1,0:T(4,128)(2,1)S(1)}, u32[]{:S(2)}, u32[]{:S(2)}) collective-permute-start(bf16[4,32,4,128]{3,2,1,0:T(4,128)(2,1)S(1)} %get-tuple-element.112), channel_id=1, source_target_pairs={{0,7},{1,0},{2,1},{3,2},{4,3},{5,4},{6,5},{7,6},{8,15},{9,8},{10,9... | collective-permute-start | bytes 393224 | tf_op jit(solution)/shard_map/ppermute | solution.py:514
  88.5 31.9 %all-to-all-start.1 = ((bf16[8,96,1536]{2,1,0:T(8,128)(2,1)}), bf16[8,96,1536]{2,1,0:T(8,128)(2,1)S(1)}, u32[]{:S(2)}, u32[]{:S(2)}) async-start(bf16[8,96,1536]{2,1,0:T(8,128)(2,1)} %pick.1), calls=%async_computation.1 | async-start | bytes 4718592 | tf_op jit(solution)/shard_map/all_to_all | solution.py:442
  98.0 30.6 %collective-permute-start.14 = (bf16[8,32,4,128]{3,2,1,0:T(4,128)(2,1)}, bf16[8,32,4,128]{3,2,1,0:T(4,128)(2,1)S(1)}, u32[]{:S(2)}, u32[]{:S(2)}) collective-permute-start(bf16[8,32,4,128]{3,2,1,0:T(4,128)(2,1)} %get-tuple-element.99), channel_id=1, source_target_pairs={{0,8},{1,9},{2,10},{3,11},{4,12},{5,13},{6,14},{7,15},{8,16},{9,17... | collective-permute-start | bytes 786440 | tf_op jit(solution)/shard_map/ppermute | solution.py:583
  99.1 29.5 %collective-permute-start.15 = (bf16[8,32,4,128]{3,2,1,0:T(4,128)(2,1)}, bf16[8,32,4,128]{3,2,1,0:T(4,128)(2,1)}, u32[]{:S(2)}, u32[]{:S(2)}) collective-permute-start(bf16[8,32,4,128]{3,2,1,0:T(4,128)(2,1)} %get-tuple-element.100), channel_id=1, source_target_pairs={{0,16},{1,17},{2,18},{3,19},{4,20},{5,21},{6,22},{7,23},{8,24},{9,... | collective-permute-start | bytes 786440 | tf_op jit(solution)/shard_map/ppermute | solution.py:583
  103.3 25.3 %collective-permute-start.16 = (bf16[8,32,4,128]{3,2,1,0:T(4,128)(2,1)}, bf16[8,32,4,128]{3,2,1,0:T(4,128)(2,1)}, u32[]{:S(2)}, u32[]{:S(2)}) collective-permute-start(bf16[8,32,4,128]{3,2,1,0:T(4,128)(2,1)} %get-tuple-element.101), channel_id=1, source_target_pairs={{0,24},{1,25},{2,26},{3,27},{4,28},{5,29},{6,30},{7,31},{8,0},{9,1... | collective-permute-start | bytes 786440 | tf_op jit(solution)/shard_map/ppermute | solution.py:583
  129.3 33.0 %all-to-all-start.2 = ((bf16[8,96,1536]{2,1,0:T(8,128)(2,1)}), bf16[8,96,1536]{2,1,0:T(8,128)(2,1)S(1)}, u32[]{:S(2)}, u32[]{:S(2)}) async-start(bf16[8,96,1536]{2,1,0:T(8,128)(2,1)} %experts.1), calls=%async_computation.2 | async-start | bytes 4718592 | tf_op jit(solution)/shard_map/all_to_all | solution.py:442
  165.3 9.0 %collective-permute-start.17 = (bf16[64,1536]{1,0:T(8,128)(2,1)S(1)}, bf16[64,1536]{1,0:T(8,128)(2,1)S(1)}, u32[]{:S(2)}, u32[]{:S(2)}) collective-permute-start(bf16[64,1536]{1,0:T(8,128)(2,1)S(1)} %get-tuple-element.105), channel_id=1, source_target_pairs={{0,8},{1,9},{2,10},{3,11},{4,12},{5,13},{6,14},{7,15},{8,16},{9,17... | collective-permute-start | bytes 589832 | tf_op jit(solution)/shard_map/ppermute | solution.py:465
  166.3 17.0 %collective-permute-start.18 = (bf16[64,1536]{1,0:T(8,128)(2,1)S(1)}, bf16[64,1536]{1,0:T(8,128)(2,1)S(1)}, u32[]{:S(2)}, u32[]{:S(2)}) collective-permute-start(bf16[64,1536]{1,0:T(8,128)(2,1)S(1)} %get-tuple-element.106), channel_id=1, source_target_pairs={{0,16},{1,17},{2,18},{3,19},{4,20},{5,21},{6,22},{7,23},{8,24},{9,... | collective-permute-start | bytes 589832 | tf_op jit(solution)/shard_map/ppermute | solution.py:465
  170.4 16.7 %collective-permute-start.19 = (bf16[64,1536]{1,0:T(8,128)(2,1)S(1)}, bf16[64,1536]{1,0:T(8,128)(2,1)S(1)}, u32[]{:S(2)}, u32[]{:S(2)}) collective-permute-start(bf16[64,1536]{1,0:T(8,128)(2,1)S(1)} %get-tuple-element.107), channel_id=1, source_target_pairs={{0,24},{1,25},{2,26},{3,27},{4,28},{5,29},{6,30},{7,31},{8,0},{9,1... | collective-permute-start | bytes 589832 | tf_op jit(solution)/shard_map/ppermute | solution.py:465
  (37 other events, 146.9 us)
Sparse Core Ops, SparseCore 0:
  9.9 29.4 all-gather.3
  41.2 29.0 all-gather.5

commit v5 on v4

--- a/solution.py
+++ b/solution.py
@@ -163,6 +163,12 @@
     return (gate / (1.0 + jnp.exp(-gate)) * up).astype(jnp.bfloat16)
 
 
+def join_kernel(key_ref, value_ref, out_ref):
+    width = key_ref.shape[1]
+    out_ref[:, :width] = key_ref[...]
+    out_ref[:, width:] = value_ref[...]
+
+
 def attention_kernel(
     z_ref,
     first_ref,
@@ -340,22 +346,19 @@
     out_ref[...] = dot(act, down_weight).astype(jnp.bfloat16)
 
 
-def hold_kernel(*refs):
-    count = (len(refs) + 1) // 2
-    copies = []
-    for from_ref, to_ref in zip(refs[: count - 1], refs[count - 1 : -1]):
-        for at in range(to_ref.shape[0]):
-            copy = pltpu.make_async_copy(from_ref.at[at], to_ref.at[at], refs[-1].at[len(copies)])
-            copy.start()
-            copies.append(copy)
-    for copy in copies:
-        copy.wait()
-
-
-def experts_kernel(rows_ref, gate_up_ref, down_ref, out_hbm, out_ref, out_sems):
+def experts_kernel(
+    rows_ref, gate_up_hbm, down_hbm, out_hbm, gate_up_ref, down_ref, out_ref, in_sems, out_sems
+):
     halves = gate_up_ref.shape[0]
     sources, rows, width = rows_ref.shape
     per_half = rows // halves
+    fetches = []
+    for half in range(halves):
+        pairs = ((gate_up_hbm, gate_up_ref), (down_hbm, down_ref))
+        for at, (from_ref, to_ref) in enumerate(pairs):
+            fetch = pltpu.make_async_copy(from_ref.at[half], to_ref.at[half], in_sems.at[at, half])
+            fetch.start()
+            fetches.append(fetch)
     copies = []
     for pair in range(halves // 2):
         both = pl.ds(2 * pair * per_half, 2 * per_half)
@@ -365,7 +368,9 @@
             half = 2 * pair + member
             own = arrived[:, member * per_half : (member + 1) * per_half]
             own = own.reshape(sources * per_half, width).astype(jnp.bfloat16)
+            fetches[2 * half].wait()
             act = silu_times(dot(own, gate_up_ref[half, 0]), dot(own, gate_up_ref[half, 1]))
+            fetches[2 * half + 1].wait()
             results.append(dot(act, down_ref[half]).reshape(sources, per_half, width))
         out_ref[:, both, :] = jnp.concatenate(results, axis=1).astype(jnp.bfloat16)
         copy = pltpu.make_async_copy(out_ref.at[:, both], out_hbm.at[:, both], out_sems.at[pair])
@@ -399,6 +404,10 @@
         z_steps = lax.rem(lax.div(me, PLANE) - lax.div(source, PLANE) + Z_SIZE, Z_SIZE)
         steps = lax.rem(lax.rem(me, PLANE) - lax.rem(source, PLANE) + PLANE, PLANE)
         to_ref[block] = from_ref[z_steps * PLANE + steps]
+
+
+def in_hbm(array):
+    return pltpu.with_memory_space_constraint(array, pltpu.HBM)
 
 
 def params(mib=16):
@@ -443,7 +452,14 @@
             array, "seq", split_axis=0, concat_axis=0, tiled=True, axis_index_groups=groups
         )
 
-    own_kv = jnp.concatenate([key_vectors, value_vectors], axis=1)
+    own_kv = pl.pallas_call(
+        join_kernel,
+        out_shape=pltpu.HBM((tokens, 2 * key_vectors.shape[1]), bf16),
+        in_specs=[VMEM] * 2,
+        out_specs=VMEM,
+        compiler_params=params(),
+        name="join",
+    )(key_vectors, value_vectors)
     behind = [from_behind(own_kv, "seq", offset) for offset in range(REACH, 0, -1)]
 
     turned_weight = lax.all_gather(
@@ -566,25 +582,12 @@
         compiler_params=params(),
         cost_estimate=cost(0, 2 * MIB),
         name="regroup",
-    )(z_scalar, *in_plane)
-    grouped, gate_up, expert_down = lax.optimization_barrier((grouped, gate_up, expert_down))
-    gate_up, down = pl.pallas_call(
-        hold_kernel,
-        out_shape=[pltpu.VMEM(gate_up.shape, bf16), pltpu.VMEM(expert_down.shape, bf16)],
-        in_specs=[HBM] * 2,
-        out_specs=[VMEM] * 2,
-        scratch_shapes=[pltpu.SemaphoreType.DMA((2 * local_halves,))],
-        compiler_params=params(4),
-        cost_estimate=cost(0, 18 * MIB),
-        name="hold",
-    )(gate_up, expert_down)
+    )(z_scalar, *[in_hbm(piece) for piece in in_plane])
     arrived_cache = [grouped[0]]
     for step in range(1, Z_SIZE):
         arrived_cache.append(lax.ppermute(grouped[step], "seq", z_pairs[step]))
 
-    arrived, gate_up, down, shared_weight = lax.optimization_barrier(
-        (arrived, gate_up, down, shared_weight)
-    )
+    arrived, shared_weight = lax.optimization_barrier((arrived, shared_weight))
     shared_part, own_mixed = pl.pallas_call(
         shared_kernel,
         out_shape=[shape((all_tokens, width), bf16), shape((tokens, width), f32)],
@@ -598,16 +601,19 @@
     returning = pl.pallas_call(
         experts_kernel,
         out_shape=pltpu.HBM((PLANE, picked, width), bf16),
-        in_specs=[VMEM] * 3,
+        in_specs=[VMEM, HBM, HBM],
         out_specs=HBM,
         scratch_shapes=[
+            pltpu.VMEM((local_halves, 2, width, half_ff), bf16),
+            pltpu.VMEM((local_halves, half_ff, width), bf16),
             pltpu.VMEM((PLANE, picked, width), bf16),
+            pltpu.SemaphoreType.DMA((2, local_halves)),
             pltpu.SemaphoreType.DMA((local_halves // 2,)),
         ],
-        compiler_params=params(20),
+        compiler_params=params(32),
         cost_estimate=cost(6 * PLANE * picked * half_ff * width, 14 * MIB),
         name="experts",
-    )(arrived, gate_up, down)
+    )(arrived, in_hbm(gate_up), in_hbm(expert_down))
     returning, arrived_cache = lax.optimization_barrier((returning, arrived_cache))
     returned = exchange(returning, planes).reshape(PLANE * picked, width)
 
@@ -632,7 +638,7 @@
         compiler_params=params(24),
         cost_estimate=cost(2 * all_tokens * PLANE * picked * width, 3 * MIB),
         name="combine",
-    )(z_scalar, mix, returned, shared_part)
+    )(z_scalar, in_hbm(mix), returned, in_hbm(shared_part))
     layer_out = pl.pallas_call(
         final_kernel,
         out_shape=shape((tokens, width), bf16),

time: 196 us -> 190 us (0.969)
  local copies, waits for them, and re-layouts: 29.5 us -> 19 us
  Pallas kernels: 20.4 us -> 25.2 us
    unnamed x73 -> x52, local copies, waits for them, and re-layouts: 24.3 us -> 11.4 us
    optimization_barrier x1, local copies, waits for them, and re-layouts: 3.79 us -> 6.28 us  [shards(): lax.optimization_barrier((gathered, cache_blocks, expert_gate_up))]
    ppermute x7, waiting for transfers between devices: 0.81 us -> 3.28 us  [shards(): piece = lax.ppermute(piece, 'seq', pairs)]
    pallas_call x1, Pallas kernels: 3.51 us -> 5.92 us  [shards(): pl.pallas_call(experts_kernel, out_shape=pltpu.HBM((PLANE, picked, width)...]
    ppermute x6, waiting for transfers between devices: 36.5 us -> 34.4 us  [along_z(): lax.ppermute(arrays[step], 'seq', z_pairs[step])]
  transfers between devices with their start and end apart: 25 -> 25, of which waited for: 9 -> 9; matrix products, arithmetic and copies ran while one was open for 5% -> 6% of each run, Pallas kernels for 10% -> 12%
where the time goes in v5:
time: 190 us; the launch traced here: 189 us
  waiting for transfers between devices  79.2 us (42%)
  starting transfers between devices  48 us (25%)
  Pallas kernels  25.2 us (13%)
  local copies, waits for them, and re-layouts  19 us (10%)
  between operations  14.4 us (8%)
  other arithmetic  3.59 us (2%)
    all_to_all x3, waiting for transfers between devices, exchange(): lax.all_to_all(array, 'seq', split_axis=0, concat_axis=0, tiled=True, axi...  40.8 us
    ppermute x6, waiting for transfers between devices, along_z(): lax.ppermute(arrays[step], 'seq', z_pairs[step])  34.4 us
    all_to_all x3, starting transfers between devices, exchange(): lax.all_to_all(array, 'seq', split_axis=0, concat_axis=0, tiled=True, axi...  14.3 us
    ppermute x4, starting transfers between devices, from_behind(): return lax.ppermute(shard, axis, pairs)  13.1 us
    unnamed x52, local copies, waits for them, and re-layouts  11.4 us
    ppermute x6, starting transfers between devices, along_z(): lax.ppermute(arrays[step], 'seq', z_pairs[step])  8.78 us
    ppermute x7, starting transfers between devices, shards(): piece = lax.ppermute(piece, 'seq', pairs)  6.55 us
    optimization_barrier x1, local copies, waits for them, and re-layouts, shards(): lax.optimization_barrier((gathered, cache_blocks, expert_gate_up))  6.28 us
  transfers between devices with their start and end apart: 25, of which 9 were waited for; matrix products, arithmetic and copies ran while one was open for 6% of the time, Pallas kernels for 12%

profile of v5, /device:TPU:10, one launch (start us, length us, event | category | flops | bytes accessed | tf_op | source)
XLA Modules:
  0.0 189.3 jit_solution(17861223098173402573)
XLA Ops:
  12.2 3.4 %collective-permute-start.2 = (bf16[64,1024]{1,0:T(8,128)(2,1)}, bf16[64,1024]{1,0:T(8,128)(2,1)S(1)}, u32[]{:S(2)}, u32[]{:S(2)}) collective-permute-start(bf16[64,1024]{1,0:T(8,128)(2,1)} %join.1.own_ref), channel_id=1, source_target_pairs={{0,2},{1,3},{2,4},{3,5},{4,6},{5,7},{6,8},{7,9},{8,10},{9,11},{10,... | collective-permute-start | bytes 393224 | tf_op jit(solution)/shard_map/ppermute | solution.py:28
  15.6 4.3 %collective-permute-start.1 = (bf16[64,1024]{1,0:T(8,128)(2,1)}, bf16[64,1024]{1,0:T(8,128)(2,1)S(1)}, u32[]{:S(2)}, u32[]{:S(2)}) collective-permute-start(bf16[64,1024]{1,0:T(8,128)(2,1)} %join.1.own_ref), channel_id=1, source_target_pairs={{0,3},{1,4},{2,5},{3,6},{4,7},{5,8},{6,9},{7,10},{8,11},{9,12},{10... | collective-permute-start | bytes 393224 | tf_op jit(solution)/shard_map/ppermute | solution.py:28
  19.9 3.4 %collective-permute-start = (bf16[64,1024]{1,0:T(8,128)(2,1)}, bf16[64,1024]{1,0:T(8,128)(2,1)S(1)}, u32[]{:S(2)}, u32[]{:S(2)}) collective-permute-start(bf16[64,1024]{1,0:T(8,128)(2,1)} %join.1.own_ref), channel_id=1, source_target_pairs={{0,4},{1,5},{2,6},{3,7},{4,8},{5,9},{6,10},{7,11},{8,12},{9,13},{1... | collective-permute-start | bytes 393224 | tf_op jit(solution)/shard_map/ppermute | solution.py:28
  29.2 3.9 %attention.1 = (bf16[64,2048]{1,0:T(8,128)(2,1)}, bf16[64,2048]{1,0:T(8,128)(2,1)}, bf16[64,2048]{1,0:T(8,128)(2,1)}, bf16[64,2048]{1,0:T(8,128)(2,1)}) custom-call(s32[1]{0:T(128)} %bitcast.z_ref, s32[1]{0:T(128)} %bitcast.1.first_ref, s32[16]{0:T(128)} %lengths_ref.1, bf16[64,1536]{1,0:T(8,128)(2,1)} %q_ref.1, bf16[64,1024]{1,0:T(8,128)(2,1)} %copy-done.17, ...), custom_call_target="tpu_custom_call" | custom-call | flops 125829120 | bytes 3145728 | tf_op jit(solution)/shard_map/attention/pallas_call | solution.py:499
  36.5 16.5 %collective-permute-done.4.refs_1_ = bf16[64,2048]{1,0:T(8,128)(2,1)S(1)} collective-permute-done((bf16[64,2048]{1,0:T(8,128)(2,1)}, bf16[64,2048]{1,0:T(8,128)(2,1)S(1)}, u32[]{:S(2)}, u32[]{:S(2)}) %collective-permute-start.4) | collective-permute-done | bytes 262176 | tf_op jit(solution)/shard_map/ppermute | solution.py:481
  53.0 3.5 %collective-permute-done.5.refs_2_ = bf16[64,2048]{1,0:T(8,128)(2,1)S(1)} collective-permute-done((bf16[64,2048]{1,0:T(8,128)(2,1)}, bf16[64,2048]{1,0:T(8,128)(2,1)S(1)}, u32[]{:S(2)}, u32[]{:S(2)}) %collective-permute-start.5) | collective-permute-done | bytes 262176 | tf_op jit(solution)/shard_map/ppermute | solution.py:481
  61.9 4.5 %all-to-all-start = ((bf16[4,256,384]{2,1,0:T(8,128)(2,1)}), bf16[4,256,384]{2,1,0:T(8,128)(2,1)S(1)}, u32[]{:S(2)}, u32[]{:S(2)}) async-start(bf16[4,256,384]{2,1,0:T(8,128)(2,1)} %get-tuple-element.59), calls=%async_computation | async-start | bytes 1572864 | tf_op jit(solution)/shard_map/all_to_all | solution.py:451
  70.9 2.4 %collective-permute-start.9 = (bf16[4,32,4,128]{3,2,1,0:T(4,128)(2,1)S(1)}, bf16[4,32,4,128]{3,2,1,0:T(4,128)(2,1)S(1)}, u32[]{:S(2)}, u32[]{:S(2)}) collective-permute-start(bf16[4,32,4,128]{3,2,1,0:T(4,128)(2,1)S(1)} %get-tuple-element.96), channel_id=1, source_target_pairs={{0,3},{1,4},{2,5},{3,6},{4,7},{5,0},{6,1},{7,2},{8,11},{9,12},{10,... | collective-permute-start | bytes 393224 | tf_op jit(solution)/shard_map/ppermute | solution.py:530
  74.3 3.3 %collective-permute-done.12.refs_6_ = bf16[4,32,4,128]{3,2,1,0:T(4,128)(2,1)S(1)} collective-permute-done((bf16[4,32,4,128]{3,2,1,0:T(4,128)(2,1)S(1)}, bf16[4,32,4,128]{3,2,1,0:T(4,128)(2,1)S(1)}, u32[]{:S(2)}, u32[]{:S(2)}) %collective-permute-start.12) | collective-permute-done | bytes 131104 | tf_op jit(solution)/shard_map/ppermute | solution.py:530
  77.6 1.9 %tables.1 = (bf16[768,256]{1,0:T(8,128)(2,1)S(1)}, bf16[256,768]{1,0:T(8,128)(2,1)S(1)}) custom-call(s32[1]{0:T(128)} %bitcast.7.parity_ref, bf16[256,128]{1,0:T(8,128)(2,1)S(1)} %get-tuple-element.60.info_ref), custom_call_target="tpu_custom_call" | custom-call | flops 3932160 | bytes 1048576 | tf_op jit(solution)/shard_map/tables/pallas_call | solution.py:549
  80.2 2.9 %all-to-all-done.mixed_ref = bf16[4,256,384]{2,1,0:T(8,128)(2,1)S(1)} async-done(((bf16[4,256,384]{2,1,0:T(8,128)(2,1)}), bf16[4,256,384]{2,1,0:T(8,128)(2,1)S(1)}, u32[]{:S(2)}, u32[]{:S(2)}) %all-to-all-start) | async-done | bytes 786464 | tf_op jit(solution)/shard_map/all_to_all | solution.py:451
  83.1 2.1 %pick.1 = bf16[8,96,1536]{2,1,0:T(8,128)(2,1)} custom-call(bf16[768,256]{1,0:T(8,128)(2,1)S(1)} %get-tuple-element.61.onehot_ref, f32[1,1536]{1,0:T(1,128)S(1)} %reshape.33.gain_ref, bf16[4,256,384]{2,1,0:T(8,128)(2,1)S(1)} %all-to-all-done.mixed_ref), custom_call_target="tpu_custom_call" | custom-call | flops 603979776 | bytes 4194304 | tf_op jit(solution)/shard_map/pick/pallas_call | solution.py:561
  86.1 4.7 %all-to-all-start.1 = ((bf16[8,96,1536]{2,1,0:T(8,128)(2,1)}), bf16[8,96,1536]{2,1,0:T(8,128)(2,1)S(1)}, u32[]{:S(2)}, u32[]{:S(2)}) async-start(bf16[8,96,1536]{2,1,0:T(8,128)(2,1)} %pick.1), calls=%async_computation.1 | async-start | bytes 4718592 | tf_op jit(solution)/shard_map/all_to_all | solution.py:451
  90.8 2.1 %regroup.1 = (bf16[8,32,4,128]{3,2,1,0:T(4,128)(2,1)S(1)}, bf16[8,32,4,128]{3,2,1,0:T(4,128)(2,1)}, bf16[8,32,4,128]{3,2,1,0:T(4,128)(2,1)}, bf16[8,32,4,128]{3,2,1,0:T(4,128)(2,1)S(1)}) custom-call(s32[1]{0:T(128)} %bitcast.z_ref, bf16[4,32,4,128]{3,2,1,0:T(4,128)(2,1)} %get-tuple-element.70.refs_0_, bf16[4,32,4,128]{3,2,1,0:T(4,128)(2,1)} %copy-done.24, ...), custom_call_target="tpu_custom_call" | custom-call | bytes 2097152 | tf_op jit(solution)/shard_map/regroup/pallas_call | solution.py:577
  94.5 4.2 %collective-permute-start.15 = (bf16[8,32,4,128]{3,2,1,0:T(4,128)(2,1)}, bf16[8,32,4,128]{3,2,1,0:T(4,128)(2,1)}, u32[]{:S(2)}, u32[]{:S(2)}) collective-permute-start(bf16[8,32,4,128]{3,2,1,0:T(4,128)(2,1)} %get-tuple-element.80), channel_id=1, source_target_pairs={{0,16},{1,17},{2,18},{3,19},{4,20},{5,21},{6,22},{7,23},{8,24},{9,... | collective-permute-start | bytes 786440 | tf_op jit(solution)/shard_map/ppermute | solution.py:588
  99.0 6.3 %copy.35 = bf16[4,1536,2,256]{3,1,2,0:T(8,128)(2,1)} copy(bf16[4,1536,2,256]{3,2,1,0:T(2,128)(2,1)} %param.26) | data formatting | bytes 12582912 | tf_op jit(solution)/shard_map/optimization_barrier | solution.py:512
  105.3 13.5 %all-to-all-done.1.rows_ref = bf16[8,96,1536]{2,1,0:T(8,128)(2,1)S(1)} async-done(((bf16[8,96,1536]{2,1,0:T(8,128)(2,1)}), bf16[8,96,1536]{2,1,0:T(8,128)(2,1)S(1)}, u32[]{:S(2)}, u32[]{:S(2)}) %all-to-all-start.1) | async-done | bytes 2359328 | tf_op jit(solution)/shard_map/all_to_all | solution.py:451
  118.8 5.9 %experts.1 = bf16[8,96,1536]{2,1,0:T(8,128)(2,1)} custom-call(bf16[8,96,1536]{2,1,0:T(8,128)(2,1)S(1)} %all-to-all-done.1.rows_ref, bf16[4,2,1536,256]{3,2,1,0:T(8,128)(2,1)} %bitcast.53, bf16[4,256,1536]{2,1,0:T(8,128)(2,1)} %down_hbm.1), custom_call_target="tpu_custom_call" | custom-call | flops 1811939328 | bytes 14680064 | tf_op jit(solution)/shard_map/experts/pallas_call | solution.py:601
  124.7 5.1 %all-to-all-start.2 = ((bf16[8,96,1536]{2,1,0:T(8,128)(2,1)}), bf16[8,96,1536]{2,1,0:T(8,128)(2,1)S(1)}, u32[]{:S(2)}, u32[]{:S(2)}) async-start(bf16[8,96,1536]{2,1,0:T(8,128)(2,1)} %experts.1), calls=%async_computation.2 | async-start | bytes 4718592 | tf_op jit(solution)/shard_map/all_to_all | solution.py:451
  133.4 24.4 %all-to-all-done.2 = bf16[8,96,1536]{2,1,0:T(8,128)(2,1)S(1)} async-done(((bf16[8,96,1536]{2,1,0:T(8,128)(2,1)}), bf16[8,96,1536]{2,1,0:T(8,128)(2,1)S(1)}, u32[]{:S(2)}, u32[]{:S(2)}) %all-to-all-start.2) | async-done | bytes 2359328 | tf_op jit(solution)/shard_map/all_to_all | solution.py:451
  157.8 2.2 %combine.1 = (bf16[64,1536]{1,0:T(8,128)(2,1)S(1)}, bf16[64,1536]{1,0:T(8,128)(2,1)S(1)}, bf16[64,1536]{1,0:T(8,128)(2,1)S(1)}, bf16[64,1536]{1,0:T(8,128)(2,1)S(1)}) custom-call(s32[1]{0:T(128)} %bitcast.z_ref, bf16[256,768]{1,0:T(8,128)(2,1)} %copy-done.3, bf16[768,1536]{1,0:T(8,128)(2,1)S(1)} %bitcast.49, bf16[256,1536]{1,0:T(8,128)(2,1)} %copy-done.2), custom_call_target="tpu_custom_call" | custom-call | flops 603979776 | bytes 3145728 | tf_op jit(solution)/shard_map/combine/pallas_call | solution.py:632
  160.8 4.2 %collective-permute-start.18 = (bf16[64,1536]{1,0:T(8,128)(2,1)S(1)}, bf16[64,1536]{1,0:T(8,128)(2,1)S(1)}, u32[]{:S(2)}, u32[]{:S(2)}) collective-permute-start(bf16[64,1536]{1,0:T(8,128)(2,1)S(1)} %get-tuple-element.86), channel_id=1, source_target_pairs={{0,16},{1,17},{2,18},{3,19},{4,20},{5,21},{6,22},{7,23},{8,24},{9,... | collective-permute-start | bytes 589832 | tf_op jit(solution)/shard_map/ppermute | solution.py:481
  169.0 8.8 %collective-permute-done.18.refs_2_ = bf16[64,1536]{1,0:T(8,128)(2,1)S(1)} collective-permute-done((bf16[64,1536]{1,0:T(8,128)(2,1)S(1)}, bf16[64,1536]{1,0:T(8,128)(2,1)S(1)}, u32[]{:S(2)}, u32[]{:S(2)}) %collective-permute-start.18) | collective-permute-done | bytes 196640 | tf_op jit(solution)/shard_map/ppermute | solution.py:481
  177.8 3.9 %collective-permute-done.19.refs_3_ = bf16[64,1536]{1,0:T(8,128)(2,1)S(1)} collective-permute-done((bf16[64,1536]{1,0:T(8,128)(2,1)S(1)}, bf16[64,1536]{1,0:T(8,128)(2,1)S(1)}, u32[]{:S(2)}, u32[]{:S(2)}) %collective-permute-start.19) | collective-permute-done | bytes 196640 | tf_op jit(solution)/shard_map/ppermute | solution.py:481
  (97 shorter events, 37.6 us)
Async XLA Ops:
  7.2 51.0 %all-gather.4.cloned.1.call-start = ((), (), s32[]{:S(2)}) async-start(), calls=%async_computation.3 | async-start | bytes 1327104 | tf_op jit(solution)/shard_map/all_gather | solution.py:465
  7.9 97.4 %all-gather.6.cloned.1.call-start = ((), (), s32[]{:S(2)}) async-start(), calls=%async_computation.4 | async-start | bytes 2654208 | tf_op jit(solution)/shard_map/all_gather | solution.py:510
  10.3 18.1 %collective-permute-start.3 = (bf16[64,1024]{1,0:T(8,128)(2,1)}, bf16[64,1024]{1,0:T(8,128)(2,1)S(1)}, u32[]{:S(2)}, u32[]{:S(2)}) collective-permute-start(bf16[64,1024]{1,0:T(8,128)(2,1)} %join.1.own_ref), channel_id=1, source_target_pairs={{0,1},{1,2},{2,3},{3,4},{4,5},{5,6},{6,7},{7,8},{8,9},{9,10},{10,1... | collective-permute-start | bytes 393224 | tf_op jit(solution)/shard_map/ppermute | solution.py:28
  12.2 16.2 %collective-permute-start.2 = (bf16[64,1024]{1,0:T(8,128)(2,1)}, bf16[64,1024]{1,0:T(8,128)(2,1)S(1)}, u32[]{:S(2)}, u32[]{:S(2)}) collective-permute-start(bf16[64,1024]{1,0:T(8,128)(2,1)} %join.1.own_ref), channel_id=1, source_target_pairs={{0,2},{1,3},{2,4},{3,5},{4,6},{5,7},{6,8},{7,9},{8,10},{9,11},{10,... | collective-permute-start | bytes 393224 | tf_op jit(solution)/shard_map/ppermute | solution.py:28
  15.6 12.8 %collective-permute-start.1 = (bf16[64,1024]{1,0:T(8,128)(2,1)}, bf16[64,1024]{1,0:T(8,128)(2,1)S(1)}, u32[]{:S(2)}, u32[]{:S(2)}) collective-permute-start(bf16[64,1024]{1,0:T(8,128)(2,1)} %join.1.own_ref), channel_id=1, source_target_pairs={{0,3},{1,4},{2,5},{3,6},{4,7},{5,8},{6,9},{7,10},{8,11},{9,12},{10... | collective-permute-start | bytes 393224 | tf_op jit(solution)/shard_map/ppermute | solution.py:28
  19.9 8.5 %collective-permute-start = (bf16[64,1024]{1,0:T(8,128)(2,1)}, bf16[64,1024]{1,0:T(8,128)(2,1)S(1)}, u32[]{:S(2)}, u32[]{:S(2)}) collective-permute-start(bf16[64,1024]{1,0:T(8,128)(2,1)} %join.1.own_ref), channel_id=1, source_target_pairs={{0,4},{1,5},{2,6},{3,7},{4,8},{5,9},{6,10},{7,11},{8,12},{9,13},{1... | collective-permute-start | bytes 393224 | tf_op jit(solution)/shard_map/ppermute | solution.py:28
  33.1 19.9 %collective-permute-start.4 = (bf16[64,2048]{1,0:T(8,128)(2,1)}, bf16[64,2048]{1,0:T(8,128)(2,1)S(1)}, u32[]{:S(2)}, u32[]{:S(2)}) collective-permute-start(bf16[64,2048]{1,0:T(8,128)(2,1)} %get-tuple-element.52), channel_id=1, source_target_pairs={{0,8},{1,9},{2,10},{3,11},{4,12},{5,13},{6,14},{7,15},{8,16},{9,17... | collective-permute-start | bytes 786440 | tf_op jit(solution)/shard_map/ppermute | solution.py:481
  34.7 21.8 %collective-permute-start.5 = (bf16[64,2048]{1,0:T(8,128)(2,1)}, bf16[64,2048]{1,0:T(8,128)(2,1)S(1)}, u32[]{:S(2)}, u32[]{:S(2)}) collective-permute-start(bf16[64,2048]{1,0:T(8,128)(2,1)} %get-tuple-element.53), channel_id=1, source_target_pairs={{0,16},{1,17},{2,18},{3,19},{4,20},{5,21},{6,22},{7,23},{8,24},{9,... | collective-permute-start | bytes 786440 | tf_op jit(solution)/shard_map/ppermute | solution.py:481
  36.0 22.2 %collective-permute-start.6 = (bf16[64,2048]{1,0:T(8,128)(2,1)}, bf16[64,2048]{1,0:T(8,128)(2,1)S(1)}, u32[]{:S(2)}, u32[]{:S(2)}) collective-permute-start(bf16[64,2048]{1,0:T(8,128)(2,1)} %get-tuple-element.54), channel_id=1, source_target_pairs={{0,24},{1,25},{2,26},{3,27},{4,28},{5,29},{6,30},{7,31},{8,0},{9,1... | collective-permute-start | bytes 786440 | tf_op jit(solution)/shard_map/ppermute | solution.py:481
  61.9 21.2 %all-to-all-start = ((bf16[4,256,384]{2,1,0:T(8,128)(2,1)}), bf16[4,256,384]{2,1,0:T(8,128)(2,1)S(1)}, u32[]{:S(2)}, u32[]{:S(2)}) async-start(bf16[4,256,384]{2,1,0:T(8,128)(2,1)} %get-tuple-element.59), calls=%async_computation | async-start | bytes 1572864 | tf_op jit(solution)/shard_map/all_to_all | solution.py:451
  67.7 9.8 %collective-permute-start.12 = (bf16[4,32,4,128]{3,2,1,0:T(4,128)(2,1)S(1)}, bf16[4,32,4,128]{3,2,1,0:T(4,128)(2,1)S(1)}, u32[]{:S(2)}, u32[]{:S(2)}) collective-permute-start(bf16[4,32,4,128]{3,2,1,0:T(4,128)(2,1)S(1)} %get-tuple-element.93), channel_id=1, source_target_pairs={{0,6},{1,7},{2,0},{3,1},{4,2},{5,3},{6,4},{7,5},{8,14},{9,15},{10,... | collective-permute-start | bytes 393224 | tf_op jit(solution)/shard_map/ppermute | solution.py:530
  69.6 15.7 %collective-permute-start.11 = (bf16[4,32,4,128]{3,2,1,0:T(4,128)(2,1)S(1)}, bf16[4,32,4,128]{3,2,1,0:T(4,128)(2,1)S(1)}, u32[]{:S(2)}, u32[]{:S(2)}) collective-permute-start(bf16[4,32,4,128]{3,2,1,0:T(4,128)(2,1)S(1)} %get-tuple-element.94), channel_id=1, source_target_pairs={{0,5},{1,6},{2,7},{3,0},{4,1},{5,2},{6,3},{7,4},{8,13},{9,14},{10,... | collective-permute-start | bytes 393224 | tf_op jit(solution)/shard_map/ppermute | solution.py:530
  70.7 14.5 %collective-permute-start.10 = (bf16[4,32,4,128]{3,2,1,0:T(4,128)(2,1)S(1)}, bf16[4,32,4,128]{3,2,1,0:T(4,128)(2,1)S(1)}, u32[]{:S(2)}, u32[]{:S(2)}) collective-permute-start(bf16[4,32,4,128]{3,2,1,0:T(4,128)(2,1)S(1)} %get-tuple-element.95), channel_id=1, source_target_pairs={{0,4},{1,5},{2,6},{3,7},{4,0},{5,1},{6,2},{7,3},{8,12},{9,13},{10,... | collective-permute-start | bytes 393224 | tf_op jit(solution)/shard_map/ppermute | solution.py:530
  70.9 14.4 %collective-permute-start.9 = (bf16[4,32,4,128]{3,2,1,0:T(4,128)(2,1)S(1)}, bf16[4,32,4,128]{3,2,1,0:T(4,128)(2,1)S(1)}, u32[]{:S(2)}, u32[]{:S(2)}) collective-permute-start(bf16[4,32,4,128]{3,2,1,0:T(4,128)(2,1)S(1)} %get-tuple-element.96), channel_id=1, source_target_pairs={{0,3},{1,4},{2,5},{3,6},{4,7},{5,0},{6,1},{7,2},{8,11},{9,12},{10,... | collective-permute-start | bytes 393224 | tf_op jit(solution)/shard_map/ppermute | solution.py:530
  73.3 12.0 %collective-permute-start.8 = (bf16[4,32,4,128]{3,2,1,0:T(4,128)(2,1)S(1)}, bf16[4,32,4,128]{3,2,1,0:T(4,128)(2,1)S(1)}, u32[]{:S(2)}, u32[]{:S(2)}) collective-permute-start(bf16[4,32,4,128]{3,2,1,0:T(4,128)(2,1)S(1)} %get-tuple-element.97), channel_id=1, source_target_pairs={{0,2},{1,3},{2,4},{3,5},{4,6},{5,7},{6,0},{7,1},{8,10},{9,11},{10,... | collective-permute-start | bytes 393224 | tf_op jit(solution)/shard_map/ppermute | solution.py:530
  77.5 7.8 %collective-permute-start.7 = (bf16[4,32,4,128]{3,2,1,0:T(4,128)(2,1)S(1)}, bf16[4,32,4,128]{3,2,1,0:T(4,128)(2,1)S(1)}, u32[]{:S(2)}, u32[]{:S(2)}) collective-permute-start(bf16[4,32,4,128]{3,2,1,0:T(4,128)(2,1)S(1)} %get-tuple-element.98), channel_id=1, source_target_pairs={{0,1},{1,2},{2,3},{3,4},{4,5},{5,6},{6,7},{7,0},{8,9},{9,10},{10,1... | collective-permute-start | bytes 393224 | tf_op jit(solution)/shard_map/ppermute | solution.py:530
  86.1 32.6 %all-to-all-start.1 = ((bf16[8,96,1536]{2,1,0:T(8,128)(2,1)}), bf16[8,96,1536]{2,1,0:T(8,128)(2,1)S(1)}, u32[]{:S(2)}, u32[]{:S(2)}) async-start(bf16[8,96,1536]{2,1,0:T(8,128)(2,1)} %pick.1), calls=%async_computation.1 | async-start | bytes 4718592 | tf_op jit(solution)/shard_map/all_to_all | solution.py:451
  93.7 31.0 %collective-permute-start.14 = (bf16[8,32,4,128]{3,2,1,0:T(4,128)(2,1)}, bf16[8,32,4,128]{3,2,1,0:T(4,128)(2,1)}, u32[]{:S(2)}, u32[]{:S(2)}) collective-permute-start(bf16[8,32,4,128]{3,2,1,0:T(4,128)(2,1)} %get-tuple-element.79), channel_id=1, source_target_pairs={{0,8},{1,9},{2,10},{3,11},{4,12},{5,13},{6,14},{7,15},{8,16},{9,17... | collective-permute-start | bytes 786440 | tf_op jit(solution)/shard_map/ppermute | solution.py:588
  94.5 30.3 %collective-permute-start.15 = (bf16[8,32,4,128]{3,2,1,0:T(4,128)(2,1)}, bf16[8,32,4,128]{3,2,1,0:T(4,128)(2,1)}, u32[]{:S(2)}, u32[]{:S(2)}) collective-permute-start(bf16[8,32,4,128]{3,2,1,0:T(4,128)(2,1)} %get-tuple-element.80), channel_id=1, source_target_pairs={{0,16},{1,17},{2,18},{3,19},{4,20},{5,21},{6,22},{7,23},{8,24},{9,... | collective-permute-start | bytes 786440 | tf_op jit(solution)/shard_map/ppermute | solution.py:588
  98.7 26.1 %collective-permute-start.16 = (bf16[8,32,4,128]{3,2,1,0:T(4,128)(2,1)S(1)}, bf16[8,32,4,128]{3,2,1,0:T(4,128)(2,1)}, u32[]{:S(2)}, u32[]{:S(2)}) collective-permute-start(bf16[8,32,4,128]{3,2,1,0:T(4,128)(2,1)S(1)} %get-tuple-element.81), channel_id=1, source_target_pairs={{0,24},{1,25},{2,26},{3,27},{4,28},{5,29},{6,30},{7,31},{8,0},{9,1... | collective-permute-start | bytes 786440 | tf_op jit(solution)/shard_map/ppermute | solution.py:588
  124.7 33.0 %all-to-all-start.2 = ((bf16[8,96,1536]{2,1,0:T(8,128)(2,1)}), bf16[8,96,1536]{2,1,0:T(8,128)(2,1)S(1)}, u32[]{:S(2)}, u32[]{:S(2)}) async-start(bf16[8,96,1536]{2,1,0:T(8,128)(2,1)} %experts.1), calls=%async_computation.2 | async-start | bytes 4718592 | tf_op jit(solution)/shard_map/all_to_all | solution.py:451
  160.0 9.0 %collective-permute-start.17 = (bf16[64,1536]{1,0:T(8,128)(2,1)S(1)}, bf16[64,1536]{1,0:T(8,128)(2,1)S(1)}, u32[]{:S(2)}, u32[]{:S(2)}) collective-permute-start(bf16[64,1536]{1,0:T(8,128)(2,1)S(1)} %get-tuple-element.85), channel_id=1, source_target_pairs={{0,8},{1,9},{2,10},{3,11},{4,12},{5,13},{6,14},{7,15},{8,16},{9,17... | collective-permute-start | bytes 589832 | tf_op jit(solution)/shard_map/ppermute | solution.py:481
  160.8 17.0 %collective-permute-start.18 = (bf16[64,1536]{1,0:T(8,128)(2,1)S(1)}, bf16[64,1536]{1,0:T(8,128)(2,1)S(1)}, u32[]{:S(2)}, u32[]{:S(2)}) collective-permute-start(bf16[64,1536]{1,0:T(8,128)(2,1)S(1)} %get-tuple-element.86), channel_id=1, source_target_pairs={{0,16},{1,17},{2,18},{3,19},{4,20},{5,21},{6,22},{7,23},{8,24},{9,... | collective-permute-start | bytes 589832 | tf_op jit(solution)/shard_map/ppermute | solution.py:481
  165.0 16.7 %collective-permute-start.19 = (bf16[64,1536]{1,0:T(8,128)(2,1)S(1)}, bf16[64,1536]{1,0:T(8,128)(2,1)S(1)}, u32[]{:S(2)}, u32[]{:S(2)}) collective-permute-start(bf16[64,1536]{1,0:T(8,128)(2,1)S(1)} %get-tuple-element.87), channel_id=1, source_target_pairs={{0,24},{1,25},{2,26},{3,27},{4,28},{5,29},{6,30},{7,31},{8,0},{9,1... | collective-permute-start | bytes 589832 | tf_op jit(solution)/shard_map/ppermute | solution.py:481
  (27 other events, 141.5 us)
Sparse Core Ops, SparseCore 0:
  9.9 31.3 all-gather.3
  43.2 29.0 all-gather.5

commit v6 on v5

--- a/solution.py
+++ b/solution.py
@@ -170,21 +170,9 @@
 
 
 def attention_kernel(
-    z_ref,
-    first_ref,
-    lengths_ref,
-    q_ref,
-    k4_ref,
-    k3_ref,
-    k2_ref,
-    k1_ref,
-    own_ref,
-    residual_ref,
-    info_ref,
-    *out_refs,
+    first_ref, lengths_ref, q_ref, k4_ref, k3_ref, k2_ref, k1_ref, own_ref, info_ref, out_ref
 ):
     tokens, width = q_ref.shape
-    part = width // Z_SIZE
     kv_width = own_ref.shape[1] // 2
     kv_heads = kv_width // HD
     group = width // HD // kv_heads
@@ -201,16 +189,7 @@
     hidden = jnp.where((key_pos >= start) & (key_pos <= query_pos), 0.0, NEGATIVE)
     hidden = jnp.concatenate([hidden] * group, axis=0)
     scale = 1.0 / math.sqrt(HD)
-    for step, out_ref in enumerate(out_refs):
-        z = lax.rem(z_ref[0] + step, Z_SIZE)
-        for column in range(Z_SIZE):
-
-            @pl.when(z == column)
-            def _(column=column, out_ref=out_ref):
-                columns = slice(column * part, (column + 1) * part)
-                out_ref[:, width : width + part] = residual_ref[:, columns]
-
-        out_ref[:, width + part :] = info_ref[...]
+    out_ref[:, width:] = info_ref[...]
     for kv in range(kv_heads):
         at = slice(kv * HD, (kv + 1) * HD)
         value_at = slice(kv_width + kv * HD, kv_width + (kv + 1) * HD)
@@ -223,8 +202,7 @@
         total = jnp.sum(weights, axis=-1, keepdims=True)
         result = (dot(weights.astype(jnp.bfloat16), value) / total).astype(jnp.bfloat16)
         for member, h in enumerate(heads):
-            for out_ref in out_refs:
-                out_ref[:, h * HD : (h + 1) * HD] = result[member * tokens : (member + 1) * tokens]
+            out_ref[:, h * HD : (h + 1) * HD] = result[member * tokens : (member + 1) * tokens]
 
 
 def route_kernel(z_ref, ids_ref, logits_ref, out_ref, turned_ref):
@@ -273,16 +251,15 @@
 
 def project_kernel(z_ref, *refs):
     sent = refs[:Z_SIZE]
-    weight_ref, mixed_ref, info_ref, rows_ref = refs[Z_SIZE:]
+    weight_ref, out_ref, info_ref, rows_ref = refs[Z_SIZE:]
     for step, sent_ref in enumerate(sent):
         rows_ref[source_z(z_ref, step)] = sent_ref[...]
     rows = jnp.concatenate([rows_ref[z] for z in range(Z_SIZE)], axis=0)
-    part, width = weight_ref.shape
-    out = dot_rows(rows[:, :width], weight_ref[...])
-    mixed = (out + rows[:, width : width + part].astype(jnp.float32)).astype(jnp.bfloat16)
+    width = weight_ref.shape[1]
+    out = dot_rows(rows[:, :width], weight_ref[...]).astype(jnp.bfloat16)
     for z in range(Z_SIZE):
-        mixed_ref[z] = mixed
-    info_ref[...] = rows[:, width + part :]
+        out_ref[z] = out
+    info_ref[...] = rows[:, width:]
 
 
 def row_codes(info, first, parity, per_device):
@@ -310,14 +287,15 @@
     mix_ref[...] = mix.astype(jnp.bfloat16)
 
 
-def norm(mixed_ref, gain_ref):
-    mixed = jnp.concatenate([mixed_ref[z] for z in range(Z_SIZE)], axis=1).astype(jnp.float32)
+def norm(projected_ref, residual_ref, gain_ref):
+    projected = jnp.concatenate([projected_ref[z] for z in range(Z_SIZE)], axis=1)
+    mixed = residual_ref[...].astype(jnp.float32) + projected.astype(jnp.float32)
     mean_square = jnp.mean(mixed * mixed, axis=-1, keepdims=True)
     return (mixed * lax.rsqrt(mean_square + EPSILON) * gain_ref[...]).astype(jnp.bfloat16)
 
 
-def pick_kernel(onehot_ref, gain_ref, mixed_ref, out_hbm, out_ref, sems):
-    normed = norm(mixed_ref, gain_ref)
+def pick_kernel(onehot_ref, gain_ref, projected_ref, residual_ref, out_hbm, out_ref, sems):
+    normed = norm(projected_ref, residual_ref, gain_ref)
     picked = out_ref.shape[1]
     copies = []
     for p in range(PLANE):
@@ -330,18 +308,20 @@
         copy.wait()
 
 
-def shared_kernel(z_ref, gain_ref, mixed_ref, weight_ref, out_ref, own_ref):
-    tokens, columns = own_ref.shape[0], mixed_ref.shape[2]
+def shared_kernel(z_ref, gain_ref, projected_ref, residual_ref, weight_ref, out_ref, own_ref):
+    tokens, columns = own_ref.shape[0], projected_ref.shape[2]
     own = pl.ds(pl.multiple_of(z_ref[0] * tokens, tokens), tokens)
     for z in range(Z_SIZE):
-        own_ref[:, z * columns : (z + 1) * columns] = mixed_ref[z, own, :].astype(jnp.float32)
+        at = slice(z * columns, (z + 1) * columns)
+        own_residual = residual_ref[own, at].astype(jnp.float32)
+        own_ref[:, at] = own_residual + projected_ref[z, own, :].astype(jnp.float32)
     parts, units, _ = weight_ref.shape
     units = units // 3
     gate_weight, up_weight, down_weight = [
         jnp.concatenate([weight_ref[p, at * units : (at + 1) * units] for p in range(parts)], axis=0)
         for at in range(3)
     ]
-    rows = norm(mixed_ref, gain_ref)
+    rows = norm(projected_ref, residual_ref, gain_ref)
     act = silu_times(dot_rows(rows, gate_weight), dot_rows(rows, up_weight))
     out_ref[...] = dot(act, down_weight).astype(jnp.bfloat16)
 
@@ -452,6 +432,9 @@
             array, "seq", split_axis=0, concat_axis=0, tiled=True, axis_index_groups=groups
         )
 
+    line_residual = lax.all_gather(
+        residual, "seq", axis=0, tiled=True, axis_index_groups=z_groups
+    )
     own_kv = pl.pallas_call(
         join_kernel,
         out_shape=pltpu.HBM((tokens, 2 * key_vectors.shape[1]), bf16),
@@ -459,7 +442,8 @@
         out_specs=VMEM,
         compiler_params=params(),
         name="join",
-    )(key_vectors, value_vectors)
+    )(in_hbm(key_vectors), in_hbm(value_vectors))
+    own_kv, out_weight = lax.optimization_barrier((own_kv, out_weight))
     behind = [from_behind(own_kv, "seq", offset) for offset in range(REACH, 0, -1)]
 
     turned_weight = lax.all_gather(
@@ -467,14 +451,14 @@
     )
     info = pl.pallas_call(
         route_kernel,
-        out_shape=shape((tokens, 128), bf16),
+        out_shape=pltpu.HBM((tokens, 128), bf16),
         in_specs=[SMEM] + [VMEM] * 2,
         out_specs=VMEM,
         scratch_shapes=[pltpu.VMEM((128, 128), f32)],
         compiler_params=params(),
         cost_estimate=cost(MIB, MIB),
         name="route",
-    )(scalar(z_index), route_ids.T, route_logits.T)
+    )(scalar(z_index), in_hbm(route_ids.T), in_hbm(route_logits.T))
 
     def along_z(arrays):
         return [arrays[0]] + [
@@ -495,20 +479,20 @@
         [jnp.transpose(shared_gate_up, (1, 2, 0)).reshape(-1, width), shared_down], axis=0
     )
 
-    sent_width = width + part + info.shape[1]
+    sent_width = width + info.shape[1]
     sent = pl.pallas_call(
         attention_kernel,
-        out_shape=[shape((tokens, sent_width), bf16)] * Z_SIZE,
-        in_specs=[SMEM] * 3 + [VMEM] * 8,
-        out_specs=[VMEM] * Z_SIZE,
+        out_shape=pltpu.HBM((tokens, sent_width), bf16),
+        in_specs=[SMEM] * 2 + [VMEM] * 7,
+        out_specs=VMEM,
         compiler_params=params(58),
         cost_estimate=cost(4 * tokens * 5 * tokens * width, 3 * MIB),
         name="attention",
-    )(z_scalar, scalar(me * tokens), lengths, queries, *behind, own_kv, residual, info)
+    )(scalar(me * tokens), in_hbm(lengths), queries, *behind, own_kv, info)
 
     sent, own_shared = lax.optimization_barrier((sent, own_shared))
     shared_weight = lax.all_gather(own_shared, "seq", axis=0, axis_index_groups=planes)
-    gathered = along_z(sent)
+    gathered = along_z([sent] * Z_SIZE)
     gathered, cache_blocks, expert_gate_up = lax.optimization_barrier(
         (gathered, cache_blocks, expert_gate_up)
     )
@@ -531,7 +515,7 @@
         in_plane.append(piece)
     gate_up = jnp.transpose(expert_gate_up, (0, 2, 1, 3))
 
-    mixed_part, info = pl.pallas_call(
+    projected_part, info = pl.pallas_call(
         project_kernel,
         out_shape=[pltpu.HBM((Z_SIZE, all_tokens, part), bf16), shape((all_tokens, 128), bf16)],
         in_specs=[SMEM] + [VMEM] * (Z_SIZE + 1),
@@ -540,8 +524,8 @@
         compiler_params=params(),
         cost_estimate=cost(2 * all_tokens * width * part, 3 * MIB),
         name="project",
-    )(z_scalar, *gathered, turned_weight)
-    mixed = exchange(mixed_part, z_groups)
+    )(z_scalar, in_hbm(gathered[0]), *gathered[1:], in_hbm(turned_weight))
+    projected = exchange(projected_part, z_groups)
 
     local_halves, _, _, half_ff = expert_gate_up.shape
     per_half = Z_SIZE * CAP
@@ -561,7 +545,7 @@
     outgoing = pl.pallas_call(
         pick_kernel,
         out_shape=pltpu.HBM((PLANE, picked, width), bf16),
-        in_specs=[VMEM] * 3,
+        in_specs=[VMEM] * 4,
         out_specs=HBM,
         scratch_shapes=[
             pltpu.VMEM((PLANE, picked, width), bf16),
@@ -570,7 +554,7 @@
         compiler_params=params(),
         cost_estimate=cost(2 * PLANE * picked * all_tokens * width, 4 * MIB),
         name="pick",
-    )(onehot, gain, mixed)
+    )(onehot, gain, projected, in_hbm(line_residual))
 
     outgoing, in_plane = lax.optimization_barrier((outgoing, in_plane))
     arrived = exchange(outgoing, planes)
@@ -591,12 +575,12 @@
     shared_part, own_mixed = pl.pallas_call(
         shared_kernel,
         out_shape=[shape((all_tokens, width), bf16), shape((tokens, width), f32)],
-        in_specs=[SMEM] + [VMEM] * 3,
+        in_specs=[SMEM] + [VMEM] * 4,
         out_specs=[VMEM] * 2,
         compiler_params=params(24),
         cost_estimate=cost(6 * all_tokens * 256 * width, 5 * MIB),
         name="shared_expert",
-    )(z_scalar, gain, mixed, shared_weight)
+    )(z_scalar, gain, projected, in_hbm(line_residual), shared_weight)
 
     returning = pl.pallas_call(
         experts_kernel,

time: 190 us -> 202 us (1.063)
  blocking collectives: 0 us -> 18.5 us
  waiting for transfers between devices: 79.2 us -> 70.1 us
  local copies, waits for them, and re-layouts: 19 us -> 12.2 us
  Pallas kernels: 25.2 us -> 30.8 us
  starting transfers between devices: 48 us -> 51.4 us
    all_gather x0 -> x1, blocking collectives: none -> 18.5 us  [shards(): lax.all_gather(residual, 'seq', axis=0, tiled=True, axis_index_groups=z_g...]
    unnamed x52 -> x40, local copies, waits for them, and re-layouts: 11.4 us -> 4.69 us
    ppermute x6, waiting for transfers between devices: 34.4 us -> 28.2 us  [along_z(): lax.ppermute(arrays[step], 'seq', z_pairs[step])]
    all_to_all x3, waiting for transfers between devices: 40.8 us -> 36.9 us  [exchange(): lax.all_to_all(array, 'seq', split_axis=0, concat_axis=0, tiled=True, axi...]
    ppermute x7, starting transfers between devices: 6.55 us -> 9.99 us  [shards(): piece = lax.ppermute(piece, 'seq', pairs)]
  transfers between devices with their start and end apart: 25 -> 25, of which waited for: 9 -> 9; matrix products, arithmetic and copies ran while one was open for 6% -> 6% of each run, Pallas kernels for 12% -> 13%
where the time goes in v6:
time: 202 us; the launch traced here: 201 us
  waiting for transfers between devices  70.1 us (35%)
  starting transfers between devices  51.4 us (25%)
  Pallas kernels  30.8 us (15%)
  blocking collectives  18.5 us (9%)
  between operations  14.4 us (7%)
  local copies, waits for them, and re-layouts  12.2 us (6%)
  other arithmetic  3.6 us (2%)
    all_to_all x3, waiting for transfers between devices, exchange(): lax.all_to_all(array, 'seq', split_axis=0, concat_axis=0, tiled=True, axi...  36.9 us
    ppermute x6, waiting for transfers between devices, along_z(): lax.ppermute(arrays[step], 'seq', z_pairs[step])  28.2 us
    all_gather x1, blocking collectives, shards(): lax.all_gather(residual, 'seq', axis=0, tiled=True, axis_index_groups=z_g...  18.5 us
    all_to_all x3, starting transfers between devices, exchange(): lax.all_to_all(array, 'seq', split_axis=0, concat_axis=0, tiled=True, axi...  13.9 us
    ppermute x4, starting transfers between devices, from_behind(): return lax.ppermute(shard, axis, pairs)  13.1 us
    ppermute x7, starting transfers between devices, shards(): piece = lax.ppermute(piece, 'seq', pairs)  9.99 us
    ppermute x6, starting transfers between devices, along_z(): lax.ppermute(arrays[step], 'seq', z_pairs[step])  9.76 us
    optimization_barrier x1, local copies, waits for them, and re-layouts, shards(): lax.optimization_barrier((gathered, cache_blocks, expert_gate_up))  6.31 us
  transfers between devices with their start and end apart: 25, of which 9 were waited for; matrix products, arithmetic and copies ran while one was open for 6% of the time, Pallas kernels for 13%

profile of v6, /device:TPU:10, one launch (start us, length us, event | category | flops | bytes accessed | tf_op | source)
XLA Modules:
  0.0 201.0 jit_solution(5023296701043614051)
XLA Ops:
  10.7 3.4 %collective-permute-start.2 = (bf16[64,1024]{1,0:T(8,128)(2,1)}, bf16[64,1024]{1,0:T(8,128)(2,1)S(1)}, u32[]{:S(2)}, u32[]{:S(2)}) collective-permute-start(bf16[64,1024]{1,0:T(8,128)(2,1)} %join.1.own_ref), channel_id=1, source_target_pairs={{0,2},{1,3},{2,4},{3,5},{4,6},{5,7},{6,8},{7,9},{8,10},{9,11},{10,... | collective-permute-start | bytes 393224 | tf_op jit(solution)/shard_map/ppermute | solution.py:28
  14.2 4.3 %collective-permute-start.1 = (bf16[64,1024]{1,0:T(8,128)(2,1)}, bf16[64,1024]{1,0:T(8,128)(2,1)S(1)}, u32[]{:S(2)}, u32[]{:S(2)}) collective-permute-start(bf16[64,1024]{1,0:T(8,128)(2,1)} %join.1.own_ref), channel_id=1, source_target_pairs={{0,3},{1,4},{2,5},{3,6},{4,7},{5,8},{6,9},{7,10},{8,11},{9,12},{10... | collective-permute-start | bytes 393224 | tf_op jit(solution)/shard_map/ppermute | solution.py:28
  18.5 3.4 %collective-permute-start = (bf16[64,1024]{1,0:T(8,128)(2,1)}, bf16[64,1024]{1,0:T(8,128)(2,1)S(1)}, u32[]{:S(2)}, u32[]{:S(2)}) collective-permute-start(bf16[64,1024]{1,0:T(8,128)(2,1)} %join.1.own_ref), channel_id=1, source_target_pairs={{0,4},{1,5},{2,6},{3,7},{4,8},{5,9},{6,10},{7,11},{8,12},{9,13},{1... | collective-permute-start | bytes 393224 | tf_op jit(solution)/shard_map/ppermute | solution.py:28
  27.1 3.3 %attention.1.refs_0_ = bf16[64,1664]{1,0:T(8,128)(2,1)} custom-call(s32[1]{0:T(128)} %bitcast.1.first_ref, s32[16]{0:T(128)} %lengths_ref.1, bf16[64,1536]{1,0:T(8,128)(2,1)} %q_ref.1, bf16[64,1024]{1,0:T(8,128)(2,1)} %copy-done.11, bf16[64,1024]{1,0:T(8,128)(2,1)} %copy-done.10, bf16[64,1024]{1,0:T(8,128)(2,1)} %copy-done.9, bf16[64,1024]{1,0:T(8,128)(2,1)} %copy-done.8, ...), custom_call_target="tpu_custom_call" | custom-call | flops 125829120 | bytes 3145728 | tf_op jit(solution)/shard_map/attention/pallas_call | solution.py:483
  30.8 2.7 %collective-permute-start.5 = (bf16[64,1664]{1,0:T(8,128)(2,1)}, bf16[64,1664]{1,0:T(8,128)(2,1)S(1)}, u32[]{:S(2)}, u32[]{:S(2)}) collective-permute-start(bf16[64,1664]{1,0:T(8,128)(2,1)} %attention.1.refs_0_), channel_id=1, source_target_pairs={{0,16},{1,17},{2,18},{3,19},{4,20},{5,21},{6,22},{7,23},{8,24},{9,... | collective-permute-start | bytes 638984 | tf_op jit(solution)/shard_map/ppermute | solution.py:465
  35.4 11.8 %collective-permute-done.6.refs_3_ = bf16[64,1664]{1,0:T(8,128)(2,1)S(1)} collective-permute-done((bf16[64,1664]{1,0:T(8,128)(2,1)}, bf16[64,1664]{1,0:T(8,128)(2,1)S(1)}, u32[]{:S(2)}, u32[]{:S(2)}) %collective-permute-start.6) | collective-permute-done | bytes 213024 | tf_op jit(solution)/shard_map/ppermute | solution.py:465
  47.2 3.6 %collective-permute-done.4.refs_1_ = bf16[64,1664]{1,0:T(8,128)(2,1)S(1)} collective-permute-done((bf16[64,1664]{1,0:T(8,128)(2,1)}, bf16[64,1664]{1,0:T(8,128)(2,1)S(1)}, u32[]{:S(2)}, u32[]{:S(2)}) %collective-permute-start.4) | collective-permute-done | bytes 213024 | tf_op jit(solution)/shard_map/ppermute | solution.py:465
  50.8 2.9 %project.1 = (bf16[4,256,384]{2,1,0:T(8,128)(2,1)}, bf16[256,128]{1,0:T(8,128)(2,1)S(1)}) custom-call(s32[1]{0:T(128)} %bitcast.z_ref, bf16[64,1664]{1,0:T(8,128)(2,1)} %attention.1.refs_0_, bf16[64,1664]{1,0:T(8,128)(2,1)S(1)} %collective-permute-done.4.refs_1_, bf16[64,1664]{1,0:T(8,128)(2,1)S(1)} %collective-permute-done.5.refs_2_, ...), custom_call_target="tpu_custom_call" | custom-call | flops 301989888 | bytes 3145728 | tf_op jit(solution)/shard_map/project/pallas_call | solution.py:518
  53.7 5.2 %all-to-all-start = ((bf16[4,256,384]{2,1,0:T(8,128)(2,1)}), bf16[4,256,384]{2,1,0:T(8,128)(2,1)S(1)}, u32[]{:S(2)}, u32[]{:S(2)}) async-start(bf16[4,256,384]{2,1,0:T(8,128)(2,1)} %get-tuple-element.49), calls=%async_computation | async-start | bytes 1572864 | tf_op jit(solution)/shard_map/all_to_all | solution.py:431
  66.4 3.7 %collective-permute-start.8 = (bf16[4,32,4,128]{3,2,1,0:T(4,128)(2,1)S(1)}, bf16[4,32,4,128]{3,2,1,0:T(4,128)(2,1)S(1)}, u32[]{:S(2)}, u32[]{:S(2)}) collective-permute-start(bf16[4,32,4,128]{3,2,1,0:T(4,128)(2,1)S(1)} %get-tuple-element.87), channel_id=1, source_target_pairs={{0,2},{1,3},{2,4},{3,5},{4,6},{5,7},{6,0},{7,1},{8,10},{9,11},{10,... | collective-permute-start | bytes 393224 | tf_op jit(solution)/shard_map/ppermute | solution.py:514
  70.1 4.7 %collective-permute-done.12.refs_6_ = bf16[4,32,4,128]{3,2,1,0:T(4,128)(2,1)S(1)} collective-permute-done((bf16[4,32,4,128]{3,2,1,0:T(4,128)(2,1)S(1)}, bf16[4,32,4,128]{3,2,1,0:T(4,128)(2,1)S(1)}, u32[]{:S(2)}, u32[]{:S(2)}) %collective-permute-start.12) | collective-permute-done | bytes 131104 | tf_op jit(solution)/shard_map/ppermute | solution.py:514
  74.8 18.5 %all_gather.13.residual_ref = bf16[256,1536]{1,0:T(8,128)(2,1)} all-gather(bf16[64,1536]{1,0:T(8,128)(2,1)S(1)} %copy-done.7), channel_id=1, replica_groups={{0,8,16,24},{1,9,17,25},{2,10,18,26},{3,11,19,27},{4,12,20,28},{5,13,21..., dimensions={0}, use_global_device_ids=true | all-gather | bytes 983040 | tf_op jit(solution)/shard_map/all_gather | solution.py:435
  95.3 3.5 %pick.1 = bf16[8,96,1536]{2,1,0:T(8,128)(2,1)} custom-call(bf16[768,256]{1,0:T(8,128)(2,1)S(1)} %get-tuple-element.51.onehot_ref, f32[1,1536]{1,0:T(1,128)S(1)} %reshape.33.gain_ref, bf16[4,256,384]{2,1,0:T(8,128)(2,1)S(1)} %all-to-all-done.projected_ref, bf16[256,1536]{1,0:T(8,128)(2,1)} %all_gather.13.residual_ref), custom_call_target="tpu_custom_call" | custom-call | flops 603979776 | bytes 4194304 | tf_op jit(solution)/shard_map/pick/pallas_call | solution.py:545
  99.8 3.6 %all-to-all-start.1 = ((bf16[8,96,1536]{2,1,0:T(8,128)(2,1)}), bf16[8,96,1536]{2,1,0:T(8,128)(2,1)S(1)}, u32[]{:S(2)}, u32[]{:S(2)}) async-start(bf16[8,96,1536]{2,1,0:T(8,128)(2,1)} %pick.1), calls=%async_computation.1 | async-start | bytes 4718592 | tf_op jit(solution)/shard_map/all_to_all | solution.py:431
  107.6 3.0 %collective-permute-start.15 = (bf16[8,32,4,128]{3,2,1,0:T(4,128)(2,1)}, bf16[8,32,4,128]{3,2,1,0:T(4,128)(2,1)}, u32[]{:S(2)}, u32[]{:S(2)}) collective-permute-start(bf16[8,32,4,128]{3,2,1,0:T(4,128)(2,1)} %get-tuple-element.70), channel_id=1, source_target_pairs={{0,16},{1,17},{2,18},{3,19},{4,20},{5,21},{6,22},{7,23},{8,24},{9,... | collective-permute-start | bytes 786440 | tf_op jit(solution)/shard_map/ppermute | solution.py:572
  110.8 6.3 %copy.35 = bf16[4,1536,2,256]{3,1,2,0:T(8,128)(2,1)} copy(bf16[4,1536,2,256]{3,2,1,0:T(2,128)(2,1)} %param.26) | data formatting | bytes 12582912 | tf_op jit(solution)/shard_map/optimization_barrier | solution.py:496
  117.1 13.9 %all-to-all-done.1.rows_ref = bf16[8,96,1536]{2,1,0:T(8,128)(2,1)S(1)} async-done(((bf16[8,96,1536]{2,1,0:T(8,128)(2,1)}), bf16[8,96,1536]{2,1,0:T(8,128)(2,1)S(1)}, u32[]{:S(2)}, u32[]{:S(2)}) %all-to-all-start.1) | async-done | bytes 2359328 | tf_op jit(solution)/shard_map/all_to_all | solution.py:431
  131.0 5.9 %experts.1 = bf16[8,96,1536]{2,1,0:T(8,128)(2,1)} custom-call(bf16[8,96,1536]{2,1,0:T(8,128)(2,1)S(1)} %all-to-all-done.1.rows_ref, bf16[4,2,1536,256]{3,2,1,0:T(8,128)(2,1)} %bitcast.51, bf16[4,256,1536]{2,1,0:T(8,128)(2,1)} %down_hbm.1), custom_call_target="tpu_custom_call" | custom-call | flops 1811939328 | bytes 14680064 | tf_op jit(solution)/shard_map/experts/pallas_call | solution.py:585
  136.9 5.0 %all-to-all-start.2 = ((bf16[8,96,1536]{2,1,0:T(8,128)(2,1)}), bf16[8,96,1536]{2,1,0:T(8,128)(2,1)S(1)}, u32[]{:S(2)}, u32[]{:S(2)}) async-start(bf16[8,96,1536]{2,1,0:T(8,128)(2,1)} %experts.1), calls=%async_computation.2 | async-start | bytes 4718592 | tf_op jit(solution)/shard_map/all_to_all | solution.py:431
  146.9 23.0 %all-to-all-done.2 = bf16[8,96,1536]{2,1,0:T(8,128)(2,1)S(1)} async-done(((bf16[8,96,1536]{2,1,0:T(8,128)(2,1)}), bf16[8,96,1536]{2,1,0:T(8,128)(2,1)S(1)}, u32[]{:S(2)}, u32[]{:S(2)}) %all-to-all-start.2) | async-done | bytes 2359328 | tf_op jit(solution)/shard_map/all_to_all | solution.py:431
  173.7 3.0 %collective-permute-start.18 = (bf16[64,1536]{1,0:T(8,128)(2,1)S(1)}, bf16[64,1536]{1,0:T(8,128)(2,1)S(1)}, u32[]{:S(2)}, u32[]{:S(2)}) collective-permute-start(bf16[64,1536]{1,0:T(8,128)(2,1)S(1)} %get-tuple-element.76), channel_id=1, source_target_pairs={{0,16},{1,17},{2,18},{3,19},{4,20},{5,21},{6,22},{7,23},{8,24},{9,... | collective-permute-start | bytes 589832 | tf_op jit(solution)/shard_map/ppermute | solution.py:465
  180.5 6.7 %collective-permute-done.17.refs_1_ = bf16[64,1536]{1,0:T(8,128)(2,1)S(1)} collective-permute-done((bf16[64,1536]{1,0:T(8,128)(2,1)S(1)}, bf16[64,1536]{1,0:T(8,128)(2,1)S(1)}, u32[]{:S(2)}, u32[]{:S(2)}) %collective-permute-start.17) | collective-permute-done | bytes 196640 | tf_op jit(solution)/shard_map/ppermute | solution.py:465
  187.2 3.5 %collective-permute-done.18.refs_2_ = bf16[64,1536]{1,0:T(8,128)(2,1)S(1)} collective-permute-done((bf16[64,1536]{1,0:T(8,128)(2,1)S(1)}, bf16[64,1536]{1,0:T(8,128)(2,1)S(1)}, u32[]{:S(2)}, u32[]{:S(2)}) %collective-permute-start.18) | collective-permute-done | bytes 196640 | tf_op jit(solution)/shard_map/ppermute | solution.py:465
  190.7 2.7 %collective-permute-done.19.refs_3_ = bf16[64,1536]{1,0:T(8,128)(2,1)S(1)} collective-permute-done((bf16[64,1536]{1,0:T(8,128)(2,1)S(1)}, bf16[64,1536]{1,0:T(8,128)(2,1)S(1)}, u32[]{:S(2)}, u32[]{:S(2)}) %collective-permute-start.19) | collective-permute-done | bytes 196640 | tf_op jit(solution)/shard_map/ppermute | solution.py:465
  (86 shorter events, 39.1 us)
Async XLA Ops:
  7.2 43.6 %all-gather.4.cloned.1.call-start = ((), (), s32[]{:S(2)}) async-start(), calls=%async_computation.3 | async-start | bytes 1327104 | tf_op jit(solution)/shard_map/all_gather | solution.py:449
  8.8 108.4 %all-gather.6.cloned.1.call-start = ((), (), s32[]{:S(2)}) async-start(), calls=%async_computation.4 | async-start | bytes 2654208 | tf_op jit(solution)/shard_map/all_gather | solution.py:494
  8.8 17.4 %collective-permute-start.3 = (bf16[64,1024]{1,0:T(8,128)(2,1)}, bf16[64,1024]{1,0:T(8,128)(2,1)S(1)}, u32[]{:S(2)}, u32[]{:S(2)}) collective-permute-start(bf16[64,1024]{1,0:T(8,128)(2,1)} %join.1.own_ref), channel_id=1, source_target_pairs={{0,1},{1,2},{2,3},{3,4},{4,5},{5,6},{6,7},{7,8},{8,9},{9,10},{10,1... | collective-permute-start | bytes 393224 | tf_op jit(solution)/shard_map/ppermute | solution.py:28
  10.7 15.5 %collective-permute-start.2 = (bf16[64,1024]{1,0:T(8,128)(2,1)}, bf16[64,1024]{1,0:T(8,128)(2,1)S(1)}, u32[]{:S(2)}, u32[]{:S(2)}) collective-permute-start(bf16[64,1024]{1,0:T(8,128)(2,1)} %join.1.own_ref), channel_id=1, source_target_pairs={{0,2},{1,3},{2,4},{3,5},{4,6},{5,7},{6,8},{7,9},{8,10},{9,11},{10,... | collective-permute-start | bytes 393224 | tf_op jit(solution)/shard_map/ppermute | solution.py:28
  14.2 12.1 %collective-permute-start.1 = (bf16[64,1024]{1,0:T(8,128)(2,1)}, bf16[64,1024]{1,0:T(8,128)(2,1)S(1)}, u32[]{:S(2)}, u32[]{:S(2)}) collective-permute-start(bf16[64,1024]{1,0:T(8,128)(2,1)} %join.1.own_ref), channel_id=1, source_target_pairs={{0,3},{1,4},{2,5},{3,6},{4,7},{5,8},{6,9},{7,10},{8,11},{9,12},{10... | collective-permute-start | bytes 393224 | tf_op jit(solution)/shard_map/ppermute | solution.py:28
  18.5 8.0 %collective-permute-start = (bf16[64,1024]{1,0:T(8,128)(2,1)}, bf16[64,1024]{1,0:T(8,128)(2,1)S(1)}, u32[]{:S(2)}, u32[]{:S(2)}) collective-permute-start(bf16[64,1024]{1,0:T(8,128)(2,1)} %join.1.own_ref), channel_id=1, source_target_pairs={{0,4},{1,5},{2,6},{3,7},{4,8},{5,9},{6,10},{7,11},{8,12},{9,13},{1... | collective-permute-start | bytes 393224 | tf_op jit(solution)/shard_map/ppermute | solution.py:28
  30.4 16.8 %collective-permute-start.6 = (bf16[64,1664]{1,0:T(8,128)(2,1)}, bf16[64,1664]{1,0:T(8,128)(2,1)S(1)}, u32[]{:S(2)}, u32[]{:S(2)}) collective-permute-start(bf16[64,1664]{1,0:T(8,128)(2,1)} %attention.1.refs_0_), channel_id=1, source_target_pairs={{0,24},{1,25},{2,26},{3,27},{4,28},{5,29},{6,30},{7,31},{8,0},{9,1... | collective-permute-start | bytes 638984 | tf_op jit(solution)/shard_map/ppermute | solution.py:465
  30.8 16.4 %collective-permute-start.5 = (bf16[64,1664]{1,0:T(8,128)(2,1)}, bf16[64,1664]{1,0:T(8,128)(2,1)S(1)}, u32[]{:S(2)}, u32[]{:S(2)}) collective-permute-start(bf16[64,1664]{1,0:T(8,128)(2,1)} %attention.1.refs_0_), channel_id=1, source_target_pairs={{0,16},{1,17},{2,18},{3,19},{4,20},{5,21},{6,22},{7,23},{8,24},{9,... | collective-permute-start | bytes 638984 | tf_op jit(solution)/shard_map/ppermute | solution.py:465
  33.5 17.3 %collective-permute-start.4 = (bf16[64,1664]{1,0:T(8,128)(2,1)}, bf16[64,1664]{1,0:T(8,128)(2,1)S(1)}, u32[]{:S(2)}, u32[]{:S(2)}) collective-permute-start(bf16[64,1664]{1,0:T(8,128)(2,1)} %attention.1.refs_0_), channel_id=1, source_target_pairs={{0,8},{1,9},{2,10},{3,11},{4,12},{5,13},{6,14},{7,15},{8,16},{9,17... | collective-permute-start | bytes 638984 | tf_op jit(solution)/shard_map/ppermute | solution.py:465
  53.7 41.7 %all-to-all-start = ((bf16[4,256,384]{2,1,0:T(8,128)(2,1)}), bf16[4,256,384]{2,1,0:T(8,128)(2,1)S(1)}, u32[]{:S(2)}, u32[]{:S(2)}) async-start(bf16[4,256,384]{2,1,0:T(8,128)(2,1)} %get-tuple-element.49), calls=%async_computation | async-start | bytes 1572864 | tf_op jit(solution)/shard_map/all_to_all | solution.py:431
  60.2 14.6 %collective-permute-start.12 = (bf16[4,32,4,128]{3,2,1,0:T(4,128)(2,1)S(1)}, bf16[4,32,4,128]{3,2,1,0:T(4,128)(2,1)S(1)}, u32[]{:S(2)}, u32[]{:S(2)}) collective-permute-start(bf16[4,32,4,128]{3,2,1,0:T(4,128)(2,1)S(1)} %get-tuple-element.83), channel_id=1, source_target_pairs={{0,6},{1,7},{2,0},{3,1},{4,2},{5,3},{6,4},{7,5},{8,14},{9,15},{10,... | collective-permute-start | bytes 393224 | tf_op jit(solution)/shard_map/ppermute | solution.py:514
  61.9 36.9 %collective-permute-start.11 = (bf16[4,32,4,128]{3,2,1,0:T(4,128)(2,1)S(1)}, bf16[4,32,4,128]{3,2,1,0:T(4,128)(2,1)S(1)}, u32[]{:S(2)}, u32[]{:S(2)}) collective-permute-start(bf16[4,32,4,128]{3,2,1,0:T(4,128)(2,1)S(1)} %get-tuple-element.84), channel_id=1, source_target_pairs={{0,5},{1,6},{2,7},{3,0},{4,1},{5,2},{6,3},{7,4},{8,13},{9,14},{10,... | collective-permute-start | bytes 393224 | tf_op jit(solution)/shard_map/ppermute | solution.py:514
  63.8 35.1 %collective-permute-start.10 = (bf16[4,32,4,128]{3,2,1,0:T(4,128)(2,1)S(1)}, bf16[4,32,4,128]{3,2,1,0:T(4,128)(2,1)S(1)}, u32[]{:S(2)}, u32[]{:S(2)}) collective-permute-start(bf16[4,32,4,128]{3,2,1,0:T(4,128)(2,1)S(1)} %get-tuple-element.85), channel_id=1, source_target_pairs={{0,4},{1,5},{2,6},{3,7},{4,0},{5,1},{6,2},{7,3},{8,12},{9,13},{10,... | collective-permute-start | bytes 393224 | tf_op jit(solution)/shard_map/ppermute | solution.py:514
  64.0 34.9 %collective-permute-start.9 = (bf16[4,32,4,128]{3,2,1,0:T(4,128)(2,1)S(1)}, bf16[4,32,4,128]{3,2,1,0:T(4,128)(2,1)S(1)}, u32[]{:S(2)}, u32[]{:S(2)}) collective-permute-start(bf16[4,32,4,128]{3,2,1,0:T(4,128)(2,1)S(1)} %get-tuple-element.86), channel_id=1, source_target_pairs={{0,3},{1,4},{2,5},{3,6},{4,7},{5,0},{6,1},{7,2},{8,11},{9,12},{10,... | collective-permute-start | bytes 393224 | tf_op jit(solution)/shard_map/ppermute | solution.py:514
  66.4 32.6 %collective-permute-start.8 = (bf16[4,32,4,128]{3,2,1,0:T(4,128)(2,1)S(1)}, bf16[4,32,4,128]{3,2,1,0:T(4,128)(2,1)S(1)}, u32[]{:S(2)}, u32[]{:S(2)}) collective-permute-start(bf16[4,32,4,128]{3,2,1,0:T(4,128)(2,1)S(1)} %get-tuple-element.87), channel_id=1, source_target_pairs={{0,2},{1,3},{2,4},{3,5},{4,6},{5,7},{6,0},{7,1},{8,10},{9,11},{10,... | collective-permute-start | bytes 393224 | tf_op jit(solution)/shard_map/ppermute | solution.py:514
  74.8 24.1 %collective-permute-start.7 = (bf16[4,32,4,128]{3,2,1,0:T(4,128)(2,1)S(1)}, bf16[4,32,4,128]{3,2,1,0:T(4,128)(2,1)S(1)}, u32[]{:S(2)}, u32[]{:S(2)}) collective-permute-start(bf16[4,32,4,128]{3,2,1,0:T(4,128)(2,1)S(1)} %get-tuple-element.88), channel_id=1, source_target_pairs={{0,1},{1,2},{2,3},{3,4},{4,5},{5,6},{6,7},{7,0},{8,9},{9,10},{10,1... | collective-permute-start | bytes 393224 | tf_op jit(solution)/shard_map/ppermute | solution.py:514
  99.8 31.2 %all-to-all-start.1 = ((bf16[8,96,1536]{2,1,0:T(8,128)(2,1)}), bf16[8,96,1536]{2,1,0:T(8,128)(2,1)S(1)}, u32[]{:S(2)}, u32[]{:S(2)}) async-start(bf16[8,96,1536]{2,1,0:T(8,128)(2,1)} %pick.1), calls=%async_computation.1 | async-start | bytes 4718592 | tf_op jit(solution)/shard_map/all_to_all | solution.py:431
  106.2 30.7 %collective-permute-start.14 = (bf16[8,32,4,128]{3,2,1,0:T(4,128)(2,1)}, bf16[8,32,4,128]{3,2,1,0:T(4,128)(2,1)}, u32[]{:S(2)}, u32[]{:S(2)}) collective-permute-start(bf16[8,32,4,128]{3,2,1,0:T(4,128)(2,1)} %get-tuple-element.69), channel_id=1, source_target_pairs={{0,8},{1,9},{2,10},{3,11},{4,12},{5,13},{6,14},{7,15},{8,16},{9,17... | collective-permute-start | bytes 786440 | tf_op jit(solution)/shard_map/ppermute | solution.py:572
  107.6 29.3 %collective-permute-start.15 = (bf16[8,32,4,128]{3,2,1,0:T(4,128)(2,1)}, bf16[8,32,4,128]{3,2,1,0:T(4,128)(2,1)}, u32[]{:S(2)}, u32[]{:S(2)}) collective-permute-start(bf16[8,32,4,128]{3,2,1,0:T(4,128)(2,1)} %get-tuple-element.70), channel_id=1, source_target_pairs={{0,16},{1,17},{2,18},{3,19},{4,20},{5,21},{6,22},{7,23},{8,24},{9,... | collective-permute-start | bytes 786440 | tf_op jit(solution)/shard_map/ppermute | solution.py:572
  110.6 26.3 %collective-permute-start.16 = (bf16[8,32,4,128]{3,2,1,0:T(4,128)(2,1)S(1)}, bf16[8,32,4,128]{3,2,1,0:T(4,128)(2,1)}, u32[]{:S(2)}, u32[]{:S(2)}) collective-permute-start(bf16[8,32,4,128]{3,2,1,0:T(4,128)(2,1)S(1)} %get-tuple-element.71), channel_id=1, source_target_pairs={{0,24},{1,25},{2,26},{3,27},{4,28},{5,29},{6,30},{7,31},{8,0},{9,1... | collective-permute-start | bytes 786440 | tf_op jit(solution)/shard_map/ppermute | solution.py:572
  136.9 33.0 %all-to-all-start.2 = ((bf16[8,96,1536]{2,1,0:T(8,128)(2,1)}), bf16[8,96,1536]{2,1,0:T(8,128)(2,1)S(1)}, u32[]{:S(2)}, u32[]{:S(2)}) async-start(bf16[8,96,1536]{2,1,0:T(8,128)(2,1)} %experts.1), calls=%async_computation.2 | async-start | bytes 4718592 | tf_op jit(solution)/shard_map/all_to_all | solution.py:431
  172.1 15.1 %collective-permute-start.17 = (bf16[64,1536]{1,0:T(8,128)(2,1)S(1)}, bf16[64,1536]{1,0:T(8,128)(2,1)S(1)}, u32[]{:S(2)}, u32[]{:S(2)}) collective-permute-start(bf16[64,1536]{1,0:T(8,128)(2,1)S(1)} %get-tuple-element.75), channel_id=1, source_target_pairs={{0,8},{1,9},{2,10},{3,11},{4,12},{5,13},{6,14},{7,15},{8,16},{9,17... | collective-permute-start | bytes 589832 | tf_op jit(solution)/shard_map/ppermute | solution.py:465
  173.7 17.0 %collective-permute-start.18 = (bf16[64,1536]{1,0:T(8,128)(2,1)S(1)}, bf16[64,1536]{1,0:T(8,128)(2,1)S(1)}, u32[]{:S(2)}, u32[]{:S(2)}) collective-permute-start(bf16[64,1536]{1,0:T(8,128)(2,1)S(1)} %get-tuple-element.76), channel_id=1, source_target_pairs={{0,16},{1,17},{2,18},{3,19},{4,20},{5,21},{6,22},{7,23},{8,24},{9,... | collective-permute-start | bytes 589832 | tf_op jit(solution)/shard_map/ppermute | solution.py:465
  176.7 16.7 %collective-permute-start.19 = (bf16[64,1536]{1,0:T(8,128)(2,1)S(1)}, bf16[64,1536]{1,0:T(8,128)(2,1)S(1)}, u32[]{:S(2)}, u32[]{:S(2)}) collective-permute-start(bf16[64,1536]{1,0:T(8,128)(2,1)S(1)} %get-tuple-element.77), channel_id=1, source_target_pairs={{0,24},{1,25},{2,26},{3,27},{4,28},{5,29},{6,30},{7,31},{8,0},{9,1... | collective-permute-start | bytes 589832 | tf_op jit(solution)/shard_map/ppermute | solution.py:465
  (21 other events, 207.4 us)
Sparse Core Ops, SparseCore 0:
  9.9 29.9 all-gather.3
  41.7 38.6 all-gather.5

commit v7 on v5

--- a/solution.py
+++ b/solution.py
@@ -459,7 +459,7 @@
         out_specs=VMEM,
         compiler_params=params(),
         name="join",
-    )(key_vectors, value_vectors)
+    )(in_hbm(key_vectors), in_hbm(value_vectors))
     behind = [from_behind(own_kv, "seq", offset) for offset in range(REACH, 0, -1)]
 
     turned_weight = lax.all_gather(
@@ -467,14 +467,14 @@
     )
     info = pl.pallas_call(
         route_kernel,
-        out_shape=shape((tokens, 128), bf16),
+        out_shape=pltpu.HBM((tokens, 128), bf16),
         in_specs=[SMEM] + [VMEM] * 2,
         out_specs=VMEM,
         scratch_shapes=[pltpu.VMEM((128, 128), f32)],
         compiler_params=params(),
         cost_estimate=cost(MIB, MIB),
         name="route",
-    )(scalar(z_index), route_ids.T, route_logits.T)
+    )(scalar(z_index), in_hbm(route_ids.T), in_hbm(route_logits.T))
 
     def along_z(arrays):
         return [arrays[0]] + [
@@ -498,13 +498,13 @@
     sent_width = width + part + info.shape[1]
     sent = pl.pallas_call(
         attention_kernel,
-        out_shape=[shape((tokens, sent_width), bf16)] * Z_SIZE,
+        out_shape=[pltpu.HBM((tokens, sent_width), bf16)] * Z_SIZE,
         in_specs=[SMEM] * 3 + [VMEM] * 8,
         out_specs=[VMEM] * Z_SIZE,
         compiler_params=params(58),
         cost_estimate=cost(4 * tokens * 5 * tokens * width, 3 * MIB),
         name="attention",
-    )(z_scalar, scalar(me * tokens), lengths, queries, *behind, own_kv, residual, info)
+    )(z_scalar, scalar(me * tokens), in_hbm(lengths), queries, *behind, own_kv, residual, info)
 
     sent, own_shared = lax.optimization_barrier((sent, own_shared))
     shared_weight = lax.all_gather(own_shared, "seq", axis=0, axis_index_groups=planes)
@@ -540,7 +540,7 @@
         compiler_params=params(),
         cost_estimate=cost(2 * all_tokens * width * part, 3 * MIB),
         name="project",
-    )(z_scalar, *gathered, turned_weight)
+    )(z_scalar, in_hbm(gathered[0]), *gathered[1:], in_hbm(turned_weight))
     mixed = exchange(mixed_part, z_groups)
 
     local_halves, _, _, half_ff = expert_gate_up.shape

time: 190 us -> 188 us (0.989)
  local copies, waits for them, and re-layouts: 19 us -> 13 us
  Pallas kernels: 25.2 us -> 28.6 us
  starting transfers between devices: 48 us -> 50.1 us
    unnamed x52 -> x38, local copies, waits for them, and re-layouts: 11.4 us -> 5.42 us
  transfers between devices with their start and end apart: 25 -> 25, of which waited for: 9 -> 10; matrix products, arithmetic and copies ran while one was open for 6% -> 6% of each run, Pallas kernels for 12% -> 14%
where the time goes in v7:
time: 188 us
  waiting for transfers between devices  78 us (41%)
  starting transfers between devices  50.1 us (27%)
  Pallas kernels  28.6 us (15%)
  between operations  14.3 us (8%)
  local copies, waits for them, and re-layouts  13 us (7%)
  other arithmetic  3.57 us (2%)
    all_to_all x3, waiting for transfers between devices, exchange(): lax.all_to_all(array, 'seq', split_axis=0, concat_axis=0, tiled=True, axi...  40.1 us
    ppermute x6, waiting for transfers between devices, along_z(): lax.ppermute(arrays[step], 'seq', z_pairs[step])  33.6 us
    all_to_all x3, starting transfers between devices, exchange(): lax.all_to_all(array, 'seq', split_axis=0, concat_axis=0, tiled=True, axi...  14.9 us
    ppermute x4, starting transfers between devices, from_behind(): return lax.ppermute(shard, axis, pairs)  13.1 us
    ppermute x6, starting transfers between devices, along_z(): lax.ppermute(arrays[step], 'seq', z_pairs[step])  9.52 us
    ppermute x7, starting transfers between devices, shards(): piece = lax.ppermute(piece, 'seq', pairs)  7.25 us
    optimization_barrier x1, local copies, waits for them, and re-layouts, shards(): lax.optimization_barrier((gathered, cache_blocks, expert_gate_up))  6.31 us
    pallas_call x1, Pallas kernels, shards(): pl.pallas_call(experts_kernel, out_shape=pltpu.HBM((PLANE, picked, width)...  5.88 us
  transfers between devices with their start and end apart: 25, of which 10 were waited for; matrix products, arithmetic and copies ran while one was open for 6% of the time, Pallas kernels for 14%

profile of v7, /device:TPU:10, one launch (start us, length us, event | category | flops | bytes accessed | tf_op | source)
XLA Modules:
  0.0 187.5 jit_solution(268380702322574741)
XLA Ops:
  11.4 3.4 %collective-permute-start.2 = (bf16[64,1024]{1,0:T(8,128)(2,1)}, bf16[64,1024]{1,0:T(8,128)(2,1)S(1)}, u32[]{:S(2)}, u32[]{:S(2)}) collective-permute-start(bf16[64,1024]{1,0:T(8,128)(2,1)} %join.1.own_ref), channel_id=1, source_target_pairs={{0,2},{1,3},{2,4},{3,5},{4,6},{5,7},{6,8},{7,9},{8,10},{9,11},{10,... | collective-permute-start | bytes 393224 | tf_op jit(solution)/shard_map/ppermute | solution.py:28
  14.8 4.3 %collective-permute-start.1 = (bf16[64,1024]{1,0:T(8,128)(2,1)}, bf16[64,1024]{1,0:T(8,128)(2,1)S(1)}, u32[]{:S(2)}, u32[]{:S(2)}) collective-permute-start(bf16[64,1024]{1,0:T(8,128)(2,1)} %join.1.own_ref), channel_id=1, source_target_pairs={{0,3},{1,4},{2,5},{3,6},{4,7},{5,8},{6,9},{7,10},{8,11},{9,12},{10... | collective-permute-start | bytes 393224 | tf_op jit(solution)/shard_map/ppermute | solution.py:28
  19.1 3.4 %collective-permute-start = (bf16[64,1024]{1,0:T(8,128)(2,1)}, bf16[64,1024]{1,0:T(8,128)(2,1)S(1)}, u32[]{:S(2)}, u32[]{:S(2)}) collective-permute-start(bf16[64,1024]{1,0:T(8,128)(2,1)} %join.1.own_ref), channel_id=1, source_target_pairs={{0,4},{1,5},{2,6},{3,7},{4,8},{5,9},{6,10},{7,11},{8,12},{9,13},{1... | collective-permute-start | bytes 393224 | tf_op jit(solution)/shard_map/ppermute | solution.py:28
  22.6 2.6 %route.1.info_ref = bf16[64,128]{1,0:T(8,128)(2,1)} custom-call(s32[1]{0:T(128)} %bitcast.z_ref, s32[6,64]{1,0:T(8,128)} %bitcast.56, f32[6,64]{1,0:T(8,128)} %bitcast.57), custom_call_target="tpu_custom_call" | custom-call | flops 1048576 | bytes 1048576 | tf_op jit(solution)/shard_map/route/pallas_call | solution.py:468
  27.7 3.8 %attention.1 = (bf16[64,2048]{1,0:T(8,128)(2,1)}, bf16[64,2048]{1,0:T(8,128)(2,1)}, bf16[64,2048]{1,0:T(8,128)(2,1)}, bf16[64,2048]{1,0:T(8,128)(2,1)}) custom-call(s32[1]{0:T(128)} %bitcast.z_ref, s32[1]{0:T(128)} %bitcast.1.first_ref, s32[16]{0:T(128)} %lengths_ref.1, bf16[64,1536]{1,0:T(8,128)(2,1)} %q_ref.1, bf16[64,1024]{1,0:T(8,128)(2,1)} %copy-done.10, ...), custom_call_target="tpu_custom_call" | custom-call | flops 125829120 | bytes 3145728 | tf_op jit(solution)/shard_map/attention/pallas_call | solution.py:499
  35.7 15.8 %collective-permute-done.4.refs_1_ = bf16[64,2048]{1,0:T(8,128)(2,1)S(1)} collective-permute-done((bf16[64,2048]{1,0:T(8,128)(2,1)}, bf16[64,2048]{1,0:T(8,128)(2,1)S(1)}, u32[]{:S(2)}, u32[]{:S(2)}) %collective-permute-start.4) | collective-permute-done | bytes 262176 | tf_op jit(solution)/shard_map/ppermute | solution.py:481
  51.5 3.5 %collective-permute-done.5.refs_2_ = bf16[64,2048]{1,0:T(8,128)(2,1)S(1)} collective-permute-done((bf16[64,2048]{1,0:T(8,128)(2,1)}, bf16[64,2048]{1,0:T(8,128)(2,1)S(1)}, u32[]{:S(2)}, u32[]{:S(2)}) %collective-permute-start.5) | collective-permute-done | bytes 262176 | tf_op jit(solution)/shard_map/ppermute | solution.py:481
  56.6 2.8 %project.1 = (bf16[4,256,384]{2,1,0:T(8,128)(2,1)}, bf16[256,128]{1,0:T(8,128)(2,1)S(1)}) custom-call(s32[1]{0:T(128)} %bitcast.z_ref, bf16[64,2048]{1,0:T(8,128)(2,1)} %get-tuple-element.55.refs_0_, bf16[64,2048]{1,0:T(8,128)(2,1)S(1)} %collective-permute-done.4.refs_1_, bf16[64,2048]{1,0:T(8,128)(2,1)S(1)} %collective-permute-done.5.refs_2_, ...), custom_call_target="tpu_custom_call" | custom-call | flops 301989888 | bytes 3145728 | tf_op jit(solution)/shard_map/project/pallas_call | solution.py:534
  59.4 4.5 %all-to-all-start = ((bf16[4,256,384]{2,1,0:T(8,128)(2,1)}), bf16[4,256,384]{2,1,0:T(8,128)(2,1)S(1)}, u32[]{:S(2)}, u32[]{:S(2)}) async-start(bf16[4,256,384]{2,1,0:T(8,128)(2,1)} %get-tuple-element.59), calls=%async_computation | async-start | bytes 1572864 | tf_op jit(solution)/shard_map/all_to_all | solution.py:451
  69.1 2.4 %collective-permute-start.9 = (bf16[4,32,4,128]{3,2,1,0:T(4,128)(2,1)S(1)}, bf16[4,32,4,128]{3,2,1,0:T(4,128)(2,1)S(1)}, u32[]{:S(2)}, u32[]{:S(2)}) collective-permute-start(bf16[4,32,4,128]{3,2,1,0:T(4,128)(2,1)S(1)} %get-tuple-element.96), channel_id=1, source_target_pairs={{0,3},{1,4},{2,5},{3,6},{4,7},{5,0},{6,1},{7,2},{8,11},{9,12},{10,... | collective-permute-start | bytes 393224 | tf_op jit(solution)/shard_map/ppermute | solution.py:530
  72.5 3.3 %collective-permute-done.12.refs_6_ = bf16[4,32,4,128]{3,2,1,0:T(4,128)(2,1)S(1)} collective-permute-done((bf16[4,32,4,128]{3,2,1,0:T(4,128)(2,1)S(1)}, bf16[4,32,4,128]{3,2,1,0:T(4,128)(2,1)S(1)}, u32[]{:S(2)}, u32[]{:S(2)}) %collective-permute-start.12) | collective-permute-done | bytes 131104 | tf_op jit(solution)/shard_map/ppermute | solution.py:530
  78.4 2.2 %all-to-all-done.mixed_ref = bf16[4,256,384]{2,1,0:T(8,128)(2,1)S(1)} async-done(((bf16[4,256,384]{2,1,0:T(8,128)(2,1)}), bf16[4,256,384]{2,1,0:T(8,128)(2,1)S(1)}, u32[]{:S(2)}, u32[]{:S(2)}) %all-to-all-start) | async-done | bytes 786464 | tf_op jit(solution)/shard_map/all_to_all | solution.py:451
  83.7 5.3 %all-to-all-start.1 = ((bf16[8,96,1536]{2,1,0:T(8,128)(2,1)}), bf16[8,96,1536]{2,1,0:T(8,128)(2,1)S(1)}, u32[]{:S(2)}, u32[]{:S(2)}) async-start(bf16[8,96,1536]{2,1,0:T(8,128)(2,1)} %pick.1), calls=%async_computation.1 | async-start | bytes 4718592 | tf_op jit(solution)/shard_map/all_to_all | solution.py:451
  89.0 2.1 %regroup.1 = (bf16[8,32,4,128]{3,2,1,0:T(4,128)(2,1)S(1)}, bf16[8,32,4,128]{3,2,1,0:T(4,128)(2,1)}, bf16[8,32,4,128]{3,2,1,0:T(4,128)(2,1)}, bf16[8,32,4,128]{3,2,1,0:T(4,128)(2,1)S(1)}) custom-call(s32[1]{0:T(128)} %bitcast.z_ref, bf16[4,32,4,128]{3,2,1,0:T(4,128)(2,1)} %get-tuple-element.70.refs_0_, bf16[4,32,4,128]{3,2,1,0:T(4,128)(2,1)} %copy-done.17, ...), custom_call_target="tpu_custom_call" | custom-call | bytes 2097152 | tf_op jit(solution)/shard_map/regroup/pallas_call | solution.py:577
  92.7 4.2 %collective-permute-start.15 = (bf16[8,32,4,128]{3,2,1,0:T(4,128)(2,1)}, bf16[8,32,4,128]{3,2,1,0:T(4,128)(2,1)}, u32[]{:S(2)}, u32[]{:S(2)}) collective-permute-start(bf16[8,32,4,128]{3,2,1,0:T(4,128)(2,1)} %get-tuple-element.80), channel_id=1, source_target_pairs={{0,16},{1,17},{2,18},{3,19},{4,20},{5,21},{6,22},{7,23},{8,24},{9,... | collective-permute-start | bytes 786440 | tf_op jit(solution)/shard_map/ppermute | solution.py:588
  97.2 6.3 %copy.35 = bf16[4,1536,2,256]{3,1,2,0:T(8,128)(2,1)} copy(bf16[4,1536,2,256]{3,2,1,0:T(2,128)(2,1)} %param.26) | data formatting | bytes 12582912 | tf_op jit(solution)/shard_map/optimization_barrier | solution.py:512
  103.5 13.5 %all-to-all-done.1.rows_ref = bf16[8,96,1536]{2,1,0:T(8,128)(2,1)S(1)} async-done(((bf16[8,96,1536]{2,1,0:T(8,128)(2,1)}), bf16[8,96,1536]{2,1,0:T(8,128)(2,1)S(1)}, u32[]{:S(2)}, u32[]{:S(2)}) %all-to-all-start.1) | async-done | bytes 2359328 | tf_op jit(solution)/shard_map/all_to_all | solution.py:451
  117.0 5.9 %experts.1 = bf16[8,96,1536]{2,1,0:T(8,128)(2,1)} custom-call(bf16[8,96,1536]{2,1,0:T(8,128)(2,1)S(1)} %all-to-all-done.1.rows_ref, bf16[4,2,1536,256]{3,2,1,0:T(8,128)(2,1)} %bitcast.51, bf16[4,256,1536]{2,1,0:T(8,128)(2,1)} %down_hbm.1), custom_call_target="tpu_custom_call" | custom-call | flops 1811939328 | bytes 14680064 | tf_op jit(solution)/shard_map/experts/pallas_call | solution.py:601
  122.9 5.1 %all-to-all-start.2 = ((bf16[8,96,1536]{2,1,0:T(8,128)(2,1)}), bf16[8,96,1536]{2,1,0:T(8,128)(2,1)S(1)}, u32[]{:S(2)}, u32[]{:S(2)}) async-start(bf16[8,96,1536]{2,1,0:T(8,128)(2,1)} %experts.1), calls=%async_computation.2 | async-start | bytes 4718592 | tf_op jit(solution)/shard_map/all_to_all | solution.py:451
  131.5 24.4 %all-to-all-done.2 = bf16[8,96,1536]{2,1,0:T(8,128)(2,1)S(1)} async-done(((bf16[8,96,1536]{2,1,0:T(8,128)(2,1)}), bf16[8,96,1536]{2,1,0:T(8,128)(2,1)S(1)}, u32[]{:S(2)}, u32[]{:S(2)}) %all-to-all-start.2) | async-done | bytes 2359328 | tf_op jit(solution)/shard_map/all_to_all | solution.py:451
  155.9 2.2 %combine.1 = (bf16[64,1536]{1,0:T(8,128)(2,1)S(1)}, bf16[64,1536]{1,0:T(8,128)(2,1)S(1)}, bf16[64,1536]{1,0:T(8,128)(2,1)S(1)}, bf16[64,1536]{1,0:T(8,128)(2,1)S(1)}) custom-call(s32[1]{0:T(128)} %bitcast.z_ref, bf16[256,768]{1,0:T(8,128)(2,1)} %copy-done.2, bf16[768,1536]{1,0:T(8,128)(2,1)S(1)} %bitcast.49, bf16[256,1536]{1,0:T(8,128)(2,1)} %copy-done.1), custom_call_target="tpu_custom_call" | custom-call | flops 603979776 | bytes 3145728 | tf_op jit(solution)/shard_map/combine/pallas_call | solution.py:632
  159.0 4.2 %collective-permute-start.18 = (bf16[64,1536]{1,0:T(8,128)(2,1)S(1)}, bf16[64,1536]{1,0:T(8,128)(2,1)S(1)}, u32[]{:S(2)}, u32[]{:S(2)}) collective-permute-start(bf16[64,1536]{1,0:T(8,128)(2,1)S(1)} %get-tuple-element.86), channel_id=1, source_target_pairs={{0,16},{1,17},{2,18},{3,19},{4,20},{5,21},{6,22},{7,23},{8,24},{9,... | collective-permute-start | bytes 589832 | tf_op jit(solution)/shard_map/ppermute | solution.py:481
  167.1 8.9 %collective-permute-done.18.refs_2_ = bf16[64,1536]{1,0:T(8,128)(2,1)S(1)} collective-permute-done((bf16[64,1536]{1,0:T(8,128)(2,1)S(1)}, bf16[64,1536]{1,0:T(8,128)(2,1)S(1)}, u32[]{:S(2)}, u32[]{:S(2)}) %collective-permute-start.18) | collective-permute-done | bytes 196640 | tf_op jit(solution)/shard_map/ppermute | solution.py:481
  176.0 3.9 %collective-permute-done.19.refs_3_ = bf16[64,1536]{1,0:T(8,128)(2,1)S(1)} collective-permute-done((bf16[64,1536]{1,0:T(8,128)(2,1)S(1)}, bf16[64,1536]{1,0:T(8,128)(2,1)S(1)}, u32[]{:S(2)}, u32[]{:S(2)}) %collective-permute-start.19) | collective-permute-done | bytes 196640 | tf_op jit(solution)/shard_map/ppermute | solution.py:481
  (83 shorter events, 35.4 us)
Async XLA Ops:
  7.2 49.4 %all-gather.4.cloned.1.call-start = ((), (), s32[]{:S(2)}) async-start(), calls=%async_computation.3 | async-start | bytes 1327104 | tf_op jit(solution)/shard_map/all_gather | solution.py:465
  7.9 95.6 %all-gather.6.cloned.1.call-start = ((), (), s32[]{:S(2)}) async-start(), calls=%async_computation.4 | async-start | bytes 2654208 | tf_op jit(solution)/shard_map/all_gather | solution.py:510
  9.5 17.4 %collective-permute-start.3 = (bf16[64,1024]{1,0:T(8,128)(2,1)}, bf16[64,1024]{1,0:T(8,128)(2,1)S(1)}, u32[]{:S(2)}, u32[]{:S(2)}) collective-permute-start(bf16[64,1024]{1,0:T(8,128)(2,1)} %join.1.own_ref), channel_id=1, source_target_pairs={{0,1},{1,2},{2,3},{3,4},{4,5},{5,6},{6,7},{7,8},{8,9},{9,10},{10,1... | collective-permute-start | bytes 393224 | tf_op jit(solution)/shard_map/ppermute | solution.py:28
  11.4 15.4 %collective-permute-start.2 = (bf16[64,1024]{1,0:T(8,128)(2,1)}, bf16[64,1024]{1,0:T(8,128)(2,1)S(1)}, u32[]{:S(2)}, u32[]{:S(2)}) collective-permute-start(bf16[64,1024]{1,0:T(8,128)(2,1)} %join.1.own_ref), channel_id=1, source_target_pairs={{0,2},{1,3},{2,4},{3,5},{4,6},{5,7},{6,8},{7,9},{8,10},{9,11},{10,... | collective-permute-start | bytes 393224 | tf_op jit(solution)/shard_map/ppermute | solution.py:28
  14.8 12.1 %collective-permute-start.1 = (bf16[64,1024]{1,0:T(8,128)(2,1)}, bf16[64,1024]{1,0:T(8,128)(2,1)S(1)}, u32[]{:S(2)}, u32[]{:S(2)}) collective-permute-start(bf16[64,1024]{1,0:T(8,128)(2,1)} %join.1.own_ref), channel_id=1, source_target_pairs={{0,3},{1,4},{2,5},{3,6},{4,7},{5,8},{6,9},{7,10},{8,11},{9,12},{10... | collective-permute-start | bytes 393224 | tf_op jit(solution)/shard_map/ppermute | solution.py:28
  19.1 8.0 %collective-permute-start = (bf16[64,1024]{1,0:T(8,128)(2,1)}, bf16[64,1024]{1,0:T(8,128)(2,1)S(1)}, u32[]{:S(2)}, u32[]{:S(2)}) collective-permute-start(bf16[64,1024]{1,0:T(8,128)(2,1)} %join.1.own_ref), channel_id=1, source_target_pairs={{0,4},{1,5},{2,6},{3,7},{4,8},{5,9},{6,10},{7,11},{8,12},{9,13},{1... | collective-permute-start | bytes 393224 | tf_op jit(solution)/shard_map/ppermute | solution.py:28
  31.6 19.9 %collective-permute-start.4 = (bf16[64,2048]{1,0:T(8,128)(2,1)}, bf16[64,2048]{1,0:T(8,128)(2,1)S(1)}, u32[]{:S(2)}, u32[]{:S(2)}) collective-permute-start(bf16[64,2048]{1,0:T(8,128)(2,1)} %get-tuple-element.52), channel_id=1, source_target_pairs={{0,8},{1,9},{2,10},{3,11},{4,12},{5,13},{6,14},{7,15},{8,16},{9,17... | collective-permute-start | bytes 786440 | tf_op jit(solution)/shard_map/ppermute | solution.py:481
  33.2 21.8 %collective-permute-start.5 = (bf16[64,2048]{1,0:T(8,128)(2,1)}, bf16[64,2048]{1,0:T(8,128)(2,1)S(1)}, u32[]{:S(2)}, u32[]{:S(2)}) collective-permute-start(bf16[64,2048]{1,0:T(8,128)(2,1)} %get-tuple-element.53), channel_id=1, source_target_pairs={{0,16},{1,17},{2,18},{3,19},{4,20},{5,21},{6,22},{7,23},{8,24},{9,... | collective-permute-start | bytes 786440 | tf_op jit(solution)/shard_map/ppermute | solution.py:481
  34.3 22.2 %collective-permute-start.6 = (bf16[64,2048]{1,0:T(8,128)(2,1)}, bf16[64,2048]{1,0:T(8,128)(2,1)S(1)}, u32[]{:S(2)}, u32[]{:S(2)}) collective-permute-start(bf16[64,2048]{1,0:T(8,128)(2,1)} %get-tuple-element.54), channel_id=1, source_target_pairs={{0,24},{1,25},{2,26},{3,27},{4,28},{5,29},{6,30},{7,31},{8,0},{9,1... | collective-permute-start | bytes 786440 | tf_op jit(solution)/shard_map/ppermute | solution.py:481
  59.4 21.3 %all-to-all-start = ((bf16[4,256,384]{2,1,0:T(8,128)(2,1)}), bf16[4,256,384]{2,1,0:T(8,128)(2,1)S(1)}, u32[]{:S(2)}, u32[]{:S(2)}) async-start(bf16[4,256,384]{2,1,0:T(8,128)(2,1)} %get-tuple-element.59), calls=%async_computation | async-start | bytes 1572864 | tf_op jit(solution)/shard_map/all_to_all | solution.py:451
  65.9 9.8 %collective-permute-start.12 = (bf16[4,32,4,128]{3,2,1,0:T(4,128)(2,1)S(1)}, bf16[4,32,4,128]{3,2,1,0:T(4,128)(2,1)S(1)}, u32[]{:S(2)}, u32[]{:S(2)}) collective-permute-start(bf16[4,32,4,128]{3,2,1,0:T(4,128)(2,1)S(1)} %get-tuple-element.93), channel_id=1, source_target_pairs={{0,6},{1,7},{2,0},{3,1},{4,2},{5,3},{6,4},{7,5},{8,14},{9,15},{10,... | collective-permute-start | bytes 393224 | tf_op jit(solution)/shard_map/ppermute | solution.py:530
  67.1 15.7 %collective-permute-start.11 = (bf16[4,32,4,128]{3,2,1,0:T(4,128)(2,1)S(1)}, bf16[4,32,4,128]{3,2,1,0:T(4,128)(2,1)S(1)}, u32[]{:S(2)}, u32[]{:S(2)}) collective-permute-start(bf16[4,32,4,128]{3,2,1,0:T(4,128)(2,1)S(1)} %get-tuple-element.94), channel_id=1, source_target_pairs={{0,5},{1,6},{2,7},{3,0},{4,1},{5,2},{6,3},{7,4},{8,13},{9,14},{10,... | collective-permute-start | bytes 393224 | tf_op jit(solution)/shard_map/ppermute | solution.py:530
  68.9 13.9 %collective-permute-start.10 = (bf16[4,32,4,128]{3,2,1,0:T(4,128)(2,1)S(1)}, bf16[4,32,4,128]{3,2,1,0:T(4,128)(2,1)S(1)}, u32[]{:S(2)}, u32[]{:S(2)}) collective-permute-start(bf16[4,32,4,128]{3,2,1,0:T(4,128)(2,1)S(1)} %get-tuple-element.95), channel_id=1, source_target_pairs={{0,4},{1,5},{2,6},{3,7},{4,0},{5,1},{6,2},{7,3},{8,12},{9,13},{10,... | collective-permute-start | bytes 393224 | tf_op jit(solution)/shard_map/ppermute | solution.py:530
  69.1 13.8 %collective-permute-start.9 = (bf16[4,32,4,128]{3,2,1,0:T(4,128)(2,1)S(1)}, bf16[4,32,4,128]{3,2,1,0:T(4,128)(2,1)S(1)}, u32[]{:S(2)}, u32[]{:S(2)}) collective-permute-start(bf16[4,32,4,128]{3,2,1,0:T(4,128)(2,1)S(1)} %get-tuple-element.96), channel_id=1, source_target_pairs={{0,3},{1,4},{2,5},{3,6},{4,7},{5,0},{6,1},{7,2},{8,11},{9,12},{10,... | collective-permute-start | bytes 393224 | tf_op jit(solution)/shard_map/ppermute | solution.py:530
  71.5 11.4 %collective-permute-start.8 = (bf16[4,32,4,128]{3,2,1,0:T(4,128)(2,1)S(1)}, bf16[4,32,4,128]{3,2,1,0:T(4,128)(2,1)S(1)}, u32[]{:S(2)}, u32[]{:S(2)}) collective-permute-start(bf16[4,32,4,128]{3,2,1,0:T(4,128)(2,1)S(1)} %get-tuple-element.97), channel_id=1, source_target_pairs={{0,2},{1,3},{2,4},{3,5},{4,6},{5,7},{6,0},{7,1},{8,10},{9,11},{10,... | collective-permute-start | bytes 393224 | tf_op jit(solution)/shard_map/ppermute | solution.py:530
  75.7 7.2 %collective-permute-start.7 = (bf16[4,32,4,128]{3,2,1,0:T(4,128)(2,1)S(1)}, bf16[4,32,4,128]{3,2,1,0:T(4,128)(2,1)S(1)}, u32[]{:S(2)}, u32[]{:S(2)}) collective-permute-start(bf16[4,32,4,128]{3,2,1,0:T(4,128)(2,1)S(1)} %get-tuple-element.98), channel_id=1, source_target_pairs={{0,1},{1,2},{2,3},{3,4},{4,5},{5,6},{6,7},{7,0},{8,9},{9,10},{10,1... | collective-permute-start | bytes 393224 | tf_op jit(solution)/shard_map/ppermute | solution.py:530
  83.7 33.3 %all-to-all-start.1 = ((bf16[8,96,1536]{2,1,0:T(8,128)(2,1)}), bf16[8,96,1536]{2,1,0:T(8,128)(2,1)S(1)}, u32[]{:S(2)}, u32[]{:S(2)}) async-start(bf16[8,96,1536]{2,1,0:T(8,128)(2,1)} %pick.1), calls=%async_computation.1 | async-start | bytes 4718592 | tf_op jit(solution)/shard_map/all_to_all | solution.py:451
  91.9 31.0 %collective-permute-start.14 = (bf16[8,32,4,128]{3,2,1,0:T(4,128)(2,1)}, bf16[8,32,4,128]{3,2,1,0:T(4,128)(2,1)}, u32[]{:S(2)}, u32[]{:S(2)}) collective-permute-start(bf16[8,32,4,128]{3,2,1,0:T(4,128)(2,1)} %get-tuple-element.79), channel_id=1, source_target_pairs={{0,8},{1,9},{2,10},{3,11},{4,12},{5,13},{6,14},{7,15},{8,16},{9,17... | collective-permute-start | bytes 786440 | tf_op jit(solution)/shard_map/ppermute | solution.py:588
  92.7 30.1 %collective-permute-start.15 = (bf16[8,32,4,128]{3,2,1,0:T(4,128)(2,1)}, bf16[8,32,4,128]{3,2,1,0:T(4,128)(2,1)}, u32[]{:S(2)}, u32[]{:S(2)}) collective-permute-start(bf16[8,32,4,128]{3,2,1,0:T(4,128)(2,1)} %get-tuple-element.80), channel_id=1, source_target_pairs={{0,16},{1,17},{2,18},{3,19},{4,20},{5,21},{6,22},{7,23},{8,24},{9,... | collective-permute-start | bytes 786440 | tf_op jit(solution)/shard_map/ppermute | solution.py:588
  96.9 26.0 %collective-permute-start.16 = (bf16[8,32,4,128]{3,2,1,0:T(4,128)(2,1)S(1)}, bf16[8,32,4,128]{3,2,1,0:T(4,128)(2,1)}, u32[]{:S(2)}, u32[]{:S(2)}) collective-permute-start(bf16[8,32,4,128]{3,2,1,0:T(4,128)(2,1)S(1)} %get-tuple-element.81), channel_id=1, source_target_pairs={{0,24},{1,25},{2,26},{3,27},{4,28},{5,29},{6,30},{7,31},{8,0},{9,1... | collective-permute-start | bytes 786440 | tf_op jit(solution)/shard_map/ppermute | solution.py:588
  122.9 33.0 %all-to-all-start.2 = ((bf16[8,96,1536]{2,1,0:T(8,128)(2,1)}), bf16[8,96,1536]{2,1,0:T(8,128)(2,1)S(1)}, u32[]{:S(2)}, u32[]{:S(2)}) async-start(bf16[8,96,1536]{2,1,0:T(8,128)(2,1)} %experts.1), calls=%async_computation.2 | async-start | bytes 4718592 | tf_op jit(solution)/shard_map/all_to_all | solution.py:451
  158.1 9.0 %collective-permute-start.17 = (bf16[64,1536]{1,0:T(8,128)(2,1)S(1)}, bf16[64,1536]{1,0:T(8,128)(2,1)S(1)}, u32[]{:S(2)}, u32[]{:S(2)}) collective-permute-start(bf16[64,1536]{1,0:T(8,128)(2,1)S(1)} %get-tuple-element.85), channel_id=1, source_target_pairs={{0,8},{1,9},{2,10},{3,11},{4,12},{5,13},{6,14},{7,15},{8,16},{9,17... | collective-permute-start | bytes 589832 | tf_op jit(solution)/shard_map/ppermute | solution.py:481
  159.0 17.0 %collective-permute-start.18 = (bf16[64,1536]{1,0:T(8,128)(2,1)S(1)}, bf16[64,1536]{1,0:T(8,128)(2,1)S(1)}, u32[]{:S(2)}, u32[]{:S(2)}) collective-permute-start(bf16[64,1536]{1,0:T(8,128)(2,1)S(1)} %get-tuple-element.86), channel_id=1, source_target_pairs={{0,16},{1,17},{2,18},{3,19},{4,20},{5,21},{6,22},{7,23},{8,24},{9,... | collective-permute-start | bytes 589832 | tf_op jit(solution)/shard_map/ppermute | solution.py:481
  163.2 16.7 %collective-permute-start.19 = (bf16[64,1536]{1,0:T(8,128)(2,1)S(1)}, bf16[64,1536]{1,0:T(8,128)(2,1)S(1)}, u32[]{:S(2)}, u32[]{:S(2)}) collective-permute-start(bf16[64,1536]{1,0:T(8,128)(2,1)S(1)} %get-tuple-element.87), channel_id=1, source_target_pairs={{0,24},{1,25},{2,26},{3,27},{4,28},{5,29},{6,30},{7,31},{8,0},{9,1... | collective-permute-start | bytes 589832 | tf_op jit(solution)/shard_map/ppermute | solution.py:481
  (20 other events, 131.5 us)
Sparse Core Ops, SparseCore 0:
  9.9 30.5 all-gather.3
  42.4 29.0 all-gather.5

commit v8 on v7

--- a/solution.py
+++ b/solution.py
@@ -201,16 +201,19 @@
     hidden = jnp.where((key_pos >= start) & (key_pos <= query_pos), 0.0, NEGATIVE)
     hidden = jnp.concatenate([hidden] * group, axis=0)
     scale = 1.0 / math.sqrt(HD)
-    for step, out_ref in enumerate(out_refs):
-        z = lax.rem(z_ref[0] + step, Z_SIZE)
+    for flip in range(Z_SIZE):
+        z = lax.bitwise_xor(z_ref[0], flip)
+        out_ref = out_refs[min(flip, 2)]
+        first_column = width if flip < 3 else width + part + HD
         for column in range(Z_SIZE):
 
             @pl.when(z == column)
-            def _(column=column, out_ref=out_ref):
+            def _(column=column, out_ref=out_ref, first_column=first_column):
                 columns = slice(column * part, (column + 1) * part)
-                out_ref[:, width : width + part] = residual_ref[:, columns]
-
-        out_ref[:, width + part :] = info_ref[...]
+                out_ref[:, first_column : first_column + part] = residual_ref[:, columns]
+
+    for out_ref in out_refs:
+        out_ref[:, width + part : width + part + HD] = info_ref[...]
     for kv in range(kv_heads):
         at = slice(kv * HD, (kv + 1) * HD)
         value_at = slice(kv_width + kv * HD, kv_width + (kv + 1) * HD)
@@ -267,17 +270,19 @@
             out[at] = piece[z]
 
 
-def source_z(z_ref, step):
-    return lax.rem(z_ref[0] + Z_SIZE - step, Z_SIZE)
-
-
 def project_kernel(z_ref, *refs):
     sent = refs[:Z_SIZE]
     weight_ref, mixed_ref, info_ref, rows_ref = refs[Z_SIZE:]
-    for step, sent_ref in enumerate(sent):
-        rows_ref[source_z(z_ref, step)] = sent_ref[...]
+    part, width = weight_ref.shape
+    for flip, sent_ref in enumerate(sent):
+        z = lax.bitwise_xor(z_ref[0], flip)
+        if flip < 3:
+            rows_ref[z] = sent_ref[:, : rows_ref.shape[2]]
+        else:
+            rows_ref[z, :, :width] = sent_ref[:, :width]
+            rows_ref[z, :, width : width + part] = sent_ref[:, width + part + HD :]
+            rows_ref[z, :, width + part :] = sent_ref[:, width + part : width + part + HD]
     rows = jnp.concatenate([rows_ref[z] for z in range(Z_SIZE)], axis=0)
-    part, width = weight_ref.shape
     out = dot_rows(rows[:, :width], weight_ref[...])
     mixed = (out + rows[:, width : width + part].astype(jnp.float32)).astype(jnp.bfloat16)
     for z in range(Z_SIZE):
@@ -498,9 +503,13 @@
     sent_width = width + part + info.shape[1]
     sent = pl.pallas_call(
         attention_kernel,
-        out_shape=[pltpu.HBM((tokens, sent_width), bf16)] * Z_SIZE,
+        out_shape=[
+            pltpu.HBM((tokens, sent_width), bf16),
+            pltpu.HBM((tokens, sent_width), bf16),
+            pltpu.HBM((tokens, sent_width + part), bf16),
+        ],
         in_specs=[SMEM] * 3 + [VMEM] * 8,
-        out_specs=[VMEM] * Z_SIZE,
+        out_specs=[VMEM] * 3,
         compiler_params=params(58),
         cost_estimate=cost(4 * tokens * 5 * tokens * width, 3 * MIB),
         name="attention",
@@ -508,7 +517,14 @@
 
     sent, own_shared = lax.optimization_barrier((sent, own_shared))
     shared_weight = lax.all_gather(own_shared, "seq", axis=0, axis_index_groups=planes)
-    gathered = along_z(sent)
+    z_swaps = [
+        [(z * PLANE + p, (z ^ flip) * PLANE + p) for z in range(Z_SIZE) for p in range(PLANE)]
+        for flip in range(Z_SIZE)
+    ]
+    far = lax.ppermute(sent[2], "seq", z_swaps[2])
+    near = lax.ppermute(sent[1], "seq", z_swaps[1])
+    passed_on = lax.ppermute(far, "seq", z_swaps[1])
+    gathered = [sent[0], near, far, passed_on]
     gathered, cache_blocks, expert_gate_up = lax.optimization_barrier(
         (gathered, cache_blocks, expert_gate_up)
     )

time: 188 us -> 195 us (1.037)
  waiting for transfers between devices: 78 us -> 82.3 us
  starting transfers between devices: 50.1 us -> 52.6 us
    ppermute x0 -> x3, waiting for transfers between devices: none -> 25.8 us  [the longest x1 13 us: shards(): far = lax.ppermute(sent[2], 'seq', z_swaps[2])]
    ppermute x6 -> x3, waiting for transfers between devices: 33.6 us -> 13 us  [along_z(): lax.ppermute(arrays[step], 'seq', z_pairs[step])]
    ppermute x0 -> x3, starting transfers between devices: none -> 4.17 us  [the longest x1 2.14 us: shards(): far = lax.ppermute(sent[2], 'seq', z_swaps[2])]
    ppermute x6 -> x3, starting transfers between devices: 9.52 us -> 5.69 us  [along_z(): lax.ppermute(arrays[step], 'seq', z_pairs[step])]
  transfers between devices with their start and end apart: 25 -> 25, of which waited for: 10 -> 9; matrix products, arithmetic and copies ran while one was open for 6% -> 6% of each run, Pallas kernels for 14% -> 13%
where the time goes in v8:
time: 195 us; the launch traced here: 194 us
  waiting for transfers between devices  82.3 us (42%)
  starting transfers between devices  52.6 us (27%)
  Pallas kernels  28.5 us (15%)
  between operations  14.3 us (7%)
  local copies, waits for them, and re-layouts  12.9 us (7%)
  other arithmetic  3.57 us (2%)
    all_to_all x3, waiting for transfers between devices, exchange(): lax.all_to_all(array, 'seq', split_axis=0, concat_axis=0, tiled=True, axi...  39.2 us
    all_to_all x3, starting transfers between devices, exchange(): lax.all_to_all(array, 'seq', split_axis=0, concat_axis=0, tiled=True, axi...  16.6 us
    ppermute x4, starting transfers between devices, from_behind(): return lax.ppermute(shard, axis, pairs)  13.1 us
    ppermute x3, waiting for transfers between devices, along_z(): lax.ppermute(arrays[step], 'seq', z_pairs[step])  13 us
    ppermute x1, waiting for transfers between devices, shards(): far = lax.ppermute(sent[2], 'seq', z_swaps[2])  13 us
    ppermute x1, waiting for transfers between devices, shards(): near = lax.ppermute(sent[1], 'seq', z_swaps[1])  12.9 us
    ppermute x7, starting transfers between devices, shards(): piece = lax.ppermute(piece, 'seq', pairs)  7.38 us
    optimization_barrier x1, local copies, waits for them, and re-layouts, shards(): lax.optimization_barrier((gathered, cache_blocks, expert_gate_up))  6.32 us
  transfers between devices with their start and end apart: 25, of which 9 were waited for; matrix products, arithmetic and copies ran while one was open for 6% of the time, Pallas kernels for 13%

profile of v8, /device:TPU:10, one launch (start us, length us, event | category | flops | bytes accessed | tf_op | source)
XLA Modules:
  0.0 194.2 jit_solution(17320271636924307935)
XLA Ops:
  11.4 3.4 %collective-permute-start.2 = (bf16[64,1024]{1,0:T(8,128)(2,1)}, bf16[64,1024]{1,0:T(8,128)(2,1)S(1)}, u32[]{:S(2)}, u32[]{:S(2)}) collective-permute-start(bf16[64,1024]{1,0:T(8,128)(2,1)} %join.1.own_ref), channel_id=1, source_target_pairs={{0,2},{1,3},{2,4},{3,5},{4,6},{5,7},{6,8},{7,9},{8,10},{9,11},{10,... | collective-permute-start | bytes 393224 | tf_op jit(solution)/shard_map/ppermute | solution.py:28
  14.8 4.3 %collective-permute-start.1 = (bf16[64,1024]{1,0:T(8,128)(2,1)}, bf16[64,1024]{1,0:T(8,128)(2,1)S(1)}, u32[]{:S(2)}, u32[]{:S(2)}) collective-permute-start(bf16[64,1024]{1,0:T(8,128)(2,1)} %join.1.own_ref), channel_id=1, source_target_pairs={{0,3},{1,4},{2,5},{3,6},{4,7},{5,8},{6,9},{7,10},{8,11},{9,12},{10... | collective-permute-start | bytes 393224 | tf_op jit(solution)/shard_map/ppermute | solution.py:28
  19.1 3.4 %collective-permute-start = (bf16[64,1024]{1,0:T(8,128)(2,1)}, bf16[64,1024]{1,0:T(8,128)(2,1)S(1)}, u32[]{:S(2)}, u32[]{:S(2)}) collective-permute-start(bf16[64,1024]{1,0:T(8,128)(2,1)} %join.1.own_ref), channel_id=1, source_target_pairs={{0,4},{1,5},{2,6},{3,7},{4,8},{5,9},{6,10},{7,11},{8,12},{9,13},{1... | collective-permute-start | bytes 393224 | tf_op jit(solution)/shard_map/ppermute | solution.py:28
  22.6 2.6 %route.1.info_ref = bf16[64,128]{1,0:T(8,128)(2,1)} custom-call(s32[1]{0:T(128)} %bitcast.z_ref, s32[6,64]{1,0:T(8,128)} %bitcast.56, f32[6,64]{1,0:T(8,128)} %bitcast.57), custom_call_target="tpu_custom_call" | custom-call | flops 1048576 | bytes 1048576 | tf_op jit(solution)/shard_map/route/pallas_call | solution.py:473
  27.8 3.6 %attention.1 = (bf16[64,2048]{1,0:T(8,128)(2,1)}, bf16[64,2048]{1,0:T(8,128)(2,1)}, bf16[64,2432]{1,0:T(8,128)(2,1)}) custom-call(s32[1]{0:T(128)} %bitcast.z_ref, s32[1]{0:T(128)} %bitcast.1.first_ref, s32[16]{0:T(128)} %lengths_ref.1, bf16[64,1536]{1,0:T(8,128)(2,1)} %q_ref.1, bf16[64,1024]{1,0:T(8,128)(2,1)} %copy-done.10, bf16[64,1024]{1,0:T(8,128)(2,1)} %copy-done.9, ...), custom_call_target="tpu_custom_call" | custom-call | flops 125829120 | bytes 3145728 | tf_op jit(solution)/shard_map/attention/pallas_call | solution.py:504
  31.4 2.1 %collective-permute-start.5 = (bf16[64,2432]{1,0:T(8,128)(2,1)}, bf16[64,2432]{1,0:T(8,128)(2,1)S(1)}, u32[]{:S(2)}, u32[]{:S(2)}) collective-permute-start(bf16[64,2432]{1,0:T(8,128)(2,1)} %get-tuple-element.50), channel_id=1, source_target_pairs={{0,16},{1,17},{2,18},{3,19},{4,20},{5,21},{6,22},{7,23},{8,24},{9,... | collective-permute-start | bytes 933896 | tf_op jit(solution)/shard_map/ppermute | solution.py:524
  33.6 13.0 %collective-permute-done.5.refs_2_ = bf16[64,2432]{1,0:T(8,128)(2,1)S(1)} collective-permute-done((bf16[64,2432]{1,0:T(8,128)(2,1)}, bf16[64,2432]{1,0:T(8,128)(2,1)S(1)}, u32[]{:S(2)}, u32[]{:S(2)}) %collective-permute-start.5) | collective-permute-done | bytes 311328 | tf_op jit(solution)/shard_map/ppermute | solution.py:524
  48.6 12.9 %collective-permute-done.4.refs_1_ = bf16[64,2048]{1,0:T(8,128)(2,1)S(1)} collective-permute-done((bf16[64,2048]{1,0:T(8,128)(2,1)}, bf16[64,2048]{1,0:T(8,128)(2,1)S(1)}, u32[]{:S(2)}, u32[]{:S(2)}) %collective-permute-start.4) | collective-permute-done | bytes 262176 | tf_op jit(solution)/shard_map/ppermute | solution.py:525
  61.4 2.9 %project.1 = (bf16[4,256,384]{2,1,0:T(8,128)(2,1)}, bf16[256,128]{1,0:T(8,128)(2,1)S(1)}) custom-call(s32[1]{0:T(128)} %bitcast.z_ref, bf16[64,2048]{1,0:T(8,128)(2,1)} %get-tuple-element.51.refs_0_, bf16[64,2048]{1,0:T(8,128)(2,1)S(1)} %collective-permute-done.4.refs_1_, bf16[64,2432]{1,0:T(8,128)(2,1)S(1)} %collective-permute-done.5.refs_2_, ...), custom_call_target="tpu_custom_call" | custom-call | flops 301989888 | bytes 3145728 | tf_op jit(solution)/shard_map/project/pallas_call | solution.py:550
  64.3 6.1 %all-to-all-start = ((bf16[4,256,384]{2,1,0:T(8,128)(2,1)}), bf16[4,256,384]{2,1,0:T(8,128)(2,1)S(1)}, u32[]{:S(2)}, u32[]{:S(2)}) async-start(bf16[4,256,384]{2,1,0:T(8,128)(2,1)} %get-tuple-element.55), calls=%async_computation | async-start | bytes 1572864 | tf_op jit(solution)/shard_map/all_to_all | solution.py:456
  75.7 2.4 %collective-permute-start.9 = (bf16[4,32,4,128]{3,2,1,0:T(4,128)(2,1)S(1)}, bf16[4,32,4,128]{3,2,1,0:T(4,128)(2,1)S(1)}, u32[]{:S(2)}, u32[]{:S(2)}) collective-permute-start(bf16[4,32,4,128]{3,2,1,0:T(4,128)(2,1)S(1)} %get-tuple-element.92), channel_id=1, source_target_pairs={{0,3},{1,4},{2,5},{3,6},{4,7},{5,0},{6,1},{7,2},{8,11},{9,12},{10,... | collective-permute-start | bytes 393224 | tf_op jit(solution)/shard_map/ppermute | solution.py:546
  79.0 3.3 %collective-permute-done.12.refs_6_ = bf16[4,32,4,128]{3,2,1,0:T(4,128)(2,1)S(1)} collective-permute-done((bf16[4,32,4,128]{3,2,1,0:T(4,128)(2,1)S(1)}, bf16[4,32,4,128]{3,2,1,0:T(4,128)(2,1)S(1)}, u32[]{:S(2)}, u32[]{:S(2)}) %collective-permute-start.12) | collective-permute-done | bytes 131104 | tf_op jit(solution)/shard_map/ppermute | solution.py:546
  89.7 5.4 %all-to-all-start.1 = ((bf16[8,96,1536]{2,1,0:T(8,128)(2,1)}), bf16[8,96,1536]{2,1,0:T(8,128)(2,1)S(1)}, u32[]{:S(2)}, u32[]{:S(2)}) async-start(bf16[8,96,1536]{2,1,0:T(8,128)(2,1)} %pick.1), calls=%async_computation.1 | async-start | bytes 4718592 | tf_op jit(solution)/shard_map/all_to_all | solution.py:456
  95.1 2.1 %regroup.1 = (bf16[8,32,4,128]{3,2,1,0:T(4,128)(2,1)S(1)}, bf16[8,32,4,128]{3,2,1,0:T(4,128)(2,1)}, bf16[8,32,4,128]{3,2,1,0:T(4,128)(2,1)}, bf16[8,32,4,128]{3,2,1,0:T(4,128)(2,1)S(1)}) custom-call(s32[1]{0:T(128)} %bitcast.z_ref, bf16[4,32,4,128]{3,2,1,0:T(4,128)(2,1)} %get-tuple-element.66.refs_0_, bf16[4,32,4,128]{3,2,1,0:T(4,128)(2,1)} %copy-done.17, ...), custom_call_target="tpu_custom_call" | custom-call | bytes 2097152 | tf_op jit(solution)/shard_map/regroup/pallas_call | solution.py:593
  99.4 4.2 %collective-permute-start.15 = (bf16[8,32,4,128]{3,2,1,0:T(4,128)(2,1)}, bf16[8,32,4,128]{3,2,1,0:T(4,128)(2,1)}, u32[]{:S(2)}, u32[]{:S(2)}) collective-permute-start(bf16[8,32,4,128]{3,2,1,0:T(4,128)(2,1)} %get-tuple-element.76), channel_id=1, source_target_pairs={{0,16},{1,17},{2,18},{3,19},{4,20},{5,21},{6,22},{7,23},{8,24},{9,... | collective-permute-start | bytes 786440 | tf_op jit(solution)/shard_map/ppermute | solution.py:604
  103.6 6.3 %copy.35 = bf16[4,1536,2,256]{3,1,2,0:T(8,128)(2,1)} copy(bf16[4,1536,2,256]{3,2,1,0:T(2,128)(2,1)} %param.26) | data formatting | bytes 12582912 | tf_op jit(solution)/shard_map/optimization_barrier | solution.py:528
  109.9 13.1 %all-to-all-done.1.rows_ref = bf16[8,96,1536]{2,1,0:T(8,128)(2,1)S(1)} async-done(((bf16[8,96,1536]{2,1,0:T(8,128)(2,1)}), bf16[8,96,1536]{2,1,0:T(8,128)(2,1)S(1)}, u32[]{:S(2)}, u32[]{:S(2)}) %all-to-all-start.1) | async-done | bytes 2359328 | tf_op jit(solution)/shard_map/all_to_all | solution.py:456
  123.1 5.9 %experts.1 = bf16[8,96,1536]{2,1,0:T(8,128)(2,1)} custom-call(bf16[8,96,1536]{2,1,0:T(8,128)(2,1)S(1)} %all-to-all-done.1.rows_ref, bf16[4,2,1536,256]{3,2,1,0:T(8,128)(2,1)} %bitcast.51, bf16[4,256,1536]{2,1,0:T(8,128)(2,1)} %down_hbm.1), custom_call_target="tpu_custom_call" | custom-call | flops 1811939328 | bytes 14680064 | tf_op jit(solution)/shard_map/experts/pallas_call | solution.py:617
  129.0 5.0 %all-to-all-start.2 = ((bf16[8,96,1536]{2,1,0:T(8,128)(2,1)}), bf16[8,96,1536]{2,1,0:T(8,128)(2,1)S(1)}, u32[]{:S(2)}, u32[]{:S(2)}) async-start(bf16[8,96,1536]{2,1,0:T(8,128)(2,1)} %experts.1), calls=%async_computation.2 | async-start | bytes 4718592 | tf_op jit(solution)/shard_map/all_to_all | solution.py:456
  137.6 24.4 %all-to-all-done.2 = bf16[8,96,1536]{2,1,0:T(8,128)(2,1)S(1)} async-done(((bf16[8,96,1536]{2,1,0:T(8,128)(2,1)}), bf16[8,96,1536]{2,1,0:T(8,128)(2,1)S(1)}, u32[]{:S(2)}, u32[]{:S(2)}) %all-to-all-start.2) | async-done | bytes 2359328 | tf_op jit(solution)/shard_map/all_to_all | solution.py:456
  162.0 2.2 %combine.1 = (bf16[64,1536]{1,0:T(8,128)(2,1)S(1)}, bf16[64,1536]{1,0:T(8,128)(2,1)S(1)}, bf16[64,1536]{1,0:T(8,128)(2,1)S(1)}, bf16[64,1536]{1,0:T(8,128)(2,1)S(1)}) custom-call(s32[1]{0:T(128)} %bitcast.z_ref, bf16[256,768]{1,0:T(8,128)(2,1)} %copy-done.2, bf16[768,1536]{1,0:T(8,128)(2,1)S(1)} %bitcast.49, bf16[256,1536]{1,0:T(8,128)(2,1)} %copy-done.1), custom_call_target="tpu_custom_call" | custom-call | flops 603979776 | bytes 3145728 | tf_op jit(solution)/shard_map/combine/pallas_call | solution.py:648
  165.7 4.2 %collective-permute-start.18 = (bf16[64,1536]{1,0:T(8,128)(2,1)S(1)}, bf16[64,1536]{1,0:T(8,128)(2,1)S(1)}, u32[]{:S(2)}, u32[]{:S(2)}) collective-permute-start(bf16[64,1536]{1,0:T(8,128)(2,1)S(1)} %get-tuple-element.82), channel_id=1, source_target_pairs={{0,16},{1,17},{2,18},{3,19},{4,20},{5,21},{6,22},{7,23},{8,24},{9,... | collective-permute-start | bytes 589832 | tf_op jit(solution)/shard_map/ppermute | solution.py:486
  173.5 9.2 %collective-permute-done.18.refs_2_ = bf16[64,1536]{1,0:T(8,128)(2,1)S(1)} collective-permute-done((bf16[64,1536]{1,0:T(8,128)(2,1)S(1)}, bf16[64,1536]{1,0:T(8,128)(2,1)S(1)}, u32[]{:S(2)}, u32[]{:S(2)}) %collective-permute-start.18) | collective-permute-done | bytes 196640 | tf_op jit(solution)/shard_map/ppermute | solution.py:486
  182.7 3.9 %collective-permute-done.19.refs_3_ = bf16[64,1536]{1,0:T(8,128)(2,1)S(1)} collective-permute-done((bf16[64,1536]{1,0:T(8,128)(2,1)S(1)}, bf16[64,1536]{1,0:T(8,128)(2,1)S(1)}, u32[]{:S(2)}, u32[]{:S(2)}) %collective-permute-start.19) | collective-permute-done | bytes 196640 | tf_op jit(solution)/shard_map/ppermute | solution.py:486
  (83 shorter events, 34.0 us)
Async XLA Ops:
  7.2 54.3 %all-gather.4.cloned.1.call-start = ((), (), s32[]{:S(2)}) async-start(), calls=%async_computation.3 | async-start | bytes 1327104 | tf_op jit(solution)/shard_map/all_gather | solution.py:470
  7.9 102.0 %all-gather.6.cloned.1.call-start = ((), (), s32[]{:S(2)}) async-start(), calls=%async_computation.4 | async-start | bytes 2654208 | tf_op jit(solution)/shard_map/all_gather | solution.py:519
  9.5 17.4 %collective-permute-start.3 = (bf16[64,1024]{1,0:T(8,128)(2,1)}, bf16[64,1024]{1,0:T(8,128)(2,1)S(1)}, u32[]{:S(2)}, u32[]{:S(2)}) collective-permute-start(bf16[64,1024]{1,0:T(8,128)(2,1)} %join.1.own_ref), channel_id=1, source_target_pairs={{0,1},{1,2},{2,3},{3,4},{4,5},{5,6},{6,7},{7,8},{8,9},{9,10},{10,1... | collective-permute-start | bytes 393224 | tf_op jit(solution)/shard_map/ppermute | solution.py:28
  11.4 15.4 %collective-permute-start.2 = (bf16[64,1024]{1,0:T(8,128)(2,1)}, bf16[64,1024]{1,0:T(8,128)(2,1)S(1)}, u32[]{:S(2)}, u32[]{:S(2)}) collective-permute-start(bf16[64,1024]{1,0:T(8,128)(2,1)} %join.1.own_ref), channel_id=1, source_target_pairs={{0,2},{1,3},{2,4},{3,5},{4,6},{5,7},{6,8},{7,9},{8,10},{9,11},{10,... | collective-permute-start | bytes 393224 | tf_op jit(solution)/shard_map/ppermute | solution.py:28
  14.8 12.1 %collective-permute-start.1 = (bf16[64,1024]{1,0:T(8,128)(2,1)}, bf16[64,1024]{1,0:T(8,128)(2,1)S(1)}, u32[]{:S(2)}, u32[]{:S(2)}) collective-permute-start(bf16[64,1024]{1,0:T(8,128)(2,1)} %join.1.own_ref), channel_id=1, source_target_pairs={{0,3},{1,4},{2,5},{3,6},{4,7},{5,8},{6,9},{7,10},{8,11},{9,12},{10... | collective-permute-start | bytes 393224 | tf_op jit(solution)/shard_map/ppermute | solution.py:28
  19.1 8.0 %collective-permute-start = (bf16[64,1024]{1,0:T(8,128)(2,1)}, bf16[64,1024]{1,0:T(8,128)(2,1)S(1)}, u32[]{:S(2)}, u32[]{:S(2)}) collective-permute-start(bf16[64,1024]{1,0:T(8,128)(2,1)} %join.1.own_ref), channel_id=1, source_target_pairs={{0,4},{1,5},{2,6},{3,7},{4,8},{5,9},{6,10},{7,11},{8,12},{9,13},{1... | collective-permute-start | bytes 393224 | tf_op jit(solution)/shard_map/ppermute | solution.py:28
  31.4 15.1 %collective-permute-start.5 = (bf16[64,2432]{1,0:T(8,128)(2,1)}, bf16[64,2432]{1,0:T(8,128)(2,1)S(1)}, u32[]{:S(2)}, u32[]{:S(2)}) collective-permute-start(bf16[64,2432]{1,0:T(8,128)(2,1)} %get-tuple-element.50), channel_id=1, source_target_pairs={{0,16},{1,17},{2,18},{3,19},{4,20},{5,21},{6,22},{7,23},{8,24},{9,... | collective-permute-start | bytes 933896 | tf_op jit(solution)/shard_map/ppermute | solution.py:524
  46.5 14.9 %collective-permute-start.6 = (bf16[64,2432]{1,0:T(8,128)(2,1)S(1)}, bf16[64,2432]{1,0:T(8,128)(2,1)S(1)}, u32[]{:S(2)}, u32[]{:S(2)}) collective-permute-start(bf16[64,2432]{1,0:T(8,128)(2,1)S(1)} %collective-permute-done.5.refs_2_), channel_id=1, source_target_pairs={{0,8},{1,9},{2,10},{3,11},{4,12},{5,13},{6,14},{7,15},{8,0},{9,1},... | collective-permute-start | bytes 933896 | tf_op jit(solution)/shard_map/ppermute | solution.py:526
  47.8 13.6 %collective-permute-start.4 = (bf16[64,2048]{1,0:T(8,128)(2,1)}, bf16[64,2048]{1,0:T(8,128)(2,1)S(1)}, u32[]{:S(2)}, u32[]{:S(2)}) collective-permute-start(bf16[64,2048]{1,0:T(8,128)(2,1)} %get-tuple-element.49), channel_id=1, source_target_pairs={{0,8},{1,9},{2,10},{3,11},{4,12},{5,13},{6,14},{7,15},{8,0},{9,1},... | collective-permute-start | bytes 786440 | tf_op jit(solution)/shard_map/ppermute | solution.py:525
  64.3 22.4 %all-to-all-start = ((bf16[4,256,384]{2,1,0:T(8,128)(2,1)}), bf16[4,256,384]{2,1,0:T(8,128)(2,1)S(1)}, u32[]{:S(2)}, u32[]{:S(2)}) async-start(bf16[4,256,384]{2,1,0:T(8,128)(2,1)} %get-tuple-element.55), calls=%async_computation | async-start | bytes 1572864 | tf_op jit(solution)/shard_map/all_to_all | solution.py:456
  71.7 10.6 %collective-permute-start.12 = (bf16[4,32,4,128]{3,2,1,0:T(4,128)(2,1)S(1)}, bf16[4,32,4,128]{3,2,1,0:T(4,128)(2,1)S(1)}, u32[]{:S(2)}, u32[]{:S(2)}) collective-permute-start(bf16[4,32,4,128]{3,2,1,0:T(4,128)(2,1)S(1)} %get-tuple-element.89), channel_id=1, source_target_pairs={{0,6},{1,7},{2,0},{3,1},{4,2},{5,3},{6,4},{7,5},{8,14},{9,15},{10,... | collective-permute-start | bytes 393224 | tf_op jit(solution)/shard_map/ppermute | solution.py:546
  73.5 15.3 %collective-permute-start.11 = (bf16[4,32,4,128]{3,2,1,0:T(4,128)(2,1)S(1)}, bf16[4,32,4,128]{3,2,1,0:T(4,128)(2,1)S(1)}, u32[]{:S(2)}, u32[]{:S(2)}) collective-permute-start(bf16[4,32,4,128]{3,2,1,0:T(4,128)(2,1)S(1)} %get-tuple-element.90), channel_id=1, source_target_pairs={{0,5},{1,6},{2,7},{3,0},{4,1},{5,2},{6,3},{7,4},{8,13},{9,14},{10,... | collective-permute-start | bytes 393224 | tf_op jit(solution)/shard_map/ppermute | solution.py:546
  75.5 13.4 %collective-permute-start.10 = (bf16[4,32,4,128]{3,2,1,0:T(4,128)(2,1)S(1)}, bf16[4,32,4,128]{3,2,1,0:T(4,128)(2,1)S(1)}, u32[]{:S(2)}, u32[]{:S(2)}) collective-permute-start(bf16[4,32,4,128]{3,2,1,0:T(4,128)(2,1)S(1)} %get-tuple-element.91), channel_id=1, source_target_pairs={{0,4},{1,5},{2,6},{3,7},{4,0},{5,1},{6,2},{7,3},{8,12},{9,13},{10,... | collective-permute-start | bytes 393224 | tf_op jit(solution)/shard_map/ppermute | solution.py:546
  75.7 13.2 %collective-permute-start.9 = (bf16[4,32,4,128]{3,2,1,0:T(4,128)(2,1)S(1)}, bf16[4,32,4,128]{3,2,1,0:T(4,128)(2,1)S(1)}, u32[]{:S(2)}, u32[]{:S(2)}) collective-permute-start(bf16[4,32,4,128]{3,2,1,0:T(4,128)(2,1)S(1)} %get-tuple-element.92), channel_id=1, source_target_pairs={{0,3},{1,4},{2,5},{3,6},{4,7},{5,0},{6,1},{7,2},{8,11},{9,12},{10,... | collective-permute-start | bytes 393224 | tf_op jit(solution)/shard_map/ppermute | solution.py:546
  78.0 10.9 %collective-permute-start.8 = (bf16[4,32,4,128]{3,2,1,0:T(4,128)(2,1)S(1)}, bf16[4,32,4,128]{3,2,1,0:T(4,128)(2,1)S(1)}, u32[]{:S(2)}, u32[]{:S(2)}) collective-permute-start(bf16[4,32,4,128]{3,2,1,0:T(4,128)(2,1)S(1)} %get-tuple-element.93), channel_id=1, source_target_pairs={{0,2},{1,3},{2,4},{3,5},{4,6},{5,7},{6,0},{7,1},{8,10},{9,11},{10,... | collective-permute-start | bytes 393224 | tf_op jit(solution)/shard_map/ppermute | solution.py:546
  82.3 6.6 %collective-permute-start.7 = (bf16[4,32,4,128]{3,2,1,0:T(4,128)(2,1)S(1)}, bf16[4,32,4,128]{3,2,1,0:T(4,128)(2,1)S(1)}, u32[]{:S(2)}, u32[]{:S(2)}) collective-permute-start(bf16[4,32,4,128]{3,2,1,0:T(4,128)(2,1)S(1)} %get-tuple-element.94), channel_id=1, source_target_pairs={{0,1},{1,2},{2,3},{3,4},{4,5},{5,6},{6,7},{7,0},{8,9},{9,10},{10,1... | collective-permute-start | bytes 393224 | tf_op jit(solution)/shard_map/ppermute | solution.py:546
  89.7 33.3 %all-to-all-start.1 = ((bf16[8,96,1536]{2,1,0:T(8,128)(2,1)}), bf16[8,96,1536]{2,1,0:T(8,128)(2,1)S(1)}, u32[]{:S(2)}, u32[]{:S(2)}) async-start(bf16[8,96,1536]{2,1,0:T(8,128)(2,1)} %pick.1), calls=%async_computation.1 | async-start | bytes 4718592 | tf_op jit(solution)/shard_map/all_to_all | solution.py:456
  98.0 31.0 %collective-permute-start.14 = (bf16[8,32,4,128]{3,2,1,0:T(4,128)(2,1)}, bf16[8,32,4,128]{3,2,1,0:T(4,128)(2,1)}, u32[]{:S(2)}, u32[]{:S(2)}) collective-permute-start(bf16[8,32,4,128]{3,2,1,0:T(4,128)(2,1)} %get-tuple-element.75), channel_id=1, source_target_pairs={{0,8},{1,9},{2,10},{3,11},{4,12},{5,13},{6,14},{7,15},{8,16},{9,17... | collective-permute-start | bytes 786440 | tf_op jit(solution)/shard_map/ppermute | solution.py:604
  99.4 29.5 %collective-permute-start.15 = (bf16[8,32,4,128]{3,2,1,0:T(4,128)(2,1)}, bf16[8,32,4,128]{3,2,1,0:T(4,128)(2,1)}, u32[]{:S(2)}, u32[]{:S(2)}) collective-permute-start(bf16[8,32,4,128]{3,2,1,0:T(4,128)(2,1)} %get-tuple-element.76), channel_id=1, source_target_pairs={{0,16},{1,17},{2,18},{3,19},{4,20},{5,21},{6,22},{7,23},{8,24},{9,... | collective-permute-start | bytes 786440 | tf_op jit(solution)/shard_map/ppermute | solution.py:604
  103.6 25.4 %collective-permute-start.16 = (bf16[8,32,4,128]{3,2,1,0:T(4,128)(2,1)S(1)}, bf16[8,32,4,128]{3,2,1,0:T(4,128)(2,1)}, u32[]{:S(2)}, u32[]{:S(2)}) collective-permute-start(bf16[8,32,4,128]{3,2,1,0:T(4,128)(2,1)S(1)} %get-tuple-element.77), channel_id=1, source_target_pairs={{0,24},{1,25},{2,26},{3,27},{4,28},{5,29},{6,30},{7,31},{8,0},{9,1... | collective-permute-start | bytes 786440 | tf_op jit(solution)/shard_map/ppermute | solution.py:604
  129.0 33.0 %all-to-all-start.2 = ((bf16[8,96,1536]{2,1,0:T(8,128)(2,1)}), bf16[8,96,1536]{2,1,0:T(8,128)(2,1)S(1)}, u32[]{:S(2)}, u32[]{:S(2)}) async-start(bf16[8,96,1536]{2,1,0:T(8,128)(2,1)} %experts.1), calls=%async_computation.2 | async-start | bytes 4718592 | tf_op jit(solution)/shard_map/all_to_all | solution.py:456
  164.2 9.4 %collective-permute-start.17 = (bf16[64,1536]{1,0:T(8,128)(2,1)S(1)}, bf16[64,1536]{1,0:T(8,128)(2,1)S(1)}, u32[]{:S(2)}, u32[]{:S(2)}) collective-permute-start(bf16[64,1536]{1,0:T(8,128)(2,1)S(1)} %get-tuple-element.81), channel_id=1, source_target_pairs={{0,8},{1,9},{2,10},{3,11},{4,12},{5,13},{6,14},{7,15},{8,16},{9,17... | collective-permute-start | bytes 589832 | tf_op jit(solution)/shard_map/ppermute | solution.py:486
  165.7 17.0 %collective-permute-start.18 = (bf16[64,1536]{1,0:T(8,128)(2,1)S(1)}, bf16[64,1536]{1,0:T(8,128)(2,1)S(1)}, u32[]{:S(2)}, u32[]{:S(2)}) collective-permute-start(bf16[64,1536]{1,0:T(8,128)(2,1)S(1)} %get-tuple-element.82), channel_id=1, source_target_pairs={{0,16},{1,17},{2,18},{3,19},{4,20},{5,21},{6,22},{7,23},{8,24},{9,... | collective-permute-start | bytes 589832 | tf_op jit(solution)/shard_map/ppermute | solution.py:486
  169.9 16.7 %collective-permute-start.19 = (bf16[64,1536]{1,0:T(8,128)(2,1)S(1)}, bf16[64,1536]{1,0:T(8,128)(2,1)S(1)}, u32[]{:S(2)}, u32[]{:S(2)}) collective-permute-start(bf16[64,1536]{1,0:T(8,128)(2,1)S(1)} %get-tuple-element.83), channel_id=1, source_target_pairs={{0,24},{1,25},{2,26},{3,27},{4,28},{5,29},{6,30},{7,31},{8,0},{9,1... | collective-permute-start | bytes 589832 | tf_op jit(solution)/shard_map/ppermute | solution.py:486
  (20 other events, 133.4 us)
Sparse Core Ops, SparseCore 0:
  9.9 30.5 all-gather.3
  42.4 29.0 all-gather.5

commit v9 on v7

--- a/solution.py
+++ b/solution.py
@@ -462,9 +462,6 @@
     )(in_hbm(key_vectors), in_hbm(value_vectors))
     behind = [from_behind(own_kv, "seq", offset) for offset in range(REACH, 0, -1)]
 
-    turned_weight = lax.all_gather(
-        out_weight.T, "seq", axis=0, tiled=True, axis_index_groups=planes
-    )
     info = pl.pallas_call(
         route_kernel,
         out_shape=pltpu.HBM((tokens, 128), bf16),
@@ -475,6 +472,11 @@
         cost_estimate=cost(MIB, MIB),
         name="route",
     )(scalar(z_index), in_hbm(route_ids.T), in_hbm(route_logits.T))
+
+    info, out_weight = lax.optimization_barrier((info, out_weight))
+    turned_weight = lax.all_gather(
+        out_weight.T, "seq", axis=0, tiled=True, axis_index_groups=planes
+    )
 
     def along_z(arrays):
         return [arrays[0]] + [

time: 188 us -> 190 us (1.011)
    ppermute x4, waiting for transfers between devices: 0.23 us -> 2.8 us  [from_behind(): return lax.ppermute(shard, axis, pairs)]
  transfers between devices with their start and end apart: 25 -> 25, of which waited for: 10 -> 10; matrix products, arithmetic and copies ran while one was open for 6% -> 6% of each run, Pallas kernels for 14% -> 12%
where the time goes in v9:
time: 190 us; the launch traced here: 189 us
  waiting for transfers between devices  79.8 us (42%)
  starting transfers between devices  50.2 us (26%)
  Pallas kernels  28.6 us (15%)
  between operations  14.3 us (8%)
  local copies, waits for them, and re-layouts  13 us (7%)
  other arithmetic  3.57 us (2%)
    all_to_all x3, waiting for transfers between devices, exchange(): lax.all_to_all(array, 'seq', split_axis=0, concat_axis=0, tiled=True, axi...  40 us
    ppermute x6, waiting for transfers between devices, along_z(): lax.ppermute(arrays[step], 'seq', z_pairs[step])  33.6 us
    all_to_all x3, starting transfers between devices, exchange(): lax.all_to_all(array, 'seq', split_axis=0, concat_axis=0, tiled=True, axi...  14.3 us
    ppermute x4, starting transfers between devices, from_behind(): return lax.ppermute(shard, axis, pairs)  13.1 us
    ppermute x6, starting transfers between devices, along_z(): lax.ppermute(arrays[step], 'seq', z_pairs[step])  9.4 us
    ppermute x7, starting transfers between devices, shards(): piece = lax.ppermute(piece, 'seq', pairs)  8.04 us
    optimization_barrier x1, local copies, waits for them, and re-layouts, shards(): lax.optimization_barrier((gathered, cache_blocks, expert_gate_up))  6.31 us
    pallas_call x1, Pallas kernels, shards(): pl.pallas_call(experts_kernel, out_shape=pltpu.HBM((PLANE, picked, width)...  5.89 us
  transfers between devices with their start and end apart: 25, of which 10 were waited for; matrix products, arithmetic and copies ran while one was open for 6% of the time, Pallas kernels for 12%

profile of v9, /device:TPU:10, one launch (start us, length us, event | category | flops | bytes accessed | tf_op | source)
XLA Modules:
  0.0 189.4 jit_solution(13065155947902440093)
XLA Ops:
  7.2 2.6 %route.1.info_ref = bf16[64,128]{1,0:T(8,128)(2,1)} custom-call(s32[1]{0:T(128)} %bitcast.z_ref, s32[6,64]{1,0:T(8,128)} %bitcast.56, f32[6,64]{1,0:T(8,128)} %bitcast.57), custom_call_target="tpu_custom_call" | custom-call | flops 1048576 | bytes 1048576 | tf_op jit(solution)/shard_map/route/pallas_call | solution.py:465
  13.3 3.4 %collective-permute-start.2 = (bf16[64,1024]{1,0:T(8,128)(2,1)}, bf16[64,1024]{1,0:T(8,128)(2,1)S(1)}, u32[]{:S(2)}, u32[]{:S(2)}) collective-permute-start(bf16[64,1024]{1,0:T(8,128)(2,1)} %join.1.own_ref), channel_id=1, source_target_pairs={{0,2},{1,3},{2,4},{3,5},{4,6},{5,7},{6,8},{7,9},{8,10},{9,11},{10,... | collective-permute-start | bytes 393224 | tf_op jit(solution)/shard_map/ppermute | solution.py:28
  16.7 4.3 %collective-permute-start.1 = (bf16[64,1024]{1,0:T(8,128)(2,1)}, bf16[64,1024]{1,0:T(8,128)(2,1)S(1)}, u32[]{:S(2)}, u32[]{:S(2)}) collective-permute-start(bf16[64,1024]{1,0:T(8,128)(2,1)} %join.1.own_ref), channel_id=1, source_target_pairs={{0,3},{1,4},{2,5},{3,6},{4,7},{5,8},{6,9},{7,10},{8,11},{9,12},{10... | collective-permute-start | bytes 393224 | tf_op jit(solution)/shard_map/ppermute | solution.py:28
  21.0 3.4 %collective-permute-start = (bf16[64,1024]{1,0:T(8,128)(2,1)}, bf16[64,1024]{1,0:T(8,128)(2,1)S(1)}, u32[]{:S(2)}, u32[]{:S(2)}) collective-permute-start(bf16[64,1024]{1,0:T(8,128)(2,1)} %join.1.own_ref), channel_id=1, source_target_pairs={{0,4},{1,5},{2,6},{3,7},{4,8},{5,9},{6,10},{7,11},{8,12},{9,13},{1... | collective-permute-start | bytes 393224 | tf_op jit(solution)/shard_map/ppermute | solution.py:28
  26.2 2.8 %collective-permute-done.k4_ref = bf16[64,1024]{1,0:T(8,128)(2,1)S(1)} collective-permute-done((bf16[64,1024]{1,0:T(8,128)(2,1)}, bf16[64,1024]{1,0:T(8,128)(2,1)S(1)}, u32[]{:S(2)}, u32[]{:S(2)}) %collective-permute-start) | collective-permute-done | bytes 131104 | tf_op jit(solution)/shard_map/ppermute | solution.py:28
  29.7 3.8 %attention.1 = (bf16[64,2048]{1,0:T(8,128)(2,1)}, bf16[64,2048]{1,0:T(8,128)(2,1)}, bf16[64,2048]{1,0:T(8,128)(2,1)}, bf16[64,2048]{1,0:T(8,128)(2,1)}) custom-call(s32[1]{0:T(128)} %bitcast.z_ref, s32[1]{0:T(128)} %bitcast.1.first_ref, s32[16]{0:T(128)} %lengths_ref.1, bf16[64,1536]{1,0:T(8,128)(2,1)} %q_ref.1, bf16[64,1024]{1,0:T(8,128)(2,1)} %copy-done.10, ...), custom_call_target="tpu_custom_call" | custom-call | flops 125829120 | bytes 3145728 | tf_op jit(solution)/shard_map/attention/pallas_call | solution.py:501
  37.5 15.7 %collective-permute-done.4.refs_1_ = bf16[64,2048]{1,0:T(8,128)(2,1)S(1)} collective-permute-done((bf16[64,2048]{1,0:T(8,128)(2,1)}, bf16[64,2048]{1,0:T(8,128)(2,1)S(1)}, u32[]{:S(2)}, u32[]{:S(2)}) %collective-permute-start.4) | collective-permute-done | bytes 262176 | tf_op jit(solution)/shard_map/ppermute | solution.py:483
  53.3 2.8 %collective-permute-done.5.refs_2_ = bf16[64,2048]{1,0:T(8,128)(2,1)S(1)} collective-permute-done((bf16[64,2048]{1,0:T(8,128)(2,1)}, bf16[64,2048]{1,0:T(8,128)(2,1)S(1)}, u32[]{:S(2)}, u32[]{:S(2)}) %collective-permute-start.5) | collective-permute-done | bytes 262176 | tf_op jit(solution)/shard_map/ppermute | solution.py:483
  56.1 2.3 %collective-permute-done.6.refs_3_ = bf16[64,2048]{1,0:T(8,128)(2,1)S(1)} collective-permute-done((bf16[64,2048]{1,0:T(8,128)(2,1)}, bf16[64,2048]{1,0:T(8,128)(2,1)S(1)}, u32[]{:S(2)}, u32[]{:S(2)}) %collective-permute-start.6) | collective-permute-done | bytes 262176 | tf_op jit(solution)/shard_map/ppermute | solution.py:483
  58.4 2.8 %project.1 = (bf16[4,256,384]{2,1,0:T(8,128)(2,1)}, bf16[256,128]{1,0:T(8,128)(2,1)S(1)}) custom-call(s32[1]{0:T(128)} %bitcast.z_ref, bf16[64,2048]{1,0:T(8,128)(2,1)} %get-tuple-element.58.refs_0_, bf16[64,2048]{1,0:T(8,128)(2,1)S(1)} %collective-permute-done.4.refs_1_, bf16[64,2048]{1,0:T(8,128)(2,1)S(1)} %collective-permute-done.5.refs_2_, ...), custom_call_target="tpu_custom_call" | custom-call | flops 301989888 | bytes 3145728 | tf_op jit(solution)/shard_map/project/pallas_call | solution.py:536
  61.2 3.8 %all-to-all-start = ((bf16[4,256,384]{2,1,0:T(8,128)(2,1)}), bf16[4,256,384]{2,1,0:T(8,128)(2,1)S(1)}, u32[]{:S(2)}, u32[]{:S(2)}) async-start(bf16[4,256,384]{2,1,0:T(8,128)(2,1)} %get-tuple-element.63), calls=%async_computation | async-start | bytes 1572864 | tf_op jit(solution)/shard_map/all_to_all | solution.py:451
  71.0 2.4 %collective-permute-start.9 = (bf16[4,32,4,128]{3,2,1,0:T(4,128)(2,1)S(1)}, bf16[4,32,4,128]{3,2,1,0:T(4,128)(2,1)S(1)}, u32[]{:S(2)}, u32[]{:S(2)}) collective-permute-start(bf16[4,32,4,128]{3,2,1,0:T(4,128)(2,1)S(1)} %get-tuple-element.100), channel_id=1, source_target_pairs={{0,3},{1,4},{2,5},{3,6},{4,7},{5,0},{6,1},{7,2},{8,11},{9,12},{10,... | collective-permute-start | bytes 393224 | tf_op jit(solution)/shard_map/ppermute | solution.py:532
  74.4 3.3 %collective-permute-done.12.refs_6_ = bf16[4,32,4,128]{3,2,1,0:T(4,128)(2,1)S(1)} collective-permute-done((bf16[4,32,4,128]{3,2,1,0:T(4,128)(2,1)S(1)}, bf16[4,32,4,128]{3,2,1,0:T(4,128)(2,1)S(1)}, u32[]{:S(2)}, u32[]{:S(2)}) %collective-permute-start.12) | collective-permute-done | bytes 131104 | tf_op jit(solution)/shard_map/ppermute | solution.py:532
  85.5 5.4 %all-to-all-start.1 = ((bf16[8,96,1536]{2,1,0:T(8,128)(2,1)}), bf16[8,96,1536]{2,1,0:T(8,128)(2,1)S(1)}, u32[]{:S(2)}, u32[]{:S(2)}) async-start(bf16[8,96,1536]{2,1,0:T(8,128)(2,1)} %pick.1), calls=%async_computation.1 | async-start | bytes 4718592 | tf_op jit(solution)/shard_map/all_to_all | solution.py:451
  94.6 4.2 %collective-permute-start.15 = (bf16[8,32,4,128]{3,2,1,0:T(4,128)(2,1)}, bf16[8,32,4,128]{3,2,1,0:T(4,128)(2,1)}, u32[]{:S(2)}, u32[]{:S(2)}) collective-permute-start(bf16[8,32,4,128]{3,2,1,0:T(4,128)(2,1)} %get-tuple-element.84), channel_id=1, source_target_pairs={{0,16},{1,17},{2,18},{3,19},{4,20},{5,21},{6,22},{7,23},{8,24},{9,... | collective-permute-start | bytes 786440 | tf_op jit(solution)/shard_map/ppermute | solution.py:590
  99.1 6.3 %copy.35 = bf16[4,1536,2,256]{3,1,2,0:T(8,128)(2,1)} copy(bf16[4,1536,2,256]{3,2,1,0:T(2,128)(2,1)} %param.26) | data formatting | bytes 12582912 | tf_op jit(solution)/shard_map/optimization_barrier | solution.py:514
  105.4 13.5 %all-to-all-done.1.rows_ref = bf16[8,96,1536]{2,1,0:T(8,128)(2,1)S(1)} async-done(((bf16[8,96,1536]{2,1,0:T(8,128)(2,1)}), bf16[8,96,1536]{2,1,0:T(8,128)(2,1)S(1)}, u32[]{:S(2)}, u32[]{:S(2)}) %all-to-all-start.1) | async-done | bytes 2359328 | tf_op jit(solution)/shard_map/all_to_all | solution.py:451
  118.9 5.9 %experts.1 = bf16[8,96,1536]{2,1,0:T(8,128)(2,1)} custom-call(bf16[8,96,1536]{2,1,0:T(8,128)(2,1)S(1)} %all-to-all-done.1.rows_ref, bf16[4,2,1536,256]{3,2,1,0:T(8,128)(2,1)} %bitcast.51, bf16[4,256,1536]{2,1,0:T(8,128)(2,1)} %down_hbm.1), custom_call_target="tpu_custom_call" | custom-call | flops 1811939328 | bytes 14680064 | tf_op jit(solution)/shard_map/experts/pallas_call | solution.py:603
  124.8 5.1 %all-to-all-start.2 = ((bf16[8,96,1536]{2,1,0:T(8,128)(2,1)}), bf16[8,96,1536]{2,1,0:T(8,128)(2,1)S(1)}, u32[]{:S(2)}, u32[]{:S(2)}) async-start(bf16[8,96,1536]{2,1,0:T(8,128)(2,1)} %experts.1), calls=%async_computation.2 | async-start | bytes 4718592 | tf_op jit(solution)/shard_map/all_to_all | solution.py:451
  133.4 24.4 %all-to-all-done.2 = bf16[8,96,1536]{2,1,0:T(8,128)(2,1)S(1)} async-done(((bf16[8,96,1536]{2,1,0:T(8,128)(2,1)}), bf16[8,96,1536]{2,1,0:T(8,128)(2,1)S(1)}, u32[]{:S(2)}, u32[]{:S(2)}) %all-to-all-start.2) | async-done | bytes 2359328 | tf_op jit(solution)/shard_map/all_to_all | solution.py:451
  157.8 2.2 %combine.1 = (bf16[64,1536]{1,0:T(8,128)(2,1)S(1)}, bf16[64,1536]{1,0:T(8,128)(2,1)S(1)}, bf16[64,1536]{1,0:T(8,128)(2,1)S(1)}, bf16[64,1536]{1,0:T(8,128)(2,1)S(1)}) custom-call(s32[1]{0:T(128)} %bitcast.z_ref, bf16[256,768]{1,0:T(8,128)(2,1)} %copy-done.2, bf16[768,1536]{1,0:T(8,128)(2,1)S(1)} %bitcast.49, bf16[256,1536]{1,0:T(8,128)(2,1)} %copy-done.1), custom_call_target="tpu_custom_call" | custom-call | flops 603979776 | bytes 3145728 | tf_op jit(solution)/shard_map/combine/pallas_call | solution.py:634
  160.9 4.2 %collective-permute-start.18 = (bf16[64,1536]{1,0:T(8,128)(2,1)S(1)}, bf16[64,1536]{1,0:T(8,128)(2,1)S(1)}, u32[]{:S(2)}, u32[]{:S(2)}) collective-permute-start(bf16[64,1536]{1,0:T(8,128)(2,1)S(1)} %get-tuple-element.90), channel_id=1, source_target_pairs={{0,16},{1,17},{2,18},{3,19},{4,20},{5,21},{6,22},{7,23},{8,24},{9,... | collective-permute-start | bytes 589832 | tf_op jit(solution)/shard_map/ppermute | solution.py:483
  169.0 8.9 %collective-permute-done.18.refs_2_ = bf16[64,1536]{1,0:T(8,128)(2,1)S(1)} collective-permute-done((bf16[64,1536]{1,0:T(8,128)(2,1)S(1)}, bf16[64,1536]{1,0:T(8,128)(2,1)S(1)}, u32[]{:S(2)}, u32[]{:S(2)}) %collective-permute-start.18) | collective-permute-done | bytes 196640 | tf_op jit(solution)/shard_map/ppermute | solution.py:483
  177.9 3.9 %collective-permute-done.19.refs_3_ = bf16[64,1536]{1,0:T(8,128)(2,1)S(1)} collective-permute-done((bf16[64,1536]{1,0:T(8,128)(2,1)S(1)}, bf16[64,1536]{1,0:T(8,128)(2,1)S(1)}, u32[]{:S(2)}, u32[]{:S(2)}) %collective-permute-start.19) | collective-permute-done | bytes 196640 | tf_op jit(solution)/shard_map/ppermute | solution.py:483
  (83 shorter events, 37.8 us)
Async XLA Ops:
  7.2 51.2 %all-gather.4.cloned.1.call-start = ((), (), s32[]{:S(2)}) async-start(), calls=%async_computation.3 | async-start | bytes 1327104 | tf_op jit(solution)/shard_map/all_gather | solution.py:477
  9.8 95.6 %all-gather.6.cloned.1.call-start = ((), (), s32[]{:S(2)}) async-start(), calls=%async_computation.4 | async-start | bytes 2654208 | tf_op jit(solution)/shard_map/all_gather | solution.py:512
  11.4 14.8 %collective-permute-start.3 = (bf16[64,1024]{1,0:T(8,128)(2,1)}, bf16[64,1024]{1,0:T(8,128)(2,1)S(1)}, u32[]{:S(2)}, u32[]{:S(2)}) collective-permute-start(bf16[64,1024]{1,0:T(8,128)(2,1)} %join.1.own_ref), channel_id=1, source_target_pairs={{0,1},{1,2},{2,3},{3,4},{4,5},{5,6},{6,7},{7,8},{8,9},{9,10},{10,1... | collective-permute-start | bytes 393224 | tf_op jit(solution)/shard_map/ppermute | solution.py:28
  13.3 12.9 %collective-permute-start.2 = (bf16[64,1024]{1,0:T(8,128)(2,1)}, bf16[64,1024]{1,0:T(8,128)(2,1)S(1)}, u32[]{:S(2)}, u32[]{:S(2)}) collective-permute-start(bf16[64,1024]{1,0:T(8,128)(2,1)} %join.1.own_ref), channel_id=1, source_target_pairs={{0,2},{1,3},{2,4},{3,5},{4,6},{5,7},{6,8},{7,9},{8,10},{9,11},{10,... | collective-permute-start | bytes 393224 | tf_op jit(solution)/shard_map/ppermute | solution.py:28
  16.7 9.5 %collective-permute-start.1 = (bf16[64,1024]{1,0:T(8,128)(2,1)}, bf16[64,1024]{1,0:T(8,128)(2,1)S(1)}, u32[]{:S(2)}, u32[]{:S(2)}) collective-permute-start(bf16[64,1024]{1,0:T(8,128)(2,1)} %join.1.own_ref), channel_id=1, source_target_pairs={{0,3},{1,4},{2,5},{3,6},{4,7},{5,8},{6,9},{7,10},{8,11},{9,12},{10... | collective-permute-start | bytes 393224 | tf_op jit(solution)/shard_map/ppermute | solution.py:28
  21.0 8.0 %collective-permute-start = (bf16[64,1024]{1,0:T(8,128)(2,1)}, bf16[64,1024]{1,0:T(8,128)(2,1)S(1)}, u32[]{:S(2)}, u32[]{:S(2)}) collective-permute-start(bf16[64,1024]{1,0:T(8,128)(2,1)} %join.1.own_ref), channel_id=1, source_target_pairs={{0,4},{1,5},{2,6},{3,7},{4,8},{5,9},{6,10},{7,11},{8,12},{9,13},{1... | collective-permute-start | bytes 393224 | tf_op jit(solution)/shard_map/ppermute | solution.py:28
  33.5 19.8 %collective-permute-start.4 = (bf16[64,2048]{1,0:T(8,128)(2,1)}, bf16[64,2048]{1,0:T(8,128)(2,1)S(1)}, u32[]{:S(2)}, u32[]{:S(2)}) collective-permute-start(bf16[64,2048]{1,0:T(8,128)(2,1)} %get-tuple-element.55), channel_id=1, source_target_pairs={{0,8},{1,9},{2,10},{3,11},{4,12},{5,13},{6,14},{7,15},{8,16},{9,17... | collective-permute-start | bytes 786440 | tf_op jit(solution)/shard_map/ppermute | solution.py:483
  35.1 21.0 %collective-permute-start.5 = (bf16[64,2048]{1,0:T(8,128)(2,1)}, bf16[64,2048]{1,0:T(8,128)(2,1)S(1)}, u32[]{:S(2)}, u32[]{:S(2)}) collective-permute-start(bf16[64,2048]{1,0:T(8,128)(2,1)} %get-tuple-element.56), channel_id=1, source_target_pairs={{0,16},{1,17},{2,18},{3,19},{4,20},{5,21},{6,22},{7,23},{8,24},{9,... | collective-permute-start | bytes 786440 | tf_op jit(solution)/shard_map/ppermute | solution.py:483
  35.6 22.8 %collective-permute-start.6 = (bf16[64,2048]{1,0:T(8,128)(2,1)}, bf16[64,2048]{1,0:T(8,128)(2,1)S(1)}, u32[]{:S(2)}, u32[]{:S(2)}) collective-permute-start(bf16[64,2048]{1,0:T(8,128)(2,1)} %get-tuple-element.57), channel_id=1, source_target_pairs={{0,24},{1,25},{2,26},{3,27},{4,28},{5,29},{6,30},{7,31},{8,0},{9,1... | collective-permute-start | bytes 786440 | tf_op jit(solution)/shard_map/ppermute | solution.py:483
  61.2 21.3 %all-to-all-start = ((bf16[4,256,384]{2,1,0:T(8,128)(2,1)}), bf16[4,256,384]{2,1,0:T(8,128)(2,1)S(1)}, u32[]{:S(2)}, u32[]{:S(2)}) async-start(bf16[4,256,384]{2,1,0:T(8,128)(2,1)} %get-tuple-element.63), calls=%async_computation | async-start | bytes 1572864 | tf_op jit(solution)/shard_map/all_to_all | solution.py:451
  67.8 9.8 %collective-permute-start.12 = (bf16[4,32,4,128]{3,2,1,0:T(4,128)(2,1)S(1)}, bf16[4,32,4,128]{3,2,1,0:T(4,128)(2,1)S(1)}, u32[]{:S(2)}, u32[]{:S(2)}) collective-permute-start(bf16[4,32,4,128]{3,2,1,0:T(4,128)(2,1)S(1)} %get-tuple-element.97), channel_id=1, source_target_pairs={{0,6},{1,7},{2,0},{3,1},{4,2},{5,3},{6,4},{7,5},{8,14},{9,15},{10,... | collective-permute-start | bytes 393224 | tf_op jit(solution)/shard_map/ppermute | solution.py:532
  68.9 15.7 %collective-permute-start.11 = (bf16[4,32,4,128]{3,2,1,0:T(4,128)(2,1)S(1)}, bf16[4,32,4,128]{3,2,1,0:T(4,128)(2,1)S(1)}, u32[]{:S(2)}, u32[]{:S(2)}) collective-permute-start(bf16[4,32,4,128]{3,2,1,0:T(4,128)(2,1)S(1)} %get-tuple-element.98), channel_id=1, source_target_pairs={{0,5},{1,6},{2,7},{3,0},{4,1},{5,2},{6,3},{7,4},{8,13},{9,14},{10,... | collective-permute-start | bytes 393224 | tf_op jit(solution)/shard_map/ppermute | solution.py:532
  70.8 13.8 %collective-permute-start.10 = (bf16[4,32,4,128]{3,2,1,0:T(4,128)(2,1)S(1)}, bf16[4,32,4,128]{3,2,1,0:T(4,128)(2,1)S(1)}, u32[]{:S(2)}, u32[]{:S(2)}) collective-permute-start(bf16[4,32,4,128]{3,2,1,0:T(4,128)(2,1)S(1)} %get-tuple-element.99), channel_id=1, source_target_pairs={{0,4},{1,5},{2,6},{3,7},{4,0},{5,1},{6,2},{7,3},{8,12},{9,13},{10,... | collective-permute-start | bytes 393224 | tf_op jit(solution)/shard_map/ppermute | solution.py:532
  71.0 13.7 %collective-permute-start.9 = (bf16[4,32,4,128]{3,2,1,0:T(4,128)(2,1)S(1)}, bf16[4,32,4,128]{3,2,1,0:T(4,128)(2,1)S(1)}, u32[]{:S(2)}, u32[]{:S(2)}) collective-permute-start(bf16[4,32,4,128]{3,2,1,0:T(4,128)(2,1)S(1)} %get-tuple-element.100), channel_id=1, source_target_pairs={{0,3},{1,4},{2,5},{3,6},{4,7},{5,0},{6,1},{7,2},{8,11},{9,12},{10,... | collective-permute-start | bytes 393224 | tf_op jit(solution)/shard_map/ppermute | solution.py:532
  73.4 11.3 %collective-permute-start.8 = (bf16[4,32,4,128]{3,2,1,0:T(4,128)(2,1)S(1)}, bf16[4,32,4,128]{3,2,1,0:T(4,128)(2,1)S(1)}, u32[]{:S(2)}, u32[]{:S(2)}) collective-permute-start(bf16[4,32,4,128]{3,2,1,0:T(4,128)(2,1)S(1)} %get-tuple-element.101), channel_id=1, source_target_pairs={{0,2},{1,3},{2,4},{3,5},{4,6},{5,7},{6,0},{7,1},{8,10},{9,11},{10,... | collective-permute-start | bytes 393224 | tf_op jit(solution)/shard_map/ppermute | solution.py:532
  77.6 7.1 %collective-permute-start.7 = (bf16[4,32,4,128]{3,2,1,0:T(4,128)(2,1)S(1)}, bf16[4,32,4,128]{3,2,1,0:T(4,128)(2,1)S(1)}, u32[]{:S(2)}, u32[]{:S(2)}) collective-permute-start(bf16[4,32,4,128]{3,2,1,0:T(4,128)(2,1)S(1)} %get-tuple-element.102), channel_id=1, source_target_pairs={{0,1},{1,2},{2,3},{3,4},{4,5},{5,6},{6,7},{7,0},{8,9},{9,10},{10,1... | collective-permute-start | bytes 393224 | tf_op jit(solution)/shard_map/ppermute | solution.py:532
  85.5 33.4 %all-to-all-start.1 = ((bf16[8,96,1536]{2,1,0:T(8,128)(2,1)}), bf16[8,96,1536]{2,1,0:T(8,128)(2,1)S(1)}, u32[]{:S(2)}, u32[]{:S(2)}) async-start(bf16[8,96,1536]{2,1,0:T(8,128)(2,1)} %pick.1), calls=%async_computation.1 | async-start | bytes 4718592 | tf_op jit(solution)/shard_map/all_to_all | solution.py:451
  93.8 31.0 %collective-permute-start.14 = (bf16[8,32,4,128]{3,2,1,0:T(4,128)(2,1)}, bf16[8,32,4,128]{3,2,1,0:T(4,128)(2,1)}, u32[]{:S(2)}, u32[]{:S(2)}) collective-permute-start(bf16[8,32,4,128]{3,2,1,0:T(4,128)(2,1)} %get-tuple-element.83), channel_id=1, source_target_pairs={{0,8},{1,9},{2,10},{3,11},{4,12},{5,13},{6,14},{7,15},{8,16},{9,17... | collective-permute-start | bytes 786440 | tf_op jit(solution)/shard_map/ppermute | solution.py:590
  94.6 30.2 %collective-permute-start.15 = (bf16[8,32,4,128]{3,2,1,0:T(4,128)(2,1)}, bf16[8,32,4,128]{3,2,1,0:T(4,128)(2,1)}, u32[]{:S(2)}, u32[]{:S(2)}) collective-permute-start(bf16[8,32,4,128]{3,2,1,0:T(4,128)(2,1)} %get-tuple-element.84), channel_id=1, source_target_pairs={{0,16},{1,17},{2,18},{3,19},{4,20},{5,21},{6,22},{7,23},{8,24},{9,... | collective-permute-start | bytes 786440 | tf_op jit(solution)/shard_map/ppermute | solution.py:590
  98.8 26.0 %collective-permute-start.16 = (bf16[8,32,4,128]{3,2,1,0:T(4,128)(2,1)S(1)}, bf16[8,32,4,128]{3,2,1,0:T(4,128)(2,1)}, u32[]{:S(2)}, u32[]{:S(2)}) collective-permute-start(bf16[8,32,4,128]{3,2,1,0:T(4,128)(2,1)S(1)} %get-tuple-element.85), channel_id=1, source_target_pairs={{0,24},{1,25},{2,26},{3,27},{4,28},{5,29},{6,30},{7,31},{8,0},{9,1... | collective-permute-start | bytes 786440 | tf_op jit(solution)/shard_map/ppermute | solution.py:590
  124.8 33.0 %all-to-all-start.2 = ((bf16[8,96,1536]{2,1,0:T(8,128)(2,1)}), bf16[8,96,1536]{2,1,0:T(8,128)(2,1)S(1)}, u32[]{:S(2)}, u32[]{:S(2)}) async-start(bf16[8,96,1536]{2,1,0:T(8,128)(2,1)} %experts.1), calls=%async_computation.2 | async-start | bytes 4718592 | tf_op jit(solution)/shard_map/all_to_all | solution.py:451
  160.0 9.0 %collective-permute-start.17 = (bf16[64,1536]{1,0:T(8,128)(2,1)S(1)}, bf16[64,1536]{1,0:T(8,128)(2,1)S(1)}, u32[]{:S(2)}, u32[]{:S(2)}) collective-permute-start(bf16[64,1536]{1,0:T(8,128)(2,1)S(1)} %get-tuple-element.89), channel_id=1, source_target_pairs={{0,8},{1,9},{2,10},{3,11},{4,12},{5,13},{6,14},{7,15},{8,16},{9,17... | collective-permute-start | bytes 589832 | tf_op jit(solution)/shard_map/ppermute | solution.py:483
  160.9 17.0 %collective-permute-start.18 = (bf16[64,1536]{1,0:T(8,128)(2,1)S(1)}, bf16[64,1536]{1,0:T(8,128)(2,1)S(1)}, u32[]{:S(2)}, u32[]{:S(2)}) collective-permute-start(bf16[64,1536]{1,0:T(8,128)(2,1)S(1)} %get-tuple-element.90), channel_id=1, source_target_pairs={{0,16},{1,17},{2,18},{3,19},{4,20},{5,21},{6,22},{7,23},{8,24},{9,... | collective-permute-start | bytes 589832 | tf_op jit(solution)/shard_map/ppermute | solution.py:483
  165.1 16.7 %collective-permute-start.19 = (bf16[64,1536]{1,0:T(8,128)(2,1)S(1)}, bf16[64,1536]{1,0:T(8,128)(2,1)S(1)}, u32[]{:S(2)}, u32[]{:S(2)}) collective-permute-start(bf16[64,1536]{1,0:T(8,128)(2,1)S(1)} %get-tuple-element.91), channel_id=1, source_target_pairs={{0,24},{1,25},{2,26},{3,27},{4,28},{5,29},{6,30},{7,31},{8,0},{9,1... | collective-permute-start | bytes 589832 | tf_op jit(solution)/shard_map/ppermute | solution.py:483
  (20 other events, 137.8 us)
Sparse Core Ops, SparseCore 0:
  9.9 32.4 all-gather.3
  44.3 29.0 all-gather.5

commit v10 on v7

--- a/solution.py
+++ b/solution.py
@@ -501,10 +501,10 @@
         out_shape=[pltpu.HBM((tokens, sent_width), bf16)] * Z_SIZE,
         in_specs=[SMEM] * 3 + [VMEM] * 8,
         out_specs=[VMEM] * Z_SIZE,
-        compiler_params=params(58),
+        compiler_params=params(),
         cost_estimate=cost(4 * tokens * 5 * tokens * width, 3 * MIB),
         name="attention",
-    )(z_scalar, scalar(me * tokens), in_hbm(lengths), queries, *behind, own_kv, residual, info)
+    )(z_scalar, scalar(me * tokens), in_hbm(lengths), in_hbm(queries), *behind, own_kv, in_hbm(residual), info)
 
     sent, own_shared = lax.optimization_barrier((sent, own_shared))
     shared_weight = lax.all_gather(own_shared, "seq", axis=0, axis_index_groups=planes)

time: 188 us -> 189 us (level)
    unnamed x38 -> x34, local copies, waits for them, and re-layouts: 5.42 us -> 6.42 us
  transfers between devices with their start and end apart: 25 -> 25, of which waited for: 10 -> 10; matrix products, arithmetic and copies ran while one was open for 6% -> 6% of each run, Pallas kernels for 14% -> 13%
where the time goes in v10:
time: 189 us; the launch traced here: 188 us
  waiting for transfers between devices  77.9 us (41%)
  starting transfers between devices  50.2 us (27%)
  Pallas kernels  28.4 us (15%)
  between operations  14.3 us (8%)
  local copies, waits for them, and re-layouts  13.9 us (7%)
  other arithmetic  3.58 us (2%)
    all_to_all x3, waiting for transfers between devices, exchange(): lax.all_to_all(array, 'seq', split_axis=0, concat_axis=0, tiled=True, axi...  40.1 us
    ppermute x6, waiting for transfers between devices, along_z(): lax.ppermute(arrays[step], 'seq', z_pairs[step])  33.6 us
    all_to_all x3, starting transfers between devices, exchange(): lax.all_to_all(array, 'seq', split_axis=0, concat_axis=0, tiled=True, axi...  14.8 us
    ppermute x4, starting transfers between devices, from_behind(): return lax.ppermute(shard, axis, pairs)  13.1 us
    ppermute x6, starting transfers between devices, along_z(): lax.ppermute(arrays[step], 'seq', z_pairs[step])  9.52 us
    ppermute x7, starting transfers between devices, shards(): piece = lax.ppermute(piece, 'seq', pairs)  7.39 us
    unnamed x34, local copies, waits for them, and re-layouts  6.42 us
    optimization_barrier x1, local copies, waits for them, and re-layouts, shards(): lax.optimization_barrier((gathered, cache_blocks, expert_gate_up))  6.31 us
  transfers between devices with their start and end apart: 25, of which 10 were waited for; matrix products, arithmetic and copies ran while one was open for 6% of the time, Pallas kernels for 13%

profile of v10, /device:TPU:10, one launch (start us, length us, event | category | flops | bytes accessed | tf_op | source)
XLA Modules:
  0.0 188.3 jit_solution(6169115265240483238)
XLA Ops:
  11.4 3.4 %collective-permute-start.2 = (bf16[64,1024]{1,0:T(8,128)(2,1)}, bf16[64,1024]{1,0:T(8,128)(2,1)S(1)}, u32[]{:S(2)}, u32[]{:S(2)}) collective-permute-start(bf16[64,1024]{1,0:T(8,128)(2,1)} %join.1.own_ref), channel_id=1, source_target_pairs={{0,2},{1,3},{2,4},{3,5},{4,6},{5,7},{6,8},{7,9},{8,10},{9,11},{10,... | collective-permute-start | bytes 393224 | tf_op jit(solution)/shard_map/ppermute | solution.py:28
  14.8 4.3 %collective-permute-start.1 = (bf16[64,1024]{1,0:T(8,128)(2,1)}, bf16[64,1024]{1,0:T(8,128)(2,1)S(1)}, u32[]{:S(2)}, u32[]{:S(2)}) collective-permute-start(bf16[64,1024]{1,0:T(8,128)(2,1)} %join.1.own_ref), channel_id=1, source_target_pairs={{0,3},{1,4},{2,5},{3,6},{4,7},{5,8},{6,9},{7,10},{8,11},{9,12},{10... | collective-permute-start | bytes 393224 | tf_op jit(solution)/shard_map/ppermute | solution.py:28
  19.1 3.4 %collective-permute-start = (bf16[64,1024]{1,0:T(8,128)(2,1)}, bf16[64,1024]{1,0:T(8,128)(2,1)S(1)}, u32[]{:S(2)}, u32[]{:S(2)}) collective-permute-start(bf16[64,1024]{1,0:T(8,128)(2,1)} %join.1.own_ref), channel_id=1, source_target_pairs={{0,4},{1,5},{2,6},{3,7},{4,8},{5,9},{6,10},{7,11},{8,12},{9,13},{1... | collective-permute-start | bytes 393224 | tf_op jit(solution)/shard_map/ppermute | solution.py:28
  22.6 2.6 %route.1.info_ref = bf16[64,128]{1,0:T(8,128)(2,1)} custom-call(s32[1]{0:T(128)} %bitcast.z_ref, s32[6,64]{1,0:T(8,128)} %bitcast.56, f32[6,64]{1,0:T(8,128)} %bitcast.57), custom_call_target="tpu_custom_call" | custom-call | flops 1048576 | bytes 1048576 | tf_op jit(solution)/shard_map/route/pallas_call | solution.py:468
  28.7 3.5 %attention.1 = (bf16[64,2048]{1,0:T(8,128)(2,1)}, bf16[64,2048]{1,0:T(8,128)(2,1)}, bf16[64,2048]{1,0:T(8,128)(2,1)}, bf16[64,2048]{1,0:T(8,128)(2,1)}) custom-call(s32[1]{0:T(128)} %bitcast.z_ref, s32[1]{0:T(128)} %bitcast.1.first_ref, s32[16]{0:T(128)} %lengths_ref.1, bf16[64,1536]{1,0:T(8,128)(2,1)} %q_ref.1, ...), custom_call_target="tpu_custom_call" | custom-call | flops 125829120 | bytes 3145728 | tf_op jit(solution)/shard_map/attention/pallas_call | solution.py:499
  36.4 15.8 %collective-permute-done.4.refs_1_ = bf16[64,2048]{1,0:T(8,128)(2,1)S(1)} collective-permute-done((bf16[64,2048]{1,0:T(8,128)(2,1)}, bf16[64,2048]{1,0:T(8,128)(2,1)S(1)}, u32[]{:S(2)}, u32[]{:S(2)}) %collective-permute-start.4) | collective-permute-done | bytes 262176 | tf_op jit(solution)/shard_map/ppermute | solution.py:481
  52.2 3.3 %collective-permute-done.5.refs_2_ = bf16[64,2048]{1,0:T(8,128)(2,1)S(1)} collective-permute-done((bf16[64,2048]{1,0:T(8,128)(2,1)}, bf16[64,2048]{1,0:T(8,128)(2,1)S(1)}, u32[]{:S(2)}, u32[]{:S(2)}) %collective-permute-start.5) | collective-permute-done | bytes 262176 | tf_op jit(solution)/shard_map/ppermute | solution.py:481
  57.3 2.8 %project.1 = (bf16[4,256,384]{2,1,0:T(8,128)(2,1)}, bf16[256,128]{1,0:T(8,128)(2,1)S(1)}) custom-call(s32[1]{0:T(128)} %bitcast.z_ref, bf16[64,2048]{1,0:T(8,128)(2,1)} %get-tuple-element.55.refs_0_, bf16[64,2048]{1,0:T(8,128)(2,1)S(1)} %collective-permute-done.4.refs_1_, bf16[64,2048]{1,0:T(8,128)(2,1)S(1)} %collective-permute-done.5.refs_2_, ...), custom_call_target="tpu_custom_call" | custom-call | flops 301989888 | bytes 3145728 | tf_op jit(solution)/shard_map/project/pallas_call | solution.py:534
  60.1 4.4 %all-to-all-start = ((bf16[4,256,384]{2,1,0:T(8,128)(2,1)}), bf16[4,256,384]{2,1,0:T(8,128)(2,1)S(1)}, u32[]{:S(2)}, u32[]{:S(2)}) async-start(bf16[4,256,384]{2,1,0:T(8,128)(2,1)} %get-tuple-element.59), calls=%async_computation | async-start | bytes 1572864 | tf_op jit(solution)/shard_map/all_to_all | solution.py:451
  69.7 2.4 %collective-permute-start.9 = (bf16[4,32,4,128]{3,2,1,0:T(4,128)(2,1)S(1)}, bf16[4,32,4,128]{3,2,1,0:T(4,128)(2,1)S(1)}, u32[]{:S(2)}, u32[]{:S(2)}) collective-permute-start(bf16[4,32,4,128]{3,2,1,0:T(4,128)(2,1)S(1)} %get-tuple-element.96), channel_id=1, source_target_pairs={{0,3},{1,4},{2,5},{3,6},{4,7},{5,0},{6,1},{7,2},{8,11},{9,12},{10,... | collective-permute-start | bytes 393224 | tf_op jit(solution)/shard_map/ppermute | solution.py:530
  73.1 3.3 %collective-permute-done.12.refs_6_ = bf16[4,32,4,128]{3,2,1,0:T(4,128)(2,1)S(1)} collective-permute-done((bf16[4,32,4,128]{3,2,1,0:T(4,128)(2,1)S(1)}, bf16[4,32,4,128]{3,2,1,0:T(4,128)(2,1)S(1)}, u32[]{:S(2)}, u32[]{:S(2)}) %collective-permute-start.12) | collective-permute-done | bytes 131104 | tf_op jit(solution)/shard_map/ppermute | solution.py:530
  79.1 2.2 %all-to-all-done.mixed_ref = bf16[4,256,384]{2,1,0:T(8,128)(2,1)S(1)} async-done(((bf16[4,256,384]{2,1,0:T(8,128)(2,1)}), bf16[4,256,384]{2,1,0:T(8,128)(2,1)S(1)}, u32[]{:S(2)}, u32[]{:S(2)}) %all-to-all-start) | async-done | bytes 786464 | tf_op jit(solution)/shard_map/all_to_all | solution.py:451
  84.3 5.4 %all-to-all-start.1 = ((bf16[8,96,1536]{2,1,0:T(8,128)(2,1)}), bf16[8,96,1536]{2,1,0:T(8,128)(2,1)S(1)}, u32[]{:S(2)}, u32[]{:S(2)}) async-start(bf16[8,96,1536]{2,1,0:T(8,128)(2,1)} %pick.1), calls=%async_computation.1 | async-start | bytes 4718592 | tf_op jit(solution)/shard_map/all_to_all | solution.py:451
  89.7 2.1 %regroup.1 = (bf16[8,32,4,128]{3,2,1,0:T(4,128)(2,1)S(1)}, bf16[8,32,4,128]{3,2,1,0:T(4,128)(2,1)}, bf16[8,32,4,128]{3,2,1,0:T(4,128)(2,1)}, bf16[8,32,4,128]{3,2,1,0:T(4,128)(2,1)S(1)}) custom-call(s32[1]{0:T(128)} %bitcast.z_ref, bf16[4,32,4,128]{3,2,1,0:T(4,128)(2,1)} %get-tuple-element.70.refs_0_, bf16[4,32,4,128]{3,2,1,0:T(4,128)(2,1)} %copy-done.15, ...), custom_call_target="tpu_custom_call" | custom-call | bytes 2097152 | tf_op jit(solution)/shard_map/regroup/pallas_call | solution.py:577
  93.4 4.2 %collective-permute-start.15 = (bf16[8,32,4,128]{3,2,1,0:T(4,128)(2,1)}, bf16[8,32,4,128]{3,2,1,0:T(4,128)(2,1)}, u32[]{:S(2)}, u32[]{:S(2)}) collective-permute-start(bf16[8,32,4,128]{3,2,1,0:T(4,128)(2,1)} %get-tuple-element.80), channel_id=1, source_target_pairs={{0,16},{1,17},{2,18},{3,19},{4,20},{5,21},{6,22},{7,23},{8,24},{9,... | collective-permute-start | bytes 786440 | tf_op jit(solution)/shard_map/ppermute | solution.py:588
  97.9 6.3 %copy.35 = bf16[4,1536,2,256]{3,1,2,0:T(8,128)(2,1)} copy(bf16[4,1536,2,256]{3,2,1,0:T(2,128)(2,1)} %param.26) | data formatting | bytes 12582912 | tf_op jit(solution)/shard_map/optimization_barrier | solution.py:512
  104.2 13.5 %all-to-all-done.1.rows_ref = bf16[8,96,1536]{2,1,0:T(8,128)(2,1)S(1)} async-done(((bf16[8,96,1536]{2,1,0:T(8,128)(2,1)}), bf16[8,96,1536]{2,1,0:T(8,128)(2,1)S(1)}, u32[]{:S(2)}, u32[]{:S(2)}) %all-to-all-start.1) | async-done | bytes 2359328 | tf_op jit(solution)/shard_map/all_to_all | solution.py:451
  117.7 5.9 %experts.1 = bf16[8,96,1536]{2,1,0:T(8,128)(2,1)} custom-call(bf16[8,96,1536]{2,1,0:T(8,128)(2,1)S(1)} %all-to-all-done.1.rows_ref, bf16[4,2,1536,256]{3,2,1,0:T(8,128)(2,1)} %bitcast.51, bf16[4,256,1536]{2,1,0:T(8,128)(2,1)} %down_hbm.1), custom_call_target="tpu_custom_call" | custom-call | flops 1811939328 | bytes 14680064 | tf_op jit(solution)/shard_map/experts/pallas_call | solution.py:601
  123.6 5.1 %all-to-all-start.2 = ((bf16[8,96,1536]{2,1,0:T(8,128)(2,1)}), bf16[8,96,1536]{2,1,0:T(8,128)(2,1)S(1)}, u32[]{:S(2)}, u32[]{:S(2)}) async-start(bf16[8,96,1536]{2,1,0:T(8,128)(2,1)} %experts.1), calls=%async_computation.2 | async-start | bytes 4718592 | tf_op jit(solution)/shard_map/all_to_all | solution.py:451
  132.2 24.4 %all-to-all-done.2 = bf16[8,96,1536]{2,1,0:T(8,128)(2,1)S(1)} async-done(((bf16[8,96,1536]{2,1,0:T(8,128)(2,1)}), bf16[8,96,1536]{2,1,0:T(8,128)(2,1)S(1)}, u32[]{:S(2)}, u32[]{:S(2)}) %all-to-all-start.2) | async-done | bytes 2359328 | tf_op jit(solution)/shard_map/all_to_all | solution.py:451
  156.7 2.2 %combine.1 = (bf16[64,1536]{1,0:T(8,128)(2,1)S(1)}, bf16[64,1536]{1,0:T(8,128)(2,1)S(1)}, bf16[64,1536]{1,0:T(8,128)(2,1)S(1)}, bf16[64,1536]{1,0:T(8,128)(2,1)S(1)}) custom-call(s32[1]{0:T(128)} %bitcast.z_ref, bf16[256,768]{1,0:T(8,128)(2,1)} %copy-done.3, bf16[768,1536]{1,0:T(8,128)(2,1)S(1)} %bitcast.49, bf16[256,1536]{1,0:T(8,128)(2,1)} %copy-done.1), custom_call_target="tpu_custom_call" | custom-call | flops 603979776 | bytes 3145728 | tf_op jit(solution)/shard_map/combine/pallas_call | solution.py:632
  159.8 4.2 %collective-permute-start.18 = (bf16[64,1536]{1,0:T(8,128)(2,1)S(1)}, bf16[64,1536]{1,0:T(8,128)(2,1)S(1)}, u32[]{:S(2)}, u32[]{:S(2)}) collective-permute-start(bf16[64,1536]{1,0:T(8,128)(2,1)S(1)} %get-tuple-element.86), channel_id=1, source_target_pairs={{0,16},{1,17},{2,18},{3,19},{4,20},{5,21},{6,22},{7,23},{8,24},{9,... | collective-permute-start | bytes 589832 | tf_op jit(solution)/shard_map/ppermute | solution.py:481
  167.9 8.9 %collective-permute-done.18.refs_2_ = bf16[64,1536]{1,0:T(8,128)(2,1)S(1)} collective-permute-done((bf16[64,1536]{1,0:T(8,128)(2,1)S(1)}, bf16[64,1536]{1,0:T(8,128)(2,1)S(1)}, u32[]{:S(2)}, u32[]{:S(2)}) %collective-permute-start.18) | collective-permute-done | bytes 196640 | tf_op jit(solution)/shard_map/ppermute | solution.py:481
  176.8 3.8 %collective-permute-done.19.refs_3_ = bf16[64,1536]{1,0:T(8,128)(2,1)S(1)} collective-permute-done((bf16[64,1536]{1,0:T(8,128)(2,1)S(1)}, bf16[64,1536]{1,0:T(8,128)(2,1)S(1)}, u32[]{:S(2)}, u32[]{:S(2)}) %collective-permute-start.19) | collective-permute-done | bytes 196640 | tf_op jit(solution)/shard_map/ppermute | solution.py:481
  (79 shorter events, 36.6 us)
Async XLA Ops:
  7.2 50.1 %all-gather.4.cloned.1.call-start = ((), (), s32[]{:S(2)}) async-start(), calls=%async_computation.3 | async-start | bytes 1327104 | tf_op jit(solution)/shard_map/all_gather | solution.py:465
  7.9 96.3 %all-gather.6.cloned.1.call-start = ((), (), s32[]{:S(2)}) async-start(), calls=%async_computation.4 | async-start | bytes 2654208 | tf_op jit(solution)/shard_map/all_gather | solution.py:510
  9.5 17.4 %collective-permute-start.3 = (bf16[64,1024]{1,0:T(8,128)(2,1)}, bf16[64,1024]{1,0:T(8,128)(2,1)S(1)}, u32[]{:S(2)}, u32[]{:S(2)}) collective-permute-start(bf16[64,1024]{1,0:T(8,128)(2,1)} %join.1.own_ref), channel_id=1, source_target_pairs={{0,1},{1,2},{2,3},{3,4},{4,5},{5,6},{6,7},{7,8},{8,9},{9,10},{10,1... | collective-permute-start | bytes 393224 | tf_op jit(solution)/shard_map/ppermute | solution.py:28
  11.4 15.5 %collective-permute-start.2 = (bf16[64,1024]{1,0:T(8,128)(2,1)}, bf16[64,1024]{1,0:T(8,128)(2,1)S(1)}, u32[]{:S(2)}, u32[]{:S(2)}) collective-permute-start(bf16[64,1024]{1,0:T(8,128)(2,1)} %join.1.own_ref), channel_id=1, source_target_pairs={{0,2},{1,3},{2,4},{3,5},{4,6},{5,7},{6,8},{7,9},{8,10},{9,11},{10,... | collective-permute-start | bytes 393224 | tf_op jit(solution)/shard_map/ppermute | solution.py:28
  14.8 12.1 %collective-permute-start.1 = (bf16[64,1024]{1,0:T(8,128)(2,1)}, bf16[64,1024]{1,0:T(8,128)(2,1)S(1)}, u32[]{:S(2)}, u32[]{:S(2)}) collective-permute-start(bf16[64,1024]{1,0:T(8,128)(2,1)} %join.1.own_ref), channel_id=1, source_target_pairs={{0,3},{1,4},{2,5},{3,6},{4,7},{5,8},{6,9},{7,10},{8,11},{9,12},{10... | collective-permute-start | bytes 393224 | tf_op jit(solution)/shard_map/ppermute | solution.py:28
  19.1 8.0 %collective-permute-start = (bf16[64,1024]{1,0:T(8,128)(2,1)}, bf16[64,1024]{1,0:T(8,128)(2,1)S(1)}, u32[]{:S(2)}, u32[]{:S(2)}) collective-permute-start(bf16[64,1024]{1,0:T(8,128)(2,1)} %join.1.own_ref), channel_id=1, source_target_pairs={{0,4},{1,5},{2,6},{3,7},{4,8},{5,9},{6,10},{7,11},{8,12},{9,13},{1... | collective-permute-start | bytes 393224 | tf_op jit(solution)/shard_map/ppermute | solution.py:28
  32.2 19.9 %collective-permute-start.4 = (bf16[64,2048]{1,0:T(8,128)(2,1)}, bf16[64,2048]{1,0:T(8,128)(2,1)S(1)}, u32[]{:S(2)}, u32[]{:S(2)}) collective-permute-start(bf16[64,2048]{1,0:T(8,128)(2,1)} %get-tuple-element.52), channel_id=1, source_target_pairs={{0,8},{1,9},{2,10},{3,11},{4,12},{5,13},{6,14},{7,15},{8,16},{9,17... | collective-permute-start | bytes 786440 | tf_op jit(solution)/shard_map/ppermute | solution.py:481
  33.9 21.6 %collective-permute-start.5 = (bf16[64,2048]{1,0:T(8,128)(2,1)}, bf16[64,2048]{1,0:T(8,128)(2,1)S(1)}, u32[]{:S(2)}, u32[]{:S(2)}) collective-permute-start(bf16[64,2048]{1,0:T(8,128)(2,1)} %get-tuple-element.53), channel_id=1, source_target_pairs={{0,16},{1,17},{2,18},{3,19},{4,20},{5,21},{6,22},{7,23},{8,24},{9,... | collective-permute-start | bytes 786440 | tf_op jit(solution)/shard_map/ppermute | solution.py:481
  34.9 22.4 %collective-permute-start.6 = (bf16[64,2048]{1,0:T(8,128)(2,1)}, bf16[64,2048]{1,0:T(8,128)(2,1)S(1)}, u32[]{:S(2)}, u32[]{:S(2)}) collective-permute-start(bf16[64,2048]{1,0:T(8,128)(2,1)} %get-tuple-element.54), channel_id=1, source_target_pairs={{0,24},{1,25},{2,26},{3,27},{4,28},{5,29},{6,30},{7,31},{8,0},{9,1... | collective-permute-start | bytes 786440 | tf_op jit(solution)/shard_map/ppermute | solution.py:481
  60.1 21.2 %all-to-all-start = ((bf16[4,256,384]{2,1,0:T(8,128)(2,1)}), bf16[4,256,384]{2,1,0:T(8,128)(2,1)S(1)}, u32[]{:S(2)}, u32[]{:S(2)}) async-start(bf16[4,256,384]{2,1,0:T(8,128)(2,1)} %get-tuple-element.59), calls=%async_computation | async-start | bytes 1572864 | tf_op jit(solution)/shard_map/all_to_all | solution.py:451
  66.6 9.8 %collective-permute-start.12 = (bf16[4,32,4,128]{3,2,1,0:T(4,128)(2,1)S(1)}, bf16[4,32,4,128]{3,2,1,0:T(4,128)(2,1)S(1)}, u32[]{:S(2)}, u32[]{:S(2)}) collective-permute-start(bf16[4,32,4,128]{3,2,1,0:T(4,128)(2,1)S(1)} %get-tuple-element.93), channel_id=1, source_target_pairs={{0,6},{1,7},{2,0},{3,1},{4,2},{5,3},{6,4},{7,5},{8,14},{9,15},{10,... | collective-permute-start | bytes 393224 | tf_op jit(solution)/shard_map/ppermute | solution.py:530
  67.7 15.8 %collective-permute-start.11 = (bf16[4,32,4,128]{3,2,1,0:T(4,128)(2,1)S(1)}, bf16[4,32,4,128]{3,2,1,0:T(4,128)(2,1)S(1)}, u32[]{:S(2)}, u32[]{:S(2)}) collective-permute-start(bf16[4,32,4,128]{3,2,1,0:T(4,128)(2,1)S(1)} %get-tuple-element.94), channel_id=1, source_target_pairs={{0,5},{1,6},{2,7},{3,0},{4,1},{5,2},{6,3},{7,4},{8,13},{9,14},{10,... | collective-permute-start | bytes 393224 | tf_op jit(solution)/shard_map/ppermute | solution.py:530
  69.6 13.9 %collective-permute-start.10 = (bf16[4,32,4,128]{3,2,1,0:T(4,128)(2,1)S(1)}, bf16[4,32,4,128]{3,2,1,0:T(4,128)(2,1)S(1)}, u32[]{:S(2)}, u32[]{:S(2)}) collective-permute-start(bf16[4,32,4,128]{3,2,1,0:T(4,128)(2,1)S(1)} %get-tuple-element.95), channel_id=1, source_target_pairs={{0,4},{1,5},{2,6},{3,7},{4,0},{5,1},{6,2},{7,3},{8,12},{9,13},{10,... | collective-permute-start | bytes 393224 | tf_op jit(solution)/shard_map/ppermute | solution.py:530
  69.7 13.7 %collective-permute-start.9 = (bf16[4,32,4,128]{3,2,1,0:T(4,128)(2,1)S(1)}, bf16[4,32,4,128]{3,2,1,0:T(4,128)(2,1)S(1)}, u32[]{:S(2)}, u32[]{:S(2)}) collective-permute-start(bf16[4,32,4,128]{3,2,1,0:T(4,128)(2,1)S(1)} %get-tuple-element.96), channel_id=1, source_target_pairs={{0,3},{1,4},{2,5},{3,6},{4,7},{5,0},{6,1},{7,2},{8,11},{9,12},{10,... | collective-permute-start | bytes 393224 | tf_op jit(solution)/shard_map/ppermute | solution.py:530
  72.1 11.4 %collective-permute-start.8 = (bf16[4,32,4,128]{3,2,1,0:T(4,128)(2,1)S(1)}, bf16[4,32,4,128]{3,2,1,0:T(4,128)(2,1)S(1)}, u32[]{:S(2)}, u32[]{:S(2)}) collective-permute-start(bf16[4,32,4,128]{3,2,1,0:T(4,128)(2,1)S(1)} %get-tuple-element.97), channel_id=1, source_target_pairs={{0,2},{1,3},{2,4},{3,5},{4,6},{5,7},{6,0},{7,1},{8,10},{9,11},{10,... | collective-permute-start | bytes 393224 | tf_op jit(solution)/shard_map/ppermute | solution.py:530
  76.4 7.2 %collective-permute-start.7 = (bf16[4,32,4,128]{3,2,1,0:T(4,128)(2,1)S(1)}, bf16[4,32,4,128]{3,2,1,0:T(4,128)(2,1)S(1)}, u32[]{:S(2)}, u32[]{:S(2)}) collective-permute-start(bf16[4,32,4,128]{3,2,1,0:T(4,128)(2,1)S(1)} %get-tuple-element.98), channel_id=1, source_target_pairs={{0,1},{1,2},{2,3},{3,4},{4,5},{5,6},{6,7},{7,0},{8,9},{9,10},{10,1... | collective-permute-start | bytes 393224 | tf_op jit(solution)/shard_map/ppermute | solution.py:530
  84.3 33.4 %all-to-all-start.1 = ((bf16[8,96,1536]{2,1,0:T(8,128)(2,1)}), bf16[8,96,1536]{2,1,0:T(8,128)(2,1)S(1)}, u32[]{:S(2)}, u32[]{:S(2)}) async-start(bf16[8,96,1536]{2,1,0:T(8,128)(2,1)} %pick.1), calls=%async_computation.1 | async-start | bytes 4718592 | tf_op jit(solution)/shard_map/all_to_all | solution.py:451
  92.6 31.0 %collective-permute-start.14 = (bf16[8,32,4,128]{3,2,1,0:T(4,128)(2,1)}, bf16[8,32,4,128]{3,2,1,0:T(4,128)(2,1)}, u32[]{:S(2)}, u32[]{:S(2)}) collective-permute-start(bf16[8,32,4,128]{3,2,1,0:T(4,128)(2,1)} %get-tuple-element.79), channel_id=1, source_target_pairs={{0,8},{1,9},{2,10},{3,11},{4,12},{5,13},{6,14},{7,15},{8,16},{9,17... | collective-permute-start | bytes 786440 | tf_op jit(solution)/shard_map/ppermute | solution.py:588
  93.4 30.2 %collective-permute-start.15 = (bf16[8,32,4,128]{3,2,1,0:T(4,128)(2,1)}, bf16[8,32,4,128]{3,2,1,0:T(4,128)(2,1)}, u32[]{:S(2)}, u32[]{:S(2)}) collective-permute-start(bf16[8,32,4,128]{3,2,1,0:T(4,128)(2,1)} %get-tuple-element.80), channel_id=1, source_target_pairs={{0,16},{1,17},{2,18},{3,19},{4,20},{5,21},{6,22},{7,23},{8,24},{9,... | collective-permute-start | bytes 786440 | tf_op jit(solution)/shard_map/ppermute | solution.py:588
  97.6 26.0 %collective-permute-start.16 = (bf16[8,32,4,128]{3,2,1,0:T(4,128)(2,1)S(1)}, bf16[8,32,4,128]{3,2,1,0:T(4,128)(2,1)}, u32[]{:S(2)}, u32[]{:S(2)}) collective-permute-start(bf16[8,32,4,128]{3,2,1,0:T(4,128)(2,1)S(1)} %get-tuple-element.81), channel_id=1, source_target_pairs={{0,24},{1,25},{2,26},{3,27},{4,28},{5,29},{6,30},{7,31},{8,0},{9,1... | collective-permute-start | bytes 786440 | tf_op jit(solution)/shard_map/ppermute | solution.py:588
  123.6 33.0 %all-to-all-start.2 = ((bf16[8,96,1536]{2,1,0:T(8,128)(2,1)}), bf16[8,96,1536]{2,1,0:T(8,128)(2,1)S(1)}, u32[]{:S(2)}, u32[]{:S(2)}) async-start(bf16[8,96,1536]{2,1,0:T(8,128)(2,1)} %experts.1), calls=%async_computation.2 | async-start | bytes 4718592 | tf_op jit(solution)/shard_map/all_to_all | solution.py:451
  158.9 9.0 %collective-permute-start.17 = (bf16[64,1536]{1,0:T(8,128)(2,1)S(1)}, bf16[64,1536]{1,0:T(8,128)(2,1)S(1)}, u32[]{:S(2)}, u32[]{:S(2)}) collective-permute-start(bf16[64,1536]{1,0:T(8,128)(2,1)S(1)} %get-tuple-element.85), channel_id=1, source_target_pairs={{0,8},{1,9},{2,10},{3,11},{4,12},{5,13},{6,14},{7,15},{8,16},{9,17... | collective-permute-start | bytes 589832 | tf_op jit(solution)/shard_map/ppermute | solution.py:481
  159.8 17.0 %collective-permute-start.18 = (bf16[64,1536]{1,0:T(8,128)(2,1)S(1)}, bf16[64,1536]{1,0:T(8,128)(2,1)S(1)}, u32[]{:S(2)}, u32[]{:S(2)}) collective-permute-start(bf16[64,1536]{1,0:T(8,128)(2,1)S(1)} %get-tuple-element.86), channel_id=1, source_target_pairs={{0,16},{1,17},{2,18},{3,19},{4,20},{5,21},{6,22},{7,23},{8,24},{9,... | collective-permute-start | bytes 589832 | tf_op jit(solution)/shard_map/ppermute | solution.py:481
  163.9 16.7 %collective-permute-start.19 = (bf16[64,1536]{1,0:T(8,128)(2,1)S(1)}, bf16[64,1536]{1,0:T(8,128)(2,1)S(1)}, u32[]{:S(2)}, u32[]{:S(2)}) collective-permute-start(bf16[64,1536]{1,0:T(8,128)(2,1)S(1)} %get-tuple-element.87), channel_id=1, source_target_pairs={{0,24},{1,25},{2,26},{3,27},{4,28},{5,29},{6,30},{7,31},{8,0},{9,1... | collective-permute-start | bytes 589832 | tf_op jit(solution)/shard_map/ppermute | solution.py:481
  (18 other events, 106.2 us)
Sparse Core Ops, SparseCore 0:
  9.9 30.5 all-gather.3
  42.4 29.0 all-gather.5

commit v11 on v7

--- a/solution.py
+++ b/solution.py
@@ -174,10 +174,10 @@
     first_ref,
     lengths_ref,
     q_ref,
+    k1_ref,
+    k2_ref,
+    k3_ref,
     k4_ref,
-    k3_ref,
-    k2_ref,
-    k1_ref,
     own_ref,
     residual_ref,
     info_ref,
@@ -460,7 +460,7 @@
         compiler_params=params(),
         name="join",
     )(in_hbm(key_vectors), in_hbm(value_vectors))
-    behind = [from_behind(own_kv, "seq", offset) for offset in range(REACH, 0, -1)]
+    behind = [from_behind(own_kv, "seq", offset) for offset in range(1, REACH + 1)]
 
     turned_weight = lax.all_gather(
         out_weight.T, "seq", axis=0, tiled=True, axis_index_groups=planes

time: 188 us -> 188 us (level)
  starting transfers between devices: 50.1 us -> 45.4 us
  waiting for transfers between devices: 78 us -> 82.4 us
    ppermute x6, waiting for transfers between devices: 33.6 us -> 36.2 us  [along_z(): lax.ppermute(arrays[step], 'seq', z_pairs[step])]
    all_to_all x3, waiting for transfers between devices: 40.1 us -> 42 us  [exchange(): lax.all_to_all(array, 'seq', split_axis=0, concat_axis=0, tiled=True, axi...]
where the time goes in v11:
time: 188 us; the launch traced here: 187 us
  waiting for transfers between devices  82.4 us (44%)
  starting transfers between devices  45.4 us (24%)
  Pallas kernels  28.6 us (15%)
  between operations  14.3 us (8%)
  local copies, waits for them, and re-layouts  13 us (7%)
  other arithmetic  3.57 us (2%)
    all_to_all x3, waiting for transfers between devices, exchange(): lax.all_to_all(array, 'seq', split_axis=0, concat_axis=0, tiled=True, axi...  42 us
    ppermute x6, waiting for transfers between devices, along_z(): lax.ppermute(arrays[step], 'seq', z_pairs[step])  36.2 us
    all_to_all x3, starting transfers between devices, exchange(): lax.all_to_all(array, 'seq', split_axis=0, concat_axis=0, tiled=True, axi...  13.5 us
    ppermute x4, starting transfers between devices, from_behind(): return lax.ppermute(shard, axis, pairs)  12 us
    ppermute x6, starting transfers between devices, along_z(): lax.ppermute(arrays[step], 'seq', z_pairs[step])  8.99 us
    optimization_barrier x1, local copies, waits for them, and re-layouts, shards(): lax.optimization_barrier((gathered, cache_blocks, expert_gate_up))  6.31 us
    pallas_call x1, Pallas kernels, shards(): pl.pallas_call(experts_kernel, out_shape=pltpu.HBM((PLANE, picked, width)...  5.88 us
    ppermute x7, starting transfers between devices, shards(): piece = lax.ppermute(piece, 'seq', pairs)  5.56 us
  transfers between devices with their start and end apart: 25, of which 10 were waited for; matrix products, arithmetic and copies ran while one was open for 6% of the time, Pallas kernels for 14%

profile of v11, /device:TPU:10, one launch (start us, length us, event | category | flops | bytes accessed | tf_op | source)
XLA Modules:
  0.0 187.3 jit_solution(11929557679001789209)
XLA Ops:
  9.5 3.4 %collective-permute-start.3 = (bf16[64,1024]{1,0:T(8,128)(2,1)}, bf16[64,1024]{1,0:T(8,128)(2,1)S(1)}, u32[]{:S(2)}, u32[]{:S(2)}) collective-permute-start(bf16[64,1024]{1,0:T(8,128)(2,1)} %join.1.own_ref), channel_id=1, source_target_pairs={{0,4},{1,5},{2,6},{3,7},{4,8},{5,9},{6,10},{7,11},{8,12},{9,13},{1... | collective-permute-start | bytes 393224 | tf_op jit(solution)/shard_map/ppermute | solution.py:28
  12.9 2.6 %collective-permute-start.2 = (bf16[64,1024]{1,0:T(8,128)(2,1)}, bf16[64,1024]{1,0:T(8,128)(2,1)S(1)}, u32[]{:S(2)}, u32[]{:S(2)}) collective-permute-start(bf16[64,1024]{1,0:T(8,128)(2,1)} %join.1.own_ref), channel_id=1, source_target_pairs={{0,3},{1,4},{2,5},{3,6},{4,7},{5,8},{6,9},{7,10},{8,11},{9,12},{10... | collective-permute-start | bytes 393224 | tf_op jit(solution)/shard_map/ppermute | solution.py:28
  15.5 3.4 %collective-permute-start.1 = (bf16[64,1024]{1,0:T(8,128)(2,1)}, bf16[64,1024]{1,0:T(8,128)(2,1)S(1)}, u32[]{:S(2)}, u32[]{:S(2)}) collective-permute-start(bf16[64,1024]{1,0:T(8,128)(2,1)} %join.1.own_ref), channel_id=1, source_target_pairs={{0,2},{1,3},{2,4},{3,5},{4,6},{5,7},{6,8},{7,9},{8,10},{9,11},{10,... | collective-permute-start | bytes 393224 | tf_op jit(solution)/shard_map/ppermute | solution.py:28
  18.9 2.6 %collective-permute-start = (bf16[64,1024]{1,0:T(8,128)(2,1)}, bf16[64,1024]{1,0:T(8,128)(2,1)S(1)}, u32[]{:S(2)}, u32[]{:S(2)}) collective-permute-start(bf16[64,1024]{1,0:T(8,128)(2,1)} %join.1.own_ref), channel_id=1, source_target_pairs={{0,1},{1,2},{2,3},{3,4},{4,5},{5,6},{6,7},{7,8},{8,9},{9,10},{10,1... | collective-permute-start | bytes 393224 | tf_op jit(solution)/shard_map/ppermute | solution.py:28
  21.5 2.6 %route.1.info_ref = bf16[64,128]{1,0:T(8,128)(2,1)} custom-call(s32[1]{0:T(128)} %bitcast.z_ref, s32[6,64]{1,0:T(8,128)} %bitcast.56, f32[6,64]{1,0:T(8,128)} %bitcast.57), custom_call_target="tpu_custom_call" | custom-call | flops 1048576 | bytes 1048576 | tf_op jit(solution)/shard_map/route/pallas_call | solution.py:468
  26.6 3.8 %attention.1 = (bf16[64,2048]{1,0:T(8,128)(2,1)}, bf16[64,2048]{1,0:T(8,128)(2,1)}, bf16[64,2048]{1,0:T(8,128)(2,1)}, bf16[64,2048]{1,0:T(8,128)(2,1)}) custom-call(s32[1]{0:T(128)} %bitcast.z_ref, s32[1]{0:T(128)} %bitcast.1.first_ref, s32[16]{0:T(128)} %lengths_ref.1, bf16[64,1536]{1,0:T(8,128)(2,1)} %q_ref.1, bf16[64,1024]{1,0:T(8,128)(2,1)} %copy-done.10, ...), custom_call_target="tpu_custom_call" | custom-call | flops 125829120 | bytes 3145728 | tf_op jit(solution)/shard_map/attention/pallas_call | solution.py:499
  34.0 5.8 %collective-permute-done.4.refs_1_ = bf16[64,2048]{1,0:T(8,128)(2,1)S(1)} collective-permute-done((bf16[64,2048]{1,0:T(8,128)(2,1)}, bf16[64,2048]{1,0:T(8,128)(2,1)S(1)}, u32[]{:S(2)}, u32[]{:S(2)}) %collective-permute-start.4) | collective-permute-done | bytes 262176 | tf_op jit(solution)/shard_map/ppermute | solution.py:481
  39.8 16.0 %collective-permute-done.5.refs_2_ = bf16[64,2048]{1,0:T(8,128)(2,1)S(1)} collective-permute-done((bf16[64,2048]{1,0:T(8,128)(2,1)}, bf16[64,2048]{1,0:T(8,128)(2,1)S(1)}, u32[]{:S(2)}, u32[]{:S(2)}) %collective-permute-start.5) | collective-permute-done | bytes 262176 | tf_op jit(solution)/shard_map/ppermute | solution.py:481
  57.5 2.8 %project.1 = (bf16[4,256,384]{2,1,0:T(8,128)(2,1)}, bf16[256,128]{1,0:T(8,128)(2,1)S(1)}) custom-call(s32[1]{0:T(128)} %bitcast.z_ref, bf16[64,2048]{1,0:T(8,128)(2,1)} %get-tuple-element.55.refs_0_, bf16[64,2048]{1,0:T(8,128)(2,1)S(1)} %collective-permute-done.4.refs_1_, bf16[64,2048]{1,0:T(8,128)(2,1)S(1)} %collective-permute-done.5.refs_2_, ...), custom_call_target="tpu_custom_call" | custom-call | flops 301989888 | bytes 3145728 | tf_op jit(solution)/shard_map/project/pallas_call | solution.py:534
  60.3 4.5 %all-to-all-start = ((bf16[4,256,384]{2,1,0:T(8,128)(2,1)}), bf16[4,256,384]{2,1,0:T(8,128)(2,1)S(1)}, u32[]{:S(2)}, u32[]{:S(2)}) async-start(bf16[4,256,384]{2,1,0:T(8,128)(2,1)} %get-tuple-element.59), calls=%async_computation | async-start | bytes 1572864 | tf_op jit(solution)/shard_map/all_to_all | solution.py:451
  68.7 2.4 %collective-permute-start.9 = (bf16[4,32,4,128]{3,2,1,0:T(4,128)(2,1)S(1)}, bf16[4,32,4,128]{3,2,1,0:T(4,128)(2,1)S(1)}, u32[]{:S(2)}, u32[]{:S(2)}) collective-permute-start(bf16[4,32,4,128]{3,2,1,0:T(4,128)(2,1)S(1)} %get-tuple-element.96), channel_id=1, source_target_pairs={{0,3},{1,4},{2,5},{3,6},{4,7},{5,0},{6,1},{7,2},{8,11},{9,12},{10,... | collective-permute-start | bytes 393224 | tf_op jit(solution)/shard_map/ppermute | solution.py:530
  71.7 3.3 %collective-permute-done.12.refs_6_ = bf16[4,32,4,128]{3,2,1,0:T(4,128)(2,1)S(1)} collective-permute-done((bf16[4,32,4,128]{3,2,1,0:T(4,128)(2,1)S(1)}, bf16[4,32,4,128]{3,2,1,0:T(4,128)(2,1)S(1)}, u32[]{:S(2)}, u32[]{:S(2)}) %collective-permute-start.12) | collective-permute-done | bytes 131104 | tf_op jit(solution)/shard_map/ppermute | solution.py:530
  77.7 4.2 %all-to-all-done.mixed_ref = bf16[4,256,384]{2,1,0:T(8,128)(2,1)S(1)} async-done(((bf16[4,256,384]{2,1,0:T(8,128)(2,1)}), bf16[4,256,384]{2,1,0:T(8,128)(2,1)S(1)}, u32[]{:S(2)}, u32[]{:S(2)}) %all-to-all-start) | async-done | bytes 786464 | tf_op jit(solution)/shard_map/all_to_all | solution.py:451
  84.9 3.9 %all-to-all-start.1 = ((bf16[8,96,1536]{2,1,0:T(8,128)(2,1)}), bf16[8,96,1536]{2,1,0:T(8,128)(2,1)S(1)}, u32[]{:S(2)}, u32[]{:S(2)}) async-start(bf16[8,96,1536]{2,1,0:T(8,128)(2,1)} %pick.1), calls=%async_computation.1 | async-start | bytes 4718592 | tf_op jit(solution)/shard_map/all_to_all | solution.py:451
  92.8 4.2 %collective-permute-start.15 = (bf16[8,32,4,128]{3,2,1,0:T(4,128)(2,1)}, bf16[8,32,4,128]{3,2,1,0:T(4,128)(2,1)}, u32[]{:S(2)}, u32[]{:S(2)}) collective-permute-start(bf16[8,32,4,128]{3,2,1,0:T(4,128)(2,1)} %get-tuple-element.80), channel_id=1, source_target_pairs={{0,16},{1,17},{2,18},{3,19},{4,20},{5,21},{6,22},{7,23},{8,24},{9,... | collective-permute-start | bytes 786440 | tf_op jit(solution)/shard_map/ppermute | solution.py:588
  97.0 6.3 %copy.35 = bf16[4,1536,2,256]{3,1,2,0:T(8,128)(2,1)} copy(bf16[4,1536,2,256]{3,2,1,0:T(2,128)(2,1)} %param.26) | data formatting | bytes 12582912 | tf_op jit(solution)/shard_map/optimization_barrier | solution.py:512
  103.3 13.5 %all-to-all-done.1.rows_ref = bf16[8,96,1536]{2,1,0:T(8,128)(2,1)S(1)} async-done(((bf16[8,96,1536]{2,1,0:T(8,128)(2,1)}), bf16[8,96,1536]{2,1,0:T(8,128)(2,1)S(1)}, u32[]{:S(2)}, u32[]{:S(2)}) %all-to-all-start.1) | async-done | bytes 2359328 | tf_op jit(solution)/shard_map/all_to_all | solution.py:451
  116.8 5.9 %experts.1 = bf16[8,96,1536]{2,1,0:T(8,128)(2,1)} custom-call(bf16[8,96,1536]{2,1,0:T(8,128)(2,1)S(1)} %all-to-all-done.1.rows_ref, bf16[4,2,1536,256]{3,2,1,0:T(8,128)(2,1)} %bitcast.51, bf16[4,256,1536]{2,1,0:T(8,128)(2,1)} %down_hbm.1), custom_call_target="tpu_custom_call" | custom-call | flops 1811939328 | bytes 14680064 | tf_op jit(solution)/shard_map/experts/pallas_call | solution.py:601
  122.7 5.1 %all-to-all-start.2 = ((bf16[8,96,1536]{2,1,0:T(8,128)(2,1)}), bf16[8,96,1536]{2,1,0:T(8,128)(2,1)S(1)}, u32[]{:S(2)}, u32[]{:S(2)}) async-start(bf16[8,96,1536]{2,1,0:T(8,128)(2,1)} %experts.1), calls=%async_computation.2 | async-start | bytes 4718592 | tf_op jit(solution)/shard_map/all_to_all | solution.py:451
  131.3 24.4 %all-to-all-done.2 = bf16[8,96,1536]{2,1,0:T(8,128)(2,1)S(1)} async-done(((bf16[8,96,1536]{2,1,0:T(8,128)(2,1)}), bf16[8,96,1536]{2,1,0:T(8,128)(2,1)S(1)}, u32[]{:S(2)}, u32[]{:S(2)}) %all-to-all-start.2) | async-done | bytes 2359328 | tf_op jit(solution)/shard_map/all_to_all | solution.py:451
  155.7 2.2 %combine.1 = (bf16[64,1536]{1,0:T(8,128)(2,1)S(1)}, bf16[64,1536]{1,0:T(8,128)(2,1)S(1)}, bf16[64,1536]{1,0:T(8,128)(2,1)S(1)}, bf16[64,1536]{1,0:T(8,128)(2,1)S(1)}) custom-call(s32[1]{0:T(128)} %bitcast.z_ref, bf16[256,768]{1,0:T(8,128)(2,1)} %copy-done.2, bf16[768,1536]{1,0:T(8,128)(2,1)S(1)} %bitcast.49, bf16[256,1536]{1,0:T(8,128)(2,1)} %copy-done.1), custom_call_target="tpu_custom_call" | custom-call | flops 603979776 | bytes 3145728 | tf_op jit(solution)/shard_map/combine/pallas_call | solution.py:632
  158.8 4.2 %collective-permute-start.18 = (bf16[64,1536]{1,0:T(8,128)(2,1)S(1)}, bf16[64,1536]{1,0:T(8,128)(2,1)S(1)}, u32[]{:S(2)}, u32[]{:S(2)}) collective-permute-start(bf16[64,1536]{1,0:T(8,128)(2,1)S(1)} %get-tuple-element.86), channel_id=1, source_target_pairs={{0,16},{1,17},{2,18},{3,19},{4,20},{5,21},{6,22},{7,23},{8,24},{9,... | collective-permute-start | bytes 589832 | tf_op jit(solution)/shard_map/ppermute | solution.py:481
  166.9 8.9 %collective-permute-done.18.refs_2_ = bf16[64,1536]{1,0:T(8,128)(2,1)S(1)} collective-permute-done((bf16[64,1536]{1,0:T(8,128)(2,1)S(1)}, bf16[64,1536]{1,0:T(8,128)(2,1)S(1)}, u32[]{:S(2)}, u32[]{:S(2)}) %collective-permute-start.18) | collective-permute-done | bytes 196640 | tf_op jit(solution)/shard_map/ppermute | solution.py:481
  175.8 3.9 %collective-permute-done.19.refs_3_ = bf16[64,1536]{1,0:T(8,128)(2,1)S(1)} collective-permute-done((bf16[64,1536]{1,0:T(8,128)(2,1)S(1)}, bf16[64,1536]{1,0:T(8,128)(2,1)S(1)}, u32[]{:S(2)}, u32[]{:S(2)}) %collective-permute-start.19) | collective-permute-done | bytes 196640 | tf_op jit(solution)/shard_map/ppermute | solution.py:481
  (83 shorter events, 33.3 us)
Async XLA Ops:
  7.2 50.3 %all-gather.4.cloned.1.call-start = ((), (), s32[]{:S(2)}) async-start(), calls=%async_computation.3 | async-start | bytes 1327104 | tf_op jit(solution)/shard_map/all_gather | solution.py:465
  7.9 95.4 %all-gather.6.cloned.1.call-start = ((), (), s32[]{:S(2)}) async-start(), calls=%async_computation.4 | async-start | bytes 2654208 | tf_op jit(solution)/shard_map/all_gather | solution.py:510
  9.5 16.3 %collective-permute-start.3 = (bf16[64,1024]{1,0:T(8,128)(2,1)}, bf16[64,1024]{1,0:T(8,128)(2,1)S(1)}, u32[]{:S(2)}, u32[]{:S(2)}) collective-permute-start(bf16[64,1024]{1,0:T(8,128)(2,1)} %join.1.own_ref), channel_id=1, source_target_pairs={{0,4},{1,5},{2,6},{3,7},{4,8},{5,9},{6,10},{7,11},{8,12},{9,13},{1... | collective-permute-start | bytes 393224 | tf_op jit(solution)/shard_map/ppermute | solution.py:28
  12.9 12.9 %collective-permute-start.2 = (bf16[64,1024]{1,0:T(8,128)(2,1)}, bf16[64,1024]{1,0:T(8,128)(2,1)S(1)}, u32[]{:S(2)}, u32[]{:S(2)}) collective-permute-start(bf16[64,1024]{1,0:T(8,128)(2,1)} %join.1.own_ref), channel_id=1, source_target_pairs={{0,3},{1,4},{2,5},{3,6},{4,7},{5,8},{6,9},{7,10},{8,11},{9,12},{10... | collective-permute-start | bytes 393224 | tf_op jit(solution)/shard_map/ppermute | solution.py:28
  15.5 10.3 %collective-permute-start.1 = (bf16[64,1024]{1,0:T(8,128)(2,1)}, bf16[64,1024]{1,0:T(8,128)(2,1)S(1)}, u32[]{:S(2)}, u32[]{:S(2)}) collective-permute-start(bf16[64,1024]{1,0:T(8,128)(2,1)} %join.1.own_ref), channel_id=1, source_target_pairs={{0,2},{1,3},{2,4},{3,5},{4,6},{5,7},{6,8},{7,9},{8,10},{9,11},{10,... | collective-permute-start | bytes 393224 | tf_op jit(solution)/shard_map/ppermute | solution.py:28
  18.9 7.1 %collective-permute-start = (bf16[64,1024]{1,0:T(8,128)(2,1)}, bf16[64,1024]{1,0:T(8,128)(2,1)S(1)}, u32[]{:S(2)}, u32[]{:S(2)}) collective-permute-start(bf16[64,1024]{1,0:T(8,128)(2,1)} %join.1.own_ref), channel_id=1, source_target_pairs={{0,1},{1,2},{2,3},{3,4},{4,5},{5,6},{6,7},{7,8},{8,9},{9,10},{10,1... | collective-permute-start | bytes 393224 | tf_op jit(solution)/shard_map/ppermute | solution.py:28
  30.4 9.4 %collective-permute-start.4 = (bf16[64,2048]{1,0:T(8,128)(2,1)}, bf16[64,2048]{1,0:T(8,128)(2,1)S(1)}, u32[]{:S(2)}, u32[]{:S(2)}) collective-permute-start(bf16[64,2048]{1,0:T(8,128)(2,1)} %get-tuple-element.52), channel_id=1, source_target_pairs={{0,8},{1,9},{2,10},{3,11},{4,12},{5,13},{6,14},{7,15},{8,16},{9,17... | collective-permute-start | bytes 786440 | tf_op jit(solution)/shard_map/ppermute | solution.py:481
  32.0 23.8 %collective-permute-start.5 = (bf16[64,2048]{1,0:T(8,128)(2,1)}, bf16[64,2048]{1,0:T(8,128)(2,1)S(1)}, u32[]{:S(2)}, u32[]{:S(2)}) collective-permute-start(bf16[64,2048]{1,0:T(8,128)(2,1)} %get-tuple-element.53), channel_id=1, source_target_pairs={{0,16},{1,17},{2,18},{3,19},{4,20},{5,21},{6,22},{7,23},{8,24},{9,... | collective-permute-start | bytes 786440 | tf_op jit(solution)/shard_map/ppermute | solution.py:481
  33.3 24.2 %collective-permute-start.6 = (bf16[64,2048]{1,0:T(8,128)(2,1)}, bf16[64,2048]{1,0:T(8,128)(2,1)S(1)}, u32[]{:S(2)}, u32[]{:S(2)}) collective-permute-start(bf16[64,2048]{1,0:T(8,128)(2,1)} %get-tuple-element.54), channel_id=1, source_target_pairs={{0,24},{1,25},{2,26},{3,27},{4,28},{5,29},{6,30},{7,31},{8,0},{9,1... | collective-permute-start | bytes 786440 | tf_op jit(solution)/shard_map/ppermute | solution.py:481
  60.3 21.6 %all-to-all-start = ((bf16[4,256,384]{2,1,0:T(8,128)(2,1)}), bf16[4,256,384]{2,1,0:T(8,128)(2,1)S(1)}, u32[]{:S(2)}, u32[]{:S(2)}) async-start(bf16[4,256,384]{2,1,0:T(8,128)(2,1)} %get-tuple-element.59), calls=%async_computation | async-start | bytes 1572864 | tf_op jit(solution)/shard_map/all_to_all | solution.py:451
  66.1 8.9 %collective-permute-start.12 = (bf16[4,32,4,128]{3,2,1,0:T(4,128)(2,1)S(1)}, bf16[4,32,4,128]{3,2,1,0:T(4,128)(2,1)S(1)}, u32[]{:S(2)}, u32[]{:S(2)}) collective-permute-start(bf16[4,32,4,128]{3,2,1,0:T(4,128)(2,1)S(1)} %get-tuple-element.93), channel_id=1, source_target_pairs={{0,6},{1,7},{2,0},{3,1},{4,2},{5,3},{6,4},{7,5},{8,14},{9,15},{10,... | collective-permute-start | bytes 393224 | tf_op jit(solution)/shard_map/ppermute | solution.py:530
  68.0 16.0 %collective-permute-start.11 = (bf16[4,32,4,128]{3,2,1,0:T(4,128)(2,1)S(1)}, bf16[4,32,4,128]{3,2,1,0:T(4,128)(2,1)S(1)}, u32[]{:S(2)}, u32[]{:S(2)}) collective-permute-start(bf16[4,32,4,128]{3,2,1,0:T(4,128)(2,1)S(1)} %get-tuple-element.94), channel_id=1, source_target_pairs={{0,5},{1,6},{2,7},{3,0},{4,1},{5,2},{6,3},{7,4},{8,13},{9,14},{10,... | collective-permute-start | bytes 393224 | tf_op jit(solution)/shard_map/ppermute | solution.py:530
  68.0 16.0 %collective-permute-start.10 = (bf16[4,32,4,128]{3,2,1,0:T(4,128)(2,1)S(1)}, bf16[4,32,4,128]{3,2,1,0:T(4,128)(2,1)S(1)}, u32[]{:S(2)}, u32[]{:S(2)}) collective-permute-start(bf16[4,32,4,128]{3,2,1,0:T(4,128)(2,1)S(1)} %get-tuple-element.95), channel_id=1, source_target_pairs={{0,4},{1,5},{2,6},{3,7},{4,0},{5,1},{6,2},{7,3},{8,12},{9,13},{10,... | collective-permute-start | bytes 393224 | tf_op jit(solution)/shard_map/ppermute | solution.py:530
  68.7 15.4 %collective-permute-start.9 = (bf16[4,32,4,128]{3,2,1,0:T(4,128)(2,1)S(1)}, bf16[4,32,4,128]{3,2,1,0:T(4,128)(2,1)S(1)}, u32[]{:S(2)}, u32[]{:S(2)}) collective-permute-start(bf16[4,32,4,128]{3,2,1,0:T(4,128)(2,1)S(1)} %get-tuple-element.96), channel_id=1, source_target_pairs={{0,3},{1,4},{2,5},{3,6},{4,7},{5,0},{6,1},{7,2},{8,11},{9,12},{10,... | collective-permute-start | bytes 393224 | tf_op jit(solution)/shard_map/ppermute | solution.py:530
  71.0 13.0 %collective-permute-start.8 = (bf16[4,32,4,128]{3,2,1,0:T(4,128)(2,1)S(1)}, bf16[4,32,4,128]{3,2,1,0:T(4,128)(2,1)S(1)}, u32[]{:S(2)}, u32[]{:S(2)}) collective-permute-start(bf16[4,32,4,128]{3,2,1,0:T(4,128)(2,1)S(1)} %get-tuple-element.97), channel_id=1, source_target_pairs={{0,2},{1,3},{2,4},{3,5},{4,6},{5,7},{6,0},{7,1},{8,10},{9,11},{10,... | collective-permute-start | bytes 393224 | tf_op jit(solution)/shard_map/ppermute | solution.py:530
  75.0 9.1 %collective-permute-start.7 = (bf16[4,32,4,128]{3,2,1,0:T(4,128)(2,1)S(1)}, bf16[4,32,4,128]{3,2,1,0:T(4,128)(2,1)S(1)}, u32[]{:S(2)}, u32[]{:S(2)}) collective-permute-start(bf16[4,32,4,128]{3,2,1,0:T(4,128)(2,1)S(1)} %get-tuple-element.98), channel_id=1, source_target_pairs={{0,1},{1,2},{2,3},{3,4},{4,5},{5,6},{6,7},{7,0},{8,9},{9,10},{10,1... | collective-permute-start | bytes 393224 | tf_op jit(solution)/shard_map/ppermute | solution.py:530
  84.9 31.9 %all-to-all-start.1 = ((bf16[8,96,1536]{2,1,0:T(8,128)(2,1)}), bf16[8,96,1536]{2,1,0:T(8,128)(2,1)S(1)}, u32[]{:S(2)}, u32[]{:S(2)}) async-start(bf16[8,96,1536]{2,1,0:T(8,128)(2,1)} %pick.1), calls=%async_computation.1 | async-start | bytes 4718592 | tf_op jit(solution)/shard_map/all_to_all | solution.py:451
  91.7 31.0 %collective-permute-start.14 = (bf16[8,32,4,128]{3,2,1,0:T(4,128)(2,1)}, bf16[8,32,4,128]{3,2,1,0:T(4,128)(2,1)}, u32[]{:S(2)}, u32[]{:S(2)}) collective-permute-start(bf16[8,32,4,128]{3,2,1,0:T(4,128)(2,1)} %get-tuple-element.79), channel_id=1, source_target_pairs={{0,8},{1,9},{2,10},{3,11},{4,12},{5,13},{6,14},{7,15},{8,16},{9,17... | collective-permute-start | bytes 786440 | tf_op jit(solution)/shard_map/ppermute | solution.py:588
  92.8 29.9 %collective-permute-start.15 = (bf16[8,32,4,128]{3,2,1,0:T(4,128)(2,1)}, bf16[8,32,4,128]{3,2,1,0:T(4,128)(2,1)}, u32[]{:S(2)}, u32[]{:S(2)}) collective-permute-start(bf16[8,32,4,128]{3,2,1,0:T(4,128)(2,1)} %get-tuple-element.80), channel_id=1, source_target_pairs={{0,16},{1,17},{2,18},{3,19},{4,20},{5,21},{6,22},{7,23},{8,24},{9,... | collective-permute-start | bytes 786440 | tf_op jit(solution)/shard_map/ppermute | solution.py:588
  97.0 25.7 %collective-permute-start.16 = (bf16[8,32,4,128]{3,2,1,0:T(4,128)(2,1)S(1)}, bf16[8,32,4,128]{3,2,1,0:T(4,128)(2,1)}, u32[]{:S(2)}, u32[]{:S(2)}) collective-permute-start(bf16[8,32,4,128]{3,2,1,0:T(4,128)(2,1)S(1)} %get-tuple-element.81), channel_id=1, source_target_pairs={{0,24},{1,25},{2,26},{3,27},{4,28},{5,29},{6,30},{7,31},{8,0},{9,1... | collective-permute-start | bytes 786440 | tf_op jit(solution)/shard_map/ppermute | solution.py:588
  122.7 33.0 %all-to-all-start.2 = ((bf16[8,96,1536]{2,1,0:T(8,128)(2,1)}), bf16[8,96,1536]{2,1,0:T(8,128)(2,1)S(1)}, u32[]{:S(2)}, u32[]{:S(2)}) async-start(bf16[8,96,1536]{2,1,0:T(8,128)(2,1)} %experts.1), calls=%async_computation.2 | async-start | bytes 4718592 | tf_op jit(solution)/shard_map/all_to_all | solution.py:451
  157.9 9.0 %collective-permute-start.17 = (bf16[64,1536]{1,0:T(8,128)(2,1)S(1)}, bf16[64,1536]{1,0:T(8,128)(2,1)S(1)}, u32[]{:S(2)}, u32[]{:S(2)}) collective-permute-start(bf16[64,1536]{1,0:T(8,128)(2,1)S(1)} %get-tuple-element.85), channel_id=1, source_target_pairs={{0,8},{1,9},{2,10},{3,11},{4,12},{5,13},{6,14},{7,15},{8,16},{9,17... | collective-permute-start | bytes 589832 | tf_op jit(solution)/shard_map/ppermute | solution.py:481
  158.8 17.0 %collective-permute-start.18 = (bf16[64,1536]{1,0:T(8,128)(2,1)S(1)}, bf16[64,1536]{1,0:T(8,128)(2,1)S(1)}, u32[]{:S(2)}, u32[]{:S(2)}) collective-permute-start(bf16[64,1536]{1,0:T(8,128)(2,1)S(1)} %get-tuple-element.86), channel_id=1, source_target_pairs={{0,16},{1,17},{2,18},{3,19},{4,20},{5,21},{6,22},{7,23},{8,24},{9,... | collective-permute-start | bytes 589832 | tf_op jit(solution)/shard_map/ppermute | solution.py:481
  163.0 16.7 %collective-permute-start.19 = (bf16[64,1536]{1,0:T(8,128)(2,1)S(1)}, bf16[64,1536]{1,0:T(8,128)(2,1)S(1)}, u32[]{:S(2)}, u32[]{:S(2)}) collective-permute-start(bf16[64,1536]{1,0:T(8,128)(2,1)S(1)} %get-tuple-element.87), channel_id=1, source_target_pairs={{0,24},{1,25},{2,26},{3,27},{4,28},{5,29},{6,30},{7,31},{8,0},{9,1... | collective-permute-start | bytes 589832 | tf_op jit(solution)/shard_map/ppermute | solution.py:481
  (20 other events, 132.7 us)
Sparse Core Ops, SparseCore 0:
  9.9 29.4 all-gather.3
  41.3 29.0 all-gather.5
